TPU v7x, 32 devices: a whole 2x2x4 slice. The times are simulated.
32 devices in a mesh: clips: 2 (over y), tm: 4 (over x, core), rows: 4 (over z).
Axes of the slice: x: 2, y: 2, z: 4, core: 2. Of those that a mesh axis runs over, the one named last changes fastest.
Arguments:
- features: bfloat16 [8, 8, 48, 384], P(('clips', 'tm'), 'rows'), parts along dimension 0, may hold values from -320 to 320
- first_gain: float32 [384], replicated, may hold values from 0.5 to 1.5
- first_shift: float32 [384], replicated, may hold values from -3 to 3
- first_kernel: bfloat16 [384, 3, 3, 3, 384], P('tm'), may hold values from -0.0625 to 0.0625
- first_bias: float32 [384], P('tm'), may hold values from -2 to 2
- second_gain: float32 [384], replicated, may hold values from 0.5 to 1.5
- second_shift: float32 [384], replicated, may hold values from -3 to 3
- second_kernel: bfloat16 [384, 3, 3, 3, 384], P('tm'), may hold values from -0.0625 to 0.0625
- second_bias: float32 [384], P('tm'), may hold values from -2 to 2
- third_gain: float32 [384], replicated, may hold values from 0.5 to 1.5
- third_shift: float32 [384], replicated, may hold values from -3 to 3
- query_weight: bfloat16 [384, 384], replicated, may hold values from -0.30618622 to 0.30618622
- key_weight: bfloat16 [384, 384], replicated, may hold values from -1.8371173 to 1.8371173
- value_weight: bfloat16 [384, 384], replicated, may hold values from -0.3125 to 0.3125
- output_weight: bfloat16 [384, 384], replicated, may hold values from -0.3125 to 0.3125
Outputs:
- decoded: bfloat16 [8, 8, 48, 384], P(('clips', 'tm'), 'rows'), parts along dimension 0
There are 2 independent parts, one for each index of `clips`. A program takes and returns all parts, laid end to end along the dimension named above; an argument that names none is the same for every part. Nothing has to cross between parts.
All inputs are finite; a program needn't handle non-finite values.
Results may differ from a plain program's by a relative error of at most 0.029.
Values may be sent and summed in bfloat16 or wider, within the bound.
No kernel may reach another device: no remote copies, remote signals or barrier semaphores. Data moves between devices by JAX's collectives and lax.ppermute only.
A program may use at most 64 MiB of HBM per device.

v0:
```python
import functools

import jax
import jax.numpy as jnp
from jax import lax
from jax.experimental import pallas as pl
from jax.experimental.pallas import tpu as pltpu
from jax.sharding import PartitionSpec as P

C = 384
GROUPS = 32
GROUP = C // GROUPS
EPSILON = 1e-06
VMEM = pl.BlockSpec(memory_space=pltpu.VMEM)
SMEM = pl.BlockSpec(memory_space=pltpu.SMEM)
F32 = jnp.float32
BF16 = jnp.bfloat16


def call(body, outs, scratch=()):
    def run(*args):
        return pl.pallas_call(
            body,
            out_shape=outs,
            in_specs=[SMEM if a.dtype == jnp.int32 else VMEM for a in args],
            out_specs=jax.tree.map(lambda _: VMEM, outs),
            scratch_shapes=scratch,
            compiler_params=pltpu.CompilerParams(vmem_limit_bytes=16 * 1024 * 1024),
        )(*args)

    return run


def struct(shape, dtype=BF16):
    return jax.ShapeDtypeStruct(shape, dtype)


def group_sums(rows):
    channels = rows.shape[-1]
    first = lax.broadcasted_iota(jnp.int32, (channels, channels), 0)
    second = lax.broadcasted_iota(jnp.int32, (channels, channels), 1)
    same = ((first * 43691) >> 19) == ((second * 43691) >> 19)
    terms = jnp.concatenate(split3(rows), axis=0).astype(BF16)
    sums = jnp.dot(terms, same.astype(BF16), preferred_element_type=F32)
    size = rows.shape[0]
    return sums[0:size] + sums[size : 2 * size] + sums[2 * size :]


def split3(value):
    high = value.astype(BF16).astype(F32)
    rest = value - high
    middle = rest.astype(BF16).astype(F32)
    return high, middle, (rest - middle).astype(BF16).astype(F32)


def merge(means, squares, count):
    mean = sum(means) / len(means)
    spread = sum(jnp.square(m - mean) for m in means)
    return mean, (sum(squares) + count * spread) / (count * len(means))


def merge_blocks(blocks, step, count):
    parts = [[b.astype(F32)[q * step : (q + 1) * step] for q in range(6)] for b in blocks]
    return merge([p[0] + p[1] + p[2] for p in parts], [p[3] + p[4] + p[5] for p in parts], count)


def silu(value):
    return value / (1.0 + jnp.exp(-value))


def plane_block(x, count):
    channels = x.shape[1]
    mean = group_sums(jnp.broadcast_to(jnp.sum(x, axis=0, keepdims=True), (8, channels)))[0:1] / count
    square = group_sums(
        jnp.broadcast_to(jnp.sum(jnp.square(x - mean), axis=0, keepdims=True), (8, channels))
    )[0:1]
    at = lax.broadcasted_iota(jnp.int32, (16, channels), 0)
    block = jnp.zeros((16, channels), F32)
    for i, term in enumerate(split3(mean) + split3(square)):
        block = jnp.where(at == i, term, block)
    return block.astype(BF16)


def first_stats(r_ref, x_ref, near_ref, far_ref, own_ref):
    _, rows, cols, channels = x_ref.shape
    own_ref[...] = plane_block(x_ref[0].astype(F32).reshape(rows * cols, channels), rows * cols * GROUP)
    odd = r_ref[0] & 1
    near_ref[...] = x_ref[0, (rows - 1) * (1 - odd)]
    far_ref[...] = x_ref[0, (rows - 1) * odd]


def frame_norm(r_ref, *refs):
    x_refs, (table_ref, *_, out_ref) = refs[:4], refs[4:]
    _, rows, cols, channels = x_refs[0].shape
    wide = [x_ref[0].astype(F32).reshape(rows * cols, channels) for x_ref in x_refs]
    count = len(wide) * rows * cols * GROUP
    mean = group_sums(eight(sum(jnp.sum(x, axis=0, keepdims=True) for x in wide)))[0:1] / count
    squares = sum(jnp.sum(jnp.square(x - mean), axis=0, keepdims=True) for x in wide)
    variance = group_sums(eight(squares))[0:1] / count
    scale = lax.rsqrt(variance + EPSILON) * table_ref[0:1]
    shift = table_ref[1:2]
    for k, x in enumerate(wide):
        value = silu((x - mean) * scale + shift).astype(BF16)
        out_ref[0, pl.ds((r_ref[0] ^ k) * rows, rows)] = value.reshape(rows, cols, channels)


def eight(row):
    return jnp.broadcast_to(row, (8, row.shape[1]))


def load(first_ref, second_ref, *outs):
    for w_ref, out_ref in zip((first_ref, second_ref), outs):
        outputs, lanes = w_ref.shape[2] // 3, out_ref.shape[2] // 3
        for i in range(3):
            for j in range(3):
                for k in range(3):
                    out_ref[i, j, k * lanes : k * lanes + outputs] = w_ref[i, j, k * outputs : (k + 1) * outputs]
                    if outputs < lanes:
                        fill = jnp.zeros((lanes - outputs, w_ref.shape[3]), BF16)
                        out_ref[i, j, k * lanes + outputs : (k + 1) * lanes] = fill


def first_norm(n, r_ref, x_ref, near_ref, far_ref, all_ref, table_ref, loaded_ref, out_ref):
    _, rows, cols, channels = x_ref.shape
    mean, variance = merge_blocks([all_ref[i] for i in range(n)], 1, rows * cols * GROUP)
    scale = lax.rsqrt(variance + EPSILON) * table_ref[0:1]
    shift = table_ref[1:2]
    r = r_ref[0]

    def active(v):
        return silu((v.astype(F32) - mean) * scale + shift)

    odd = r & 1
    for row in range(rows):
        out_ref[0, 1 + row] = active(x_ref[0, row]).astype(BF16)
    out_ref[0, (1 + rows) * (1 - odd)] = active(near_ref[0:cols]).astype(BF16)
    beyond = jnp.logical_or(r == 0, r == n - 1)
    out_ref[0, (1 + rows) * odd] = jnp.where(beyond, 0.0, active(far_ref[0:cols])).astype(BF16)


def add_taps(total_ref, a_ref, w_ref, lanes, first, last):
    _, padded, cols, channels = a_ref.shape
    rows = padded - 2
    plane = rows * cols
    frames = total_ref.shape[0] // plane
    for i in (2, 1, 0):
        count = min(last, frames - (2 - i)) - first
        if count <= 0:
            continue
        window = jnp.concatenate(
            [a_ref[0:count, j : j + rows].reshape(count * plane, channels) for j in range(3)], axis=1
        )
        weight = jnp.concatenate([w_ref[i, j, :, lanes] for j in range(3)], axis=1)
        start = (first + 2 - i) * plane
        total_ref[start : start + count * plane] += lax.dot_general(
            window, weight, (((1,), (1,)), ((), ())), preferred_element_type=F32
        )


def finish(total_ref, cols, bias_ref):
    positions = total_ref.shape[0]
    outputs, lanes = bias_ref.shape[0], total_ref.shape[1] // 3
    col = lax.broadcasted_iota(jnp.int32, (positions // cols, cols, outputs), 1).reshape(positions, outputs)
    left = pltpu.roll(total_ref[:, 0:outputs], 1, 0)
    right = pltpu.roll(total_ref[:, 2 * lanes : 2 * lanes + outputs], positions - 1, 0)
    result = total_ref[:, lanes : lanes + outputs]
    result = result + jnp.where(col > 0, left, 0.0) + jnp.where(col < cols - 1, right, 0.0)
    return (result + bias_ref[...].reshape(1, outputs)).astype(BF16)


def on_half(m_ref, other, body):
    half = m_ref[0] >> 1
    for h in (0, 1):
        pl.when(half == (1 - h if other else h))(functools.partial(body, h))


def hand_on(x_ref, after_ref, out_ref):
    out_ref[...] = x_ref[...]


def frame_taps(total_ref, near_total_ref, pair, w_ref, first):
    frames, plane, width = total_ref.shape
    _, padded, cols, channels = pair.shape
    windows = [
        jnp.concatenate(
            [pair[g, j : j + padded - 2].reshape(plane, channels) for j in range(3)], axis=1
        )
        for g in range(2)
    ]
    for t in range(frames):
        total = None if near_total_ref is None else near_total_ref[t]
        for g in range(2):
            i = 2 - (t - first - g)
            if not 0 <= i <= 2:
                continue
            weight = jnp.concatenate([w_ref[i, j] for j in range(3)], axis=1)
            term = lax.dot_general(
                windows[g], weight, (((1,), (1,)), ((), ())), preferred_element_type=F32
            )
            total = term if total is None else total + term
        total_ref[t] = jnp.zeros((plane, width), F32) if total is None else total


def lay_out(m_ref, own_ref, mate_ref, pair):
    odd = m_ref[0] & 1
    height = own_ref.shape[1]
    for at, ref in ((odd, own_ref), (1 - odd, mate_ref)):
        pair[at, 0] = jnp.zeros(pair.shape[2:], BF16)
        pair[at, 1 : height + 1] = ref[0]
        pair[at, height + 1] = jnp.zeros(pair.shape[2:], BF16)


def first_conv_near(m_ref, own_ref, mate_ref, w_ref, total_ref, pair):
    lay_out(m_ref, own_ref, mate_ref, pair)
    on_half(m_ref, False, lambda h: frame_taps(total_ref, None, pair, w_ref, 2 * h))


def first_conv_rest(
    r_ref, m_ref, near_total_ref, own_ref, mate_ref, w_ref, bias_ref, table_ref, out_ref, pair, total, conv1, rows8
):
    lay_out(m_ref, own_ref, mate_ref, pair)
    on_half(m_ref, True, lambda h: frame_taps(total, near_total_ref, pair, w_ref, 2 * h))
    frames, height, cols, outputs = conv1.shape
    count = height * cols * GROUP
    rows8[...] = jnp.zeros(rows8.shape, F32)
    for t in range(frames):
        result = finish(total.at[t], cols, bias_ref)
        conv1[t] = result.reshape(height, cols, outputs)
        rows8[t : t + 1] = jnp.sum(result.astype(F32), axis=0, keepdims=True)
    mean = group_sums(rows8[...]) / count
    for t in range(frames):
        wide = conv1[t].astype(F32).reshape(height * cols, outputs)
        rows8[t : t + 1] = jnp.sum(jnp.square(wide - mean[t : t + 1]), axis=0, keepdims=True)
    variance = group_sums(rows8[...]) / count
    gain, shift = (own_part(table_ref[i : i + 1], m_ref[0], outputs) for i in (2, 3))
    scale = lax.rsqrt(variance + EPSILON) * gain
    padded = out_ref.shape[1]
    rows = padded - 2
    planes = [[] for _ in range(frames)]
    for row in range(padded):
        at = r_ref[0] * rows + row - 1
        inside = jnp.logical_and(at >= 0, at < height)
        at = jnp.clip(at, 0, height - 1)
        for t in range(frames):
            value = silu((conv1[t, at].astype(F32) - mean[t : t + 1]) * scale[t : t + 1] + shift)
            planes[t].append(jnp.where(inside, value, 0.0))
    write_packed(planes, out_ref)


def first_conv(r_ref, a_ref, w_ref, bias_ref, out_ref, near_ref, far_ref, block_ref, total, rows8):
    total[...] = jnp.zeros(total.shape, F32)
    add_taps(total, a_ref, w_ref, slice(None), 0, a_ref.shape[0])
    block_ref[...] = first_finish(total, bias_ref, out_ref, rows8)
    frames, rows, cols, _ = out_ref.shape
    odd = r_ref[0] & 1
    for f in range(frames):
        near_ref[f * cols : (f + 1) * cols] = out_ref[f, (rows - 1) * (1 - odd)]
        far_ref[f * cols : (f + 1) * cols] = out_ref[f, (rows - 1) * odd]


def first_finish(total_ref, bias_ref, out_ref, rows8):
    frames, rows, cols, outputs = out_ref.shape
    plane = rows * cols
    result = finish(total_ref, cols, bias_ref)
    out_ref[...] = result.reshape(frames, rows, cols, outputs)
    wide = result.astype(F32).reshape(frames, plane, outputs)
    rows8[...] = jnp.zeros(rows8.shape, F32)
    for f in range(frames):
        rows8[f : f + 1] = jnp.sum(wide[f], axis=0, keepdims=True)
    mean = group_sums(rows8[...]) / (plane * GROUP)
    for f in range(frames):
        rows8[f : f + 1] = jnp.sum(jnp.square(wide[f] - mean[f : f + 1]), axis=0, keepdims=True)
    square = group_sums(rows8[...])
    return jnp.concatenate(split3(mean) + split3(square), axis=0).astype(BF16)


def second_norm(n, r_ref, m_ref, x_ref, near_ref, far_ref, all_ref, table_ref, out_ref):
    frames, rows, cols, channels = x_ref.shape
    gain, shift = (own_part(table_ref[i : i + 1], m_ref[0], channels) for i in (2, 3))
    step = 8 * (-(-frames // 8))
    mean, variance = merge_blocks([all_ref[i] for i in range(n)], step, rows * cols * GROUP)
    scale = lax.rsqrt(variance + EPSILON) * gain
    r = r_ref[0]
    odd = r & 1
    beyond = jnp.logical_or(r == 0, r == n - 1)
    planes = []
    for f in range(frames):

        def active(v):
            return silu((v.astype(F32) - mean[f : f + 1]) * scale[f : f + 1] + shift)

        near = active(near_ref[f * cols : (f + 1) * cols])
        far = jnp.where(beyond, 0.0, active(far_ref[f * cols : (f + 1) * cols]))
        above, below = jnp.where(odd == 1, near, far), jnp.where(odd == 1, far, near)
        planes.append([above] + [active(x_ref[f, row]) for row in range(rows)] + [below])
    write_packed(planes, out_ref)


def write_packed(planes, out_ref):
    frames, channels = len(planes), planes[0][0].shape[1]
    padded = len(planes[0])
    if packs(frames, channels):
        piece = channels // (frames - 1)
        for f in range(frames - 1):
            for row in range(padded):
                extra = planes[-1][row][:, f * piece : (f + 1) * piece]
                out_ref[f, row] = jnp.concatenate([planes[f][row], extra], axis=1).astype(BF16)
    else:
        for f in range(frames):
            for row in range(padded):
                out_ref[f, row] = planes[f][row].astype(BF16)


def packs(frames, channels):
    return channels % (frames - 1) == 0 and channels + channels // (frames - 1) == 128


def packed_shape(frames, rows, cols, channels):
    if packs(frames, channels):
        return (frames - 1, rows, cols, 128)
    return (frames, rows, cols, channels)


def own_part(row, which, size):
    result = row[:, 0:size]
    for i in range(1, row.shape[1] // size):
        result = jnp.where(which == i, row[:, i * size : (i + 1) * size], result)
    return result


def unpack(part_ref, f, row, part, frames):
    if not packs(frames, part):
        return part_ref[f, row]
    if f < frames - 1:
        return part_ref[f, row][:, 0:part]
    return jnp.concatenate([part_ref[g, row][:, part:] for g in range(frames - 1)], axis=1)


def pair_taps(h, total_ref, even_ref, odd_ref, w_ref, a_ref):
    frames, padded, cols, lanes = a_ref.shape
    channels = w_ref.shape[3]
    part = channels // 4
    fill = jnp.zeros((cols, lanes - 2 * part), BF16)
    for f in range(frames):
        for row in range(padded):
            pieces = [unpack(ref, f, row, part, frames) for ref in (even_ref, odd_ref)]
            a_ref[f, row] = jnp.concatenate([fill] + pieces if h else pieces + [fill], axis=1)
    where = slice(channels - lanes, channels) if h else slice(0, lanes)
    add_taps(total_ref, a_ref, w_ref, where, 0, frames)


def in_order(m_ref, own_ref, mate_ref, both):
    odd = m_ref[0] & 1
    both[odd] = own_ref[...]
    both[1 - odd] = mate_ref[...]
    return both.at[0], both.at[1]


def second_conv_near(m_ref, own_ref, mate_ref, w_ref, total_ref, both, a_ref):
    even, odd = in_order(m_ref, own_ref, mate_ref, both)
    total_ref[...] = jnp.zeros(total_ref.shape, F32)
    on_half(m_ref, False, lambda h: pair_taps(h, total_ref, even, odd, w_ref, a_ref))


def second_conv_rest(m_ref, near_total_ref, own_ref, mate_ref, w_ref, bias_ref, *refs):
    outs, (both, a_ref, total, held) = refs[:-4], refs[-4:]
    even, odd = in_order(m_ref, own_ref, mate_ref, both)
    total[...] = near_total_ref[...]
    on_half(m_ref, True, lambda h: pair_taps(h, total, even, odd, w_ref, a_ref))
    second_finish(m_ref, total, a_ref.shape[2], bias_ref, outs, held)


def second_conv(m_ref, parts_ref, w_ref, bias_ref, *refs):
    outs, (a_ref, total, held) = refs[:-3], refs[-3:]
    count = parts_ref.shape[0]
    frames, padded, cols, channels = a_ref.shape
    for f in range(frames):
        for row in range(padded):
            pieces = [unpack(parts_ref.at[m], f, row, channels // count, frames) for m in range(count)]
            a_ref[f, row] = jnp.concatenate(pieces, axis=1)
    total[...] = jnp.zeros(total.shape, F32)
    add_taps(total, a_ref, w_ref, slice(None), 0, frames)
    second_finish(m_ref, total, cols, bias_ref, outs, held)


def second_finish(m_ref, total_ref, cols, bias_ref, outs, held):
    held[...] = finish(total_ref, cols, bias_ref).reshape(held.shape)
    for k, out_ref in enumerate(outs):
        out_ref[...] = held[m_ref[0] ^ k]


def add_hidden(m_ref, x_ref, *refs):
    parts, (out_ref, held) = refs[:-2], refs[-2:]
    _, rows, cols, channels = x_ref.shape
    for k, part in enumerate(parts):
        held[k] = part[...].astype(F32)
    update = jnp.concatenate([held[m_ref[0] ^ m] for m in range(len(parts))], axis=1)
    out_ref[...] = (x_ref[0].reshape(rows * cols, channels).astype(F32) + update).astype(BF16)


def attention(own_ref, *refs):
    others, (table_ref, wq_ref, wk_ref, wv_ref, wo_ref, out_ref) = refs[:-6], refs[-6:]
    channels = own_ref.shape[-1]
    gain, shift = table_ref[4:5], table_ref[5:6]
    own = own_ref[...].astype(F32)
    blocks = [o[...].reshape(-1, channels).astype(F32) for o in others]
    wide = blocks[0] if len(blocks) == 1 else jnp.concatenate([own] + blocks, axis=0)
    positions = wide.shape[0]
    count = positions * GROUP
    mean = group_sums(jnp.broadcast_to(jnp.sum(wide, axis=0, keepdims=True), (8, channels)))[0:1] / count
    centered = wide - mean
    variance = (
        group_sums(jnp.broadcast_to(jnp.sum(centered * centered, axis=0, keepdims=True), (8, channels)))[0:1]
        / count
    )
    scale = lax.rsqrt(variance + EPSILON) * gain
    normed = (centered * scale + shift).astype(BF16)
    mine = ((own - mean) * scale + shift).astype(BF16)
    dot = functools.partial(jnp.dot, preferred_element_type=F32)
    queries = (dot(mine, wq_ref[...]) * C ** (-0.5)).astype(BF16)
    keys = dot(normed, wk_ref[...]).astype(BF16)
    values = dot(normed, wv_ref[...]).astype(BF16)
    scores = lax.dot_general(queries, keys, (((1,), (1,)), ((), ())), preferred_element_type=F32)
    peak = jnp.max(scores, axis=-1, keepdims=True)
    weights = jnp.exp(scores - peak)
    total = jnp.sum(weights, axis=-1, keepdims=True)
    attended = (dot(weights.astype(BF16), values) / total).astype(BF16)
    out_ref[...] = (own + dot(attended, wo_ref[...])).astype(BF16)


def swapped(value, axis, partner):
    return lax.ppermute(value, axis, [(i, partner(i)) for i in range(lax.axis_size(axis))])


def around(near, far, block):
    n = lax.axis_size("rows")
    return (
        swapped(near, "rows", lambda i: i ^ 1),
        swapped(far, "rows", lambda i: ((i + 1) ^ 1) - 1 if 0 < i < n - 1 else n - 1 - i),
        lax.all_gather(block, "rows"),
    )


def per_device(
    features,
    first_gain,
    first_shift,
    first_kernel,
    first_bias,
    second_gain,
    second_shift,
    second_kernel,
    second_bias,
    third_gain,
    third_shift,
    query_weight,
    key_weight,
    value_weight,
    output_weight,
):
    _, rows, cols, channels = features.shape
    n, frames = lax.axis_size("rows"), lax.axis_size("tm")
    outputs = first_kernel.shape[0]
    plane = rows * cols
    r = lax.axis_index("rows").astype(jnp.int32).reshape(1)
    m = lax.axis_index("tm").astype(jnp.int32).reshape(1)

    def taps(kernel):
        return jnp.transpose(kernel, (1, 2, 3, 0, 4)).reshape(3, 3, 3 * outputs, channels)

    row = lax.broadcasted_iota(jnp.int32, (8, channels), 0)
    table = jnp.zeros((8, channels), F32)
    for i, vector in enumerate([first_gain, first_shift, second_gain, second_shift, third_gain, third_shift]):
        table = jnp.where(row == i, vector[None, :], table)

    split = n == 4 and frames == 4 and channels == 4 * outputs and 2 * outputs <= 256 < channels
    lanes = 128 * (-(-outputs // 128)) if split else outputs
    loaded = struct((3, 3, 3 * lanes, channels))
    weights1, weights2 = call(load, (loaded, loaded))(taps(first_kernel), taps(second_kernel))
    step = 8 * (-(-frames // 8))
    size = 6 * step
    stats_scratch = pltpu.VMEM((step, outputs), F32)
    total = struct((frames * plane, 3 * lanes), F32)
    total_scratch = pltpu.VMEM(total.shape, F32)
    active2_struct = struct(packed_shape(frames, rows + 2, cols, outputs))
    if split:
        blocks = [features] + [swapped(features, "rows", lambda i, k=k: i ^ k) for k in (1, 2, 3)]
        blocks_across = [swapped(block, "tm", lambda i: i ^ 2) for block in blocks]
        frame = struct((1, n * rows, cols, channels))
        active1 = call(frame_norm, frame)(r, *blocks, table, weights1, *blocks_across[:3])
        mate = swapped(active1, "tm", lambda i: i ^ 1)
        pair = pltpu.VMEM((2, n * rows + 2, cols, channels), BF16)
        tall = struct((frames, n * plane, 3 * lanes), F32)
        near_total = call(first_conv_near, tall, (pair,))(m, active1, mate, weights1)
        across = call(frame_norm, frame)(r, *blocks_across, table, near_total)
        beside = swapped(across, "tm", lambda i: i ^ 1)
        active2 = call(
            first_conv_rest,
            active2_struct,
            (
                pair,
                pltpu.VMEM(tall.shape, F32),
                pltpu.VMEM((frames, n * rows, cols, outputs), BF16),
                stats_scratch,
            ),
        )(r, m, near_total, across, beside, weights1, first_bias, table)
    else:
        halo = struct((cols, channels))
        near, far, block = call(first_stats, (halo, halo, struct((16, channels))))(r, features)
        active1 = call(functools.partial(first_norm, n), struct((1, rows + 2, cols, channels)))(
            r, features, *around(near, far, block), table, weights1
        )
        clip = lax.all_gather(active1, "tm", axis=0, tiled=True)
        halo = struct((frames * cols, outputs))
        conv1, near, far, block = call(
            first_conv,
            (struct((frames, rows, cols, outputs)), halo, halo, struct((size, outputs))),
            (total_scratch, stats_scratch),
        )(r, clip, weights1, first_bias)
        active2 = call(functools.partial(second_norm, n), active2_struct)(
            r, m, conv1, *around(near, far, block), table
        )

    piece = struct((plane, outputs))
    held = pltpu.VMEM((frames, plane, outputs), BF16)
    if split:
        both = pltpu.VMEM((2, *active2.shape), BF16)
        half = pltpu.VMEM((frames, rows + 2, cols, 256), BF16)
        across = swapped(active2, "tm", lambda i: i ^ 2)
        mate = swapped(active2, "tm", lambda i: i ^ 1)
        near_total = call(second_conv_near, total, (both, half))(m, active2, mate, weights2)
        beside = swapped(call(hand_on, struct(across.shape))(across, near_total), "tm", lambda i: i ^ 1)
        pieces = call(second_conv_rest, [piece] * frames, (both, half, total_scratch, held))(
            m, near_total, across, beside, weights2, second_bias
        )
    else:
        parts = lax.all_gather(active2, "tm")
        whole = pltpu.VMEM((frames, rows + 2, cols, channels), BF16)
        pieces = call(second_conv, [piece] * frames, (whole, total_scratch, held))(m, parts, weights2, second_bias)
    pieces = [pieces[0]] + [swapped(pieces[k], "tm", lambda i, k=k: i ^ k) for k in range(1, frames)]
    hidden = call(add_hidden, struct((plane, channels)), (pltpu.VMEM((frames, plane, outputs), F32),))(
        m, features, *pieces
    )
    if n == 4:
        others = [swapped(hidden, "rows", lambda i, k=k: i ^ k) for k in (1, 2, 3)]
    else:
        others = [lax.all_gather(hidden, "rows")]
    decoded = call(attention, struct((plane, channels)))(
        hidden,
        *others,
        table,
        query_weight,
        key_weight,
        value_weight,
        output_weight,
    )
    return decoded.reshape(features.shape)


def solution(mesh):
    in_specs = (
        P(("clips", "tm"), "rows", None, None),
        P(),
        P(),
        P("tm", None, None, None, None),
        P("tm"),
        P(),
        P(),
        P("tm", None, None, None, None),
        P("tm"),
        P(),
        P(),
        P(),
        P(),
        P(),
        P(),
    )
    out_specs = P(("clips", "tm"), "rows", None, None)
    return jax.shard_map(
        per_device, mesh=mesh, in_specs=in_specs, out_specs=out_specs, check_vma=False
    )
```

profile of v0, /device:TPU:0, one launch (start us, length us, event | category | flops | bytes accessed | tf_op | source)
XLA Modules:
  0.0 59.0 jit_solution(5483853033179748500)
XLA Ops:
  0.0 2.9 %collective-permute-start.3 = (bf16[1,2,48,384]{3,2,1,0:T(8,128)(2,1)}, bf16[1,2,48,384]{3,2,1,0:T(8,128)(2,1)S(1)}, u32[]{:S(2)}, u32[]{:S(2)}) collective-permute-start(bf16[1,2,48,384]{3,2,1,0:T(8,128)(2,1)} %x_ref.1), channel_id=1, source_target_pairs={{0,8},{4,12},{8,0},{12,4},{1,9},{5,13},{9,1},{13,5},{2,10},{6,14},... | collective-permute-start | bytes 221192 | tf_op jit(solution)/shard_map/ppermute | solution.py:432
  2.9 3.6 %collective-permute-start.2 = (bf16[1,2,48,384]{3,2,1,0:T(8,128)(2,1)}, bf16[1,2,48,384]{3,2,1,0:T(8,128)(2,1)S(1)}, u32[]{:S(2)}, u32[]{:S(2)}) collective-permute-start(bf16[1,2,48,384]{3,2,1,0:T(8,128)(2,1)} %x_ref.1), channel_id=1, source_target_pairs={{0,3},{1,2},{2,1},{3,0},{4,7},{5,6},{6,5},{7,4},{8,11},{9,10},{10,... | collective-permute-start | bytes 221192 | tf_op jit(solution)/shard_map/ppermute | solution.py:432
  6.5 0.0 collective-permute-start.1
  6.5 0.8 %collective-permute-start = (bf16[1,2,48,384]{3,2,1,0:T(8,128)(2,1)}, bf16[1,2,48,384]{3,2,1,0:T(8,128)(2,1)S(1)}, u32[]{:S(2)}, u32[]{:S(2)}) collective-permute-start(bf16[1,2,48,384]{3,2,1,0:T(8,128)(2,1)} %x_ref.1), channel_id=1, source_target_pairs={{0,1},{1,0},{2,3},{3,2},{4,5},{5,4},{6,7},{7,6},{8,9},{9,8},{10,11... | collective-permute-start | bytes 221192 | tf_op jit(solution)/shard_map/ppermute | solution.py:432
  7.4 5.4 %collective-permute-done.1.refs_2_ = bf16[1,2,48,384]{3,2,1,0:T(8,128)(2,1)S(1)} collective-permute-done((bf16[1,2,48,384]{3,2,1,0:T(8,128)(2,1)}, bf16[1,2,48,384]{3,2,1,0:T(8,128)(2,1)S(1)}, u32[]{:S(2)}, u32[]{:S(2)}) %collective-permute-start.1) | collective-permute-done | bytes 73760 | tf_op jit(solution)/shard_map/ppermute | solution.py:432
  12.7 0.5 collective-permute-start.5
  13.3 0.0 collective-permute-done.refs_1_
  13.3 1.5 %collective-permute-start.4 = (bf16[1,2,48,384]{3,2,1,0:T(8,128)(2,1)S(1)}, bf16[1,2,48,384]{3,2,1,0:T(8,128)(2,1)S(1)}, u32[]{:S(2)}, u32[]{:S(2)}) collective-permute-start(bf16[1,2,48,384]{3,2,1,0:T(8,128)(2,1)S(1)} %collective-permute-done.refs_1_), channel_id=1, source_target_pairs={{0,8},{4,12},{8,0},{12,4},{1,9},{5,13},{9,1},{13,5},{2,10},{6,14},... | collective-permute-start | bytes 221192 | tf_op jit(solution)/shard_map/ppermute | solution.py:432
  14.8 0.8 %select_select_fusion.refs_4_.table_ref.refs_3_ = f32[8,384]{1,0:T(8,128)S(1)} fusion(f32[384]{0:T(512)} %param.16, f32[384]{0:T(512)} %param.17, f32[384]{0:T(512)} %param.20, f32[384]{0:T(512)} %param.21, f32[384]{0:T(512)} %param.24, f32[384]{0:T(512)} %param.25, pred[8]{0:T(512)(128)(4,1)S(1)} %get-tuple-element.17, pred[8]{0:T(512)(128)(4,1)S(1)} %get-tuple-element.18, ...), kind=kLoop, calls=%fused_computation | loop fusion | flops 18432 | bytes 21552 | tf_op jit(solution)/shard_map/jit(_where)/select_n | solution.py:474
  15.6 1.5 %copy-done.2 = bf16[96,3,3,3,384]{4,0,3,2,1:T(8,128)(2,1)S(1)} copy-done((bf16[96,3,3,3,384]{4,0,3,2,1:T(8,128)(2,1)S(1)}, bf16[96,3,3,3,384]{4,0,3,2,1:T(8,128)(2,1)}, u32[]{:S(2)}) %copy-start.2) | copy-done | bytes 1990680
  17.1 1.6 %copy-done.3 = bf16[96,3,3,3,384]{4,0,3,2,1:T(8,128)(2,1)S(1)} copy-done((bf16[96,3,3,3,384]{4,0,3,2,1:T(8,128)(2,1)S(1)}, bf16[96,3,3,3,384]{4,0,3,2,1:T(8,128)(2,1)}, u32[]{:S(2)}) %copy-start.3) | copy-done | bytes 1990680
  18.7 0.5 shard_map.145
  19.2 1.5 %copy-done = bf16[3,3,384,384]{3,2,1,0:T(8,128)(2,1)} copy-done((bf16[3,3,384,384]{3,2,1,0:T(8,128)(2,1)}, bf16[3,3,384,384]{3,2,1,0:T(8,128)(2,1)S(1)}, u32[]{:S(2)}) %copy-start) | copy-done | bytes 2654232
  20.7 0.7 %shard_map.146.own_ref = bf16[1,8,48,384]{3,2,1,0:T(8,128)(2,1)S(1)} custom-call(s32[1]{0:T(128)} %bitcast.1.r_ref, bf16[1,2,48,384]{3,2,1,0:T(8,128)(2,1)S(1)} %copy-done.4, bf16[1,2,48,384]{3,2,1,0:T(8,128)(2,1)S(1)} %collective-permute-done.refs_1_, bf16[1,2,48,384]{3,2,1,0:T(8,128)(2,1)S(1)} %collective-permute-done.1.refs_2_, ...), custom_call_target="tpu_custom_call" | custom-call | tf_op jit(solution)/shard_map/pallas_call | solution.py:22
  21.4 0.0 copy-start.9
  21.4 0.6 %copy-done.9 = bf16[1,2,48,384]{3,2,1,0:T(8,128)(2,1)} copy-done((bf16[1,2,48,384]{3,2,1,0:T(8,128)(2,1)}, bf16[1,2,48,384]{3,2,1,0:T(8,128)(2,1)S(1)}, u32[]{:S(2)}) %copy-start.9) | copy-done | bytes 73752
  22.0 0.5 collective-permute-start.7
  22.5 1.0 %collective-permute-done.6.mate_ref = bf16[1,8,48,384]{3,2,1,0:T(8,128)(2,1)S(1)} collective-permute-done((bf16[1,8,48,384]{3,2,1,0:T(8,128)(2,1)S(1)}, bf16[1,8,48,384]{3,2,1,0:T(8,128)(2,1)S(1)}, u32[]{:S(2)}, u32[]{:S(2)}) %collective-permute-start.6) | collective-permute-done | bytes 294944 | tf_op jit(solution)/shard_map/ppermute | solution.py:432
  23.6 3.2 %shard_map.147.refs_5_.near_total_ref = f32[4,384,384]{2,1,0:T(8,128)S(1)} custom-call(s32[1]{0:T(128)} %bitcast.m_ref, bf16[1,8,48,384]{3,2,1,0:T(8,128)(2,1)S(1)} %shard_map.146.own_ref, bf16[1,8,48,384]{3,2,1,0:T(8,128)(2,1)S(1)} %collective-permute-done.6.mate_ref, bf16[3,3,384,384]{3,2,1,0:T(8,128)(2,1)S(1)} %get-tuple-element.11.refs_5_.w_ref), custom_call_target="tpu_custom_call" | custom-call | tf_op jit(solution)/shard_map/pallas_call | solution.py:22
  26.8 0.0 copy-start.10
  26.8 0.2 collective-permute-done.7.refs_3_
  27.0 1.6 %shard_map.148.own_ref = bf16[1,8,48,384]{3,2,1,0:T(8,128)(2,1)S(1)} custom-call(s32[1]{0:T(128)} %bitcast.1.r_ref, bf16[1,2,48,384]{3,2,1,0:T(8,128)(2,1)S(1)} %collective-permute-done.3.refs_6_.refs_0_, bf16[1,2,48,384]{3,2,1,0:T(8,128)(2,1)S(1)} %collective-permute-done.4.refs_7_.refs_1_, ...), custom_call_target="tpu_custom_call" | custom-call | tf_op jit(solution)/shard_map/pallas_call | solution.py:22
  28.6 0.1 collective-permute-start.8
  28.7 1.6 %collective-permute-done.8.mate_ref = bf16[1,8,48,384]{3,2,1,0:T(8,128)(2,1)S(1)} collective-permute-done((bf16[1,8,48,384]{3,2,1,0:T(8,128)(2,1)S(1)}, bf16[1,8,48,384]{3,2,1,0:T(8,128)(2,1)S(1)}, u32[]{:S(2)}, u32[]{:S(2)}) %collective-permute-start.8) | collective-permute-done | bytes 294944 | tf_op jit(solution)/shard_map/ppermute | solution.py:432
  30.2 2.8 %shard_map.149.own_ref = bf16[3,4,48,128]{3,2,1,0:T(8,128)(2,1)S(1)} custom-call(s32[1]{0:T(128)} %bitcast.1.r_ref, s32[1]{0:T(128)} %bitcast.m_ref, f32[4,384,384]{2,1,0:T(8,128)S(1)} %shard_map.147.refs_5_.near_total_ref, bf16[1,8,48,384]{3,2,1,0:T(8,128)(2,1)S(1)} %shard_map.148.own_ref, bf16[1,8,48,384]{3,2,1,0:T(8,128)(2,1)S(1)} %collective-permute-done.8.mate_ref, ...), custom_call_target="tpu_custom_call" | custom-call | tf_op jit(solution)/shard_map/pallas_call | solution.py:22
  33.1 0.0 copy-start.11
  33.1 0.2 collective-permute-start.9
  33.3 2.0 %collective-permute-start.10 = (bf16[3,4,48,128]{3,2,1,0:T(8,128)(2,1)S(1)}, bf16[3,4,48,128]{3,2,1,0:T(8,128)(2,1)S(1)}, u32[]{:S(2)}, u32[]{:S(2)}) collective-permute-start(bf16[3,4,48,128]{3,2,1,0:T(8,128)(2,1)S(1)} %shard_map.149.own_ref), channel_id=1, source_target_pairs={{0,8},{4,12},{8,0},{12,4},{1,9},{5,13},{9,1},{13,5},{2,10},{6,14},... | collective-permute-start | bytes 442376 | tf_op jit(solution)/shard_map/ppermute | solution.py:432
  35.2 1.2 %shard_map.150.after_ref.near_total_ref = f32[384,384]{1,0:T(8,128)S(1)} custom-call(s32[1]{0:T(128)} %bitcast.m_ref, bf16[3,4,48,128]{3,2,1,0:T(8,128)(2,1)S(1)} %shard_map.149.own_ref, bf16[3,4,48,128]{3,2,1,0:T(8,128)(2,1)S(1)} %collective-permute-done.9.mate_ref, bf16[3,3,384,384]{3,2,1,0:T(8,128)(2,1)S(1)} %copy-done.1), custom_call_target="tpu_custom_call" | custom-call | tf_op jit(solution)/shard_map/pallas_call | solution.py:22
  36.4 0.0 copy-start.5
  36.5 0.0 copy-start.6
  36.5 0.0 copy-start.7
  36.5 0.0 copy-start.8
  36.5 3.1 %collective-permute-done.10.x_ref.own_ref = bf16[3,4,48,128]{3,2,1,0:T(8,128)(2,1)S(1)} collective-permute-done((bf16[3,4,48,128]{3,2,1,0:T(8,128)(2,1)S(1)}, bf16[3,4,48,128]{3,2,1,0:T(8,128)(2,1)S(1)}, u32[]{:S(2)}, u32[]{:S(2)}) %collective-permute-start.10) | collective-permute-done | bytes 147488 | tf_op jit(solution)/shard_map/ppermute | solution.py:432
  39.6 0.1 collective-permute-start.11
  39.7 1.4 %collective-permute-done.11.mate_ref = bf16[3,4,48,128]{3,2,1,0:T(8,128)(2,1)S(1)} collective-permute-done((bf16[3,4,48,128]{3,2,1,0:T(8,128)(2,1)S(1)}, bf16[3,4,48,128]{3,2,1,0:T(8,128)(2,1)S(1)}, u32[]{:S(2)}, u32[]{:S(2)}) %collective-permute-start.11) | collective-permute-done | bytes 147488 | tf_op jit(solution)/shard_map/ppermute | solution.py:432
  41.1 1.1 %shard_map.152 = (bf16[96,96]{1,0:T(8,128)(2,1)S(1)}, bf16[96,96]{1,0:T(8,128)(2,1)S(1)}, bf16[96,96]{1,0:T(8,128)(2,1)S(1)}, bf16[96,96]{1,0:T(8,128)(2,1)S(1)}) custom-call(s32[1]{0:T(128)} %bitcast.m_ref, f32[384,384]{1,0:T(8,128)S(1)} %shard_map.150.after_ref.near_total_ref, bf16[3,4,48,128]{3,2,1,0:T(8,128)(2,1)S(1)} %collective-permute-done.10.x_ref.own_ref, ...), custom_call_target="tpu_custom_call" | custom-call | tf_op jit(solution)/shard_map/pallas_call | solution.py:22
  42.2 0.2 collective-permute-start.12
  42.4 1.7 %collective-permute-start.13 = (bf16[96,96]{1,0:T(8,128)(2,1)S(1)}, bf16[96,96]{1,0:T(8,128)(2,1)S(1)}, u32[]{:S(2)}, u32[]{:S(2)}) collective-permute-start(bf16[96,96]{1,0:T(8,128)(2,1)S(1)} %get-tuple-element.15), channel_id=1, source_target_pairs={{0,8},{4,12},{8,0},{12,4},{1,9},{5,13},{9,1},{13,5},{2,10},{6,14},... | collective-permute-start | bytes 55304 | tf_op jit(solution)/shard_map/ppermute | solution.py:432
  44.1 0.0 collective-permute-start.14
  44.2 2.1 %collective-permute-done.13.refs_2_ = bf16[96,96]{1,0:T(8,128)(2,1)S(1)} collective-permute-done((bf16[96,96]{1,0:T(8,128)(2,1)S(1)}, bf16[96,96]{1,0:T(8,128)(2,1)S(1)}, u32[]{:S(2)}, u32[]{:S(2)}) %collective-permute-start.13) | collective-permute-done | bytes 18464 | tf_op jit(solution)/shard_map/ppermute | solution.py:432
  46.3 1.1 %collective-permute-done.14.refs_3_ = bf16[96,96]{1,0:T(8,128)(2,1)S(1)} collective-permute-done((bf16[96,96]{1,0:T(8,128)(2,1)S(1)}, bf16[96,96]{1,0:T(8,128)(2,1)S(1)}, u32[]{:S(2)}, u32[]{:S(2)}) %collective-permute-start.14) | collective-permute-done | bytes 18464 | tf_op jit(solution)/shard_map/ppermute | solution.py:432
  47.4 0.1 shard_map.153.own_ref
  47.5 2.7 %collective-permute-start.17 = (bf16[96,384]{1,0:T(8,128)(2,1)S(1)}, bf16[96,384]{1,0:T(8,128)(2,1)S(1)}, u32[]{:S(2)}, u32[]{:S(2)}) collective-permute-start(bf16[96,384]{1,0:T(8,128)(2,1)S(1)} %shard_map.153.own_ref), channel_id=1, source_target_pairs={{0,3},{1,2},{2,1},{3,0},{4,7},{5,6},{6,5},{7,4},{8,11},{9,10},{10,... | collective-permute-start | bytes 221192 | tf_op jit(solution)/shard_map/ppermute | solution.py:432
  50.2 1.8 %collective-permute-start.15 = (bf16[96,384]{1,0:T(8,128)(2,1)S(1)}, bf16[96,384]{1,0:T(8,128)(2,1)S(1)}, u32[]{:S(2)}, u32[]{:S(2)}) collective-permute-start(bf16[96,384]{1,0:T(8,128)(2,1)S(1)} %shard_map.153.own_ref), channel_id=1, source_target_pairs={{0,1},{1,0},{2,3},{3,2},{4,5},{5,4},{6,7},{7,6},{8,9},{9,8},{10,11... | collective-permute-start | bytes 221192 | tf_op jit(solution)/shard_map/ppermute | solution.py:432
  52.0 2.6 %collective-permute-done.17.refs_2_ = bf16[96,384]{1,0:T(8,128)(2,1)S(1)} collective-permute-done((bf16[96,384]{1,0:T(8,128)(2,1)S(1)}, bf16[96,384]{1,0:T(8,128)(2,1)S(1)}, u32[]{:S(2)}, u32[]{:S(2)}) %collective-permute-start.17) | collective-permute-done | bytes 73760 | tf_op jit(solution)/shard_map/ppermute | solution.py:432
  54.6 2.3 %collective-permute-done.16.refs_1_ = bf16[96,384]{1,0:T(8,128)(2,1)S(1)} collective-permute-done((bf16[96,384]{1,0:T(8,128)(2,1)S(1)}, bf16[96,384]{1,0:T(8,128)(2,1)S(1)}, u32[]{:S(2)}, u32[]{:S(2)}) %collective-permute-start.16) | collective-permute-done | bytes 73760 | tf_op jit(solution)/shard_map/ppermute | solution.py:432
  56.9 2.2 %shard_map.154 = bf16[96,384]{1,0:T(8,128)(2,1)} custom-call(bf16[96,384]{1,0:T(8,128)(2,1)S(1)} %shard_map.153.own_ref, bf16[96,384]{1,0:T(8,128)(2,1)S(1)} %collective-permute-done.15.refs_0_, bf16[96,384]{1,0:T(8,128)(2,1)S(1)} %collective-permute-done.16.refs_1_, bf16[96,384]{1,0:T(8,128)(2,1)S(1)} %collective-permute-done.17.refs_2_, ...), custom_call_target="tpu_custom_call" | custom-call | tf_op jit(solution)/shard_map/pallas_call | solution.py:22
  (26 shorter events, 0.1 us)
Async XLA Ops:
  0.0 20.7 %collective-permute-start.3 = (bf16[1,2,48,384]{3,2,1,0:T(8,128)(2,1)}, bf16[1,2,48,384]{3,2,1,0:T(8,128)(2,1)S(1)}, u32[]{:S(2)}, u32[]{:S(2)}) collective-permute-start(bf16[1,2,48,384]{3,2,1,0:T(8,128)(2,1)} %x_ref.1), channel_id=1, source_target_pairs={{0,8},{4,12},{8,0},{12,4},{1,9},{5,13},{9,1},{13,5},{2,10},{6,14},... | collective-permute-start | bytes 221192 | tf_op jit(solution)/shard_map/ppermute | solution.py:432
  2.9 17.7 %collective-permute-start.2 = (bf16[1,2,48,384]{3,2,1,0:T(8,128)(2,1)}, bf16[1,2,48,384]{3,2,1,0:T(8,128)(2,1)S(1)}, u32[]{:S(2)}, u32[]{:S(2)}) collective-permute-start(bf16[1,2,48,384]{3,2,1,0:T(8,128)(2,1)} %x_ref.1), channel_id=1, source_target_pairs={{0,3},{1,2},{2,1},{3,0},{4,7},{5,6},{6,5},{7,4},{8,11},{9,10},{10,... | collective-permute-start | bytes 221192 | tf_op jit(solution)/shard_map/ppermute | solution.py:432
  6.5 6.2 %collective-permute-start.1 = (bf16[1,2,48,384]{3,2,1,0:T(8,128)(2,1)}, bf16[1,2,48,384]{3,2,1,0:T(8,128)(2,1)S(1)}, u32[]{:S(2)}, u32[]{:S(2)}) collective-permute-start(bf16[1,2,48,384]{3,2,1,0:T(8,128)(2,1)} %x_ref.1), channel_id=1, source_target_pairs={{0,2},{1,3},{2,0},{3,1},{4,6},{5,7},{6,4},{7,5},{8,10},{9,11},{10,... | collective-permute-start | bytes 221192 | tf_op jit(solution)/shard_map/ppermute | solution.py:432
  6.5 6.7 %collective-permute-start = (bf16[1,2,48,384]{3,2,1,0:T(8,128)(2,1)}, bf16[1,2,48,384]{3,2,1,0:T(8,128)(2,1)S(1)}, u32[]{:S(2)}, u32[]{:S(2)}) collective-permute-start(bf16[1,2,48,384]{3,2,1,0:T(8,128)(2,1)} %x_ref.1), channel_id=1, source_target_pairs={{0,1},{1,0},{2,3},{3,2},{4,5},{5,4},{6,7},{7,6},{8,9},{9,8},{10,11... | collective-permute-start | bytes 221192 | tf_op jit(solution)/shard_map/ppermute | solution.py:432
  12.7 7.9 %collective-permute-start.5 = (bf16[1,2,48,384]{3,2,1,0:T(8,128)(2,1)S(1)}, bf16[1,2,48,384]{3,2,1,0:T(8,128)(2,1)S(1)}, u32[]{:S(2)}, u32[]{:S(2)}) collective-permute-start(bf16[1,2,48,384]{3,2,1,0:T(8,128)(2,1)S(1)} %collective-permute-done.1.refs_2_), channel_id=1, source_target_pairs={{0,8},{4,12},{8,0},{12,4},{1,9},{5,13},{9,1},{13,5},{2,10},{6,14},... | collective-permute-start | bytes 221192 | tf_op jit(solution)/shard_map/ppermute | solution.py:432
  13.3 7.4 %collective-permute-start.4 = (bf16[1,2,48,384]{3,2,1,0:T(8,128)(2,1)S(1)}, bf16[1,2,48,384]{3,2,1,0:T(8,128)(2,1)S(1)}, u32[]{:S(2)}, u32[]{:S(2)}) collective-permute-start(bf16[1,2,48,384]{3,2,1,0:T(8,128)(2,1)S(1)} %collective-permute-done.refs_1_), channel_id=1, source_target_pairs={{0,8},{4,12},{8,0},{12,4},{1,9},{5,13},{9,1},{13,5},{2,10},{6,14},... | collective-permute-start | bytes 221192 | tf_op jit(solution)/shard_map/ppermute | solution.py:432
  15.6 1.6 %copy-start.2 = (bf16[96,3,3,3,384]{4,0,3,2,1:T(8,128)(2,1)S(1)}, bf16[96,3,3,3,384]{4,0,3,2,1:T(8,128)(2,1)}, u32[]{:S(2)}) copy-start(bf16[96,3,3,3,384]{4,0,3,2,1:T(8,128)(2,1)} %param.18) | copy-start | bytes 5971972
  17.1 1.6 %copy-start.3 = (bf16[96,3,3,3,384]{4,0,3,2,1:T(8,128)(2,1)S(1)}, bf16[96,3,3,3,384]{4,0,3,2,1:T(8,128)(2,1)}, u32[]{:S(2)}) copy-start(bf16[96,3,3,3,384]{4,0,3,2,1:T(8,128)(2,1)} %param.22) | copy-start | bytes 5971972
  18.7 2.0 %copy-start.4 = (bf16[1,2,48,384]{3,2,1,0:T(8,128)(2,1)S(1)}, bf16[1,2,48,384]{3,2,1,0:T(8,128)(2,1)}, u32[]{:S(2)}) copy-start(bf16[1,2,48,384]{3,2,1,0:T(8,128)(2,1)} %x_ref.1) | copy-start | bytes 221188
  19.2 1.5 %copy-start = (bf16[3,3,384,384]{3,2,1,0:T(8,128)(2,1)}, bf16[3,3,384,384]{3,2,1,0:T(8,128)(2,1)S(1)}, u32[]{:S(2)}) copy-start(bf16[3,3,384,384]{3,2,1,0:T(8,128)(2,1)S(1)} %get-tuple-element.12.w_ref) | copy-start | bytes 7962628
  21.4 0.6 %copy-start.9 = (bf16[1,2,48,384]{3,2,1,0:T(8,128)(2,1)}, bf16[1,2,48,384]{3,2,1,0:T(8,128)(2,1)S(1)}, u32[]{:S(2)}) copy-start(bf16[1,2,48,384]{3,2,1,0:T(8,128)(2,1)S(1)} %collective-permute-done.2.refs_3_) | copy-start | bytes 221188
  22.0 1.6 %collective-permute-start.6 = (bf16[1,8,48,384]{3,2,1,0:T(8,128)(2,1)S(1)}, bf16[1,8,48,384]{3,2,1,0:T(8,128)(2,1)S(1)}, u32[]{:S(2)}, u32[]{:S(2)}) collective-permute-start(bf16[1,8,48,384]{3,2,1,0:T(8,128)(2,1)S(1)} %shard_map.146.own_ref), channel_id=1, source_target_pairs={{0,4},{4,0},{8,12},{12,8},{1,5},{5,1},{9,13},{13,9},{2,6},{6,2},{1... | collective-permute-start | bytes 884744 | tf_op jit(solution)/shard_map/ppermute | solution.py:432
  22.0 5.0 %collective-permute-start.7 = (bf16[1,2,48,384]{3,2,1,0:T(8,128)(2,1)}, bf16[1,2,48,384]{3,2,1,0:T(8,128)(2,1)}, u32[]{:S(2)}, u32[]{:S(2)}) collective-permute-start(bf16[1,2,48,384]{3,2,1,0:T(8,128)(2,1)} %copy-done.9), channel_id=1, source_target_pairs={{0,8},{4,12},{8,0},{12,4},{1,9},{5,13},{9,1},{13,5},{2,10},{6,14},... | collective-permute-start | bytes 221192 | tf_op jit(solution)/shard_map/ppermute | solution.py:432
  26.8 3.4 %copy-start.10 = (f32[96]{0:T(128)S(1)}, f32[96]{0:T(128)}, u32[]{:S(2)}) copy-start(f32[96]{0:T(128)} %bias_ref.2) | copy-start | bytes 1156
  28.6 6.7 %copy-start.1 = (bf16[3,3,384,384]{3,2,1,0:T(8,128)(2,1)S(1)}, bf16[3,3,384,384]{3,2,1,0:T(8,128)(2,1)}, u32[]{:S(2)}) copy-start(bf16[3,3,384,384]{3,2,1,0:T(8,128)(2,1)} %copy-done) | copy-start | bytes 7962628
  28.6 1.6 %collective-permute-start.8 = (bf16[1,8,48,384]{3,2,1,0:T(8,128)(2,1)S(1)}, bf16[1,8,48,384]{3,2,1,0:T(8,128)(2,1)S(1)}, u32[]{:S(2)}, u32[]{:S(2)}) collective-permute-start(bf16[1,8,48,384]{3,2,1,0:T(8,128)(2,1)S(1)} %shard_map.148.own_ref), channel_id=1, source_target_pairs={{0,4},{4,0},{8,12},{12,8},{1,5},{5,1},{9,13},{13,9},{2,6},{6,2},{1... | collective-permute-start | bytes 884744 | tf_op jit(solution)/shard_map/ppermute | solution.py:432
  33.1 8.0 %copy-start.11 = (f32[96]{0:T(128)S(1)}, f32[96]{0:T(128)}, u32[]{:S(2)}) copy-start(f32[96]{0:T(128)} %bias_ref.3) | copy-start | bytes 1156
  33.1 2.2 %collective-permute-start.9 = (bf16[3,4,48,128]{3,2,1,0:T(8,128)(2,1)S(1)}, bf16[3,4,48,128]{3,2,1,0:T(8,128)(2,1)S(1)}, u32[]{:S(2)}, u32[]{:S(2)}) collective-permute-start(bf16[3,4,48,128]{3,2,1,0:T(8,128)(2,1)S(1)} %shard_map.149.own_ref), channel_id=1, source_target_pairs={{0,4},{4,0},{8,12},{12,8},{1,5},{5,1},{9,13},{13,9},{2,6},{6,2},{1... | collective-permute-start | bytes 442376 | tf_op jit(solution)/shard_map/ppermute | solution.py:432
  33.3 6.3 %collective-permute-start.10 = (bf16[3,4,48,128]{3,2,1,0:T(8,128)(2,1)S(1)}, bf16[3,4,48,128]{3,2,1,0:T(8,128)(2,1)S(1)}, u32[]{:S(2)}, u32[]{:S(2)}) collective-permute-start(bf16[3,4,48,128]{3,2,1,0:T(8,128)(2,1)S(1)} %shard_map.149.own_ref), channel_id=1, source_target_pairs={{0,8},{4,12},{8,0},{12,4},{1,9},{5,13},{9,1},{13,5},{2,10},{6,14},... | collective-permute-start | bytes 442376 | tf_op jit(solution)/shard_map/ppermute | solution.py:432
  36.4 20.4 %copy-start.5 = (bf16[384,384]{1,0:T(8,128)(2,1)S(1)}, bf16[384,384]{1,0:T(8,128)(2,1)}, u32[]{:S(2)}) copy-start(bf16[384,384]{1,0:T(8,128)(2,1)} %refs_4_.1) | copy-start | bytes 884740
  36.5 20.4 %copy-start.6 = (bf16[384,384]{1,0:T(8,128)(2,1)S(1)}, bf16[384,384]{1,0:T(8,128)(2,1)}, u32[]{:S(2)}) copy-start(bf16[384,384]{1,0:T(8,128)(2,1)} %refs_5_.1) | copy-start | bytes 884740
  36.5 20.4 %copy-start.7 = (bf16[384,384]{1,0:T(8,128)(2,1)S(1)}, bf16[384,384]{1,0:T(8,128)(2,1)}, u32[]{:S(2)}) copy-start(bf16[384,384]{1,0:T(8,128)(2,1)} %refs_6_.1) | copy-start | bytes 884740
  36.5 20.4 %copy-start.8 = (bf16[384,384]{1,0:T(8,128)(2,1)S(1)}, bf16[384,384]{1,0:T(8,128)(2,1)}, u32[]{:S(2)}) copy-start(bf16[384,384]{1,0:T(8,128)(2,1)} %refs_7_.1) | copy-start | bytes 884740
  39.6 1.4 %collective-permute-start.11 = (bf16[3,4,48,128]{3,2,1,0:T(8,128)(2,1)S(1)}, bf16[3,4,48,128]{3,2,1,0:T(8,128)(2,1)S(1)}, u32[]{:S(2)}, u32[]{:S(2)}) collective-permute-start(bf16[3,4,48,128]{3,2,1,0:T(8,128)(2,1)S(1)} %shard_map.151), channel_id=1, source_target_pairs={{0,4},{4,0},{8,12},{12,8},{1,5},{5,1},{9,13},{13,9},{2,6},{6,2},{1... | collective-permute-start | bytes 442376 | tf_op jit(solution)/shard_map/ppermute | solution.py:432
  42.2 1.9 %collective-permute-start.12 = (bf16[96,96]{1,0:T(8,128)(2,1)S(1)}, bf16[96,96]{1,0:T(8,128)(2,1)S(1)}, u32[]{:S(2)}, u32[]{:S(2)}) collective-permute-start(bf16[96,96]{1,0:T(8,128)(2,1)S(1)} %get-tuple-element.14), channel_id=1, source_target_pairs={{0,4},{4,0},{8,12},{12,8},{1,5},{5,1},{9,13},{13,9},{2,6},{6,2},{1... | collective-permute-start | bytes 55304 | tf_op jit(solution)/shard_map/ppermute | solution.py:432
  42.4 3.8 %collective-permute-start.13 = (bf16[96,96]{1,0:T(8,128)(2,1)S(1)}, bf16[96,96]{1,0:T(8,128)(2,1)S(1)}, u32[]{:S(2)}, u32[]{:S(2)}) collective-permute-start(bf16[96,96]{1,0:T(8,128)(2,1)S(1)} %get-tuple-element.15), channel_id=1, source_target_pairs={{0,8},{4,12},{8,0},{12,4},{1,9},{5,13},{9,1},{13,5},{2,10},{6,14},... | collective-permute-start | bytes 55304 | tf_op jit(solution)/shard_map/ppermute | solution.py:432
  44.1 3.3 %collective-permute-start.14 = (bf16[96,96]{1,0:T(8,128)(2,1)S(1)}, bf16[96,96]{1,0:T(8,128)(2,1)S(1)}, u32[]{:S(2)}, u32[]{:S(2)}) collective-permute-start(bf16[96,96]{1,0:T(8,128)(2,1)S(1)} %get-tuple-element.16), channel_id=1, source_target_pairs={{0,12},{4,8},{8,4},{12,0},{1,13},{5,9},{9,5},{13,1},{2,14},{6,10},... | collective-permute-start | bytes 55304 | tf_op jit(solution)/shard_map/ppermute | solution.py:432
  47.5 7.0 %collective-permute-start.17 = (bf16[96,384]{1,0:T(8,128)(2,1)S(1)}, bf16[96,384]{1,0:T(8,128)(2,1)S(1)}, u32[]{:S(2)}, u32[]{:S(2)}) collective-permute-start(bf16[96,384]{1,0:T(8,128)(2,1)S(1)} %shard_map.153.own_ref), channel_id=1, source_target_pairs={{0,3},{1,2},{2,1},{3,0},{4,7},{5,6},{6,5},{7,4},{8,11},{9,10},{10,... | collective-permute-start | bytes 221192 | tf_op jit(solution)/shard_map/ppermute | solution.py:432
  50.2 6.6 %collective-permute-start.16 = (bf16[96,384]{1,0:T(8,128)(2,1)S(1)}, bf16[96,384]{1,0:T(8,128)(2,1)S(1)}, u32[]{:S(2)}, u32[]{:S(2)}) collective-permute-start(bf16[96,384]{1,0:T(8,128)(2,1)S(1)} %shard_map.153.own_ref), channel_id=1, source_target_pairs={{0,2},{1,3},{2,0},{3,1},{4,6},{5,7},{6,4},{7,5},{8,10},{9,11},{10,... | collective-permute-start | bytes 221192 | tf_op jit(solution)/shard_map/ppermute | solution.py:432
  50.2 6.6 %collective-permute-start.15 = (bf16[96,384]{1,0:T(8,128)(2,1)S(1)}, bf16[96,384]{1,0:T(8,128)(2,1)S(1)}, u32[]{:S(2)}, u32[]{:S(2)}) collective-permute-start(bf16[96,384]{1,0:T(8,128)(2,1)S(1)} %shard_map.153.own_ref), channel_id=1, source_target_pairs={{0,1},{1,0},{2,3},{3,2},{4,5},{5,4},{6,7},{7,6},{8,9},{9,8},{10,11... | collective-permute-start | bytes 221192 | tf_op jit(solution)/shard_map/ppermute | solution.py:432
where the time goes:
time: 59.3 us; the launch traced here: 59 us
  waiting for transfers between devices  20.8 us (35%)
  starting transfers between devices  18.6 us (31%)
  Pallas kernels  13.3 us (22%)
  local copies, waits for them, and re-layouts  5.26 us (9%)
  other arithmetic  0.86 us (1%)
    ppermute x18, waiting for transfers between devices, swapped(): lax.ppermute(value, axis, [(i, partner(i)) for i in range(lax.axis_size(a...  20.8 us
    ppermute x18, starting transfers between devices, swapped(): lax.ppermute(value, axis, [(i, partner(i)) for i in range(lax.axis_size(a...  18.6 us
    pallas_call x10, Pallas kernels, run(): pl.pallas_call(body, out_shape=outs, in_specs=[SMEM if a.dtype == jnp.int...  13.3 us
    unnamed x24, local copies, waits for them, and re-layouts  5.26 us
  transfers between devices with their start and end apart: 18, of which 10 were waited for; matrix products, arithmetic and copies ran while one was open for 1% of the time, Pallas kernels for 8%

commit v1 on v0

--- a/solution.py
+++ b/solution.py
@@ -108,16 +108,16 @@
     return jnp.broadcast_to(row, (8, row.shape[1]))
 
 
-def load(first_ref, second_ref, *outs):
-    for w_ref, out_ref in zip((first_ref, second_ref), outs):
-        outputs, lanes = w_ref.shape[2] // 3, out_ref.shape[2] // 3
-        for i in range(3):
-            for j in range(3):
-                for k in range(3):
-                    out_ref[i, j, k * lanes : k * lanes + outputs] = w_ref[i, j, k * outputs : (k + 1) * outputs]
-                    if outputs < lanes:
-                        fill = jnp.zeros((lanes - outputs, w_ref.shape[3]), BF16)
-                        out_ref[i, j, k * lanes + outputs : (k + 1) * lanes] = fill
+def load(w_ref, *refs):
+    out_ref = refs[-1]
+    outputs, lanes = w_ref.shape[2] // 3, out_ref.shape[2] // 3
+    for i in range(3):
+        for j in range(3):
+            for k in range(3):
+                out_ref[i, j, k * lanes : k * lanes + outputs] = w_ref[i, j, k * outputs : (k + 1) * outputs]
+                if outputs < lanes:
+                    fill = jnp.zeros((lanes - outputs, w_ref.shape[3]), BF16)
+                    out_ref[i, j, k * lanes + outputs : (k + 1) * lanes] = fill
 
 
 def first_norm(n, r_ref, x_ref, near_ref, far_ref, all_ref, table_ref, loaded_ref, out_ref):
@@ -476,7 +476,7 @@
     split = n == 4 and frames == 4 and channels == 4 * outputs and 2 * outputs <= 256 < channels
     lanes = 128 * (-(-outputs // 128)) if split else outputs
     loaded = struct((3, 3, 3 * lanes, channels))
-    weights1, weights2 = call(load, (loaded, loaded))(taps(first_kernel), taps(second_kernel))
+    weights1 = call(load, loaded)(taps(first_kernel))
     step = 8 * (-(-frames // 8))
     size = 6 * step
     stats_scratch = pltpu.VMEM((step, outputs), F32)
@@ -484,10 +484,14 @@
     total_scratch = pltpu.VMEM(total.shape, F32)
     active2_struct = struct(packed_shape(frames, rows + 2, cols, outputs))
     if split:
-        blocks = [features] + [swapped(features, "rows", lambda i, k=k: i ^ k) for k in (1, 2, 3)]
-        blocks_across = [swapped(block, "tm", lambda i: i ^ 2) for block in blocks]
+        held_back = call(hand_on, struct(features.shape))(features, table)
+        blocks = [held_back] + [
+            swapped(held_back if k == 3 else features, "rows", lambda i, k=k: i ^ k) for k in (1, 2, 3)
+        ]
+        sent = [held_back, call(hand_on, struct(features.shape))(blocks[1], weights1), *blocks[2:]]
+        blocks_across = [swapped(block, "tm", lambda i: i ^ 2) for block in sent]
         frame = struct((1, n * rows, cols, channels))
-        active1 = call(frame_norm, frame)(r, *blocks, table, weights1, *blocks_across[:3])
+        active1 = call(frame_norm, frame)(r, *blocks, table, weights1, *blocks_across[:2])
         mate = swapped(active1, "tm", lambda i: i ^ 1)
         pair = pltpu.VMEM((2, n * rows + 2, cols, channels), BF16)
         tall = struct((frames, n * plane, 3 * lanes), F32)
@@ -521,6 +525,7 @@
             r, m, conv1, *around(near, far, block), table
         )
 
+    weights2 = call(load, loaded)(taps(second_kernel), active2)
     piece = struct((plane, outputs))
     held = pltpu.VMEM((frames, plane, outputs), BF16)
     if split:

time: 59.3 us -> 56.5 us (0.953)
  local copies, waits for them, and re-layouts: 5.26 us -> 1.6 us
  Pallas kernels: 13.3 us -> 15.2 us
  waiting for transfers between devices: 20.8 us -> 19.8 us
    unnamed x24 -> x16, local copies, waits for them, and re-layouts: 5.26 us -> 1.6 us
    pallas_call x10 -> x13, Pallas kernels: 13.3 us -> 15.2 us  [run(): pl.pallas_call(body, out_shape=outs, in_specs=[SMEM if a.dtype == jnp.int...]
    ppermute x18, waiting for transfers between devices: 20.8 us -> 19.8 us  [swapped(): lax.ppermute(value, axis, [(i, partner(i)) for i in range(lax.axis_size(a...]
  transfers between devices with their start and end apart: 18 -> 18, of which waited for: 10 -> 10; matrix products, arithmetic and copies ran while one was open for 1% -> 2% of each run, Pallas kernels for 8% -> 10%
where the time goes in v1:
time: 56.5 us; the launch traced here: 56.2 us
  waiting for transfers between devices  19.8 us (35%)
  starting transfers between devices  18.5 us (33%)
  Pallas kernels  15.2 us (27%)
  local copies, waits for them, and re-layouts  1.6 us (3%)
  other arithmetic  0.86 us (2%)
    ppermute x18, waiting for transfers between devices, swapped(): lax.ppermute(value, axis, [(i, partner(i)) for i in range(lax.axis_size(a...  19.8 us
    ppermute x18, starting transfers between devices, swapped(): lax.ppermute(value, axis, [(i, partner(i)) for i in range(lax.axis_size(a...  18.5 us
    pallas_call x13, Pallas kernels, run(): pl.pallas_call(body, out_shape=outs, in_specs=[SMEM if a.dtype == jnp.int...  15.2 us
    unnamed x16, local copies, waits for them, and re-layouts  1.6 us
  transfers between devices with their start and end apart: 18, of which 10 were waited for; matrix products, arithmetic and copies ran while one was open for 2% of the time, Pallas kernels for 10%

profile of v1, /device:TPU:0, one launch (start us, length us, event | category | flops | bytes accessed | tf_op | source)
XLA Modules:
  0.0 56.2 jit_solution(11760998759051132710)
XLA Ops:
  0.0 3.0 %collective-permute-start = (bf16[1,2,48,384]{3,2,1,0:T(8,128)(2,1)}, bf16[1,2,48,384]{3,2,1,0:T(8,128)(2,1)S(1)}, u32[]{:S(2)}, u32[]{:S(2)}) collective-permute-start(bf16[1,2,48,384]{3,2,1,0:T(8,128)(2,1)} %x_ref.3), channel_id=1, source_target_pairs={{0,1},{1,0},{2,3},{3,2},{4,5},{5,4},{6,7},{7,6},{8,9},{9,8},{10,11... | collective-permute-start | bytes 221192 | tf_op jit(solution)/shard_map/ppermute | solution.py:432
  3.0 0.8 %select_select_fusion.after_ref.refs_4_.table_ref.refs_3_ = f32[8,384]{1,0:T(8,128)S(1)} fusion(f32[384]{0:T(512)} %param.16, f32[384]{0:T(512)} %param.17, f32[384]{0:T(512)} %param.20, f32[384]{0:T(512)} %param.21, f32[384]{0:T(512)} %param.24, f32[384]{0:T(512)} %param.25, pred[8]{0:T(512)(128)(4,1)S(1)} %get-tuple-element.13, ...), kind=kLoop, calls=%fused_computation | loop fusion | flops 18432 | bytes 21552 | tf_op jit(solution)/shard_map/jit(_where)/select_n | solution.py:474
  3.9 0.9 %shard_map.145.refs_0_ = bf16[1,2,48,384]{3,2,1,0:T(8,128)(2,1)S(1)} custom-call(bf16[1,2,48,384]{3,2,1,0:T(8,128)(2,1)} %x_ref.3, f32[8,384]{1,0:T(8,128)S(1)} %select_select_fusion.after_ref.refs_4_.table_ref.refs_3_), custom_call_target="tpu_custom_call" | custom-call | tf_op jit(solution)/shard_map/pallas_call | solution.py:22
  4.8 1.5 %collective-permute-start.3 = (bf16[1,2,48,384]{3,2,1,0:T(8,128)(2,1)S(1)}, bf16[1,2,48,384]{3,2,1,0:T(8,128)(2,1)S(1)}, u32[]{:S(2)}, u32[]{:S(2)}) collective-permute-start(bf16[1,2,48,384]{3,2,1,0:T(8,128)(2,1)S(1)} %shard_map.145.refs_0_), channel_id=1, source_target_pairs={{0,8},{4,12},{8,0},{12,4},{1,9},{5,13},{9,1},{13,5},{2,10},{6,14},... | collective-permute-start | bytes 221192 | tf_op jit(solution)/shard_map/ppermute | solution.py:432
  6.3 2.5 %collective-permute-start.2 = (bf16[1,2,48,384]{3,2,1,0:T(8,128)(2,1)S(1)}, bf16[1,2,48,384]{3,2,1,0:T(8,128)(2,1)S(1)}, u32[]{:S(2)}, u32[]{:S(2)}) collective-permute-start(bf16[1,2,48,384]{3,2,1,0:T(8,128)(2,1)S(1)} %shard_map.145.refs_0_), channel_id=1, source_target_pairs={{0,3},{1,2},{2,1},{3,0},{4,7},{5,6},{6,5},{7,4},{8,11},{9,10},{10,... | collective-permute-start | bytes 221192 | tf_op jit(solution)/shard_map/ppermute | solution.py:432
  8.8 0.1 collective-permute-start.1
  8.9 1.6 %copy-done = bf16[96,3,3,3,384]{4,0,3,2,1:T(8,128)(2,1)S(1)} copy-done((bf16[96,3,3,3,384]{4,0,3,2,1:T(8,128)(2,1)S(1)}, bf16[96,3,3,3,384]{4,0,3,2,1:T(8,128)(2,1)}, u32[]{:S(2)}) %copy-start) | copy-done | bytes 1990680
  10.4 0.2 shard_map.146.after_ref.refs_5_.w_ref
  10.7 0.6 %collective-permute-start.4 = (bf16[1,2,48,384]{3,2,1,0:T(8,128)(2,1)S(1)}, bf16[1,2,48,384]{3,2,1,0:T(8,128)(2,1)S(1)}, u32[]{:S(2)}, u32[]{:S(2)}) collective-permute-start(bf16[1,2,48,384]{3,2,1,0:T(8,128)(2,1)S(1)} %shard_map.147), channel_id=1, source_target_pairs={{0,8},{4,12},{8,0},{12,4},{1,9},{5,13},{9,1},{13,5},{2,10},{6,14},... | collective-permute-start | bytes 221192 | tf_op jit(solution)/shard_map/ppermute | solution.py:432
  11.3 2.0 %collective-permute-done.2.refs_3_ = bf16[1,2,48,384]{3,2,1,0:T(8,128)(2,1)S(1)} collective-permute-done((bf16[1,2,48,384]{3,2,1,0:T(8,128)(2,1)S(1)}, bf16[1,2,48,384]{3,2,1,0:T(8,128)(2,1)S(1)}, u32[]{:S(2)}, u32[]{:S(2)}) %collective-permute-start.2) | collective-permute-done | bytes 73760 | tf_op jit(solution)/shard_map/ppermute | solution.py:432
  13.2 2.2 %collective-permute-done.1.refs_2_ = bf16[1,2,48,384]{3,2,1,0:T(8,128)(2,1)S(1)} collective-permute-done((bf16[1,2,48,384]{3,2,1,0:T(8,128)(2,1)}, bf16[1,2,48,384]{3,2,1,0:T(8,128)(2,1)S(1)}, u32[]{:S(2)}, u32[]{:S(2)}) %collective-permute-start.1) | collective-permute-done | bytes 73760 | tf_op jit(solution)/shard_map/ppermute | solution.py:432
  15.5 0.7 %shard_map.148.own_ref = bf16[1,8,48,384]{3,2,1,0:T(8,128)(2,1)S(1)} custom-call(s32[1]{0:T(128)} %bitcast.1.r_ref, bf16[1,2,48,384]{3,2,1,0:T(8,128)(2,1)S(1)} %shard_map.145.refs_0_, bf16[1,2,48,384]{3,2,1,0:T(8,128)(2,1)S(1)} %collective-permute-done.x_ref.refs_1_, bf16[1,2,48,384]{3,2,1,0:T(8,128)(2,1)S(1)} %collective-permute-done.1.refs_2_, ...), custom_call_target="tpu_custom_call" | custom-call | tf_op jit(solution)/shard_map/pallas_call | solution.py:22
  16.2 0.1 collective-permute-start.5
  16.2 0.6 %collective-permute-start.7 = (bf16[1,2,48,384]{3,2,1,0:T(8,128)(2,1)S(1)}, bf16[1,2,48,384]{3,2,1,0:T(8,128)(2,1)}, u32[]{:S(2)}, u32[]{:S(2)}) collective-permute-start(bf16[1,2,48,384]{3,2,1,0:T(8,128)(2,1)S(1)} %collective-permute-done.2.refs_3_), channel_id=1, source_target_pairs={{0,8},{4,12},{8,0},{12,4},{1,9},{5,13},{9,1},{13,5},{2,10},{6,14},... | collective-permute-start | bytes 221192 | tf_op jit(solution)/shard_map/ppermute | solution.py:432
  16.8 1.5 %collective-permute-start.6 = (bf16[1,2,48,384]{3,2,1,0:T(8,128)(2,1)S(1)}, bf16[1,2,48,384]{3,2,1,0:T(8,128)(2,1)}, u32[]{:S(2)}, u32[]{:S(2)}) collective-permute-start(bf16[1,2,48,384]{3,2,1,0:T(8,128)(2,1)S(1)} %collective-permute-done.1.refs_2_), channel_id=1, source_target_pairs={{0,8},{4,12},{8,0},{12,4},{1,9},{5,13},{9,1},{13,5},{2,10},{6,14},... | collective-permute-start | bytes 221192 | tf_op jit(solution)/shard_map/ppermute | solution.py:432
  18.3 3.2 %shard_map.149.refs_5_.near_total_ref = f32[4,384,384]{2,1,0:T(8,128)S(1)} custom-call(s32[1]{0:T(128)} %bitcast.m_ref, bf16[1,8,48,384]{3,2,1,0:T(8,128)(2,1)S(1)} %shard_map.148.own_ref, bf16[1,8,48,384]{3,2,1,0:T(8,128)(2,1)S(1)} %collective-permute-done.5.mate_ref, bf16[3,3,384,384]{3,2,1,0:T(8,128)(2,1)S(1)} %shard_map.146.after_ref.refs_5_.w_ref), custom_call_target="tpu_custom_call" | custom-call | tf_op jit(solution)/shard_map/pallas_call | solution.py:22
  21.5 0.0 copy-start.6
  21.5 1.1 %collective-permute-done.6.refs_2_ = bf16[1,2,48,384]{3,2,1,0:T(8,128)(2,1)} collective-permute-done((bf16[1,2,48,384]{3,2,1,0:T(8,128)(2,1)S(1)}, bf16[1,2,48,384]{3,2,1,0:T(8,128)(2,1)}, u32[]{:S(2)}, u32[]{:S(2)}) %collective-permute-start.6) | collective-permute-done | bytes 73760 | tf_op jit(solution)/shard_map/ppermute | solution.py:432
  22.6 1.6 %shard_map.150.own_ref = bf16[1,8,48,384]{3,2,1,0:T(8,128)(2,1)S(1)} custom-call(s32[1]{0:T(128)} %bitcast.1.r_ref, bf16[1,2,48,384]{3,2,1,0:T(8,128)(2,1)S(1)} %collective-permute-done.3.refs_6_.refs_0_, bf16[1,2,48,384]{3,2,1,0:T(8,128)(2,1)S(1)} %collective-permute-done.4.refs_7_.refs_1_, bf16[1,2,48,384]{3,2,1,0:T(8,128)(2,1)} %collective-permute-done.6.refs_2_, ...), custom_call_target="tpu_custom_call" | custom-call | tf_op jit(solution)/shard_map/pallas_call | solution.py:22
  24.2 0.0 copy-start.1
  24.2 0.1 collective-permute-start.8
  24.3 1.6 %collective-permute-done.8.mate_ref = bf16[1,8,48,384]{3,2,1,0:T(8,128)(2,1)S(1)} collective-permute-done((bf16[1,8,48,384]{3,2,1,0:T(8,128)(2,1)S(1)}, bf16[1,8,48,384]{3,2,1,0:T(8,128)(2,1)S(1)}, u32[]{:S(2)}, u32[]{:S(2)}) %collective-permute-start.8) | collective-permute-done | bytes 294944 | tf_op jit(solution)/shard_map/ppermute | solution.py:432
  25.9 2.8 %shard_map.151.refs_0_.own_ref = bf16[3,4,48,128]{3,2,1,0:T(8,128)(2,1)S(1)} custom-call(s32[1]{0:T(128)} %bitcast.1.r_ref, s32[1]{0:T(128)} %bitcast.m_ref, f32[4,384,384]{2,1,0:T(8,128)S(1)} %shard_map.149.refs_5_.near_total_ref, bf16[1,8,48,384]{3,2,1,0:T(8,128)(2,1)S(1)} %shard_map.150.own_ref, ...), custom_call_target="tpu_custom_call" | custom-call | tf_op jit(solution)/shard_map/pallas_call | solution.py:22
  28.7 0.2 collective-permute-start.9
  28.9 1.9 %collective-permute-start.10 = (bf16[3,4,48,128]{3,2,1,0:T(8,128)(2,1)S(1)}, bf16[3,4,48,128]{3,2,1,0:T(8,128)(2,1)S(1)}, u32[]{:S(2)}, u32[]{:S(2)}) collective-permute-start(bf16[3,4,48,128]{3,2,1,0:T(8,128)(2,1)S(1)} %shard_map.151.refs_0_.own_ref), channel_id=1, source_target_pairs={{0,8},{4,12},{8,0},{12,4},{1,9},{5,13},{9,1},{13,5},{2,10},{6,14},... | collective-permute-start | bytes 442376 | tf_op jit(solution)/shard_map/ppermute | solution.py:432
  30.8 0.2 shard_map.152.w_ref
  31.1 0.0 copy-start.7
  31.1 1.2 %shard_map.153.after_ref.near_total_ref = f32[384,384]{1,0:T(8,128)S(1)} custom-call(s32[1]{0:T(128)} %bitcast.m_ref, bf16[3,4,48,128]{3,2,1,0:T(8,128)(2,1)S(1)} %shard_map.151.refs_0_.own_ref, bf16[3,4,48,128]{3,2,1,0:T(8,128)(2,1)S(1)} %collective-permute-done.9.mate_ref, bf16[3,3,384,384]{3,2,1,0:T(8,128)(2,1)S(1)} %shard_map.152.w_ref), custom_call_target="tpu_custom_call" | custom-call | tf_op jit(solution)/shard_map/pallas_call | solution.py:22
  32.3 0.0 copy-start.2
  32.3 0.0 copy-start.3
  32.3 0.0 copy-start.4
  32.3 0.0 copy-start.5
  32.4 2.8 %collective-permute-done.10.x_ref.own_ref = bf16[3,4,48,128]{3,2,1,0:T(8,128)(2,1)S(1)} collective-permute-done((bf16[3,4,48,128]{3,2,1,0:T(8,128)(2,1)S(1)}, bf16[3,4,48,128]{3,2,1,0:T(8,128)(2,1)S(1)}, u32[]{:S(2)}, u32[]{:S(2)}) %collective-permute-start.10) | collective-permute-done | bytes 147488 | tf_op jit(solution)/shard_map/ppermute | solution.py:432
  35.2 0.1 collective-permute-start.11
  35.3 1.4 %collective-permute-done.11.mate_ref = bf16[3,4,48,128]{3,2,1,0:T(8,128)(2,1)S(1)} collective-permute-done((bf16[3,4,48,128]{3,2,1,0:T(8,128)(2,1)S(1)}, bf16[3,4,48,128]{3,2,1,0:T(8,128)(2,1)S(1)}, u32[]{:S(2)}, u32[]{:S(2)}) %collective-permute-start.11) | collective-permute-done | bytes 147488 | tf_op jit(solution)/shard_map/ppermute | solution.py:432
  36.7 1.2 %shard_map.155 = (bf16[96,96]{1,0:T(8,128)(2,1)S(1)}, bf16[96,96]{1,0:T(8,128)(2,1)S(1)}, bf16[96,96]{1,0:T(8,128)(2,1)S(1)}, bf16[96,96]{1,0:T(8,128)(2,1)S(1)}) custom-call(s32[1]{0:T(128)} %bitcast.m_ref, f32[384,384]{1,0:T(8,128)S(1)} %shard_map.153.after_ref.near_total_ref, bf16[3,4,48,128]{3,2,1,0:T(8,128)(2,1)S(1)} %collective-permute-done.10.x_ref.own_ref, ...), custom_call_target="tpu_custom_call" | custom-call | tf_op jit(solution)/shard_map/pallas_call | solution.py:22
  37.8 0.2 collective-permute-start.12
  38.0 1.7 %collective-permute-start.13 = (bf16[96,96]{1,0:T(8,128)(2,1)S(1)}, bf16[96,96]{1,0:T(8,128)(2,1)S(1)}, u32[]{:S(2)}, u32[]{:S(2)}) collective-permute-start(bf16[96,96]{1,0:T(8,128)(2,1)S(1)} %get-tuple-element.11), channel_id=1, source_target_pairs={{0,8},{4,12},{8,0},{12,4},{1,9},{5,13},{9,1},{13,5},{2,10},{6,14},... | collective-permute-start | bytes 55304 | tf_op jit(solution)/shard_map/ppermute | solution.py:432
  39.7 0.0 collective-permute-start.14
  39.8 2.1 %collective-permute-done.13.refs_2_ = bf16[96,96]{1,0:T(8,128)(2,1)S(1)} collective-permute-done((bf16[96,96]{1,0:T(8,128)(2,1)S(1)}, bf16[96,96]{1,0:T(8,128)(2,1)S(1)}, u32[]{:S(2)}, u32[]{:S(2)}) %collective-permute-start.13) | collective-permute-done | bytes 18464 | tf_op jit(solution)/shard_map/ppermute | solution.py:432
  41.9 1.1 %collective-permute-done.14.refs_3_ = bf16[96,96]{1,0:T(8,128)(2,1)S(1)} collective-permute-done((bf16[96,96]{1,0:T(8,128)(2,1)S(1)}, bf16[96,96]{1,0:T(8,128)(2,1)S(1)}, u32[]{:S(2)}, u32[]{:S(2)}) %collective-permute-start.14) | collective-permute-done | bytes 18464 | tf_op jit(solution)/shard_map/ppermute | solution.py:432
  43.0 1.0 %shard_map.156.own_ref = bf16[96,384]{1,0:T(8,128)(2,1)S(1)} custom-call(s32[1]{0:T(128)} %bitcast.m_ref, bf16[1,2,48,384]{3,2,1,0:T(8,128)(2,1)} %x_ref.3, bf16[96,96]{1,0:T(8,128)(2,1)S(1)} %get-tuple-element.9.refs_0_, bf16[96,96]{1,0:T(8,128)(2,1)S(1)} %collective-permute-done.12.refs_1_, bf16[96,96]{1,0:T(8,128)(2,1)S(1)} %collective-permute-done.13.refs_2_, ...), custom_call_target="tpu_custom_call" | custom-call | tf_op jit(solution)/shard_map/pallas_call | solution.py:22
  44.0 2.6 %collective-permute-start.17 = (bf16[96,384]{1,0:T(8,128)(2,1)S(1)}, bf16[96,384]{1,0:T(8,128)(2,1)S(1)}, u32[]{:S(2)}, u32[]{:S(2)}) collective-permute-start(bf16[96,384]{1,0:T(8,128)(2,1)S(1)} %shard_map.156.own_ref), channel_id=1, source_target_pairs={{0,3},{1,2},{2,1},{3,0},{4,7},{5,6},{6,5},{7,4},{8,11},{9,10},{10,... | collective-permute-start | bytes 221192 | tf_op jit(solution)/shard_map/ppermute | solution.py:432
  46.6 0.3 collective-permute-start.16
  47.0 1.5 %collective-permute-start.15 = (bf16[96,384]{1,0:T(8,128)(2,1)S(1)}, bf16[96,384]{1,0:T(8,128)(2,1)S(1)}, u32[]{:S(2)}, u32[]{:S(2)}) collective-permute-start(bf16[96,384]{1,0:T(8,128)(2,1)S(1)} %shard_map.156.own_ref), channel_id=1, source_target_pairs={{0,1},{1,0},{2,3},{3,2},{4,5},{5,4},{6,7},{7,6},{8,9},{9,8},{10,11... | collective-permute-start | bytes 221192 | tf_op jit(solution)/shard_map/ppermute | solution.py:432
  48.5 2.3 %collective-permute-done.17.refs_2_ = bf16[96,384]{1,0:T(8,128)(2,1)S(1)} collective-permute-done((bf16[96,384]{1,0:T(8,128)(2,1)S(1)}, bf16[96,384]{1,0:T(8,128)(2,1)S(1)}, u32[]{:S(2)}, u32[]{:S(2)}) %collective-permute-start.17) | collective-permute-done | bytes 73760 | tf_op jit(solution)/shard_map/ppermute | solution.py:432
  50.8 3.3 %collective-permute-done.16.refs_1_ = bf16[96,384]{1,0:T(8,128)(2,1)S(1)} collective-permute-done((bf16[96,384]{1,0:T(8,128)(2,1)S(1)}, bf16[96,384]{1,0:T(8,128)(2,1)S(1)}, u32[]{:S(2)}, u32[]{:S(2)}) %collective-permute-start.16) | collective-permute-done | bytes 73760 | tf_op jit(solution)/shard_map/ppermute | solution.py:432
  54.1 2.2 %shard_map.157 = bf16[96,384]{1,0:T(8,128)(2,1)} custom-call(bf16[96,384]{1,0:T(8,128)(2,1)S(1)} %shard_map.156.own_ref, bf16[96,384]{1,0:T(8,128)(2,1)S(1)} %collective-permute-done.15.refs_0_, bf16[96,384]{1,0:T(8,128)(2,1)S(1)} %collective-permute-done.16.refs_1_, bf16[96,384]{1,0:T(8,128)(2,1)S(1)} %collective-permute-done.17.refs_2_, ...), custom_call_target="tpu_custom_call" | custom-call | tf_op jit(solution)/shard_map/pallas_call | solution.py:22
  (21 shorter events, 0.1 us)
Async XLA Ops:
  0.0 10.7 %collective-permute-start = (bf16[1,2,48,384]{3,2,1,0:T(8,128)(2,1)}, bf16[1,2,48,384]{3,2,1,0:T(8,128)(2,1)S(1)}, u32[]{:S(2)}, u32[]{:S(2)}) collective-permute-start(bf16[1,2,48,384]{3,2,1,0:T(8,128)(2,1)} %x_ref.3), channel_id=1, source_target_pairs={{0,1},{1,0},{2,3},{3,2},{4,5},{5,4},{6,7},{7,6},{8,9},{9,8},{10,11... | collective-permute-start | bytes 221192 | tf_op jit(solution)/shard_map/ppermute | solution.py:432
  4.8 6.5 %collective-permute-start.3 = (bf16[1,2,48,384]{3,2,1,0:T(8,128)(2,1)S(1)}, bf16[1,2,48,384]{3,2,1,0:T(8,128)(2,1)S(1)}, u32[]{:S(2)}, u32[]{:S(2)}) collective-permute-start(bf16[1,2,48,384]{3,2,1,0:T(8,128)(2,1)S(1)} %shard_map.145.refs_0_), channel_id=1, source_target_pairs={{0,8},{4,12},{8,0},{12,4},{1,9},{5,13},{9,1},{13,5},{2,10},{6,14},... | collective-permute-start | bytes 221192 | tf_op jit(solution)/shard_map/ppermute | solution.py:432
  6.3 7.0 %collective-permute-start.2 = (bf16[1,2,48,384]{3,2,1,0:T(8,128)(2,1)S(1)}, bf16[1,2,48,384]{3,2,1,0:T(8,128)(2,1)S(1)}, u32[]{:S(2)}, u32[]{:S(2)}) collective-permute-start(bf16[1,2,48,384]{3,2,1,0:T(8,128)(2,1)S(1)} %shard_map.145.refs_0_), channel_id=1, source_target_pairs={{0,3},{1,2},{2,1},{3,0},{4,7},{5,6},{6,5},{7,4},{8,11},{9,10},{10,... | collective-permute-start | bytes 221192 | tf_op jit(solution)/shard_map/ppermute | solution.py:432
  8.8 6.7 %collective-permute-start.1 = (bf16[1,2,48,384]{3,2,1,0:T(8,128)(2,1)}, bf16[1,2,48,384]{3,2,1,0:T(8,128)(2,1)S(1)}, u32[]{:S(2)}, u32[]{:S(2)}) collective-permute-start(bf16[1,2,48,384]{3,2,1,0:T(8,128)(2,1)} %x_ref.3), channel_id=1, source_target_pairs={{0,2},{1,3},{2,0},{3,1},{4,6},{5,7},{6,4},{7,5},{8,10},{9,11},{10,... | collective-permute-start | bytes 221192 | tf_op jit(solution)/shard_map/ppermute | solution.py:432
  8.9 1.6 %copy-start = (bf16[96,3,3,3,384]{4,0,3,2,1:T(8,128)(2,1)S(1)}, bf16[96,3,3,3,384]{4,0,3,2,1:T(8,128)(2,1)}, u32[]{:S(2)}) copy-start(bf16[96,3,3,3,384]{4,0,3,2,1:T(8,128)(2,1)} %param.18) | copy-start | bytes 5971972
  10.7 4.8 %collective-permute-start.4 = (bf16[1,2,48,384]{3,2,1,0:T(8,128)(2,1)S(1)}, bf16[1,2,48,384]{3,2,1,0:T(8,128)(2,1)S(1)}, u32[]{:S(2)}, u32[]{:S(2)}) collective-permute-start(bf16[1,2,48,384]{3,2,1,0:T(8,128)(2,1)S(1)} %shard_map.147), channel_id=1, source_target_pairs={{0,8},{4,12},{8,0},{12,4},{1,9},{5,13},{9,1},{13,5},{2,10},{6,14},... | collective-permute-start | bytes 221192 | tf_op jit(solution)/shard_map/ppermute | solution.py:432
  16.2 2.2 %collective-permute-start.5 = (bf16[1,8,48,384]{3,2,1,0:T(8,128)(2,1)S(1)}, bf16[1,8,48,384]{3,2,1,0:T(8,128)(2,1)S(1)}, u32[]{:S(2)}, u32[]{:S(2)}) collective-permute-start(bf16[1,8,48,384]{3,2,1,0:T(8,128)(2,1)S(1)} %shard_map.148.own_ref), channel_id=1, source_target_pairs={{0,4},{4,0},{8,12},{12,8},{1,5},{5,1},{9,13},{13,9},{2,6},{6,2},{1... | collective-permute-start | bytes 884744 | tf_op jit(solution)/shard_map/ppermute | solution.py:432
  16.2 5.3 %collective-permute-start.7 = (bf16[1,2,48,384]{3,2,1,0:T(8,128)(2,1)S(1)}, bf16[1,2,48,384]{3,2,1,0:T(8,128)(2,1)}, u32[]{:S(2)}, u32[]{:S(2)}) collective-permute-start(bf16[1,2,48,384]{3,2,1,0:T(8,128)(2,1)S(1)} %collective-permute-done.2.refs_3_), channel_id=1, source_target_pairs={{0,8},{4,12},{8,0},{12,4},{1,9},{5,13},{9,1},{13,5},{2,10},{6,14},... | collective-permute-start | bytes 221192 | tf_op jit(solution)/shard_map/ppermute | solution.py:432
  16.8 5.8 %collective-permute-start.6 = (bf16[1,2,48,384]{3,2,1,0:T(8,128)(2,1)S(1)}, bf16[1,2,48,384]{3,2,1,0:T(8,128)(2,1)}, u32[]{:S(2)}, u32[]{:S(2)}) collective-permute-start(bf16[1,2,48,384]{3,2,1,0:T(8,128)(2,1)S(1)} %collective-permute-done.1.refs_2_), channel_id=1, source_target_pairs={{0,8},{4,12},{8,0},{12,4},{1,9},{5,13},{9,1},{13,5},{2,10},{6,14},... | collective-permute-start | bytes 221192 | tf_op jit(solution)/shard_map/ppermute | solution.py:432
  21.5 4.4 %copy-start.6 = (f32[96]{0:T(128)S(1)}, f32[96]{0:T(128)}, u32[]{:S(2)}) copy-start(f32[96]{0:T(128)} %bias_ref.2) | copy-start | bytes 1156
  24.2 6.6 %copy-start.1 = (bf16[96,3,3,3,384]{4,0,3,2,1:T(8,128)(2,1)S(1)}, bf16[96,3,3,3,384]{4,0,3,2,1:T(8,128)(2,1)}, u32[]{:S(2)}) copy-start(bf16[96,3,3,3,384]{4,0,3,2,1:T(8,128)(2,1)} %param.22) | copy-start | bytes 5971972
  24.2 1.6 %collective-permute-start.8 = (bf16[1,8,48,384]{3,2,1,0:T(8,128)(2,1)S(1)}, bf16[1,8,48,384]{3,2,1,0:T(8,128)(2,1)S(1)}, u32[]{:S(2)}, u32[]{:S(2)}) collective-permute-start(bf16[1,8,48,384]{3,2,1,0:T(8,128)(2,1)S(1)} %shard_map.150.own_ref), channel_id=1, source_target_pairs={{0,4},{4,0},{8,12},{12,8},{1,5},{5,1},{9,13},{13,9},{2,6},{6,2},{1... | collective-permute-start | bytes 884744 | tf_op jit(solution)/shard_map/ppermute | solution.py:432
  28.7 2.4 %collective-permute-start.9 = (bf16[3,4,48,128]{3,2,1,0:T(8,128)(2,1)S(1)}, bf16[3,4,48,128]{3,2,1,0:T(8,128)(2,1)S(1)}, u32[]{:S(2)}, u32[]{:S(2)}) collective-permute-start(bf16[3,4,48,128]{3,2,1,0:T(8,128)(2,1)S(1)} %shard_map.151.refs_0_.own_ref), channel_id=1, source_target_pairs={{0,4},{4,0},{8,12},{12,8},{1,5},{5,1},{9,13},{13,9},{2,6},{6,2},{1... | collective-permute-start | bytes 442376 | tf_op jit(solution)/shard_map/ppermute | solution.py:432
  28.9 6.3 %collective-permute-start.10 = (bf16[3,4,48,128]{3,2,1,0:T(8,128)(2,1)S(1)}, bf16[3,4,48,128]{3,2,1,0:T(8,128)(2,1)S(1)}, u32[]{:S(2)}, u32[]{:S(2)}) collective-permute-start(bf16[3,4,48,128]{3,2,1,0:T(8,128)(2,1)S(1)} %shard_map.151.refs_0_.own_ref), channel_id=1, source_target_pairs={{0,8},{4,12},{8,0},{12,4},{1,9},{5,13},{9,1},{13,5},{2,10},{6,14},... | collective-permute-start | bytes 442376 | tf_op jit(solution)/shard_map/ppermute | solution.py:432
  31.1 5.6 %copy-start.7 = (f32[96]{0:T(128)S(1)}, f32[96]{0:T(128)}, u32[]{:S(2)}) copy-start(f32[96]{0:T(128)} %bias_ref.3) | copy-start | bytes 1156
  32.3 21.7 %copy-start.2 = (bf16[384,384]{1,0:T(8,128)(2,1)S(1)}, bf16[384,384]{1,0:T(8,128)(2,1)}, u32[]{:S(2)}) copy-start(bf16[384,384]{1,0:T(8,128)(2,1)} %refs_4_.1) | copy-start | bytes 884740
  32.3 21.7 %copy-start.3 = (bf16[384,384]{1,0:T(8,128)(2,1)S(1)}, bf16[384,384]{1,0:T(8,128)(2,1)}, u32[]{:S(2)}) copy-start(bf16[384,384]{1,0:T(8,128)(2,1)} %refs_5_.1) | copy-start | bytes 884740
  32.3 21.7 %copy-start.4 = (bf16[384,384]{1,0:T(8,128)(2,1)S(1)}, bf16[384,384]{1,0:T(8,128)(2,1)}, u32[]{:S(2)}) copy-start(bf16[384,384]{1,0:T(8,128)(2,1)} %refs_6_.1) | copy-start | bytes 884740
  32.3 21.7 %copy-start.5 = (bf16[384,384]{1,0:T(8,128)(2,1)S(1)}, bf16[384,384]{1,0:T(8,128)(2,1)}, u32[]{:S(2)}) copy-start(bf16[384,384]{1,0:T(8,128)(2,1)} %refs_7_.1) | copy-start | bytes 884740
  35.2 1.4 %collective-permute-start.11 = (bf16[3,4,48,128]{3,2,1,0:T(8,128)(2,1)S(1)}, bf16[3,4,48,128]{3,2,1,0:T(8,128)(2,1)S(1)}, u32[]{:S(2)}, u32[]{:S(2)}) collective-permute-start(bf16[3,4,48,128]{3,2,1,0:T(8,128)(2,1)S(1)} %shard_map.154), channel_id=1, source_target_pairs={{0,4},{4,0},{8,12},{12,8},{1,5},{5,1},{9,13},{13,9},{2,6},{6,2},{1... | collective-permute-start | bytes 442376 | tf_op jit(solution)/shard_map/ppermute | solution.py:432
  37.8 1.9 %collective-permute-start.12 = (bf16[96,96]{1,0:T(8,128)(2,1)S(1)}, bf16[96,96]{1,0:T(8,128)(2,1)S(1)}, u32[]{:S(2)}, u32[]{:S(2)}) collective-permute-start(bf16[96,96]{1,0:T(8,128)(2,1)S(1)} %get-tuple-element.10), channel_id=1, source_target_pairs={{0,4},{4,0},{8,12},{12,8},{1,5},{5,1},{9,13},{13,9},{2,6},{6,2},{1... | collective-permute-start | bytes 55304 | tf_op jit(solution)/shard_map/ppermute | solution.py:432
  38.0 3.8 %collective-permute-start.13 = (bf16[96,96]{1,0:T(8,128)(2,1)S(1)}, bf16[96,96]{1,0:T(8,128)(2,1)S(1)}, u32[]{:S(2)}, u32[]{:S(2)}) collective-permute-start(bf16[96,96]{1,0:T(8,128)(2,1)S(1)} %get-tuple-element.11), channel_id=1, source_target_pairs={{0,8},{4,12},{8,0},{12,4},{1,9},{5,13},{9,1},{13,5},{2,10},{6,14},... | collective-permute-start | bytes 55304 | tf_op jit(solution)/shard_map/ppermute | solution.py:432
  39.7 3.3 %collective-permute-start.14 = (bf16[96,96]{1,0:T(8,128)(2,1)S(1)}, bf16[96,96]{1,0:T(8,128)(2,1)S(1)}, u32[]{:S(2)}, u32[]{:S(2)}) collective-permute-start(bf16[96,96]{1,0:T(8,128)(2,1)S(1)} %get-tuple-element.12), channel_id=1, source_target_pairs={{0,12},{4,8},{8,4},{12,0},{1,13},{5,9},{9,5},{13,1},{2,14},{6,10},... | collective-permute-start | bytes 55304 | tf_op jit(solution)/shard_map/ppermute | solution.py:432
  44.0 6.7 %collective-permute-start.17 = (bf16[96,384]{1,0:T(8,128)(2,1)S(1)}, bf16[96,384]{1,0:T(8,128)(2,1)S(1)}, u32[]{:S(2)}, u32[]{:S(2)}) collective-permute-start(bf16[96,384]{1,0:T(8,128)(2,1)S(1)} %shard_map.156.own_ref), channel_id=1, source_target_pairs={{0,3},{1,2},{2,1},{3,0},{4,7},{5,6},{6,5},{7,4},{8,11},{9,10},{10,... | collective-permute-start | bytes 221192 | tf_op jit(solution)/shard_map/ppermute | solution.py:432
  46.6 7.4 %collective-permute-start.16 = (bf16[96,384]{1,0:T(8,128)(2,1)S(1)}, bf16[96,384]{1,0:T(8,128)(2,1)S(1)}, u32[]{:S(2)}, u32[]{:S(2)}) collective-permute-start(bf16[96,384]{1,0:T(8,128)(2,1)S(1)} %shard_map.156.own_ref), channel_id=1, source_target_pairs={{0,2},{1,3},{2,0},{3,1},{4,6},{5,7},{6,4},{7,5},{8,10},{9,11},{10,... | collective-permute-start | bytes 221192 | tf_op jit(solution)/shard_map/ppermute | solution.py:432
  47.0 7.1 %collective-permute-start.15 = (bf16[96,384]{1,0:T(8,128)(2,1)S(1)}, bf16[96,384]{1,0:T(8,128)(2,1)S(1)}, u32[]{:S(2)}, u32[]{:S(2)}) collective-permute-start(bf16[96,384]{1,0:T(8,128)(2,1)S(1)} %shard_map.156.own_ref), channel_id=1, source_target_pairs={{0,1},{1,0},{2,3},{3,2},{4,5},{5,4},{6,7},{7,6},{8,9},{9,8},{10,11... | collective-permute-start | bytes 221192 | tf_op jit(solution)/shard_map/ppermute | solution.py:432

commit v2 on v1

--- a/solution.py
+++ b/solution.py
@@ -89,10 +89,9 @@
     far_ref[...] = x_ref[0, (rows - 1) * odd]
 
 
-def frame_norm(r_ref, *refs):
-    x_refs, (table_ref, *_, out_ref) = refs[:4], refs[4:]
-    _, rows, cols, channels = x_refs[0].shape
-    wide = [x_ref[0].astype(F32).reshape(rows * cols, channels) for x_ref in x_refs]
+def frame_norm(r_ref, blocks, table_ref, out_ref):
+    rows, cols, channels = blocks[0].shape
+    wide = [block.astype(F32).reshape(rows * cols, channels) for block in blocks]
     count = len(wide) * rows * cols * GROUP
     mean = group_sums(eight(sum(jnp.sum(x, axis=0, keepdims=True) for x in wide)))[0:1] / count
     squares = sum(jnp.sum(jnp.square(x - mean), axis=0, keepdims=True) for x in wide)
@@ -102,6 +101,22 @@
     for k, x in enumerate(wide):
         value = silu((x - mean) * scale + shift).astype(BF16)
         out_ref[0, pl.ds((r_ref[0] ^ k) * rows, rows)] = value.reshape(rows, cols, channels)
+
+
+def own_frame(
+    r_ref, own_ref, one_ref, two_ref, three_ref, across_ref, across_one_ref, table_ref, after_ref, out_ref, raw_ref, held_ref
+):
+    blocks = [ref[0] for ref in (own_ref, one_ref, two_ref, three_ref)]
+    rows = blocks[0].shape[0]
+    for k, block in enumerate(blocks):
+        raw_ref[pl.ds((r_ref[0] ^ k) * rows, rows)] = block
+    held_ref[0] = across_ref[0]
+    held_ref[1] = across_one_ref[0]
+    frame_norm(r_ref, blocks, table_ref, out_ref)
+
+
+def across_frame(r_ref, held_ref, two_ref, three_ref, table_ref, after_ref, out_ref):
+    frame_norm(r_ref, [held_ref[0], held_ref[1], two_ref[0], three_ref[0]], table_ref, out_ref)
 
 
 def eight(row):
@@ -178,27 +193,26 @@
     out_ref[...] = x_ref[...]
 
 
-def frame_taps(total_ref, near_total_ref, pair, w_ref, first):
-    frames, plane, width = total_ref.shape
-    _, padded, cols, channels = pair.shape
-    windows = [
-        jnp.concatenate(
-            [pair[g, j : j + padded - 2].reshape(plane, channels) for j in range(3)], axis=1
-        )
-        for g in range(2)
-    ]
+def frame_taps(total_ref, base_ref, a_ref, held, w_ref, lanes=slice(None)):
+    frames, plane, _ = total_ref.shape
+    _, padded, cols, channels = a_ref.shape
+    written = []
     for t in range(frames):
-        total = None if near_total_ref is None else near_total_ref[t]
-        for g in range(2):
-            i = 2 - (t - first - g)
-            if not 0 <= i <= 2:
-                continue
-            weight = jnp.concatenate([w_ref[i, j] for j in range(3)], axis=1)
-            term = lax.dot_general(
-                windows[g], weight, (((1,), (1,)), ((), ())), preferred_element_type=F32
+        total = None if base_ref is None else base_ref[t]
+        terms = [(g, 2 - (t - f)) for g, f in enumerate(held) if 0 <= t - f <= 2]
+        for g, i in terms:
+            window = jnp.concatenate(
+                [a_ref[g, j : j + padded - 2].reshape(plane, channels) for j in range(3)], axis=1
             )
+            weight = jnp.concatenate([w_ref[i, j, :, lanes] for j in range(3)], axis=1)
+            term = lax.dot_general(window, weight, (((1,), (1,)), ((), ())), preferred_element_type=F32)
             total = term if total is None else total + term
-        total_ref[t] = jnp.zeros((plane, width), F32) if total is None else total
+        if terms:
+            total_ref[t] = total
+            written.append(t)
+        elif base_ref is None:
+            total_ref[t] = jnp.zeros(total_ref.shape[1:], F32)
+    return written
 
 
 def lay_out(m_ref, own_ref, mate_ref, pair):
@@ -212,14 +226,21 @@
 
 def first_conv_near(m_ref, own_ref, mate_ref, w_ref, total_ref, pair):
     lay_out(m_ref, own_ref, mate_ref, pair)
-    on_half(m_ref, False, lambda h: frame_taps(total_ref, None, pair, w_ref, 2 * h))
+    on_half(m_ref, False, lambda h: frame_taps(total_ref, None, pair, (2 * h, 2 * h + 1), w_ref) and None)
 
 
 def first_conv_rest(
-    r_ref, m_ref, near_total_ref, own_ref, mate_ref, w_ref, bias_ref, table_ref, out_ref, pair, total, conv1, rows8
+    m_ref, near_total_ref, own_ref, mate_ref, w_ref, bias_ref, table_ref, out_ref, early_ref, late_ref, pair, total, conv1, rows8
 ):
     lay_out(m_ref, own_ref, mate_ref, pair)
-    on_half(m_ref, True, lambda h: frame_taps(total, near_total_ref, pair, w_ref, 2 * h))
+
+    def other(h):
+        written = frame_taps(total, near_total_ref, pair, (2 * h, 2 * h + 1), w_ref)
+        for t in range(total.shape[0]):
+            if t not in written:
+                total[t] = near_total_ref[t]
+
+    on_half(m_ref, True, other)
     frames, height, cols, outputs = conv1.shape
     count = height * cols * GROUP
     rows8[...] = jnp.zeros(rows8.shape, F32)
@@ -234,17 +255,13 @@
     variance = group_sums(rows8[...]) / count
     gain, shift = (own_part(table_ref[i : i + 1], m_ref[0], outputs) for i in (2, 3))
     scale = lax.rsqrt(variance + EPSILON) * gain
-    padded = out_ref.shape[1]
-    rows = padded - 2
-    planes = [[] for _ in range(frames)]
-    for row in range(padded):
-        at = r_ref[0] * rows + row - 1
-        inside = jnp.logical_and(at >= 0, at < height)
-        at = jnp.clip(at, 0, height - 1)
-        for t in range(frames):
-            value = silu((conv1[t, at].astype(F32) - mean[t : t + 1]) * scale[t : t + 1] + shift)
-            planes[t].append(jnp.where(inside, value, 0.0))
+    planes = []
+    for t in range(frames):
+        rows = [conv1[t, row].astype(F32) - mean[t : t + 1] for row in range(height)]
+        planes.append([silu(row * scale[t : t + 1] + shift) for row in rows])
     write_packed(planes, out_ref)
+    early_ref[...] = out_ref[0:2]
+    late_ref[...] = out_ref[2:]
 
 
 def first_conv(r_ref, a_ref, w_ref, bias_ref, out_ref, near_ref, far_ref, block_ref, total, rows8):
@@ -336,38 +353,82 @@
     return jnp.concatenate([part_ref[g, row][:, part:] for g in range(frames - 1)], axis=1)
 
 
-def pair_taps(h, total_ref, even_ref, odd_ref, w_ref, a_ref):
-    frames, padded, cols, lanes = a_ref.shape
-    channels = w_ref.shape[3]
-    part = channels // 4
-    fill = jnp.zeros((cols, lanes - 2 * part), BF16)
-    for f in range(frames):
-        for row in range(padded):
-            pieces = [unpack(ref, f, row, part, frames) for ref in (even_ref, odd_ref)]
-            a_ref[f, row] = jnp.concatenate([fill] + pieces if h else pieces + [fill], axis=1)
-    where = slice(channels - lanes, channels) if h else slice(0, lanes)
-    add_taps(total_ref, a_ref, w_ref, where, 0, frames)
-
-
-def in_order(m_ref, own_ref, mate_ref, both):
+def half_channels(h, parts, held, a_ref):
+    _, padded, cols, lanes = a_ref.shape
+    for g, f in enumerate(held):
+        a_ref[g, 0] = jnp.zeros((cols, lanes), BF16)
+        a_ref[g, padded - 1] = jnp.zeros((cols, lanes), BF16)
+        for row in range(padded - 2):
+            pieces = []
+            for planes in parts:
+                if f < len(planes):
+                    pieces.append(planes[f][row][:, 0:96])
+                else:
+                    pieces += [plane[row][:, 96:] for plane in planes]
+            fill = jnp.zeros((cols, lanes - 192), BF16)
+            a_ref[g, row + 1] = jnp.concatenate([fill] + pieces if h else pieces + [fill], axis=1)
+
+
+def half_lanes(h, lanes, channels):
+    return slice(channels - lanes, channels) if h else slice(0, lanes)
+
+
+def second_conv_near(m_ref, own_ref, mate_ref, w_ref, total_ref, both, a_ref):
     odd = m_ref[0] & 1
     both[odd] = own_ref[...]
     both[1 - odd] = mate_ref[...]
-    return both.at[0], both.at[1]
-
-
-def second_conv_near(m_ref, own_ref, mate_ref, w_ref, total_ref, both, a_ref):
-    even, odd = in_order(m_ref, own_ref, mate_ref, both)
-    total_ref[...] = jnp.zeros(total_ref.shape, F32)
-    on_half(m_ref, False, lambda h: pair_taps(h, total_ref, even, odd, w_ref, a_ref))
-
-
-def second_conv_rest(m_ref, near_total_ref, own_ref, mate_ref, w_ref, bias_ref, *refs):
-    outs, (both, a_ref, total, held) = refs[:-4], refs[-4:]
-    even, odd = in_order(m_ref, own_ref, mate_ref, both)
-    total[...] = near_total_ref[...]
-    on_half(m_ref, True, lambda h: pair_taps(h, total, even, odd, w_ref, a_ref))
-    second_finish(m_ref, total, a_ref.shape[2], bias_ref, outs, held)
+    lanes, channels = a_ref.shape[3], w_ref.shape[3]
+
+    def body(h):
+        parts = [[both.at[c, g] for g in range(both.shape[1])] for c in (0, 1)]
+        held = range(total_ref.shape[0])
+        half_channels(h, parts, held, a_ref)
+        frame_taps(total_ref, None, a_ref, held, w_ref, half_lanes(h, lanes, channels))
+
+    on_half(m_ref, False, body)
+
+
+def second_conv_early(m_ref, near_total_ref, own_ref, mate_ref, w_ref, total_ref, both, a_ref):
+    odd = m_ref[0] & 1
+    both[odd] = own_ref[...]
+    both[1 - odd] = mate_ref[...]
+    lanes, channels = a_ref.shape[3], w_ref.shape[3]
+
+    def body(h):
+        parts = [[both.at[c, g] for g in range(both.shape[1])] for c in (0, 1)]
+        half_channels(h, parts, (0, 1), a_ref)
+        frame_taps(total_ref, near_total_ref, a_ref, (0, 1), w_ref, half_lanes(h, lanes, channels))
+
+    on_half(m_ref, True, body)
+
+
+def second_conv_late(
+    m_ref, total_ref, own_ref, mate_ref, own_last_ref, mate_last_ref, w_ref, bias_ref, *refs
+):
+    outs, (both, last, a_ref, total, done) = refs[:-5], refs[-5:]
+    odd = m_ref[0] & 1
+    both[odd] = own_ref[...]
+    both[1 - odd] = mate_ref[...]
+    last[odd] = own_last_ref[...]
+    last[1 - odd] = mate_last_ref[...]
+    lanes, channels = a_ref.shape[3], w_ref.shape[3]
+
+    def body(h):
+        parts = [[both.at[c, 0], both.at[c, 1], last.at[c, 0]] for c in (0, 1)]
+        half_channels(h, parts, (2, 3), a_ref)
+        frame_taps(total, total_ref, a_ref, (2, 3), w_ref, half_lanes(h, lanes, channels))
+
+    on_half(m_ref, True, body)
+    cols = a_ref.shape[2]
+    for t in range(total.shape[0]):
+        done[t] = finish((total if t >= 2 else total_ref).at[t], cols, bias_ref)
+    quarter = done.shape[1] // 4
+    for k, out_ref in enumerate(outs):
+        frame = m_ref[0] ^ k
+        tail = done[frame, 3 * quarter :]
+        for b in range(3):
+            at = slice(b * quarter, (b + 1) * quarter)
+            out_ref[at] = jnp.concatenate([done[frame, at], tail[:, 32 * b : 32 * b + 32]], axis=1)
 
 
 def second_conv(m_ref, parts_ref, w_ref, bias_ref, *refs):
@@ -398,21 +459,40 @@
     out_ref[...] = (x_ref[0].reshape(rows * cols, channels).astype(F32) + update).astype(BF16)
 
 
-def attention(own_ref, *refs):
-    others, (table_ref, wq_ref, wk_ref, wv_ref, wo_ref, out_ref) = refs[:-6], refs[-6:]
-    channels = own_ref.shape[-1]
+def attention(own_ref, all_ref, table_ref, wq_ref, wk_ref, wv_ref, wo_ref, out_ref):
+    wide = all_ref[...].reshape(-1, own_ref.shape[-1]).astype(F32)
+    out_ref[...] = attend(own_ref[...].astype(F32), wide, table_ref, wq_ref, wk_ref, wv_ref, wo_ref)
+
+
+def frame_attention(
+    r_ref, m_ref, raw_ref, p0, p1, p2, p3, table_ref, wq_ref, wk_ref, wv_ref, wo_ref, out_ref, held, hidden
+):
+    height, cols, channels = raw_ref.shape
+    rows = height // 4
+    quarter = rows * cols
+    for k, piece in enumerate((p0, p1, p2, p3)):
+        held[k] = piece[...]
+    for b in range(4):
+        pieces = []
+        for source in range(4):
+            k = m_ref[0] ^ source
+            if b < 3:
+                pieces.append(held[k, b * quarter : (b + 1) * quarter, 0:96])
+            else:
+                pieces += [held[k, g * quarter : (g + 1) * quarter, 96:] for g in range(3)]
+        update = jnp.concatenate(pieces, axis=1).astype(F32)
+        raw = raw_ref[b * rows : (b + 1) * rows].reshape(quarter, channels).astype(F32)
+        hidden[b * quarter : (b + 1) * quarter] = (raw + update).astype(BF16).astype(F32)
+    own = hidden[pl.ds(r_ref[0] * quarter, quarter)]
+    out_ref[...] = attend(own, hidden[...], table_ref, wq_ref, wk_ref, wv_ref, wo_ref)
+
+
+def attend(own, wide, table_ref, wq_ref, wk_ref, wv_ref, wo_ref):
     gain, shift = table_ref[4:5], table_ref[5:6]
-    own = own_ref[...].astype(F32)
-    blocks = [o[...].reshape(-1, channels).astype(F32) for o in others]
-    wide = blocks[0] if len(blocks) == 1 else jnp.concatenate([own] + blocks, axis=0)
-    positions = wide.shape[0]
-    count = positions * GROUP
-    mean = group_sums(jnp.broadcast_to(jnp.sum(wide, axis=0, keepdims=True), (8, channels)))[0:1] / count
+    count = wide.shape[0] * GROUP
+    mean = group_sums(eight(jnp.sum(wide, axis=0, keepdims=True)))[0:1] / count
     centered = wide - mean
-    variance = (
-        group_sums(jnp.broadcast_to(jnp.sum(centered * centered, axis=0, keepdims=True), (8, channels)))[0:1]
-        / count
-    )
+    variance = group_sums(eight(jnp.sum(centered * centered, axis=0, keepdims=True)))[0:1] / count
     scale = lax.rsqrt(variance + EPSILON) * gain
     normed = (centered * scale + shift).astype(BF16)
     mine = ((own - mean) * scale + shift).astype(BF16)
@@ -425,7 +505,7 @@
     weights = jnp.exp(scores - peak)
     total = jnp.sum(weights, axis=-1, keepdims=True)
     attended = (dot(weights.astype(BF16), values) / total).astype(BF16)
-    out_ref[...] = (own + dot(attended, wo_ref[...])).astype(BF16)
+    return (own + dot(attended, wo_ref[...])).astype(BF16)
 
 
 def swapped(value, axis, partner):
@@ -473,7 +553,7 @@
     for i, vector in enumerate([first_gain, first_shift, second_gain, second_shift, third_gain, third_shift]):
         table = jnp.where(row == i, vector[None, :], table)
 
-    split = n == 4 and frames == 4 and channels == 4 * outputs and 2 * outputs <= 256 < channels
+    split = n == 4 and frames == 4 and channels == 384 and packs(frames, outputs)
     lanes = 128 * (-(-outputs // 128)) if split else outputs
     loaded = struct((3, 3, 3 * lanes, channels))
     weights1 = call(load, loaded)(taps(first_kernel))
@@ -484,30 +564,63 @@
     total_scratch = pltpu.VMEM(total.shape, F32)
     active2_struct = struct(packed_shape(frames, rows + 2, cols, outputs))
     if split:
-        held_back = call(hand_on, struct(features.shape))(features, table)
-        blocks = [held_back] + [
-            swapped(held_back if k == 3 else features, "rows", lambda i, k=k: i ^ k) for k in (1, 2, 3)
-        ]
-        sent = [held_back, call(hand_on, struct(features.shape))(blocks[1], weights1), *blocks[2:]]
-        blocks_across = [swapped(block, "tm", lambda i: i ^ 2) for block in sent]
-        frame = struct((1, n * rows, cols, channels))
-        active1 = call(frame_norm, frame)(r, *blocks, table, weights1, *blocks_across[:2])
-        mate = swapped(active1, "tm", lambda i: i ^ 1)
-        pair = pltpu.VMEM((2, n * rows + 2, cols, channels), BF16)
+        def over_rows(value, k):
+            return swapped(value, "rows", lambda i: i ^ k)
+
+        def over_x(value):
+            return swapped(value, "tm", lambda i: i ^ 2)
+
+        def over_core(value):
+            return swapped(value, "tm", lambda i: i ^ 1)
+
+        def held_until(value, after):
+            return call(hand_on, struct(value.shape))(value, after)
+
+        height = n * rows
+        one, two, three = (over_rows(features, k) for k in (1, 2, 3))
+        across, across_one = over_x(features), over_x(held_until(one, weights1))
+        frame = struct((1, height, cols, channels))
+        active1, raw, held = call(
+            own_frame, (frame, struct((height, cols, channels)), struct((2, rows, cols, channels)))
+        )(r, features, one, two, three, across, across_one, table, weights1)
+        across_two, across_three = over_x(two), over_x(three)
+        mate = over_core(active1)
+        pair = pltpu.VMEM((2, height + 2, cols, channels), BF16)
         tall = struct((frames, n * plane, 3 * lanes), F32)
+        tall_scratch = pltpu.VMEM(tall.shape, F32)
         near_total = call(first_conv_near, tall, (pair,))(m, active1, mate, weights1)
-        across = call(frame_norm, frame)(r, *blocks_across, table, near_total)
-        beside = swapped(across, "tm", lambda i: i ^ 1)
-        active2 = call(
+        across = call(across_frame, frame)(r, held, across_two, across_three, table, near_total)
+        active2, early, late = call(
             first_conv_rest,
-            active2_struct,
-            (
-                pair,
-                pltpu.VMEM(tall.shape, F32),
-                pltpu.VMEM((frames, n * rows, cols, outputs), BF16),
-                stats_scratch,
-            ),
-        )(r, m, near_total, across, beside, weights1, first_bias, table)
+            tuple(struct((k, height, cols, 128)) for k in (frames - 1, 2, frames - 3)),
+            (pair, tall_scratch, pltpu.VMEM((frames, height, cols, outputs), BF16), stats_scratch),
+        )(m, near_total, across, over_core(across), weights1, first_bias, table)
+
+        weights2 = call(load, loaded)(taps(second_kernel), active2)
+        early, late = over_x(early), over_x(late)
+        mate = over_core(active2)
+        both = pltpu.VMEM((2, frames - 1, height, cols, 128), BF16)
+        all_frames, two_frames = (pltpu.VMEM((k, height + 2, cols, 256), BF16) for k in (frames, 2))
+        near_total = call(second_conv_near, tall, (both, all_frames))(m, active2, mate, weights2)
+        early_beside = over_core(held_until(early, near_total))
+        late_beside = over_core(held_until(late, near_total))
+        both = pltpu.VMEM((2, 2, height, cols, 128), BF16)
+        last = pltpu.VMEM((2, 1, height, cols, 128), BF16)
+        early_total = call(second_conv_early, tall, (both, two_frames))(
+            m, near_total, early, early_beside, weights2
+        )
+        piece = struct((3 * plane, 128))
+        pieces = call(
+            second_conv_late,
+            [piece] * frames,
+            (both, last, two_frames, tall_scratch, pltpu.VMEM((frames, n * plane, outputs), BF16)),
+        )(m, early_total, early, early_beside, late, late_beside, weights2, second_bias)
+        pieces = [pieces[0]] + [swapped(pieces[k], "tm", lambda i, k=k: i ^ k) for k in range(1, frames)]
+        decoded = call(
+            frame_attention,
+            struct((plane, channels)),
+            (pltpu.VMEM((frames, 3 * plane, 128), BF16), pltpu.VMEM((n * plane, channels), F32)),
+        )(r, m, raw, *pieces, table, query_weight, key_weight, value_weight, output_weight)
     else:
         halo = struct((cols, channels))
         near, far, block = call(first_stats, (halo, halo, struct((16, channels))))(r, features)
@@ -525,40 +638,19 @@
             r, m, conv1, *around(near, far, block), table
         )
 
-    weights2 = call(load, loaded)(taps(second_kernel), active2)
-    piece = struct((plane, outputs))
-    held = pltpu.VMEM((frames, plane, outputs), BF16)
-    if split:
-        both = pltpu.VMEM((2, *active2.shape), BF16)
-        half = pltpu.VMEM((frames, rows + 2, cols, 256), BF16)
-        across = swapped(active2, "tm", lambda i: i ^ 2)
-        mate = swapped(active2, "tm", lambda i: i ^ 1)
-        near_total = call(second_conv_near, total, (both, half))(m, active2, mate, weights2)
-        beside = swapped(call(hand_on, struct(across.shape))(across, near_total), "tm", lambda i: i ^ 1)
-        pieces = call(second_conv_rest, [piece] * frames, (both, half, total_scratch, held))(
-            m, near_total, across, beside, weights2, second_bias
-        )
-    else:
+        weights2 = taps(second_kernel)
+        piece = struct((plane, outputs))
+        done = pltpu.VMEM((frames, plane, outputs), BF16)
         parts = lax.all_gather(active2, "tm")
         whole = pltpu.VMEM((frames, rows + 2, cols, channels), BF16)
-        pieces = call(second_conv, [piece] * frames, (whole, total_scratch, held))(m, parts, weights2, second_bias)
-    pieces = [pieces[0]] + [swapped(pieces[k], "tm", lambda i, k=k: i ^ k) for k in range(1, frames)]
-    hidden = call(add_hidden, struct((plane, channels)), (pltpu.VMEM((frames, plane, outputs), F32),))(
-        m, features, *pieces
-    )
-    if n == 4:
-        others = [swapped(hidden, "rows", lambda i, k=k: i ^ k) for k in (1, 2, 3)]
-    else:
-        others = [lax.all_gather(hidden, "rows")]
-    decoded = call(attention, struct((plane, channels)))(
-        hidden,
-        *others,
-        table,
-        query_weight,
-        key_weight,
-        value_weight,
-        output_weight,
-    )
+        pieces = call(second_conv, [piece] * frames, (whole, total_scratch, done))(m, parts, weights2, second_bias)
+        pieces = [pieces[0]] + [swapped(pieces[k], "tm", lambda i, k=k: i ^ k) for k in range(1, frames)]
+        hidden = call(add_hidden, struct((plane, channels)), (pltpu.VMEM((frames, plane, outputs), F32),))(
+            m, features, *pieces
+        )
+        decoded = call(attention, struct((plane, channels)))(
+            hidden, lax.all_gather(hidden, "rows"), table, query_weight, key_weight, value_weight, output_weight
+        )
     return decoded.reshape(features.shape)
 
 

time: 56.5 us -> 56.1 us (level)
  waiting for transfers between devices: 19.8 us -> 14.4 us
  Pallas kernels: 15.2 us -> 19.2 us
  local copies, waits for them, and re-layouts: 1.6 us -> 5.31 us
  starting transfers between devices: 18.5 us -> 16.5 us
  other arithmetic: 0.86 us -> 0.1 us
    ppermute x18 -> x17, waiting for transfers between devices: 19.8 us -> 14.4 us  [swapped(): lax.ppermute(value, axis, [(i, partner(i)) for i in range(lax.axis_size(a...]
    pallas_call x13, Pallas kernels: 15.2 us -> 19.2 us  [run(): pl.pallas_call(body, out_shape=outs, in_specs=[SMEM if a.dtype == jnp.int...]
    unnamed x16 -> x42, local copies, waits for them, and re-layouts: 1.6 us -> 5.31 us
    ppermute x18 -> x17, starting transfers between devices: 18.5 us -> 16.5 us  [swapped(): lax.ppermute(value, axis, [(i, partner(i)) for i in range(lax.axis_size(a...]
    select_n x1, other arithmetic: 0.85 us -> 0.08 us  [per_device(): table = jnp.where(row == i, vector[None, :], table)]
  transfers between devices with their start and end apart: 18 -> 17, of which waited for: 10 -> 9; matrix products, arithmetic and copies ran while one was open for 2% -> 0% of each run, Pallas kernels for 10% -> 16%
where the time goes in v2:
time: 56.1 us; the launch traced here: 55.8 us
  Pallas kernels  19.2 us (34%)
  starting transfers between devices  16.5 us (29%)
  waiting for transfers between devices  14.4 us (26%)
  local copies, waits for them, and re-layouts  5.31 us (9%)
    pallas_call x13, Pallas kernels, run(): pl.pallas_call(body, out_shape=outs, in_specs=[SMEM if a.dtype == jnp.int...  19.2 us
    ppermute x17, starting transfers between devices, swapped(): lax.ppermute(value, axis, [(i, partner(i)) for i in range(lax.axis_size(a...  16.5 us
    ppermute x17, waiting for transfers between devices, swapped(): lax.ppermute(value, axis, [(i, partner(i)) for i in range(lax.axis_size(a...  14.4 us
    unnamed x42, local copies, waits for them, and re-layouts  5.31 us
  transfers between devices with their start and end apart: 17, of which 9 were waited for; matrix products, arithmetic and copies ran while one was open for 0% of the time, Pallas kernels for 16%

profile of v2, /device:TPU:0, one launch (start us, length us, event | category | flops | bytes accessed | tf_op | source)
XLA Modules:
  0.0 55.8 jit_solution(11231988382265387705)
XLA Ops:
  0.0 5.0 %collective-permute-start.2 = (bf16[1,2,48,384]{3,2,1,0:T(8,128)(2,1)}, bf16[1,2,48,384]{3,2,1,0:T(8,128)(2,1)}, u32[]{:S(2)}, u32[]{:S(2)}) collective-permute-start(bf16[1,2,48,384]{3,2,1,0:T(8,128)(2,1)} %own_ref.1), channel_id=1, source_target_pairs={{0,3},{1,2},{2,1},{3,0},{4,7},{5,6},{6,5},{7,4},{8,11},{9,10},{10,... | collective-permute-start | bytes 221192 | tf_op jit(solution)/shard_map/ppermute | solution.py:512
  5.1 0.6 %collective-permute-start = (bf16[1,2,48,384]{3,2,1,0:T(8,128)(2,1)}, bf16[1,2,48,384]{3,2,1,0:T(8,128)(2,1)S(1)}, u32[]{:S(2)}, u32[]{:S(2)}) collective-permute-start(bf16[1,2,48,384]{3,2,1,0:T(8,128)(2,1)} %own_ref.1), channel_id=1, source_target_pairs={{0,1},{1,0},{2,3},{3,2},{4,5},{5,4},{6,7},{7,6},{8,9},{9,8},{10,11... | collective-permute-start | bytes 221192 | tf_op jit(solution)/shard_map/ppermute | solution.py:512
  5.6 1.7 %collective-permute-start.3 = (bf16[1,2,48,384]{3,2,1,0:T(8,128)(2,1)}, bf16[1,2,48,384]{3,2,1,0:T(8,128)(2,1)S(1)}, u32[]{:S(2)}, u32[]{:S(2)}) collective-permute-start(bf16[1,2,48,384]{3,2,1,0:T(8,128)(2,1)} %own_ref.1), channel_id=1, source_target_pairs={{0,8},{4,12},{8,0},{12,4},{1,9},{5,13},{9,1},{13,5},{2,10},{6,14},... | collective-permute-start | bytes 221192 | tf_op jit(solution)/shard_map/ppermute | solution.py:512
  7.4 1.5 %copy-done = bf16[96,3,3,3,384]{4,0,3,2,1:T(8,128)(2,1)S(1)} copy-done((bf16[96,3,3,3,384]{4,0,3,2,1:T(8,128)(2,1)S(1)}, bf16[96,3,3,3,384]{4,0,3,2,1:T(8,128)(2,1)}, u32[]{:S(2)}) %copy-start) | copy-done | bytes 1990680
  8.9 0.2 shard_map.145.after_ref.w_ref
  9.1 0.0 copy-start.15
  9.1 0.0 copy-start.16
  9.2 0.0 copy-start.17
  9.2 0.0 copy-start.18
  9.2 0.0 copy-start.19
  9.2 0.0 copy-start.8
  9.2 0.9 %collective-permute-done.x_ref.one_ref = bf16[1,2,48,384]{3,2,1,0:T(8,128)(2,1)S(1)} collective-permute-done((bf16[1,2,48,384]{3,2,1,0:T(8,128)(2,1)}, bf16[1,2,48,384]{3,2,1,0:T(8,128)(2,1)S(1)}, u32[]{:S(2)}, u32[]{:S(2)}) %collective-permute-start) | collective-permute-done | bytes 73760 | tf_op jit(solution)/shard_map/ppermute | solution.py:512
  10.1 1.5 %collective-permute-start.4 = (bf16[1,2,48,384]{3,2,1,0:T(8,128)(2,1)S(1)}, bf16[1,2,48,384]{3,2,1,0:T(8,128)(2,1)S(1)}, u32[]{:S(2)}, u32[]{:S(2)}) collective-permute-start(bf16[1,2,48,384]{3,2,1,0:T(8,128)(2,1)S(1)} %shard_map.146), channel_id=1, source_target_pairs={{0,8},{4,12},{8,0},{12,4},{1,9},{5,13},{9,1},{13,5},{2,10},{6,14},... | collective-permute-start | bytes 221192 | tf_op jit(solution)/shard_map/ppermute | solution.py:512
  11.6 0.1 select_select_fusion.table_ref
  11.8 0.6 %copy-done.9 = bf16[1,2,48,384]{3,2,1,0:T(8,128)(2,1)} copy-done((bf16[1,2,48,384]{3,2,1,0:T(8,128)(2,1)}, bf16[1,2,48,384]{3,2,1,0:T(8,128)(2,1)S(1)}, u32[]{:S(2)}) %copy-start.9) | copy-done | bytes 73752
  12.4 2.1 %collective-permute-done.4.across_one_ref = bf16[1,2,48,384]{3,2,1,0:T(8,128)(2,1)S(1)} collective-permute-done((bf16[1,2,48,384]{3,2,1,0:T(8,128)(2,1)S(1)}, bf16[1,2,48,384]{3,2,1,0:T(8,128)(2,1)S(1)}, u32[]{:S(2)}, u32[]{:S(2)}) %collective-permute-start.4) | collective-permute-done | bytes 73760 | tf_op jit(solution)/shard_map/ppermute | solution.py:512
  14.5 0.6 %copy-done.11 = bf16[1,2,48,384]{3,2,1,0:T(8,128)(2,1)} copy-done((bf16[1,2,48,384]{3,2,1,0:T(8,128)(2,1)}, bf16[1,2,48,384]{3,2,1,0:T(8,128)(2,1)S(1)}, u32[]{:S(2)}) %copy-start.11) | copy-done | bytes 73752
  15.1 0.9 %copy-done.10 = bf16[1,2,48,384]{3,2,1,0:T(8,128)(2,1)S(1)} copy-done((bf16[1,2,48,384]{3,2,1,0:T(8,128)(2,1)S(1)}, bf16[1,2,48,384]{3,2,1,0:T(8,128)(2,1)}, u32[]{:S(2)}) %copy-start.10) | copy-done | bytes 73752
  16.0 0.9 %copy-done.12 = bf16[1,2,48,384]{3,2,1,0:T(8,128)(2,1)S(1)} copy-done((bf16[1,2,48,384]{3,2,1,0:T(8,128)(2,1)S(1)}, bf16[1,2,48,384]{3,2,1,0:T(8,128)(2,1)}, u32[]{:S(2)}) %copy-start.12) | copy-done | bytes 73752
  16.9 1.6 %shard_map.147 = (bf16[1,8,48,384]{3,2,1,0:T(8,128)(2,1)S(1)}, bf16[8,48,384]{2,1,0:T(8,128)(2,1)S(1)}, bf16[2,2,48,384]{3,2,1,0:T(8,128)(2,1)S(1)}) custom-call(s32[1]{0:T(128)} %bitcast.r_ref, bf16[1,2,48,384]{3,2,1,0:T(8,128)(2,1)S(1)} %copy-done.8, bf16[1,2,48,384]{3,2,1,0:T(8,128)(2,1)S(1)} %collective-permute-done.x_ref.one_ref, ...), custom_call_target="tpu_custom_call" | custom-call | tf_op jit(solution)/shard_map/pallas_call | solution.py:22
  18.5 0.6 %copy-done.6 = bf16[2,2,48,384]{3,2,1,0:T(8,128)(2,1)} copy-done((bf16[2,2,48,384]{3,2,1,0:T(8,128)(2,1)}, bf16[2,2,48,384]{3,2,1,0:T(8,128)(2,1)S(1)}, u32[]{:S(2)}) %copy-start.6) | copy-done | bytes 147480
  19.2 1.5 %collective-permute-start.7 = (bf16[1,2,48,384]{3,2,1,0:T(8,128)(2,1)}, bf16[1,2,48,384]{3,2,1,0:T(8,128)(2,1)}, u32[]{:S(2)}, u32[]{:S(2)}) collective-permute-start(bf16[1,2,48,384]{3,2,1,0:T(8,128)(2,1)} %collective-permute-done.2.three_ref), channel_id=1, source_target_pairs={{0,8},{4,12},{8,0},{12,4},{1,9},{5,13},{9,1},{13,5},{2,10},{6,14},... | collective-permute-start | bytes 221192 | tf_op jit(solution)/shard_map/ppermute | solution.py:512
  20.7 0.5 collective-permute-start.6
  21.2 3.2 %shard_map.148.after_ref.near_total_ref = f32[4,384,384]{2,1,0:T(8,128)S(1)} custom-call(s32[1]{0:T(128)} %bitcast.1.m_ref, bf16[1,8,48,384]{3,2,1,0:T(8,128)(2,1)S(1)} %get-tuple-element.16.own_ref, bf16[1,8,48,384]{3,2,1,0:T(8,128)(2,1)S(1)} %collective-permute-done.5.mate_ref, bf16[3,3,384,384]{3,2,1,0:T(8,128)(2,1)S(1)} %shard_map.145.after_ref.w_ref), custom_call_target="tpu_custom_call" | custom-call | tf_op jit(solution)/shard_map/pallas_call | solution.py:22
  24.4 0.2 collective-permute-done.7.three_ref
  24.6 1.2 %collective-permute-done.6.two_ref = bf16[1,2,48,384]{3,2,1,0:T(8,128)(2,1)} collective-permute-done((bf16[1,2,48,384]{3,2,1,0:T(8,128)(2,1)}, bf16[1,2,48,384]{3,2,1,0:T(8,128)(2,1)}, u32[]{:S(2)}, u32[]{:S(2)}) %collective-permute-start.6) | collective-permute-done | bytes 73760 | tf_op jit(solution)/shard_map/ppermute | solution.py:512
  25.7 1.6 %shard_map.149.own_ref = bf16[1,8,48,384]{3,2,1,0:T(8,128)(2,1)S(1)} custom-call(s32[1]{0:T(128)} %bitcast.r_ref, bf16[2,2,48,384]{3,2,1,0:T(8,128)(2,1)S(1)} %copy-done.7, bf16[1,2,48,384]{3,2,1,0:T(8,128)(2,1)} %collective-permute-done.6.two_ref, bf16[1,2,48,384]{3,2,1,0:T(8,128)(2,1)} %collective-permute-done.7.three_ref, ...), custom_call_target="tpu_custom_call" | custom-call | tf_op jit(solution)/shard_map/pallas_call | solution.py:22
  27.4 0.1 collective-permute-start.8
  27.4 1.6 %collective-permute-done.8.mate_ref = bf16[1,8,48,384]{3,2,1,0:T(8,128)(2,1)S(1)} collective-permute-done((bf16[1,8,48,384]{3,2,1,0:T(8,128)(2,1)S(1)}, bf16[1,8,48,384]{3,2,1,0:T(8,128)(2,1)S(1)}, u32[]{:S(2)}, u32[]{:S(2)}) %collective-permute-start.8) | collective-permute-done | bytes 294944 | tf_op jit(solution)/shard_map/ppermute | solution.py:512
  29.0 3.0 %shard_map.150 = (bf16[3,8,48,128]{3,2,1,0:T(8,128)(2,1)S(1)}, bf16[2,8,48,128]{3,2,1,0:T(8,128)(2,1)S(1)}, bf16[1,8,48,128]{3,2,1,0:T(8,128)(2,1)S(1)}) custom-call(s32[1]{0:T(128)} %bitcast.1.m_ref, f32[4,384,384]{2,1,0:T(8,128)S(1)} %shard_map.148.after_ref.near_total_ref, bf16[1,8,48,384]{3,2,1,0:T(8,128)(2,1)S(1)} %shard_map.149.own_ref, ...), custom_call_target="tpu_custom_call" | custom-call | tf_op jit(solution)/shard_map/pallas_call | solution.py:22
  32.0 0.2 collective-permute-start.9
  32.2 2.9 %collective-permute-start.10 = (bf16[2,8,48,128]{3,2,1,0:T(8,128)(2,1)S(1)}, bf16[2,8,48,128]{3,2,1,0:T(8,128)(2,1)S(1)}, u32[]{:S(2)}, u32[]{:S(2)}) collective-permute-start(bf16[2,8,48,128]{3,2,1,0:T(8,128)(2,1)S(1)} %get-tuple-element.19), channel_id=1, source_target_pairs={{0,8},{4,12},{8,0},{12,4},{1,9},{5,13},{9,1},{13,5},{2,10},{6,14},... | collective-permute-start | bytes 589832 | tf_op jit(solution)/shard_map/ppermute | solution.py:512
  35.1 0.0 collective-permute-start.12
  35.2 0.2 shard_map.151.w_ref
  35.4 3.2 %shard_map.152.after_ref.near_total_ref = f32[4,384,384]{2,1,0:T(8,128)S(1)} custom-call(s32[1]{0:T(128)} %bitcast.1.m_ref, bf16[3,8,48,128]{3,2,1,0:T(8,128)(2,1)S(1)} %get-tuple-element.18.refs_0_.own_ref, bf16[3,8,48,128]{3,2,1,0:T(8,128)(2,1)S(1)} %collective-permute-done.9.mate_ref, bf16[3,3,384,384]{3,2,1,0:T(8,128)(2,1)S(1)} %shard_map.151.w_ref), custom_call_target="tpu_custom_call" | custom-call | tf_op jit(solution)/shard_map/pallas_call | solution.py:22
  38.6 2.3 %collective-permute-done.10.x_ref.own_ref = bf16[2,8,48,128]{3,2,1,0:T(8,128)(2,1)S(1)} collective-permute-done((bf16[2,8,48,128]{3,2,1,0:T(8,128)(2,1)S(1)}, bf16[2,8,48,128]{3,2,1,0:T(8,128)(2,1)S(1)}, u32[]{:S(2)}, u32[]{:S(2)}) %collective-permute-start.10) | collective-permute-done | bytes 196640 | tf_op jit(solution)/shard_map/ppermute | solution.py:512
  40.9 0.1 collective-permute-start.11
  40.9 1.7 %collective-permute-done.12.x_ref.own_last_ref = bf16[1,8,48,128]{3,2,1,0:T(8,128)(2,1)S(1)} collective-permute-done((bf16[1,8,48,128]{3,2,1,0:T(8,128)(2,1)S(1)}, bf16[1,8,48,128]{3,2,1,0:T(8,128)(2,1)S(1)}, u32[]{:S(2)}, u32[]{:S(2)}) %collective-permute-start.12) | collective-permute-done | bytes 98336 | tf_op jit(solution)/shard_map/ppermute | solution.py:512
  42.7 0.1 collective-permute-start.13
  42.8 2.1 %shard_map.154.total_ref = f32[4,384,384]{2,1,0:T(8,128)S(1)} custom-call(s32[1]{0:T(128)} %bitcast.1.m_ref, f32[4,384,384]{2,1,0:T(8,128)S(1)} %shard_map.152.after_ref.near_total_ref, bf16[2,8,48,128]{3,2,1,0:T(8,128)(2,1)S(1)} %collective-permute-done.10.x_ref.own_ref, bf16[2,8,48,128]{3,2,1,0:T(8,128)(2,1)S(1)} %collective-permute-done.11.mate_ref, ...), custom_call_target="tpu_custom_call" | custom-call | tf_op jit(solution)/shard_map/pallas_call | solution.py:22
  44.9 0.0 copy-start.3
  44.9 0.0 copy-start.4
  44.9 1.7 %shard_map.156 = (bf16[288,128]{1,0:T(8,128)(2,1)S(1)}, bf16[288,128]{1,0:T(8,128)(2,1)S(1)}, bf16[288,128]{1,0:T(8,128)(2,1)S(1)}, bf16[288,128]{1,0:T(8,128)(2,1)S(1)}) custom-call(s32[1]{0:T(128)} %bitcast.1.m_ref, f32[4,384,384]{2,1,0:T(8,128)S(1)} %shard_map.154.total_ref, bf16[2,8,48,128]{3,2,1,0:T(8,128)(2,1)S(1)} %collective-permute-done.10.x_ref.own_ref, ...), custom_call_target="tpu_custom_call" | custom-call | tf_op jit(solution)/shard_map/pallas_call | solution.py:22
  46.6 0.5 collective-permute-start.14
  47.1 1.7 %collective-permute-start.15 = (bf16[288,128]{1,0:T(8,128)(2,1)S(1)}, bf16[288,128]{1,0:T(8,128)(2,1)S(1)}, u32[]{:S(2)}, u32[]{:S(2)}) collective-permute-start(bf16[288,128]{1,0:T(8,128)(2,1)S(1)} %get-tuple-element.23), channel_id=1, source_target_pairs={{0,8},{4,12},{8,0},{12,4},{1,9},{5,13},{9,1},{13,5},{2,10},{6,14},... | collective-permute-start | bytes 221192 | tf_op jit(solution)/shard_map/ppermute | solution.py:512
  48.9 2.6 %collective-permute-done.15.p2 = bf16[288,128]{1,0:T(8,128)(2,1)S(1)} collective-permute-done((bf16[288,128]{1,0:T(8,128)(2,1)S(1)}, bf16[288,128]{1,0:T(8,128)(2,1)S(1)}, u32[]{:S(2)}, u32[]{:S(2)}) %collective-permute-start.15) | collective-permute-done | bytes 73760 | tf_op jit(solution)/shard_map/ppermute | solution.py:512
  51.5 1.9 %collective-permute-done.16.p3 = bf16[288,128]{1,0:T(8,128)(2,1)S(1)} collective-permute-done((bf16[288,128]{1,0:T(8,128)(2,1)S(1)}, bf16[288,128]{1,0:T(8,128)(2,1)S(1)}, u32[]{:S(2)}, u32[]{:S(2)}) %collective-permute-start.16) | collective-permute-done | bytes 73760 | tf_op jit(solution)/shard_map/ppermute | solution.py:512
  53.4 2.4 %shard_map.157 = bf16[96,384]{1,0:T(8,128)(2,1)} custom-call(s32[1]{0:T(128)} %bitcast.r_ref, s32[1]{0:T(128)} %bitcast.1.m_ref, bf16[8,48,384]{2,1,0:T(8,128)(2,1)S(1)} %get-tuple-element.15.raw_ref, bf16[288,128]{1,0:T(8,128)(2,1)S(1)} %get-tuple-element.21.p0, bf16[288,128]{1,0:T(8,128)(2,1)S(1)} %collective-permute-done.14.p1, ...), custom_call_target="tpu_custom_call" | custom-call | tf_op jit(solution)/shard_map/pallas_call | solution.py:22
  (45 shorter events, 0.1 us)
Async XLA Ops:
  0.0 11.7 %collective-permute-start.2 = (bf16[1,2,48,384]{3,2,1,0:T(8,128)(2,1)}, bf16[1,2,48,384]{3,2,1,0:T(8,128)(2,1)}, u32[]{:S(2)}, u32[]{:S(2)}) collective-permute-start(bf16[1,2,48,384]{3,2,1,0:T(8,128)(2,1)} %own_ref.1), channel_id=1, source_target_pairs={{0,3},{1,2},{2,1},{3,0},{4,7},{5,6},{6,5},{7,4},{8,11},{9,10},{10,... | collective-permute-start | bytes 221192 | tf_op jit(solution)/shard_map/ppermute | solution.py:512
  5.0 6.7 %collective-permute-start.1 = (bf16[1,2,48,384]{3,2,1,0:T(8,128)(2,1)}, bf16[1,2,48,384]{3,2,1,0:T(8,128)(2,1)}, u32[]{:S(2)}, u32[]{:S(2)}) collective-permute-start(bf16[1,2,48,384]{3,2,1,0:T(8,128)(2,1)} %own_ref.1), channel_id=1, source_target_pairs={{0,2},{1,3},{2,0},{3,1},{4,6},{5,7},{6,4},{7,5},{8,10},{9,11},{10,... | collective-permute-start | bytes 221192 | tf_op jit(solution)/shard_map/ppermute | solution.py:512
  5.1 5.0 %collective-permute-start = (bf16[1,2,48,384]{3,2,1,0:T(8,128)(2,1)}, bf16[1,2,48,384]{3,2,1,0:T(8,128)(2,1)S(1)}, u32[]{:S(2)}, u32[]{:S(2)}) collective-permute-start(bf16[1,2,48,384]{3,2,1,0:T(8,128)(2,1)} %own_ref.1), channel_id=1, source_target_pairs={{0,1},{1,0},{2,3},{3,2},{4,5},{5,4},{6,7},{7,6},{8,9},{9,8},{10,11... | collective-permute-start | bytes 221192 | tf_op jit(solution)/shard_map/ppermute | solution.py:512
  5.6 6.1 %collective-permute-start.3 = (bf16[1,2,48,384]{3,2,1,0:T(8,128)(2,1)}, bf16[1,2,48,384]{3,2,1,0:T(8,128)(2,1)S(1)}, u32[]{:S(2)}, u32[]{:S(2)}) collective-permute-start(bf16[1,2,48,384]{3,2,1,0:T(8,128)(2,1)} %own_ref.1), channel_id=1, source_target_pairs={{0,8},{4,12},{8,0},{12,4},{1,9},{5,13},{9,1},{13,5},{2,10},{6,14},... | collective-permute-start | bytes 221192 | tf_op jit(solution)/shard_map/ppermute | solution.py:512
  7.3 1.6 %copy-start = (bf16[96,3,3,3,384]{4,0,3,2,1:T(8,128)(2,1)S(1)}, bf16[96,3,3,3,384]{4,0,3,2,1:T(8,128)(2,1)}, u32[]{:S(2)}) copy-start(bf16[96,3,3,3,384]{4,0,3,2,1:T(8,128)(2,1)} %param.18) | copy-start | bytes 5971972
  9.1 2.5 %copy-start.15 = (f32[384]{0:T(512)S(1)}, f32[384]{0:T(512)}, u32[]{:S(2)}) copy-start(f32[384]{0:T(512)} %param.16) | copy-start | bytes 4612
  9.1 2.5 %copy-start.16 = (f32[384]{0:T(512)S(1)}, f32[384]{0:T(512)}, u32[]{:S(2)}) copy-start(f32[384]{0:T(512)} %param.17) | copy-start | bytes 4612
  9.2 2.5 %copy-start.17 = (f32[384]{0:T(512)S(1)}, f32[384]{0:T(512)}, u32[]{:S(2)}) copy-start(f32[384]{0:T(512)} %param.20) | copy-start | bytes 4612
  9.2 2.4 %copy-start.18 = (f32[384]{0:T(512)S(1)}, f32[384]{0:T(512)}, u32[]{:S(2)}) copy-start(f32[384]{0:T(512)} %param.21) | copy-start | bytes 4612
  9.2 2.4 %copy-start.19 = (f32[384]{0:T(512)S(1)}, f32[384]{0:T(512)}, u32[]{:S(2)}) copy-start(f32[384]{0:T(512)} %param.24) | copy-start | bytes 4612
  9.2 2.4 %copy-start.20 = (f32[384]{0:T(512)S(1)}, f32[384]{0:T(512)}, u32[]{:S(2)}) copy-start(f32[384]{0:T(512)} %param.25) | copy-start | bytes 4612
  9.2 5.9 %copy-start.8 = (bf16[1,2,48,384]{3,2,1,0:T(8,128)(2,1)S(1)}, bf16[1,2,48,384]{3,2,1,0:T(8,128)(2,1)}, u32[]{:S(2)}) copy-start(bf16[1,2,48,384]{3,2,1,0:T(8,128)(2,1)} %own_ref.1) | copy-start | bytes 221188
  10.1 4.4 %collective-permute-start.4 = (bf16[1,2,48,384]{3,2,1,0:T(8,128)(2,1)S(1)}, bf16[1,2,48,384]{3,2,1,0:T(8,128)(2,1)S(1)}, u32[]{:S(2)}, u32[]{:S(2)}) collective-permute-start(bf16[1,2,48,384]{3,2,1,0:T(8,128)(2,1)S(1)} %shard_map.146), channel_id=1, source_target_pairs={{0,8},{4,12},{8,0},{12,4},{1,9},{5,13},{9,1},{13,5},{2,10},{6,14},... | collective-permute-start | bytes 221192 | tf_op jit(solution)/shard_map/ppermute | solution.py:512
  11.7 0.6 %copy-start.9 = (bf16[1,2,48,384]{3,2,1,0:T(8,128)(2,1)}, bf16[1,2,48,384]{3,2,1,0:T(8,128)(2,1)S(1)}, u32[]{:S(2)}) copy-start(bf16[1,2,48,384]{3,2,1,0:T(8,128)(2,1)S(1)} %collective-permute-done.3.across_ref) | copy-start | bytes 221188
  14.5 0.6 %copy-start.11 = (bf16[1,2,48,384]{3,2,1,0:T(8,128)(2,1)}, bf16[1,2,48,384]{3,2,1,0:T(8,128)(2,1)S(1)}, u32[]{:S(2)}) copy-start(bf16[1,2,48,384]{3,2,1,0:T(8,128)(2,1)S(1)} %collective-permute-done.4.across_one_ref) | copy-start | bytes 221188
  15.1 0.9 %copy-start.10 = (bf16[1,2,48,384]{3,2,1,0:T(8,128)(2,1)S(1)}, bf16[1,2,48,384]{3,2,1,0:T(8,128)(2,1)}, u32[]{:S(2)}) copy-start(bf16[1,2,48,384]{3,2,1,0:T(8,128)(2,1)} %copy-done.9) | copy-start | bytes 221188
  16.0 0.9 %copy-start.12 = (bf16[1,2,48,384]{3,2,1,0:T(8,128)(2,1)S(1)}, bf16[1,2,48,384]{3,2,1,0:T(8,128)(2,1)}, u32[]{:S(2)}) copy-start(bf16[1,2,48,384]{3,2,1,0:T(8,128)(2,1)} %copy-done.11) | copy-start | bytes 221188
  18.5 0.7 %copy-start.6 = (bf16[2,2,48,384]{3,2,1,0:T(8,128)(2,1)}, bf16[2,2,48,384]{3,2,1,0:T(8,128)(2,1)S(1)}, u32[]{:S(2)}) copy-start(bf16[2,2,48,384]{3,2,1,0:T(8,128)(2,1)S(1)} %get-tuple-element.17.held_ref) | copy-start | bytes 442372
  19.2 2.0 %collective-permute-start.5 = (bf16[1,8,48,384]{3,2,1,0:T(8,128)(2,1)S(1)}, bf16[1,8,48,384]{3,2,1,0:T(8,128)(2,1)S(1)}, u32[]{:S(2)}, u32[]{:S(2)}) collective-permute-start(bf16[1,8,48,384]{3,2,1,0:T(8,128)(2,1)S(1)} %get-tuple-element.16.own_ref), channel_id=1, source_target_pairs={{0,4},{4,0},{8,12},{12,8},{1,5},{5,1},{9,13},{13,9},{2,6},{6,2},{1... | collective-permute-start | bytes 884744 | tf_op jit(solution)/shard_map/ppermute | solution.py:512
  19.2 5.4 %collective-permute-start.7 = (bf16[1,2,48,384]{3,2,1,0:T(8,128)(2,1)}, bf16[1,2,48,384]{3,2,1,0:T(8,128)(2,1)}, u32[]{:S(2)}, u32[]{:S(2)}) collective-permute-start(bf16[1,2,48,384]{3,2,1,0:T(8,128)(2,1)} %collective-permute-done.2.three_ref), channel_id=1, source_target_pairs={{0,8},{4,12},{8,0},{12,4},{1,9},{5,13},{9,1},{13,5},{2,10},{6,14},... | collective-permute-start | bytes 221192 | tf_op jit(solution)/shard_map/ppermute | solution.py:512
  20.7 5.1 %collective-permute-start.6 = (bf16[1,2,48,384]{3,2,1,0:T(8,128)(2,1)}, bf16[1,2,48,384]{3,2,1,0:T(8,128)(2,1)}, u32[]{:S(2)}, u32[]{:S(2)}) collective-permute-start(bf16[1,2,48,384]{3,2,1,0:T(8,128)(2,1)} %collective-permute-done.1.two_ref), channel_id=1, source_target_pairs={{0,8},{4,12},{8,0},{12,4},{1,9},{5,13},{9,1},{13,5},{2,10},{6,14},... | collective-permute-start | bytes 221192 | tf_op jit(solution)/shard_map/ppermute | solution.py:512
  21.2 4.5 %copy-start.7 = (bf16[2,2,48,384]{3,2,1,0:T(8,128)(2,1)S(1)}, bf16[2,2,48,384]{3,2,1,0:T(8,128)(2,1)}, u32[]{:S(2)}) copy-start(bf16[2,2,48,384]{3,2,1,0:T(8,128)(2,1)} %copy-done.6) | copy-start | bytes 442372
  24.4 4.6 %copy-start.14 = (f32[96]{0:T(128)S(1)}, f32[96]{0:T(128)}, u32[]{:S(2)}) copy-start(f32[96]{0:T(128)} %bias_ref.2) | copy-start | bytes 1156
  27.3 7.8 %copy-start.1 = (bf16[96,3,3,3,384]{4,0,3,2,1:T(8,128)(2,1)S(1)}, bf16[96,3,3,3,384]{4,0,3,2,1:T(8,128)(2,1)}, u32[]{:S(2)}) copy-start(bf16[96,3,3,3,384]{4,0,3,2,1:T(8,128)(2,1)} %param.22) | copy-start | bytes 5971972
  27.4 1.6 %collective-permute-start.8 = (bf16[1,8,48,384]{3,2,1,0:T(8,128)(2,1)S(1)}, bf16[1,8,48,384]{3,2,1,0:T(8,128)(2,1)S(1)}, u32[]{:S(2)}, u32[]{:S(2)}) collective-permute-start(bf16[1,8,48,384]{3,2,1,0:T(8,128)(2,1)S(1)} %shard_map.149.own_ref), channel_id=1, source_target_pairs={{0,4},{4,0},{8,12},{12,8},{1,5},{5,1},{9,13},{13,9},{2,6},{6,2},{1... | collective-permute-start | bytes 884744 | tf_op jit(solution)/shard_map/ppermute | solution.py:512
  32.0 3.4 %collective-permute-start.9 = (bf16[3,8,48,128]{3,2,1,0:T(8,128)(2,1)S(1)}, bf16[3,8,48,128]{3,2,1,0:T(8,128)(2,1)S(1)}, u32[]{:S(2)}, u32[]{:S(2)}) collective-permute-start(bf16[3,8,48,128]{3,2,1,0:T(8,128)(2,1)S(1)} %get-tuple-element.18.refs_0_.own_ref), channel_id=1, source_target_pairs={{0,4},{4,0},{8,12},{12,8},{1,5},{5,1},{9,13},{13,9},{2,6},{6,2},{1... | collective-permute-start | bytes 884744 | tf_op jit(solution)/shard_map/ppermute | solution.py:512
  32.2 8.7 %collective-permute-start.10 = (bf16[2,8,48,128]{3,2,1,0:T(8,128)(2,1)S(1)}, bf16[2,8,48,128]{3,2,1,0:T(8,128)(2,1)S(1)}, u32[]{:S(2)}, u32[]{:S(2)}) collective-permute-start(bf16[2,8,48,128]{3,2,1,0:T(8,128)(2,1)S(1)} %get-tuple-element.19), channel_id=1, source_target_pairs={{0,8},{4,12},{8,0},{12,4},{1,9},{5,13},{9,1},{13,5},{2,10},{6,14},... | collective-permute-start | bytes 589832 | tf_op jit(solution)/shard_map/ppermute | solution.py:512
  35.1 7.5 %collective-permute-start.12 = (bf16[1,8,48,128]{3,2,1,0:T(8,128)(2,1)S(1)}, bf16[1,8,48,128]{3,2,1,0:T(8,128)(2,1)S(1)}, u32[]{:S(2)}, u32[]{:S(2)}) collective-permute-start(bf16[1,8,48,128]{3,2,1,0:T(8,128)(2,1)S(1)} %get-tuple-element.20), channel_id=1, source_target_pairs={{0,8},{4,12},{8,0},{12,4},{1,9},{5,13},{9,1},{13,5},{2,10},{6,14},... | collective-permute-start | bytes 294920 | tf_op jit(solution)/shard_map/ppermute | solution.py:512
  40.9 1.9 %collective-permute-start.11 = (bf16[2,8,48,128]{3,2,1,0:T(8,128)(2,1)S(1)}, bf16[2,8,48,128]{3,2,1,0:T(8,128)(2,1)S(1)}, u32[]{:S(2)}, u32[]{:S(2)}) collective-permute-start(bf16[2,8,48,128]{3,2,1,0:T(8,128)(2,1)S(1)} %shard_map.153), channel_id=1, source_target_pairs={{0,4},{4,0},{8,12},{12,8},{1,5},{5,1},{9,13},{13,9},{2,6},{6,2},{1... | collective-permute-start | bytes 589832 | tf_op jit(solution)/shard_map/ppermute | solution.py:512
  42.7 2.3 %copy-start.13 = (f32[96]{0:T(128)S(1)}, f32[96]{0:T(128)}, u32[]{:S(2)}) copy-start(f32[96]{0:T(128)} %bias_ref.3) | copy-start | bytes 1156
  42.7 2.3 %collective-permute-start.13 = (bf16[1,8,48,128]{3,2,1,0:T(8,128)(2,1)S(1)}, bf16[1,8,48,128]{3,2,1,0:T(8,128)(2,1)S(1)}, u32[]{:S(2)}, u32[]{:S(2)}) collective-permute-start(bf16[1,8,48,128]{3,2,1,0:T(8,128)(2,1)S(1)} %shard_map.155), channel_id=1, source_target_pairs={{0,4},{4,0},{8,12},{12,8},{1,5},{5,1},{9,13},{13,9},{2,6},{6,2},{1... | collective-permute-start | bytes 294920 | tf_op jit(solution)/shard_map/ppermute | solution.py:512
  44.9 8.5 %copy-start.2 = (bf16[384,384]{1,0:T(8,128)(2,1)S(1)}, bf16[384,384]{1,0:T(8,128)(2,1)}, u32[]{:S(2)}) copy-start(bf16[384,384]{1,0:T(8,128)(2,1)} %wq_ref.1) | copy-start | bytes 884740
  44.9 8.5 %copy-start.3 = (bf16[384,384]{1,0:T(8,128)(2,1)S(1)}, bf16[384,384]{1,0:T(8,128)(2,1)}, u32[]{:S(2)}) copy-start(bf16[384,384]{1,0:T(8,128)(2,1)} %wk_ref.1) | copy-start | bytes 884740
  44.9 8.5 %copy-start.4 = (bf16[384,384]{1,0:T(8,128)(2,1)S(1)}, bf16[384,384]{1,0:T(8,128)(2,1)}, u32[]{:S(2)}) copy-start(bf16[384,384]{1,0:T(8,128)(2,1)} %wv_ref.1) | copy-start | bytes 884740
  44.9 8.5 %copy-start.5 = (bf16[384,384]{1,0:T(8,128)(2,1)S(1)}, bf16[384,384]{1,0:T(8,128)(2,1)}, u32[]{:S(2)}) copy-start(bf16[384,384]{1,0:T(8,128)(2,1)} %wo_ref.1) | copy-start | bytes 884740
  46.6 2.3 %collective-permute-start.14 = (bf16[288,128]{1,0:T(8,128)(2,1)S(1)}, bf16[288,128]{1,0:T(8,128)(2,1)S(1)}, u32[]{:S(2)}, u32[]{:S(2)}) collective-permute-start(bf16[288,128]{1,0:T(8,128)(2,1)S(1)} %get-tuple-element.22), channel_id=1, source_target_pairs={{0,4},{4,0},{8,12},{12,8},{1,5},{5,1},{9,13},{13,9},{2,6},{6,2},{1... | collective-permute-start | bytes 221192 | tf_op jit(solution)/shard_map/ppermute | solution.py:512
  47.1 4.4 %collective-permute-start.15 = (bf16[288,128]{1,0:T(8,128)(2,1)S(1)}, bf16[288,128]{1,0:T(8,128)(2,1)S(1)}, u32[]{:S(2)}, u32[]{:S(2)}) collective-permute-start(bf16[288,128]{1,0:T(8,128)(2,1)S(1)} %get-tuple-element.23), channel_id=1, source_target_pairs={{0,8},{4,12},{8,0},{12,4},{1,9},{5,13},{9,1},{13,5},{2,10},{6,14},... | collective-permute-start | bytes 221192 | tf_op jit(solution)/shard_map/ppermute | solution.py:512
  48.9 4.5 %collective-permute-start.16 = (bf16[288,128]{1,0:T(8,128)(2,1)S(1)}, bf16[288,128]{1,0:T(8,128)(2,1)S(1)}, u32[]{:S(2)}, u32[]{:S(2)}) collective-permute-start(bf16[288,128]{1,0:T(8,128)(2,1)S(1)} %get-tuple-element.24), channel_id=1, source_target_pairs={{0,12},{4,8},{8,4},{12,0},{1,13},{5,9},{9,5},{13,1},{2,14},{6,10},... | collective-permute-start | bytes 221192 | tf_op jit(solution)/shard_map/ppermute | solution.py:512

commit v3 on v2

--- a/solution.py
+++ b/solution.py
@@ -12,21 +12,30 @@
 GROUP = C // GROUPS
 EPSILON = 1e-06
 VMEM = pl.BlockSpec(memory_space=pltpu.VMEM)
-SMEM = pl.BlockSpec(memory_space=pltpu.SMEM)
 F32 = jnp.float32
 BF16 = jnp.bfloat16
 
 
+class Axis:
+    def __init__(self, name):
+        self.name = name
+
+    def __getitem__(self, _):
+        return lax.axis_index(self.name)
+
+
 def call(body, outs, scratch=()):
     def run(*args):
+        axes = [a for a in args if isinstance(a, Axis)]
+        arrays = args[len(axes) :]
         return pl.pallas_call(
-            body,
+            functools.partial(body, *axes),
             out_shape=outs,
-            in_specs=[SMEM if a.dtype == jnp.int32 else VMEM for a in args],
+            in_specs=[VMEM for _ in arrays],
             out_specs=jax.tree.map(lambda _: VMEM, outs),
             scratch_shapes=scratch,
             compiler_params=pltpu.CompilerParams(vmem_limit_bytes=16 * 1024 * 1024),
-        )(*args)
+        )(*arrays)
 
     return run
 
@@ -542,8 +551,7 @@
     n, frames = lax.axis_size("rows"), lax.axis_size("tm")
     outputs = first_kernel.shape[0]
     plane = rows * cols
-    r = lax.axis_index("rows").astype(jnp.int32).reshape(1)
-    m = lax.axis_index("tm").astype(jnp.int32).reshape(1)
+    r, m = Axis("rows"), Axis("tm")
 
     def taps(kernel):
         return jnp.transpose(kernel, (1, 2, 3, 0, 4)).reshape(3, 3, 3 * outputs, channels)

time: 56.1 us -> 50.8 us (0.906)
  local copies, waits for them, and re-layouts: 5.31 us -> 1.64 us
  Pallas kernels: 19.2 us -> 17.2 us
    unnamed x42 -> x30, local copies, waits for them, and re-layouts: 5.31 us -> 1.64 us
    pallas_call x13, Pallas kernels: 19.2 us -> 17.2 us  [run(): pl.pallas_call(functools.partial(body, *axes), out_shape=outs, in_specs=[...]
  transfers between devices with their start and end apart: 17 -> 17, of which waited for: 9 -> 8; matrix products, arithmetic and copies ran while one was open for 0% -> 0% of each run, Pallas kernels for 16% -> 18%
where the time goes in v3:
time: 50.8 us; the launch traced here: 50.6 us
  Pallas kernels  17.2 us (34%)
  starting transfers between devices  16.7 us (33%)
  waiting for transfers between devices  14.7 us (29%)
  local copies, waits for them, and re-layouts  1.64 us (3%)
    pallas_call x13, Pallas kernels, run(): pl.pallas_call(functools.partial(body, *axes), out_shape=outs, in_specs=[...  17.2 us
    ppermute x17, starting transfers between devices, swapped(): lax.ppermute(value, axis, [(i, partner(i)) for i in range(lax.axis_size(a...  16.7 us
    ppermute x17, waiting for transfers between devices, swapped(): lax.ppermute(value, axis, [(i, partner(i)) for i in range(lax.axis_size(a...  14.7 us
    unnamed x30, local copies, waits for them, and re-layouts  1.64 us
  transfers between devices with their start and end apart: 17, of which 8 were waited for; matrix products, arithmetic and copies ran while one was open for 0% of the time, Pallas kernels for 18%

profile of v3, /device:TPU:0, one launch (start us, length us, event | category | flops | bytes accessed | tf_op | source)
XLA Modules:
  0.0 50.6 jit_solution(434188752410367018)
XLA Ops:
  0.0 5.0 %collective-permute-start.2 = (bf16[1,2,48,384]{3,2,1,0:T(8,128)(2,1)}, bf16[1,2,48,384]{3,2,1,0:T(8,128)(2,1)S(1)}, u32[]{:S(2)}, u32[]{:S(2)}) collective-permute-start(bf16[1,2,48,384]{3,2,1,0:T(8,128)(2,1)} %own_ref.1), channel_id=1, source_target_pairs={{0,3},{1,2},{2,1},{3,0},{4,7},{5,6},{6,5},{7,4},{8,11},{9,10},{10,... | collective-permute-start | bytes 221192 | tf_op jit(solution)/shard_map/ppermute | solution.py:521
  5.1 0.6 %collective-permute-start = (bf16[1,2,48,384]{3,2,1,0:T(8,128)(2,1)}, bf16[1,2,48,384]{3,2,1,0:T(8,128)(2,1)S(1)}, u32[]{:S(2)}, u32[]{:S(2)}) collective-permute-start(bf16[1,2,48,384]{3,2,1,0:T(8,128)(2,1)} %own_ref.1), channel_id=1, source_target_pairs={{0,1},{1,0},{2,3},{3,2},{4,5},{5,4},{6,7},{7,6},{8,9},{9,8},{10,11... | collective-permute-start | bytes 221192 | tf_op jit(solution)/shard_map/ppermute | solution.py:521
  5.6 1.7 %collective-permute-start.3 = (bf16[1,2,48,384]{3,2,1,0:T(8,128)(2,1)}, bf16[1,2,48,384]{3,2,1,0:T(8,128)(2,1)S(1)}, u32[]{:S(2)}, u32[]{:S(2)}) collective-permute-start(bf16[1,2,48,384]{3,2,1,0:T(8,128)(2,1)} %own_ref.1), channel_id=1, source_target_pairs={{0,8},{4,12},{8,0},{12,4},{1,9},{5,13},{9,1},{13,5},{2,10},{6,14},... | collective-permute-start | bytes 221192 | tf_op jit(solution)/shard_map/ppermute | solution.py:521
  7.4 1.5 %copy-done = bf16[96,3,3,3,384]{4,0,3,2,1:T(8,128)(2,1)S(1)} copy-done((bf16[96,3,3,3,384]{4,0,3,2,1:T(8,128)(2,1)S(1)}, bf16[96,3,3,3,384]{4,0,3,2,1:T(8,128)(2,1)}, u32[]{:S(2)}) %copy-start) | copy-done | bytes 1990680
  8.9 0.2 shard_map.145.after_ref.w_ref
  9.1 0.0 copy-start.9
  9.1 0.0 copy-start.10
  9.2 0.0 copy-start.11
  9.2 0.0 copy-start.12
  9.2 0.0 copy-start.13
  9.2 0.0 copy-start.14
  9.2 0.0 copy-start.6
  9.2 0.9 %collective-permute-done.x_ref.one_ref = bf16[1,2,48,384]{3,2,1,0:T(8,128)(2,1)S(1)} collective-permute-done((bf16[1,2,48,384]{3,2,1,0:T(8,128)(2,1)}, bf16[1,2,48,384]{3,2,1,0:T(8,128)(2,1)S(1)}, u32[]{:S(2)}, u32[]{:S(2)}) %collective-permute-start) | collective-permute-done | bytes 73760 | tf_op jit(solution)/shard_map/ppermute | solution.py:521
  10.1 1.5 %collective-permute-start.4 = (bf16[1,2,48,384]{3,2,1,0:T(8,128)(2,1)S(1)}, bf16[1,2,48,384]{3,2,1,0:T(8,128)(2,1)S(1)}, u32[]{:S(2)}, u32[]{:S(2)}) collective-permute-start(bf16[1,2,48,384]{3,2,1,0:T(8,128)(2,1)S(1)} %shard_map.146), channel_id=1, source_target_pairs={{0,8},{4,12},{8,0},{12,4},{1,9},{5,13},{9,1},{13,5},{2,10},{6,14},... | collective-permute-start | bytes 221192 | tf_op jit(solution)/shard_map/ppermute | solution.py:521
  11.6 0.1 select_select_fusion.table_ref
  11.7 2.7 %collective-permute-done.4.across_one_ref = bf16[1,2,48,384]{3,2,1,0:T(8,128)(2,1)S(1)} collective-permute-done((bf16[1,2,48,384]{3,2,1,0:T(8,128)(2,1)S(1)}, bf16[1,2,48,384]{3,2,1,0:T(8,128)(2,1)S(1)}, u32[]{:S(2)}, u32[]{:S(2)}) %collective-permute-start.4) | collective-permute-done | bytes 73760 | tf_op jit(solution)/shard_map/ppermute | solution.py:521
  14.5 0.7 %shard_map.147 = (bf16[1,8,48,384]{3,2,1,0:T(8,128)(2,1)S(1)}, bf16[8,48,384]{2,1,0:T(8,128)(2,1)S(1)}, bf16[2,2,48,384]{3,2,1,0:T(8,128)(2,1)S(1)}) custom-call(bf16[1,2,48,384]{3,2,1,0:T(8,128)(2,1)S(1)} %copy-done.6, bf16[1,2,48,384]{3,2,1,0:T(8,128)(2,1)S(1)} %collective-permute-done.x_ref.one_ref, ...), custom_call_target="tpu_custom_call" | custom-call | tf_op jit(solution)/shard_map/pallas_call | solution.py:31
  15.2 0.1 collective-permute-start.5
  15.3 1.6 %collective-permute-start.7 = (bf16[1,2,48,384]{3,2,1,0:T(8,128)(2,1)S(1)}, bf16[1,2,48,384]{3,2,1,0:T(8,128)(2,1)S(1)}, u32[]{:S(2)}, u32[]{:S(2)}) collective-permute-start(bf16[1,2,48,384]{3,2,1,0:T(8,128)(2,1)S(1)} %collective-permute-done.2.three_ref), channel_id=1, source_target_pairs={{0,8},{4,12},{8,0},{12,4},{1,9},{5,13},{9,1},{13,5},{2,10},{6,14},... | collective-permute-start | bytes 221192 | tf_op jit(solution)/shard_map/ppermute | solution.py:521
  16.8 0.5 %collective-permute-start.6 = (bf16[1,2,48,384]{3,2,1,0:T(8,128)(2,1)S(1)}, bf16[1,2,48,384]{3,2,1,0:T(8,128)(2,1)S(1)}, u32[]{:S(2)}, u32[]{:S(2)}) collective-permute-start(bf16[1,2,48,384]{3,2,1,0:T(8,128)(2,1)S(1)} %collective-permute-done.1.two_ref), channel_id=1, source_target_pairs={{0,8},{4,12},{8,0},{12,4},{1,9},{5,13},{9,1},{13,5},{2,10},{6,14},... | collective-permute-start | bytes 221192 | tf_op jit(solution)/shard_map/ppermute | solution.py:521
  17.4 3.2 %shard_map.148.after_ref.near_total_ref = f32[4,384,384]{2,1,0:T(8,128)S(1)} custom-call(bf16[1,8,48,384]{3,2,1,0:T(8,128)(2,1)S(1)} %get-tuple-element.16.own_ref, bf16[1,8,48,384]{3,2,1,0:T(8,128)(2,1)S(1)} %collective-permute-done.5.mate_ref, bf16[3,3,384,384]{3,2,1,0:T(8,128)(2,1)S(1)} %shard_map.145.after_ref.w_ref), custom_call_target="tpu_custom_call" | custom-call | tf_op jit(solution)/shard_map/pallas_call | solution.py:31
  20.6 0.0 copy-start.7
  20.6 0.9 %collective-permute-done.6.two_ref = bf16[1,2,48,384]{3,2,1,0:T(8,128)(2,1)S(1)} collective-permute-done((bf16[1,2,48,384]{3,2,1,0:T(8,128)(2,1)S(1)}, bf16[1,2,48,384]{3,2,1,0:T(8,128)(2,1)S(1)}, u32[]{:S(2)}, u32[]{:S(2)}) %collective-permute-start.6) | collective-permute-done | bytes 73760 | tf_op jit(solution)/shard_map/ppermute | solution.py:521
  21.5 0.7 %shard_map.149.own_ref = bf16[1,8,48,384]{3,2,1,0:T(8,128)(2,1)S(1)} custom-call(bf16[2,2,48,384]{3,2,1,0:T(8,128)(2,1)S(1)} %get-tuple-element.17.held_ref, bf16[1,2,48,384]{3,2,1,0:T(8,128)(2,1)S(1)} %collective-permute-done.6.two_ref, bf16[1,2,48,384]{3,2,1,0:T(8,128)(2,1)S(1)} %collective-permute-done.7.three_ref, ...), custom_call_target="tpu_custom_call" | custom-call | tf_op jit(solution)/shard_map/pallas_call | solution.py:31
  22.2 0.0 copy-start.1
  22.2 0.1 collective-permute-start.8
  22.3 1.6 %collective-permute-done.8.mate_ref = bf16[1,8,48,384]{3,2,1,0:T(8,128)(2,1)S(1)} collective-permute-done((bf16[1,8,48,384]{3,2,1,0:T(8,128)(2,1)S(1)}, bf16[1,8,48,384]{3,2,1,0:T(8,128)(2,1)S(1)}, u32[]{:S(2)}, u32[]{:S(2)}) %collective-permute-start.8) | collective-permute-done | bytes 294944 | tf_op jit(solution)/shard_map/ppermute | solution.py:521
  23.9 3.0 %shard_map.150 = (bf16[3,8,48,128]{3,2,1,0:T(8,128)(2,1)S(1)}, bf16[2,8,48,128]{3,2,1,0:T(8,128)(2,1)S(1)}, bf16[1,8,48,128]{3,2,1,0:T(8,128)(2,1)S(1)}) custom-call(f32[4,384,384]{2,1,0:T(8,128)S(1)} %shard_map.148.after_ref.near_total_ref, bf16[1,8,48,384]{3,2,1,0:T(8,128)(2,1)S(1)} %shard_map.149.own_ref, ...), custom_call_target="tpu_custom_call" | custom-call | tf_op jit(solution)/shard_map/pallas_call | solution.py:31
  26.9 0.2 collective-permute-start.9
  27.1 3.0 %collective-permute-start.10 = (bf16[2,8,48,128]{3,2,1,0:T(8,128)(2,1)S(1)}, bf16[2,8,48,128]{3,2,1,0:T(8,128)(2,1)S(1)}, u32[]{:S(2)}, u32[]{:S(2)}) collective-permute-start(bf16[2,8,48,128]{3,2,1,0:T(8,128)(2,1)S(1)} %get-tuple-element.19), channel_id=1, source_target_pairs={{0,8},{4,12},{8,0},{12,4},{1,9},{5,13},{9,1},{13,5},{2,10},{6,14},... | collective-permute-start | bytes 589832 | tf_op jit(solution)/shard_map/ppermute | solution.py:521
  30.1 0.0 collective-permute-start.12
  30.1 0.2 shard_map.151.w_ref
  30.3 3.2 %shard_map.152.after_ref.near_total_ref = f32[4,384,384]{2,1,0:T(8,128)S(1)} custom-call(bf16[3,8,48,128]{3,2,1,0:T(8,128)(2,1)S(1)} %get-tuple-element.18.refs_0_.own_ref, bf16[3,8,48,128]{3,2,1,0:T(8,128)(2,1)S(1)} %collective-permute-done.9.mate_ref, bf16[3,3,384,384]{3,2,1,0:T(8,128)(2,1)S(1)} %shard_map.151.w_ref), custom_call_target="tpu_custom_call" | custom-call | tf_op jit(solution)/shard_map/pallas_call | solution.py:31
  33.5 2.3 %collective-permute-done.10.x_ref.own_ref = bf16[2,8,48,128]{3,2,1,0:T(8,128)(2,1)S(1)} collective-permute-done((bf16[2,8,48,128]{3,2,1,0:T(8,128)(2,1)S(1)}, bf16[2,8,48,128]{3,2,1,0:T(8,128)(2,1)S(1)}, u32[]{:S(2)}, u32[]{:S(2)}) %collective-permute-start.10) | collective-permute-done | bytes 196640 | tf_op jit(solution)/shard_map/ppermute | solution.py:521
  35.8 0.1 collective-permute-start.11
  35.9 1.7 %collective-permute-done.12.x_ref.own_last_ref = bf16[1,8,48,128]{3,2,1,0:T(8,128)(2,1)S(1)} collective-permute-done((bf16[1,8,48,128]{3,2,1,0:T(8,128)(2,1)S(1)}, bf16[1,8,48,128]{3,2,1,0:T(8,128)(2,1)S(1)}, u32[]{:S(2)}, u32[]{:S(2)}) %collective-permute-start.12) | collective-permute-done | bytes 98336 | tf_op jit(solution)/shard_map/ppermute | solution.py:521
  37.6 0.0 copy-start.8
  37.6 0.1 collective-permute-start.13
  37.7 2.1 %shard_map.154.total_ref = f32[4,384,384]{2,1,0:T(8,128)S(1)} custom-call(f32[4,384,384]{2,1,0:T(8,128)S(1)} %shard_map.152.after_ref.near_total_ref, bf16[2,8,48,128]{3,2,1,0:T(8,128)(2,1)S(1)} %collective-permute-done.10.x_ref.own_ref, bf16[2,8,48,128]{3,2,1,0:T(8,128)(2,1)S(1)} %collective-permute-done.11.mate_ref, ...), custom_call_target="tpu_custom_call" | custom-call | tf_op jit(solution)/shard_map/pallas_call | solution.py:31
  39.8 0.0 copy-start.2
  39.8 0.0 copy-start.4
  39.8 0.0 copy-start.5
  39.9 1.6 %shard_map.156 = (bf16[288,128]{1,0:T(8,128)(2,1)S(1)}, bf16[288,128]{1,0:T(8,128)(2,1)S(1)}, bf16[288,128]{1,0:T(8,128)(2,1)S(1)}, bf16[288,128]{1,0:T(8,128)(2,1)S(1)}) custom-call(f32[4,384,384]{2,1,0:T(8,128)S(1)} %shard_map.154.total_ref, bf16[2,8,48,128]{3,2,1,0:T(8,128)(2,1)S(1)} %collective-permute-done.10.x_ref.own_ref, ...), custom_call_target="tpu_custom_call" | custom-call | tf_op jit(solution)/shard_map/pallas_call | solution.py:31
  41.4 0.6 %collective-permute-start.14 = (bf16[288,128]{1,0:T(8,128)(2,1)S(1)}, bf16[288,128]{1,0:T(8,128)(2,1)S(1)}, u32[]{:S(2)}, u32[]{:S(2)}) collective-permute-start(bf16[288,128]{1,0:T(8,128)(2,1)S(1)} %get-tuple-element.22), channel_id=1, source_target_pairs={{0,4},{4,0},{8,12},{12,8},{1,5},{5,1},{9,13},{13,9},{2,6},{6,2},{1... | collective-permute-start | bytes 221192 | tf_op jit(solution)/shard_map/ppermute | solution.py:521
  42.0 1.7 %collective-permute-start.15 = (bf16[288,128]{1,0:T(8,128)(2,1)S(1)}, bf16[288,128]{1,0:T(8,128)(2,1)S(1)}, u32[]{:S(2)}, u32[]{:S(2)}) collective-permute-start(bf16[288,128]{1,0:T(8,128)(2,1)S(1)} %get-tuple-element.23), channel_id=1, source_target_pairs={{0,8},{4,12},{8,0},{12,4},{1,9},{5,13},{9,1},{13,5},{2,10},{6,14},... | collective-permute-start | bytes 221192 | tf_op jit(solution)/shard_map/ppermute | solution.py:521
  43.7 2.6 %collective-permute-done.15.p2 = bf16[288,128]{1,0:T(8,128)(2,1)S(1)} collective-permute-done((bf16[288,128]{1,0:T(8,128)(2,1)S(1)}, bf16[288,128]{1,0:T(8,128)(2,1)S(1)}, u32[]{:S(2)}, u32[]{:S(2)}) %collective-permute-start.15) | collective-permute-done | bytes 73760 | tf_op jit(solution)/shard_map/ppermute | solution.py:521
  46.3 1.9 %collective-permute-done.16.p3 = bf16[288,128]{1,0:T(8,128)(2,1)S(1)} collective-permute-done((bf16[288,128]{1,0:T(8,128)(2,1)S(1)}, bf16[288,128]{1,0:T(8,128)(2,1)S(1)}, u32[]{:S(2)}, u32[]{:S(2)}) %collective-permute-start.16) | collective-permute-done | bytes 73760 | tf_op jit(solution)/shard_map/ppermute | solution.py:521
  48.3 2.3 %shard_map.157 = bf16[96,384]{1,0:T(8,128)(2,1)} custom-call(bf16[8,48,384]{2,1,0:T(8,128)(2,1)S(1)} %get-tuple-element.15.raw_ref, bf16[288,128]{1,0:T(8,128)(2,1)S(1)} %get-tuple-element.21.p0, bf16[288,128]{1,0:T(8,128)(2,1)S(1)} %collective-permute-done.14.p1, bf16[288,128]{1,0:T(8,128)(2,1)S(1)} %collective-permute-done.15.p2, ...), custom_call_target="tpu_custom_call" | custom-call | tf_op jit(solution)/shard_map/pallas_call | solution.py:31
  (33 shorter events, 0.1 us)
Async XLA Ops:
  0.0 11.7 %collective-permute-start.2 = (bf16[1,2,48,384]{3,2,1,0:T(8,128)(2,1)}, bf16[1,2,48,384]{3,2,1,0:T(8,128)(2,1)S(1)}, u32[]{:S(2)}, u32[]{:S(2)}) collective-permute-start(bf16[1,2,48,384]{3,2,1,0:T(8,128)(2,1)} %own_ref.1), channel_id=1, source_target_pairs={{0,3},{1,2},{2,1},{3,0},{4,7},{5,6},{6,5},{7,4},{8,11},{9,10},{10,... | collective-permute-start | bytes 221192 | tf_op jit(solution)/shard_map/ppermute | solution.py:521
  5.0 6.7 %collective-permute-start.1 = (bf16[1,2,48,384]{3,2,1,0:T(8,128)(2,1)}, bf16[1,2,48,384]{3,2,1,0:T(8,128)(2,1)S(1)}, u32[]{:S(2)}, u32[]{:S(2)}) collective-permute-start(bf16[1,2,48,384]{3,2,1,0:T(8,128)(2,1)} %own_ref.1), channel_id=1, source_target_pairs={{0,2},{1,3},{2,0},{3,1},{4,6},{5,7},{6,4},{7,5},{8,10},{9,11},{10,... | collective-permute-start | bytes 221192 | tf_op jit(solution)/shard_map/ppermute | solution.py:521
  5.1 5.0 %collective-permute-start = (bf16[1,2,48,384]{3,2,1,0:T(8,128)(2,1)}, bf16[1,2,48,384]{3,2,1,0:T(8,128)(2,1)S(1)}, u32[]{:S(2)}, u32[]{:S(2)}) collective-permute-start(bf16[1,2,48,384]{3,2,1,0:T(8,128)(2,1)} %own_ref.1), channel_id=1, source_target_pairs={{0,1},{1,0},{2,3},{3,2},{4,5},{5,4},{6,7},{7,6},{8,9},{9,8},{10,11... | collective-permute-start | bytes 221192 | tf_op jit(solution)/shard_map/ppermute | solution.py:521
  5.6 6.1 %collective-permute-start.3 = (bf16[1,2,48,384]{3,2,1,0:T(8,128)(2,1)}, bf16[1,2,48,384]{3,2,1,0:T(8,128)(2,1)S(1)}, u32[]{:S(2)}, u32[]{:S(2)}) collective-permute-start(bf16[1,2,48,384]{3,2,1,0:T(8,128)(2,1)} %own_ref.1), channel_id=1, source_target_pairs={{0,8},{4,12},{8,0},{12,4},{1,9},{5,13},{9,1},{13,5},{2,10},{6,14},... | collective-permute-start | bytes 221192 | tf_op jit(solution)/shard_map/ppermute | solution.py:521
  7.3 1.6 %copy-start = (bf16[96,3,3,3,384]{4,0,3,2,1:T(8,128)(2,1)S(1)}, bf16[96,3,3,3,384]{4,0,3,2,1:T(8,128)(2,1)}, u32[]{:S(2)}) copy-start(bf16[96,3,3,3,384]{4,0,3,2,1:T(8,128)(2,1)} %param.18) | copy-start | bytes 5971972
  9.1 2.5 %copy-start.9 = (f32[384]{0:T(512)S(1)}, f32[384]{0:T(512)}, u32[]{:S(2)}) copy-start(f32[384]{0:T(512)} %param.16) | copy-start | bytes 4612
  9.1 2.5 %copy-start.10 = (f32[384]{0:T(512)S(1)}, f32[384]{0:T(512)}, u32[]{:S(2)}) copy-start(f32[384]{0:T(512)} %param.17) | copy-start | bytes 4612
  9.2 2.5 %copy-start.11 = (f32[384]{0:T(512)S(1)}, f32[384]{0:T(512)}, u32[]{:S(2)}) copy-start(f32[384]{0:T(512)} %param.20) | copy-start | bytes 4612
  9.2 2.4 %copy-start.12 = (f32[384]{0:T(512)S(1)}, f32[384]{0:T(512)}, u32[]{:S(2)}) copy-start(f32[384]{0:T(512)} %param.21) | copy-start | bytes 4612
  9.2 2.4 %copy-start.13 = (f32[384]{0:T(512)S(1)}, f32[384]{0:T(512)}, u32[]{:S(2)}) copy-start(f32[384]{0:T(512)} %param.24) | copy-start | bytes 4612
  9.2 2.4 %copy-start.14 = (f32[384]{0:T(512)S(1)}, f32[384]{0:T(512)}, u32[]{:S(2)}) copy-start(f32[384]{0:T(512)} %param.25) | copy-start | bytes 4612
  9.2 5.3 %copy-start.6 = (bf16[1,2,48,384]{3,2,1,0:T(8,128)(2,1)S(1)}, bf16[1,2,48,384]{3,2,1,0:T(8,128)(2,1)}, u32[]{:S(2)}) copy-start(bf16[1,2,48,384]{3,2,1,0:T(8,128)(2,1)} %own_ref.1) | copy-start | bytes 221188
  10.1 4.4 %collective-permute-start.4 = (bf16[1,2,48,384]{3,2,1,0:T(8,128)(2,1)S(1)}, bf16[1,2,48,384]{3,2,1,0:T(8,128)(2,1)S(1)}, u32[]{:S(2)}, u32[]{:S(2)}) collective-permute-start(bf16[1,2,48,384]{3,2,1,0:T(8,128)(2,1)S(1)} %shard_map.146), channel_id=1, source_target_pairs={{0,8},{4,12},{8,0},{12,4},{1,9},{5,13},{9,1},{13,5},{2,10},{6,14},... | collective-permute-start | bytes 221192 | tf_op jit(solution)/shard_map/ppermute | solution.py:521
  15.2 2.2 %collective-permute-start.5 = (bf16[1,8,48,384]{3,2,1,0:T(8,128)(2,1)S(1)}, bf16[1,8,48,384]{3,2,1,0:T(8,128)(2,1)S(1)}, u32[]{:S(2)}, u32[]{:S(2)}) collective-permute-start(bf16[1,8,48,384]{3,2,1,0:T(8,128)(2,1)S(1)} %get-tuple-element.16.own_ref), channel_id=1, source_target_pairs={{0,4},{4,0},{8,12},{12,8},{1,5},{5,1},{9,13},{13,9},{2,6},{6,2},{1... | collective-permute-start | bytes 884744 | tf_op jit(solution)/shard_map/ppermute | solution.py:521
  15.3 5.3 %collective-permute-start.7 = (bf16[1,2,48,384]{3,2,1,0:T(8,128)(2,1)S(1)}, bf16[1,2,48,384]{3,2,1,0:T(8,128)(2,1)S(1)}, u32[]{:S(2)}, u32[]{:S(2)}) collective-permute-start(bf16[1,2,48,384]{3,2,1,0:T(8,128)(2,1)S(1)} %collective-permute-done.2.three_ref), channel_id=1, source_target_pairs={{0,8},{4,12},{8,0},{12,4},{1,9},{5,13},{9,1},{13,5},{2,10},{6,14},... | collective-permute-start | bytes 221192 | tf_op jit(solution)/shard_map/ppermute | solution.py:521
  16.8 4.7 %collective-permute-start.6 = (bf16[1,2,48,384]{3,2,1,0:T(8,128)(2,1)S(1)}, bf16[1,2,48,384]{3,2,1,0:T(8,128)(2,1)S(1)}, u32[]{:S(2)}, u32[]{:S(2)}) collective-permute-start(bf16[1,2,48,384]{3,2,1,0:T(8,128)(2,1)S(1)} %collective-permute-done.1.two_ref), channel_id=1, source_target_pairs={{0,8},{4,12},{8,0},{12,4},{1,9},{5,13},{9,1},{13,5},{2,10},{6,14},... | collective-permute-start | bytes 221192 | tf_op jit(solution)/shard_map/ppermute | solution.py:521
  20.6 3.3 %copy-start.7 = (f32[96]{0:T(128)S(1)}, f32[96]{0:T(128)}, u32[]{:S(2)}) copy-start(f32[96]{0:T(128)} %bias_ref.2) | copy-start | bytes 1156
  22.2 7.9 %copy-start.1 = (bf16[96,3,3,3,384]{4,0,3,2,1:T(8,128)(2,1)S(1)}, bf16[96,3,3,3,384]{4,0,3,2,1:T(8,128)(2,1)}, u32[]{:S(2)}) copy-start(bf16[96,3,3,3,384]{4,0,3,2,1:T(8,128)(2,1)} %param.22) | copy-start | bytes 5971972
  22.2 1.6 %collective-permute-start.8 = (bf16[1,8,48,384]{3,2,1,0:T(8,128)(2,1)S(1)}, bf16[1,8,48,384]{3,2,1,0:T(8,128)(2,1)S(1)}, u32[]{:S(2)}, u32[]{:S(2)}) collective-permute-start(bf16[1,8,48,384]{3,2,1,0:T(8,128)(2,1)S(1)} %shard_map.149.own_ref), channel_id=1, source_target_pairs={{0,4},{4,0},{8,12},{12,8},{1,5},{5,1},{9,13},{13,9},{2,6},{6,2},{1... | collective-permute-start | bytes 884744 | tf_op jit(solution)/shard_map/ppermute | solution.py:521
  26.9 3.4 %collective-permute-start.9 = (bf16[3,8,48,128]{3,2,1,0:T(8,128)(2,1)S(1)}, bf16[3,8,48,128]{3,2,1,0:T(8,128)(2,1)S(1)}, u32[]{:S(2)}, u32[]{:S(2)}) collective-permute-start(bf16[3,8,48,128]{3,2,1,0:T(8,128)(2,1)S(1)} %get-tuple-element.18.refs_0_.own_ref), channel_id=1, source_target_pairs={{0,4},{4,0},{8,12},{12,8},{1,5},{5,1},{9,13},{13,9},{2,6},{6,2},{1... | collective-permute-start | bytes 884744 | tf_op jit(solution)/shard_map/ppermute | solution.py:521
  27.1 8.7 %collective-permute-start.10 = (bf16[2,8,48,128]{3,2,1,0:T(8,128)(2,1)S(1)}, bf16[2,8,48,128]{3,2,1,0:T(8,128)(2,1)S(1)}, u32[]{:S(2)}, u32[]{:S(2)}) collective-permute-start(bf16[2,8,48,128]{3,2,1,0:T(8,128)(2,1)S(1)} %get-tuple-element.19), channel_id=1, source_target_pairs={{0,8},{4,12},{8,0},{12,4},{1,9},{5,13},{9,1},{13,5},{2,10},{6,14},... | collective-permute-start | bytes 589832 | tf_op jit(solution)/shard_map/ppermute | solution.py:521
  30.1 7.5 %collective-permute-start.12 = (bf16[1,8,48,128]{3,2,1,0:T(8,128)(2,1)S(1)}, bf16[1,8,48,128]{3,2,1,0:T(8,128)(2,1)S(1)}, u32[]{:S(2)}, u32[]{:S(2)}) collective-permute-start(bf16[1,8,48,128]{3,2,1,0:T(8,128)(2,1)S(1)} %get-tuple-element.20), channel_id=1, source_target_pairs={{0,8},{4,12},{8,0},{12,4},{1,9},{5,13},{9,1},{13,5},{2,10},{6,14},... | collective-permute-start | bytes 294920 | tf_op jit(solution)/shard_map/ppermute | solution.py:521
  35.8 1.9 %collective-permute-start.11 = (bf16[2,8,48,128]{3,2,1,0:T(8,128)(2,1)S(1)}, bf16[2,8,48,128]{3,2,1,0:T(8,128)(2,1)S(1)}, u32[]{:S(2)}, u32[]{:S(2)}) collective-permute-start(bf16[2,8,48,128]{3,2,1,0:T(8,128)(2,1)S(1)} %shard_map.153), channel_id=1, source_target_pairs={{0,4},{4,0},{8,12},{12,8},{1,5},{5,1},{9,13},{13,9},{2,6},{6,2},{1... | collective-permute-start | bytes 589832 | tf_op jit(solution)/shard_map/ppermute | solution.py:521
  37.6 2.2 %copy-start.8 = (f32[96]{0:T(128)S(1)}, f32[96]{0:T(128)}, u32[]{:S(2)}) copy-start(f32[96]{0:T(128)} %bias_ref.3) | copy-start | bytes 1156
  37.6 2.2 %collective-permute-start.13 = (bf16[1,8,48,128]{3,2,1,0:T(8,128)(2,1)S(1)}, bf16[1,8,48,128]{3,2,1,0:T(8,128)(2,1)S(1)}, u32[]{:S(2)}, u32[]{:S(2)}) collective-permute-start(bf16[1,8,48,128]{3,2,1,0:T(8,128)(2,1)S(1)} %shard_map.155), channel_id=1, source_target_pairs={{0,4},{4,0},{8,12},{12,8},{1,5},{5,1},{9,13},{13,9},{2,6},{6,2},{1... | collective-permute-start | bytes 294920 | tf_op jit(solution)/shard_map/ppermute | solution.py:521
  39.8 8.5 %copy-start.2 = (bf16[384,384]{1,0:T(8,128)(2,1)S(1)}, bf16[384,384]{1,0:T(8,128)(2,1)}, u32[]{:S(2)}) copy-start(bf16[384,384]{1,0:T(8,128)(2,1)} %wq_ref.1) | copy-start | bytes 884740
  39.8 8.5 %copy-start.3 = (bf16[384,384]{1,0:T(8,128)(2,1)S(1)}, bf16[384,384]{1,0:T(8,128)(2,1)}, u32[]{:S(2)}) copy-start(bf16[384,384]{1,0:T(8,128)(2,1)} %wk_ref.1) | copy-start | bytes 884740
  39.8 8.5 %copy-start.4 = (bf16[384,384]{1,0:T(8,128)(2,1)S(1)}, bf16[384,384]{1,0:T(8,128)(2,1)}, u32[]{:S(2)}) copy-start(bf16[384,384]{1,0:T(8,128)(2,1)} %wv_ref.1) | copy-start | bytes 884740
  39.8 8.5 %copy-start.5 = (bf16[384,384]{1,0:T(8,128)(2,1)S(1)}, bf16[384,384]{1,0:T(8,128)(2,1)}, u32[]{:S(2)}) copy-start(bf16[384,384]{1,0:T(8,128)(2,1)} %wo_ref.1) | copy-start | bytes 884740
  41.4 2.3 %collective-permute-start.14 = (bf16[288,128]{1,0:T(8,128)(2,1)S(1)}, bf16[288,128]{1,0:T(8,128)(2,1)S(1)}, u32[]{:S(2)}, u32[]{:S(2)}) collective-permute-start(bf16[288,128]{1,0:T(8,128)(2,1)S(1)} %get-tuple-element.22), channel_id=1, source_target_pairs={{0,4},{4,0},{8,12},{12,8},{1,5},{5,1},{9,13},{13,9},{2,6},{6,2},{1... | collective-permute-start | bytes 221192 | tf_op jit(solution)/shard_map/ppermute | solution.py:521
  42.0 4.4 %collective-permute-start.15 = (bf16[288,128]{1,0:T(8,128)(2,1)S(1)}, bf16[288,128]{1,0:T(8,128)(2,1)S(1)}, u32[]{:S(2)}, u32[]{:S(2)}) collective-permute-start(bf16[288,128]{1,0:T(8,128)(2,1)S(1)} %get-tuple-element.23), channel_id=1, source_target_pairs={{0,8},{4,12},{8,0},{12,4},{1,9},{5,13},{9,1},{13,5},{2,10},{6,14},... | collective-permute-start | bytes 221192 | tf_op jit(solution)/shard_map/ppermute | solution.py:521
  43.7 4.5 %collective-permute-start.16 = (bf16[288,128]{1,0:T(8,128)(2,1)S(1)}, bf16[288,128]{1,0:T(8,128)(2,1)S(1)}, u32[]{:S(2)}, u32[]{:S(2)}) collective-permute-start(bf16[288,128]{1,0:T(8,128)(2,1)S(1)} %get-tuple-element.24), channel_id=1, source_target_pairs={{0,12},{4,8},{8,4},{12,0},{1,13},{5,9},{9,5},{13,1},{2,14},{6,10},... | collective-permute-start | bytes 221192 | tf_op jit(solution)/shard_map/ppermute | solution.py:521

commit v4 on v3

--- a/solution.py
+++ b/solution.py
@@ -98,8 +98,11 @@
     far_ref[...] = x_ref[0, (rows - 1) * odd]
 
 
-def frame_norm(r_ref, blocks, table_ref, out_ref):
+def own_frame(r_ref, own_ref, one_ref, two_ref, three_ref, table_ref, after_ref, out_ref, raw_ref):
+    blocks = [ref[0] for ref in (own_ref, one_ref, two_ref, three_ref)]
     rows, cols, channels = blocks[0].shape
+    for k, block in enumerate(blocks):
+        raw_ref[pl.ds((r_ref[0] ^ k) * rows, rows)] = block
     wide = [block.astype(F32).reshape(rows * cols, channels) for block in blocks]
     count = len(wide) * rows * cols * GROUP
     mean = group_sums(eight(sum(jnp.sum(x, axis=0, keepdims=True) for x in wide)))[0:1] / count
@@ -110,22 +113,6 @@
     for k, x in enumerate(wide):
         value = silu((x - mean) * scale + shift).astype(BF16)
         out_ref[0, pl.ds((r_ref[0] ^ k) * rows, rows)] = value.reshape(rows, cols, channels)
-
-
-def own_frame(
-    r_ref, own_ref, one_ref, two_ref, three_ref, across_ref, across_one_ref, table_ref, after_ref, out_ref, raw_ref, held_ref
-):
-    blocks = [ref[0] for ref in (own_ref, one_ref, two_ref, three_ref)]
-    rows = blocks[0].shape[0]
-    for k, block in enumerate(blocks):
-        raw_ref[pl.ds((r_ref[0] ^ k) * rows, rows)] = block
-    held_ref[0] = across_ref[0]
-    held_ref[1] = across_one_ref[0]
-    frame_norm(r_ref, blocks, table_ref, out_ref)
-
-
-def across_frame(r_ref, held_ref, two_ref, three_ref, table_ref, after_ref, out_ref):
-    frame_norm(r_ref, [held_ref[0], held_ref[1], two_ref[0], three_ref[0]], table_ref, out_ref)
 
 
 def eight(row):
@@ -205,7 +192,6 @@
 def frame_taps(total_ref, base_ref, a_ref, held, w_ref, lanes=slice(None)):
     frames, plane, _ = total_ref.shape
     _, padded, cols, channels = a_ref.shape
-    written = []
     for t in range(frames):
         total = None if base_ref is None else base_ref[t]
         terms = [(g, 2 - (t - f)) for g, f in enumerate(held) if 0 <= t - f <= 2]
@@ -216,12 +202,7 @@
             weight = jnp.concatenate([w_ref[i, j, :, lanes] for j in range(3)], axis=1)
             term = lax.dot_general(window, weight, (((1,), (1,)), ((), ())), preferred_element_type=F32)
             total = term if total is None else total + term
-        if terms:
-            total_ref[t] = total
-            written.append(t)
-        elif base_ref is None:
-            total_ref[t] = jnp.zeros(total_ref.shape[1:], F32)
-    return written
+        total_ref[t] = jnp.zeros(total_ref.shape[1:], F32) if total is None else total
 
 
 def lay_out(m_ref, own_ref, mate_ref, pair):
@@ -235,21 +216,29 @@
 
 def first_conv_near(m_ref, own_ref, mate_ref, w_ref, total_ref, pair):
     lay_out(m_ref, own_ref, mate_ref, pair)
-    on_half(m_ref, False, lambda h: frame_taps(total_ref, None, pair, (2 * h, 2 * h + 1), w_ref) and None)
+    on_half(m_ref, False, lambda h: frame_taps(total_ref, None, pair, (2 * h, 2 * h + 1), w_ref))
+
+
+def add_frame(m_ref, flip, a_ref, base_ref, w_ref, total_ref, rimmed):
+    height = a_ref.shape[1]
+    rimmed[0, 0] = jnp.zeros(rimmed.shape[2:], BF16)
+    rimmed[0, 1 : height + 1] = a_ref[0]
+    rimmed[0, height + 1] = jnp.zeros(rimmed.shape[2:], BF16)
+    for f in range(total_ref.shape[0]):
+
+        @pl.when((m_ref[0] ^ flip) == f)
+        def _(f=f):
+            frame_taps(total_ref, base_ref, rimmed, (f,), w_ref)
+
+
+def first_conv_across(m_ref, near_total_ref, a_ref, w_ref, total_ref, rimmed):
+    add_frame(m_ref, 2, a_ref, near_total_ref, w_ref, total_ref, rimmed)
 
 
 def first_conv_rest(
-    m_ref, near_total_ref, own_ref, mate_ref, w_ref, bias_ref, table_ref, out_ref, early_ref, late_ref, pair, total, conv1, rows8
+    m_ref, base_ref, a_ref, w_ref, bias_ref, table_ref, out_ref, early_ref, late_ref, rimmed, total, conv1, rows8
 ):
-    lay_out(m_ref, own_ref, mate_ref, pair)
-
-    def other(h):
-        written = frame_taps(total, near_total_ref, pair, (2 * h, 2 * h + 1), w_ref)
-        for t in range(total.shape[0]):
-            if t not in written:
-                total[t] = near_total_ref[t]
-
-    on_half(m_ref, True, other)
+    add_frame(m_ref, 3, a_ref, base_ref, w_ref, total, rimmed)
     frames, height, cols, outputs = conv1.shape
     count = height * cols * GROUP
     rows8[...] = jnp.zeros(rows8.shape, F32)
@@ -586,23 +575,22 @@
 
         height = n * rows
         one, two, three = (over_rows(features, k) for k in (1, 2, 3))
-        across, across_one = over_x(features), over_x(held_until(one, weights1))
         frame = struct((1, height, cols, channels))
-        active1, raw, held = call(
-            own_frame, (frame, struct((height, cols, channels)), struct((2, rows, cols, channels)))
-        )(r, features, one, two, three, across, across_one, table, weights1)
-        across_two, across_three = over_x(two), over_x(three)
-        mate = over_core(active1)
-        pair = pltpu.VMEM((2, height + 2, cols, channels), BF16)
+        active1, raw = call(own_frame, (frame, struct((height, cols, channels))))(
+            r, features, one, two, three, table, weights1
+        )
+        across, mate = over_x(active1), over_core(active1)
+        pair, rimmed = (pltpu.VMEM((k, height + 2, cols, channels), BF16) for k in (2, 1))
         tall = struct((frames, n * plane, 3 * lanes), F32)
         tall_scratch = pltpu.VMEM(tall.shape, F32)
         near_total = call(first_conv_near, tall, (pair,))(m, active1, mate, weights1)
-        across = call(across_frame, frame)(r, held, across_two, across_three, table, near_total)
+        beside = over_core(held_until(across, near_total))
+        across_total = call(first_conv_across, tall, (rimmed,))(m, near_total, across, weights1)
         active2, early, late = call(
             first_conv_rest,
             tuple(struct((k, height, cols, 128)) for k in (frames - 1, 2, frames - 3)),
-            (pair, tall_scratch, pltpu.VMEM((frames, height, cols, outputs), BF16), stats_scratch),
-        )(m, near_total, across, over_core(across), weights1, first_bias, table)
+            (rimmed, tall_scratch, pltpu.VMEM((frames, height, cols, outputs), BF16), stats_scratch),
+        )(m, across_total, beside, weights1, first_bias, table)
 
         weights2 = call(load, loaded)(taps(second_kernel), active2)
         early, late = over_x(early), over_x(late)

time: 50.8 us -> 49.8 us (0.980)
  starting transfers between devices: 16.7 us -> 12.9 us
  waiting for transfers between devices: 14.7 us -> 17 us
  other arithmetic: 0.1 us -> 0.86 us
    ppermute x17 -> x14, starting transfers between devices: 16.7 us -> 12.9 us  [swapped(): lax.ppermute(value, axis, [(i, partner(i)) for i in range(lax.axis_size(a...]
    ppermute x17 -> x14, waiting for transfers between devices: 14.7 us -> 17 us  [swapped(): lax.ppermute(value, axis, [(i, partner(i)) for i in range(lax.axis_size(a...]
    select_n x1, other arithmetic: 0.08 us -> 0.85 us  [per_device(): table = jnp.where(row == i, vector[None, :], table)]
    unnamed x30 -> x18, local copies, waits for them, and re-layouts: 1.64 us -> 1.6 us
  transfers between devices with their start and end apart: 17 -> 14, of which waited for: 8 -> 8; matrix products, arithmetic and copies ran while one was open for 0% -> 2% of each run, Pallas kernels for 18% -> 20%
where the time goes in v4:
time: 49.8 us; the launch traced here: 49.6 us
  Pallas kernels  17.1 us (34%)
  waiting for transfers between devices  17 us (34%)
  starting transfers between devices  12.9 us (26%)
  local copies, waits for them, and re-layouts  1.6 us (3%)
  other arithmetic  0.86 us (2%)
    pallas_call x13, Pallas kernels, run(): pl.pallas_call(functools.partial(body, *axes), out_shape=outs, in_specs=[...  17.1 us
    ppermute x14, waiting for transfers between devices, swapped(): lax.ppermute(value, axis, [(i, partner(i)) for i in range(lax.axis_size(a...  17 us
    ppermute x14, starting transfers between devices, swapped(): lax.ppermute(value, axis, [(i, partner(i)) for i in range(lax.axis_size(a...  12.9 us
    unnamed x18, local copies, waits for them, and re-layouts  1.6 us
  transfers between devices with their start and end apart: 14, of which 8 were waited for; matrix products, arithmetic and copies ran while one was open for 2% of the time, Pallas kernels for 20%

profile of v4, /device:TPU:0, one launch (start us, length us, event | category | flops | bytes accessed | tf_op | source)
XLA Modules:
  0.0 49.6 jit_solution(16566410181180200503)
XLA Ops:
  0.0 4.0 %collective-permute-start.1 = (bf16[1,2,48,384]{3,2,1,0:T(8,128)(2,1)}, bf16[1,2,48,384]{3,2,1,0:T(8,128)(2,1)S(1)}, u32[]{:S(2)}, u32[]{:S(2)}) collective-permute-start(bf16[1,2,48,384]{3,2,1,0:T(8,128)(2,1)} %own_ref.1), channel_id=1, source_target_pairs={{0,2},{1,3},{2,0},{3,1},{4,6},{5,7},{6,4},{7,5},{8,10},{9,11},{10,... | collective-permute-start | bytes 221192 | tf_op jit(solution)/shard_map/ppermute | solution.py:510
  4.0 1.6 %collective-permute-start = (bf16[1,2,48,384]{3,2,1,0:T(8,128)(2,1)}, bf16[1,2,48,384]{3,2,1,0:T(8,128)(2,1)S(1)}, u32[]{:S(2)}, u32[]{:S(2)}) collective-permute-start(bf16[1,2,48,384]{3,2,1,0:T(8,128)(2,1)} %own_ref.1), channel_id=1, source_target_pairs={{0,1},{1,0},{2,3},{3,2},{4,5},{5,4},{6,7},{7,6},{8,9},{9,8},{10,11... | collective-permute-start | bytes 221192 | tf_op jit(solution)/shard_map/ppermute | solution.py:510
  5.6 0.0 collective-permute-start.2
  5.6 0.8 %select_select_fusion.table_ref = f32[8,384]{1,0:T(8,128)S(1)} fusion(f32[384]{0:T(512)} %param.16, f32[384]{0:T(512)} %param.17, f32[384]{0:T(512)} %param.20, f32[384]{0:T(512)} %param.21, f32[384]{0:T(512)} %param.24, f32[384]{0:T(512)} %param.25, pred[8]{0:T(512)(128)(4,1)S(1)} %get-tuple-element.23, pred[8]{0:T(512)(128)(4,1)S(1)} %get-tuple-element.24, ...), kind=kLoop, calls=%fused_computation | loop fusion | flops 18432 | bytes 21552 | tf_op jit(solution)/shard_map/jit(_where)/select_n | solution.py:551
  6.5 1.5 %copy-done = bf16[96,3,3,3,384]{4,0,3,2,1:T(8,128)(2,1)S(1)} copy-done((bf16[96,3,3,3,384]{4,0,3,2,1:T(8,128)(2,1)S(1)}, bf16[96,3,3,3,384]{4,0,3,2,1:T(8,128)(2,1)}, u32[]{:S(2)}) %copy-start) | copy-done | bytes 1990680
  8.0 0.2 shard_map.145.after_ref.w_ref
  8.3 0.0 collective-permute-done.1.two_ref
  8.3 0.3 collective-permute-done.one_ref
  8.6 3.4 %collective-permute-done.2.three_ref = bf16[1,2,48,384]{3,2,1,0:T(8,128)(2,1)S(1)} collective-permute-done((bf16[1,2,48,384]{3,2,1,0:T(8,128)(2,1)}, bf16[1,2,48,384]{3,2,1,0:T(8,128)(2,1)S(1)}, u32[]{:S(2)}, u32[]{:S(2)}) %collective-permute-start.2) | collective-permute-done | bytes 73760 | tf_op jit(solution)/shard_map/ppermute | solution.py:510
  12.0 0.7 %shard_map.146 = (bf16[1,8,48,384]{3,2,1,0:T(8,128)(2,1)S(1)}, bf16[8,48,384]{2,1,0:T(8,128)(2,1)S(1)}) custom-call(bf16[1,2,48,384]{3,2,1,0:T(8,128)(2,1)S(1)} %copy-done.6, bf16[1,2,48,384]{3,2,1,0:T(8,128)(2,1)S(1)} %collective-permute-done.one_ref, bf16[1,2,48,384]{3,2,1,0:T(8,128)(2,1)S(1)} %collective-permute-done.1.two_ref, ...), custom_call_target="tpu_custom_call" | custom-call | tf_op jit(solution)/shard_map/pallas_call | solution.py:31
  12.7 0.1 collective-permute-start.3
  12.8 1.6 %collective-permute-start.4 = (bf16[1,8,48,384]{3,2,1,0:T(8,128)(2,1)S(1)}, bf16[1,8,48,384]{3,2,1,0:T(8,128)(2,1)S(1)}, u32[]{:S(2)}, u32[]{:S(2)}) collective-permute-start(bf16[1,8,48,384]{3,2,1,0:T(8,128)(2,1)S(1)} %get-tuple-element.15.own_ref), channel_id=1, source_target_pairs={{0,8},{4,12},{8,0},{12,4},{1,9},{5,13},{9,1},{13,5},{2,10},{6,14},... | collective-permute-start | bytes 884744 | tf_op jit(solution)/shard_map/ppermute | solution.py:510
  14.3 0.0 collective-permute-done.3.mate_ref
  14.4 3.2 %shard_map.147.near_total_ref.after_ref = f32[4,384,384]{2,1,0:T(8,128)S(1)} custom-call(bf16[1,8,48,384]{3,2,1,0:T(8,128)(2,1)S(1)} %get-tuple-element.15.own_ref, bf16[1,8,48,384]{3,2,1,0:T(8,128)(2,1)S(1)} %collective-permute-done.3.mate_ref, bf16[3,3,384,384]{3,2,1,0:T(8,128)(2,1)S(1)} %shard_map.145.after_ref.w_ref), custom_call_target="tpu_custom_call" | custom-call | tf_op jit(solution)/shard_map/pallas_call | solution.py:31
  17.5 4.7 %collective-permute-done.4.a_ref.x_ref = bf16[1,8,48,384]{3,2,1,0:T(8,128)(2,1)S(1)} collective-permute-done((bf16[1,8,48,384]{3,2,1,0:T(8,128)(2,1)S(1)}, bf16[1,8,48,384]{3,2,1,0:T(8,128)(2,1)S(1)}, u32[]{:S(2)}, u32[]{:S(2)}) %collective-permute-start.4) | collective-permute-done | bytes 294944 | tf_op jit(solution)/shard_map/ppermute | solution.py:510
  22.2 0.0 copy-start.7
  22.2 0.1 collective-permute-start.5
  22.3 1.3 %shard_map.148.base_ref = f32[4,384,384]{2,1,0:T(8,128)S(1)} custom-call(f32[4,384,384]{2,1,0:T(8,128)S(1)} %shard_map.147.near_total_ref.after_ref, bf16[1,8,48,384]{3,2,1,0:T(8,128)(2,1)S(1)} %collective-permute-done.4.a_ref.x_ref, bf16[3,3,384,384]{3,2,1,0:T(8,128)(2,1)S(1)} %shard_map.145.after_ref.w_ref), custom_call_target="tpu_custom_call" | custom-call | tf_op jit(solution)/shard_map/pallas_call | solution.py:31
  23.6 0.0 copy-start.1
  23.6 0.3 collective-permute-done.5.a_ref
  23.9 0.0 copy-done.7
  23.9 2.2 %shard_map.150 = (bf16[3,8,48,128]{3,2,1,0:T(8,128)(2,1)S(1)}, bf16[2,8,48,128]{3,2,1,0:T(8,128)(2,1)S(1)}, bf16[1,8,48,128]{3,2,1,0:T(8,128)(2,1)S(1)}) custom-call(f32[4,384,384]{2,1,0:T(8,128)S(1)} %shard_map.148.base_ref, bf16[1,8,48,384]{3,2,1,0:T(8,128)(2,1)S(1)} %collective-permute-done.5.a_ref, ...), custom_call_target="tpu_custom_call" | custom-call | tf_op jit(solution)/shard_map/pallas_call | solution.py:31
  26.1 0.6 %collective-permute-start.6 = (bf16[3,8,48,128]{3,2,1,0:T(8,128)(2,1)S(1)}, bf16[3,8,48,128]{3,2,1,0:T(8,128)(2,1)S(1)}, u32[]{:S(2)}, u32[]{:S(2)}) collective-permute-start(bf16[3,8,48,128]{3,2,1,0:T(8,128)(2,1)S(1)} %get-tuple-element.16.refs_0_.own_ref), channel_id=1, source_target_pairs={{0,4},{4,0},{8,12},{12,8},{1,5},{5,1},{9,13},{13,9},{2,6},{6,2},{1... | collective-permute-start | bytes 884744 | tf_op jit(solution)/shard_map/ppermute | solution.py:510
  26.8 2.5 %collective-permute-start.7 = (bf16[2,8,48,128]{3,2,1,0:T(8,128)(2,1)S(1)}, bf16[2,8,48,128]{3,2,1,0:T(8,128)(2,1)S(1)}, u32[]{:S(2)}, u32[]{:S(2)}) collective-permute-start(bf16[2,8,48,128]{3,2,1,0:T(8,128)(2,1)S(1)} %get-tuple-element.17), channel_id=1, source_target_pairs={{0,8},{4,12},{8,0},{12,4},{1,9},{5,13},{9,1},{13,5},{2,10},{6,14},... | collective-permute-start | bytes 589832 | tf_op jit(solution)/shard_map/ppermute | solution.py:510
  29.2 0.0 collective-permute-start.9
  29.3 0.2 shard_map.151.w_ref
  29.5 0.0 collective-permute-done.6.mate_ref
  29.5 3.0 %shard_map.152.after_ref.near_total_ref = f32[4,384,384]{2,1,0:T(8,128)S(1)} custom-call(bf16[3,8,48,128]{3,2,1,0:T(8,128)(2,1)S(1)} %get-tuple-element.16.refs_0_.own_ref, bf16[3,8,48,128]{3,2,1,0:T(8,128)(2,1)S(1)} %collective-permute-done.6.mate_ref, bf16[3,3,384,384]{3,2,1,0:T(8,128)(2,1)S(1)} %shard_map.151.w_ref), custom_call_target="tpu_custom_call" | custom-call | tf_op jit(solution)/shard_map/pallas_call | solution.py:31
  32.5 2.4 %collective-permute-done.7.x_ref.own_ref = bf16[2,8,48,128]{3,2,1,0:T(8,128)(2,1)S(1)} collective-permute-done((bf16[2,8,48,128]{3,2,1,0:T(8,128)(2,1)S(1)}, bf16[2,8,48,128]{3,2,1,0:T(8,128)(2,1)S(1)}, u32[]{:S(2)}, u32[]{:S(2)}) %collective-permute-start.7) | collective-permute-done | bytes 196640 | tf_op jit(solution)/shard_map/ppermute | solution.py:510
  34.9 0.1 collective-permute-start.8
  35.0 1.5 %collective-permute-done.9.x_ref.own_last_ref = bf16[1,8,48,128]{3,2,1,0:T(8,128)(2,1)S(1)} collective-permute-done((bf16[1,8,48,128]{3,2,1,0:T(8,128)(2,1)S(1)}, bf16[1,8,48,128]{3,2,1,0:T(8,128)(2,1)S(1)}, u32[]{:S(2)}, u32[]{:S(2)}) %collective-permute-start.9) | collective-permute-done | bytes 98336 | tf_op jit(solution)/shard_map/ppermute | solution.py:510
  36.5 0.0 copy-start.8
  36.5 0.1 collective-permute-start.10
  36.6 0.0 collective-permute-done.8.mate_ref
  36.6 2.1 %shard_map.154.total_ref = f32[4,384,384]{2,1,0:T(8,128)S(1)} custom-call(f32[4,384,384]{2,1,0:T(8,128)S(1)} %shard_map.152.after_ref.near_total_ref, bf16[2,8,48,128]{3,2,1,0:T(8,128)(2,1)S(1)} %collective-permute-done.7.x_ref.own_ref, bf16[2,8,48,128]{3,2,1,0:T(8,128)(2,1)S(1)} %collective-permute-done.8.mate_ref, ...), custom_call_target="tpu_custom_call" | custom-call | tf_op jit(solution)/shard_map/pallas_call | solution.py:31
  38.7 0.0 copy-start.2
  38.7 0.0 copy-start.3
  38.7 0.0 copy-start.4
  38.7 0.0 copy-start.5
  38.7 0.0 collective-permute-done.10.mate_last_ref
  38.8 1.8 %shard_map.156 = (bf16[288,128]{1,0:T(8,128)(2,1)S(1)}, bf16[288,128]{1,0:T(8,128)(2,1)S(1)}, bf16[288,128]{1,0:T(8,128)(2,1)S(1)}, bf16[288,128]{1,0:T(8,128)(2,1)S(1)}) custom-call(f32[4,384,384]{2,1,0:T(8,128)S(1)} %shard_map.154.total_ref, bf16[2,8,48,128]{3,2,1,0:T(8,128)(2,1)S(1)} %collective-permute-done.7.x_ref.own_ref, ...), custom_call_target="tpu_custom_call" | custom-call | tf_op jit(solution)/shard_map/pallas_call | solution.py:31
  40.6 0.6 %collective-permute-start.11 = (bf16[288,128]{1,0:T(8,128)(2,1)S(1)}, bf16[288,128]{1,0:T(8,128)(2,1)S(1)}, u32[]{:S(2)}, u32[]{:S(2)}) collective-permute-start(bf16[288,128]{1,0:T(8,128)(2,1)S(1)} %get-tuple-element.20), channel_id=1, source_target_pairs={{0,4},{4,0},{8,12},{12,8},{1,5},{5,1},{9,13},{13,9},{2,6},{6,2},{1... | collective-permute-start | bytes 221192 | tf_op jit(solution)/shard_map/ppermute | solution.py:510
  41.1 1.7 %collective-permute-start.12 = (bf16[288,128]{1,0:T(8,128)(2,1)S(1)}, bf16[288,128]{1,0:T(8,128)(2,1)S(1)}, u32[]{:S(2)}, u32[]{:S(2)}) collective-permute-start(bf16[288,128]{1,0:T(8,128)(2,1)S(1)} %get-tuple-element.21), channel_id=1, source_target_pairs={{0,8},{4,12},{8,0},{12,4},{1,9},{5,13},{9,1},{13,5},{2,10},{6,14},... | collective-permute-start | bytes 221192 | tf_op jit(solution)/shard_map/ppermute | solution.py:510
  42.8 0.0 collective-permute-start.13
  42.8 0.0 collective-permute-done.11.p1
  42.8 2.6 %collective-permute-done.12.p2 = bf16[288,128]{1,0:T(8,128)(2,1)S(1)} collective-permute-done((bf16[288,128]{1,0:T(8,128)(2,1)S(1)}, bf16[288,128]{1,0:T(8,128)(2,1)S(1)}, u32[]{:S(2)}, u32[]{:S(2)}) %collective-permute-start.12) | collective-permute-done | bytes 73760 | tf_op jit(solution)/shard_map/ppermute | solution.py:510
  45.5 1.8 %collective-permute-done.13.p3 = bf16[288,128]{1,0:T(8,128)(2,1)S(1)} collective-permute-done((bf16[288,128]{1,0:T(8,128)(2,1)S(1)}, bf16[288,128]{1,0:T(8,128)(2,1)S(1)}, u32[]{:S(2)}, u32[]{:S(2)}) %collective-permute-start.13) | collective-permute-done | bytes 73760 | tf_op jit(solution)/shard_map/ppermute | solution.py:510
  47.3 2.3 %shard_map.157 = bf16[96,384]{1,0:T(8,128)(2,1)} custom-call(bf16[8,48,384]{2,1,0:T(8,128)(2,1)S(1)} %get-tuple-element.14.raw_ref, bf16[288,128]{1,0:T(8,128)(2,1)S(1)} %get-tuple-element.19.p0, bf16[288,128]{1,0:T(8,128)(2,1)S(1)} %collective-permute-done.11.p1, bf16[288,128]{1,0:T(8,128)(2,1)S(1)} %collective-permute-done.12.p2, ...), custom_call_target="tpu_custom_call" | custom-call | tf_op jit(solution)/shard_map/pallas_call | solution.py:31
  (15 shorter events, 0.1 us)
Async XLA Ops:
  0.0 8.3 %collective-permute-start.1 = (bf16[1,2,48,384]{3,2,1,0:T(8,128)(2,1)}, bf16[1,2,48,384]{3,2,1,0:T(8,128)(2,1)S(1)}, u32[]{:S(2)}, u32[]{:S(2)}) collective-permute-start(bf16[1,2,48,384]{3,2,1,0:T(8,128)(2,1)} %own_ref.1), channel_id=1, source_target_pairs={{0,2},{1,3},{2,0},{3,1},{4,6},{5,7},{6,4},{7,5},{8,10},{9,11},{10,... | collective-permute-start | bytes 221192 | tf_op jit(solution)/shard_map/ppermute | solution.py:510
  4.0 4.6 %collective-permute-start = (bf16[1,2,48,384]{3,2,1,0:T(8,128)(2,1)}, bf16[1,2,48,384]{3,2,1,0:T(8,128)(2,1)S(1)}, u32[]{:S(2)}, u32[]{:S(2)}) collective-permute-start(bf16[1,2,48,384]{3,2,1,0:T(8,128)(2,1)} %own_ref.1), channel_id=1, source_target_pairs={{0,1},{1,0},{2,3},{3,2},{4,5},{5,4},{6,7},{7,6},{8,9},{9,8},{10,11... | collective-permute-start | bytes 221192 | tf_op jit(solution)/shard_map/ppermute | solution.py:510
  5.6 6.4 %collective-permute-start.2 = (bf16[1,2,48,384]{3,2,1,0:T(8,128)(2,1)}, bf16[1,2,48,384]{3,2,1,0:T(8,128)(2,1)S(1)}, u32[]{:S(2)}, u32[]{:S(2)}) collective-permute-start(bf16[1,2,48,384]{3,2,1,0:T(8,128)(2,1)} %own_ref.1), channel_id=1, source_target_pairs={{0,3},{1,2},{2,1},{3,0},{4,7},{5,6},{6,5},{7,4},{8,11},{9,10},{10,... | collective-permute-start | bytes 221192 | tf_op jit(solution)/shard_map/ppermute | solution.py:510
  6.5 1.6 %copy-start = (bf16[96,3,3,3,384]{4,0,3,2,1:T(8,128)(2,1)S(1)}, bf16[96,3,3,3,384]{4,0,3,2,1:T(8,128)(2,1)}, u32[]{:S(2)}) copy-start(bf16[96,3,3,3,384]{4,0,3,2,1:T(8,128)(2,1)} %param.18) | copy-start | bytes 5971972
  8.0 3.9 %copy-start.6 = (bf16[1,2,48,384]{3,2,1,0:T(8,128)(2,1)S(1)}, bf16[1,2,48,384]{3,2,1,0:T(8,128)(2,1)}, u32[]{:S(2)}) copy-start(bf16[1,2,48,384]{3,2,1,0:T(8,128)(2,1)} %own_ref.1) | copy-start | bytes 221188
  12.7 1.6 %collective-permute-start.3 = (bf16[1,8,48,384]{3,2,1,0:T(8,128)(2,1)S(1)}, bf16[1,8,48,384]{3,2,1,0:T(8,128)(2,1)S(1)}, u32[]{:S(2)}, u32[]{:S(2)}) collective-permute-start(bf16[1,8,48,384]{3,2,1,0:T(8,128)(2,1)S(1)} %get-tuple-element.15.own_ref), channel_id=1, source_target_pairs={{0,4},{4,0},{8,12},{12,8},{1,5},{5,1},{9,13},{13,9},{2,6},{6,2},{1... | collective-permute-start | bytes 884744 | tf_op jit(solution)/shard_map/ppermute | solution.py:510
  12.8 9.4 %collective-permute-start.4 = (bf16[1,8,48,384]{3,2,1,0:T(8,128)(2,1)S(1)}, bf16[1,8,48,384]{3,2,1,0:T(8,128)(2,1)S(1)}, u32[]{:S(2)}, u32[]{:S(2)}) collective-permute-start(bf16[1,8,48,384]{3,2,1,0:T(8,128)(2,1)S(1)} %get-tuple-element.15.own_ref), channel_id=1, source_target_pairs={{0,8},{4,12},{8,0},{12,4},{1,9},{5,13},{9,1},{13,5},{2,10},{6,14},... | collective-permute-start | bytes 884744 | tf_op jit(solution)/shard_map/ppermute | solution.py:510
  22.2 1.7 %copy-start.7 = (f32[96]{0:T(128)S(1)}, f32[96]{0:T(128)}, u32[]{:S(2)}) copy-start(f32[96]{0:T(128)} %bias_ref.2) | copy-start | bytes 1156
  22.2 1.6 %collective-permute-start.5 = (bf16[1,8,48,384]{3,2,1,0:T(8,128)(2,1)S(1)}, bf16[1,8,48,384]{3,2,1,0:T(8,128)(2,1)S(1)}, u32[]{:S(2)}, u32[]{:S(2)}) collective-permute-start(bf16[1,8,48,384]{3,2,1,0:T(8,128)(2,1)S(1)} %shard_map.149), channel_id=1, source_target_pairs={{0,4},{4,0},{8,12},{12,8},{1,5},{5,1},{9,13},{13,9},{2,6},{6,2},{1... | collective-permute-start | bytes 884744 | tf_op jit(solution)/shard_map/ppermute | solution.py:510
  23.6 5.7 %copy-start.1 = (bf16[96,3,3,3,384]{4,0,3,2,1:T(8,128)(2,1)S(1)}, bf16[96,3,3,3,384]{4,0,3,2,1:T(8,128)(2,1)}, u32[]{:S(2)}) copy-start(bf16[96,3,3,3,384]{4,0,3,2,1:T(8,128)(2,1)} %param.22) | copy-start | bytes 5971972
  26.1 3.4 %collective-permute-start.6 = (bf16[3,8,48,128]{3,2,1,0:T(8,128)(2,1)S(1)}, bf16[3,8,48,128]{3,2,1,0:T(8,128)(2,1)S(1)}, u32[]{:S(2)}, u32[]{:S(2)}) collective-permute-start(bf16[3,8,48,128]{3,2,1,0:T(8,128)(2,1)S(1)} %get-tuple-element.16.refs_0_.own_ref), channel_id=1, source_target_pairs={{0,4},{4,0},{8,12},{12,8},{1,5},{5,1},{9,13},{13,9},{2,6},{6,2},{1... | collective-permute-start | bytes 884744 | tf_op jit(solution)/shard_map/ppermute | solution.py:510
  26.8 8.2 %collective-permute-start.7 = (bf16[2,8,48,128]{3,2,1,0:T(8,128)(2,1)S(1)}, bf16[2,8,48,128]{3,2,1,0:T(8,128)(2,1)S(1)}, u32[]{:S(2)}, u32[]{:S(2)}) collective-permute-start(bf16[2,8,48,128]{3,2,1,0:T(8,128)(2,1)S(1)} %get-tuple-element.17), channel_id=1, source_target_pairs={{0,8},{4,12},{8,0},{12,4},{1,9},{5,13},{9,1},{13,5},{2,10},{6,14},... | collective-permute-start | bytes 589832 | tf_op jit(solution)/shard_map/ppermute | solution.py:510
  29.2 7.3 %collective-permute-start.9 = (bf16[1,8,48,128]{3,2,1,0:T(8,128)(2,1)S(1)}, bf16[1,8,48,128]{3,2,1,0:T(8,128)(2,1)S(1)}, u32[]{:S(2)}, u32[]{:S(2)}) collective-permute-start(bf16[1,8,48,128]{3,2,1,0:T(8,128)(2,1)S(1)} %get-tuple-element.18), channel_id=1, source_target_pairs={{0,8},{4,12},{8,0},{12,4},{1,9},{5,13},{9,1},{13,5},{2,10},{6,14},... | collective-permute-start | bytes 294920 | tf_op jit(solution)/shard_map/ppermute | solution.py:510
  34.9 1.6 %collective-permute-start.8 = (bf16[2,8,48,128]{3,2,1,0:T(8,128)(2,1)S(1)}, bf16[2,8,48,128]{3,2,1,0:T(8,128)(2,1)S(1)}, u32[]{:S(2)}, u32[]{:S(2)}) collective-permute-start(bf16[2,8,48,128]{3,2,1,0:T(8,128)(2,1)S(1)} %shard_map.153), channel_id=1, source_target_pairs={{0,4},{4,0},{8,12},{12,8},{1,5},{5,1},{9,13},{13,9},{2,6},{6,2},{1... | collective-permute-start | bytes 589832 | tf_op jit(solution)/shard_map/ppermute | solution.py:510
  36.5 2.2 %copy-start.8 = (f32[96]{0:T(128)S(1)}, f32[96]{0:T(128)}, u32[]{:S(2)}) copy-start(f32[96]{0:T(128)} %bias_ref.3) | copy-start | bytes 1156
  36.5 2.2 %collective-permute-start.10 = (bf16[1,8,48,128]{3,2,1,0:T(8,128)(2,1)S(1)}, bf16[1,8,48,128]{3,2,1,0:T(8,128)(2,1)S(1)}, u32[]{:S(2)}, u32[]{:S(2)}) collective-permute-start(bf16[1,8,48,128]{3,2,1,0:T(8,128)(2,1)S(1)} %shard_map.155), channel_id=1, source_target_pairs={{0,4},{4,0},{8,12},{12,8},{1,5},{5,1},{9,13},{13,9},{2,6},{6,2},{1... | collective-permute-start | bytes 294920 | tf_op jit(solution)/shard_map/ppermute | solution.py:510
  38.7 8.6 %copy-start.2 = (bf16[384,384]{1,0:T(8,128)(2,1)S(1)}, bf16[384,384]{1,0:T(8,128)(2,1)}, u32[]{:S(2)}) copy-start(bf16[384,384]{1,0:T(8,128)(2,1)} %wq_ref.1) | copy-start | bytes 884740
  38.7 8.6 %copy-start.3 = (bf16[384,384]{1,0:T(8,128)(2,1)S(1)}, bf16[384,384]{1,0:T(8,128)(2,1)}, u32[]{:S(2)}) copy-start(bf16[384,384]{1,0:T(8,128)(2,1)} %wk_ref.1) | copy-start | bytes 884740
  38.7 8.6 %copy-start.4 = (bf16[384,384]{1,0:T(8,128)(2,1)S(1)}, bf16[384,384]{1,0:T(8,128)(2,1)}, u32[]{:S(2)}) copy-start(bf16[384,384]{1,0:T(8,128)(2,1)} %wv_ref.1) | copy-start | bytes 884740
  38.7 8.6 %copy-start.5 = (bf16[384,384]{1,0:T(8,128)(2,1)S(1)}, bf16[384,384]{1,0:T(8,128)(2,1)}, u32[]{:S(2)}) copy-start(bf16[384,384]{1,0:T(8,128)(2,1)} %wo_ref.1) | copy-start | bytes 884740
  40.6 2.3 %collective-permute-start.11 = (bf16[288,128]{1,0:T(8,128)(2,1)S(1)}, bf16[288,128]{1,0:T(8,128)(2,1)S(1)}, u32[]{:S(2)}, u32[]{:S(2)}) collective-permute-start(bf16[288,128]{1,0:T(8,128)(2,1)S(1)} %get-tuple-element.20), channel_id=1, source_target_pairs={{0,4},{4,0},{8,12},{12,8},{1,5},{5,1},{9,13},{13,9},{2,6},{6,2},{1... | collective-permute-start | bytes 221192 | tf_op jit(solution)/shard_map/ppermute | solution.py:510
  41.1 4.4 %collective-permute-start.12 = (bf16[288,128]{1,0:T(8,128)(2,1)S(1)}, bf16[288,128]{1,0:T(8,128)(2,1)S(1)}, u32[]{:S(2)}, u32[]{:S(2)}) collective-permute-start(bf16[288,128]{1,0:T(8,128)(2,1)S(1)} %get-tuple-element.21), channel_id=1, source_target_pairs={{0,8},{4,12},{8,0},{12,4},{1,9},{5,13},{9,1},{13,5},{2,10},{6,14},... | collective-permute-start | bytes 221192 | tf_op jit(solution)/shard_map/ppermute | solution.py:510
  42.8 4.5 %collective-permute-start.13 = (bf16[288,128]{1,0:T(8,128)(2,1)S(1)}, bf16[288,128]{1,0:T(8,128)(2,1)S(1)}, u32[]{:S(2)}, u32[]{:S(2)}) collective-permute-start(bf16[288,128]{1,0:T(8,128)(2,1)S(1)} %get-tuple-element.22), channel_id=1, source_target_pairs={{0,12},{4,8},{8,4},{12,0},{1,13},{5,9},{9,5},{13,1},{2,14},{6,10},... | collective-permute-start | bytes 221192 | tf_op jit(solution)/shard_map/ppermute | solution.py:510

commit v5 on v4

--- a/solution.py
+++ b/solution.py
@@ -24,7 +24,7 @@
         return lax.axis_index(self.name)
 
 
-def call(body, outs, scratch=()):
+def call(body, outs, scratch=(), cost=None):
     def run(*args):
         axes = [a for a in args if isinstance(a, Axis)]
         arrays = args[len(axes) :]
@@ -35,6 +35,7 @@
             out_specs=jax.tree.map(lambda _: VMEM, outs),
             scratch_shapes=scratch,
             compiler_params=pltpu.CompilerParams(vmem_limit_bytes=16 * 1024 * 1024),
+            cost_estimate=cost,
         )(*arrays)
 
     return run
@@ -98,11 +99,24 @@
     far_ref[...] = x_ref[0, (rows - 1) * odd]
 
 
-def own_frame(r_ref, own_ref, one_ref, two_ref, three_ref, table_ref, after_ref, out_ref, raw_ref):
+def own_frame(
+    r_ref, own_ref, one_ref, two_ref, three_ref, table_ref, loaded_ref, across_ref, out_ref, raw_ref, blocks_ref
+):
     blocks = [ref[0] for ref in (own_ref, one_ref, two_ref, three_ref)]
-    rows, cols, channels = blocks[0].shape
+    rows = blocks[0].shape[0]
     for k, block in enumerate(blocks):
         raw_ref[pl.ds((r_ref[0] ^ k) * rows, rows)] = block
+        if k > 0:
+            blocks_ref[k - 1] = block
+    frame_norm(r_ref, blocks, table_ref, out_ref)
+
+
+def across_frame(r_ref, own_ref, blocks_ref, table_ref, after_ref, out_ref):
+    frame_norm(r_ref, [own_ref[0]] + [blocks_ref[k] for k in range(3)], table_ref, out_ref)
+
+
+def frame_norm(r_ref, blocks, table_ref, out_ref):
+    rows, cols, channels = blocks[0].shape
     wide = [block.astype(F32).reshape(rows * cols, channels) for block in blocks]
     count = len(wide) * rows * cols * GROUP
     mean = group_sums(eight(sum(jnp.sum(x, axis=0, keepdims=True) for x in wide)))[0:1] / count
@@ -189,10 +203,10 @@
     out_ref[...] = x_ref[...]
 
 
-def frame_taps(total_ref, base_ref, a_ref, held, w_ref, lanes=slice(None)):
+def frame_taps(total_ref, base_ref, a_ref, held, w_ref, lanes=slice(None), first=0):
     frames, plane, _ = total_ref.shape
     _, padded, cols, channels = a_ref.shape
-    for t in range(frames):
+    for t in range(first, first + frames):
         total = None if base_ref is None else base_ref[t]
         terms = [(g, 2 - (t - f)) for g, f in enumerate(held) if 0 <= t - f <= 2]
         for g, i in terms:
@@ -202,7 +216,7 @@
             weight = jnp.concatenate([w_ref[i, j, :, lanes] for j in range(3)], axis=1)
             term = lax.dot_general(window, weight, (((1,), (1,)), ((), ())), preferred_element_type=F32)
             total = term if total is None else total + term
-        total_ref[t] = jnp.zeros(total_ref.shape[1:], F32) if total is None else total
+        total_ref[t - first] = jnp.zeros(total_ref.shape[1:], F32) if total is None else total
 
 
 def lay_out(m_ref, own_ref, mate_ref, pair):
@@ -219,26 +233,36 @@
     on_half(m_ref, False, lambda h: frame_taps(total_ref, None, pair, (2 * h, 2 * h + 1), w_ref))
 
 
-def add_frame(m_ref, flip, a_ref, base_ref, w_ref, total_ref, rimmed):
+def add_frame(m_ref, flip, a_ref, base_ref, w_ref, total_ref, rimmed, first=0):
     height = a_ref.shape[1]
     rimmed[0, 0] = jnp.zeros(rimmed.shape[2:], BF16)
     rimmed[0, 1 : height + 1] = a_ref[0]
     rimmed[0, height + 1] = jnp.zeros(rimmed.shape[2:], BF16)
-    for f in range(total_ref.shape[0]):
+    for f in range(base_ref.shape[0]):
 
         @pl.when((m_ref[0] ^ flip) == f)
         def _(f=f):
-            frame_taps(total_ref, base_ref, rimmed, (f,), w_ref)
+            frame_taps(total_ref, base_ref, rimmed, (f,), w_ref, first=first)
 
 
 def first_conv_across(m_ref, near_total_ref, a_ref, w_ref, total_ref, rimmed):
     add_frame(m_ref, 2, a_ref, near_total_ref, w_ref, total_ref, rimmed)
 
 
+def first_conv_early(m_ref, base_ref, a_ref, w_ref, bias_ref, table_ref, out_ref, *scratch):
+    first_conv_rest(0, m_ref, base_ref, a_ref, w_ref, bias_ref, table_ref, out_ref, *scratch)
+
+
+def first_conv_late(m_ref, base_ref, a_ref, w_ref, bias_ref, table_ref, early_ref, out_ref, all_ref, *scratch):
+    first_conv_rest(2, m_ref, base_ref, a_ref, w_ref, bias_ref, table_ref, out_ref, *scratch)
+    all_ref[0:2] = early_ref[...]
+    all_ref[2:4] = out_ref[...]
+
+
 def first_conv_rest(
-    m_ref, base_ref, a_ref, w_ref, bias_ref, table_ref, out_ref, early_ref, late_ref, rimmed, total, conv1, rows8
+    first, m_ref, base_ref, a_ref, w_ref, bias_ref, table_ref, out_ref, rimmed, total, conv1, rows8
 ):
-    add_frame(m_ref, 3, a_ref, base_ref, w_ref, total, rimmed)
+    add_frame(m_ref, 3, a_ref, base_ref, w_ref, total, rimmed, first)
     frames, height, cols, outputs = conv1.shape
     count = height * cols * GROUP
     rows8[...] = jnp.zeros(rows8.shape, F32)
@@ -253,13 +277,13 @@
     variance = group_sums(rows8[...]) / count
     gain, shift = (own_part(table_ref[i : i + 1], m_ref[0], outputs) for i in (2, 3))
     scale = lax.rsqrt(variance + EPSILON) * gain
-    planes = []
     for t in range(frames):
         rows = [conv1[t, row].astype(F32) - mean[t : t + 1] for row in range(height)]
-        planes.append([silu(row * scale[t : t + 1] + shift) for row in rows])
-    write_packed(planes, out_ref)
-    early_ref[...] = out_ref[0:2]
-    late_ref[...] = out_ref[2:]
+        rows = [silu(row * scale[t : t + 1] + shift) for row in rows]
+        for q in range(height // 4):
+            for g in range(3):
+                extra = rows[4 * q + 3][:, 32 * g : 32 * g + 32]
+                out_ref[t, 3 * q + g] = jnp.concatenate([rows[4 * q + g], extra], axis=1).astype(BF16)
 
 
 def first_conv(r_ref, a_ref, w_ref, bias_ref, out_ref, near_ref, far_ref, block_ref, total, rows8):
@@ -351,72 +375,51 @@
     return jnp.concatenate([part_ref[g, row][:, part:] for g in range(frames - 1)], axis=1)
 
 
-def half_channels(h, parts, held, a_ref):
-    _, padded, cols, lanes = a_ref.shape
-    for g, f in enumerate(held):
-        a_ref[g, 0] = jnp.zeros((cols, lanes), BF16)
-        a_ref[g, padded - 1] = jnp.zeros((cols, lanes), BF16)
+def half_channels(h, parts, a_ref):
+    frames, padded, cols, lanes = a_ref.shape
+    fill = jnp.zeros((cols, lanes - 192), BF16)
+    for f in range(frames):
+        a_ref[f, 0] = jnp.zeros((cols, lanes), BF16)
+        a_ref[f, padded - 1] = jnp.zeros((cols, lanes), BF16)
         for row in range(padded - 2):
+            q, i = divmod(row, 4)
             pieces = []
-            for planes in parts:
-                if f < len(planes):
-                    pieces.append(planes[f][row][:, 0:96])
+            for part in parts:
+                if i < 3:
+                    pieces.append(part[f, 3 * q + i][:, 0:96])
                 else:
-                    pieces += [plane[row][:, 96:] for plane in planes]
-            fill = jnp.zeros((cols, lanes - 192), BF16)
-            a_ref[g, row + 1] = jnp.concatenate([fill] + pieces if h else pieces + [fill], axis=1)
+                    pieces += [part[f, 3 * q + g][:, 96:] for g in range(3)]
+            a_ref[f, row + 1] = jnp.concatenate([fill] + pieces if h else pieces + [fill], axis=1)
 
 
 def half_lanes(h, lanes, channels):
     return slice(channels - lanes, channels) if h else slice(0, lanes)
 
 
-def second_conv_near(m_ref, own_ref, mate_ref, w_ref, total_ref, both, a_ref):
+def half_taps(m_ref, other, own_ref, mate_ref, held, base_ref, w_ref, total_ref, both, a_ref):
     odd = m_ref[0] & 1
     both[odd] = own_ref[...]
     both[1 - odd] = mate_ref[...]
     lanes, channels = a_ref.shape[3], w_ref.shape[3]
 
     def body(h):
-        parts = [[both.at[c, g] for g in range(both.shape[1])] for c in (0, 1)]
-        held = range(total_ref.shape[0])
-        half_channels(h, parts, held, a_ref)
-        frame_taps(total_ref, None, a_ref, held, w_ref, half_lanes(h, lanes, channels))
-
-    on_half(m_ref, False, body)
+        half_channels(h, (both.at[0], both.at[1]), a_ref)
+        frame_taps(total_ref, base_ref, a_ref, held, w_ref, half_lanes(h, lanes, channels))
+
+    on_half(m_ref, other, body)
+
+
+def second_conv_near(m_ref, own_ref, mate_ref, w_ref, total_ref, both, a_ref):
+    half_taps(m_ref, False, own_ref, mate_ref, (0, 1, 2, 3), None, w_ref, total_ref, both, a_ref)
 
 
 def second_conv_early(m_ref, near_total_ref, own_ref, mate_ref, w_ref, total_ref, both, a_ref):
-    odd = m_ref[0] & 1
-    both[odd] = own_ref[...]
-    both[1 - odd] = mate_ref[...]
-    lanes, channels = a_ref.shape[3], w_ref.shape[3]
-
-    def body(h):
-        parts = [[both.at[c, g] for g in range(both.shape[1])] for c in (0, 1)]
-        half_channels(h, parts, (0, 1), a_ref)
-        frame_taps(total_ref, near_total_ref, a_ref, (0, 1), w_ref, half_lanes(h, lanes, channels))
-
-    on_half(m_ref, True, body)
-
-
-def second_conv_late(
-    m_ref, total_ref, own_ref, mate_ref, own_last_ref, mate_last_ref, w_ref, bias_ref, *refs
-):
-    outs, (both, last, a_ref, total, done) = refs[:-5], refs[-5:]
-    odd = m_ref[0] & 1
-    both[odd] = own_ref[...]
-    both[1 - odd] = mate_ref[...]
-    last[odd] = own_last_ref[...]
-    last[1 - odd] = mate_last_ref[...]
-    lanes, channels = a_ref.shape[3], w_ref.shape[3]
-
-    def body(h):
-        parts = [[both.at[c, 0], both.at[c, 1], last.at[c, 0]] for c in (0, 1)]
-        half_channels(h, parts, (2, 3), a_ref)
-        frame_taps(total, total_ref, a_ref, (2, 3), w_ref, half_lanes(h, lanes, channels))
-
-    on_half(m_ref, True, body)
+    half_taps(m_ref, True, own_ref, mate_ref, (0, 1), near_total_ref, w_ref, total_ref, both, a_ref)
+
+
+def second_conv_late(m_ref, total_ref, own_ref, mate_ref, w_ref, bias_ref, *refs):
+    outs, (both, a_ref, total, done) = refs[:-4], refs[-4:]
+    half_taps(m_ref, True, own_ref, mate_ref, (2, 3), total_ref, w_ref, total, both, a_ref)
     cols = a_ref.shape[2]
     for t in range(total.shape[0]):
         done[t] = finish((total if t >= 2 else total_ref).at[t], cols, bias_ref)
@@ -576,32 +579,38 @@
         height = n * rows
         one, two, three = (over_rows(features, k) for k in (1, 2, 3))
         frame = struct((1, height, cols, channels))
-        active1, raw = call(own_frame, (frame, struct((height, cols, channels))))(
-            r, features, one, two, three, table, weights1
-        )
-        across, mate = over_x(active1), over_core(active1)
+        across_own = over_x(features)
+        active1, raw, blocks = call(
+            own_frame, (frame, struct((height, cols, channels)), struct((n - 1, rows, cols, channels)))
+        )(r, features, one, two, three, table, weights1, across_own)
+        across_blocks, mate = over_x(blocks), over_core(active1)
         pair, rimmed = (pltpu.VMEM((k, height + 2, cols, channels), BF16) for k in (2, 1))
         tall = struct((frames, n * plane, 3 * lanes), F32)
-        tall_scratch = pltpu.VMEM(tall.shape, F32)
         near_total = call(first_conv_near, tall, (pair,))(m, active1, mate, weights1)
-        beside = over_core(held_until(across, near_total))
+        across = call(across_frame, frame)(r, across_own, across_blocks, table, near_total)
+        beside = over_core(across)
         across_total = call(first_conv_across, tall, (rimmed,))(m, near_total, across, weights1)
-        active2, early, late = call(
-            first_conv_rest,
-            tuple(struct((k, height, cols, 128)) for k in (frames - 1, 2, frames - 3)),
-            (rimmed, tall_scratch, pltpu.VMEM((frames, height, cols, outputs), BF16), stats_scratch),
-        )(m, across_total, beside, weights1, first_bias, table)
-
-        weights2 = call(load, loaded)(taps(second_kernel), active2)
-        early, late = over_x(early), over_x(late)
-        mate = over_core(active2)
-        both = pltpu.VMEM((2, frames - 1, height, cols, 128), BF16)
-        all_frames, two_frames = (pltpu.VMEM((k, height + 2, cols, 256), BF16) for k in (frames, 2))
-        near_total = call(second_conv_near, tall, (both, all_frames))(m, active2, mate, weights2)
-        early_beside = over_core(held_until(early, near_total))
+        scratch = (
+            rimmed,
+            pltpu.VMEM((2, n * plane, 3 * lanes), F32),
+            pltpu.VMEM((2, height, cols, outputs), BF16),
+            stats_scratch,
+        )
+        packed = struct((2, 3 * height // 4, cols, 128))
+        packed_all = struct((4, 3 * height // 4, cols, 128))
+        early = call(first_conv_early, packed, scratch)(m, across_total, beside, weights1, first_bias, table)
+        late, active2 = call(first_conv_late, (packed, packed_all), scratch)(
+            m, across_total, beside, weights1, first_bias, table, early
+        )
+
+        early, late, mate = over_x(early), over_x(late), over_core(active2)
+        long = pl.CostEstimate(flops=10**10, bytes_accessed=4 * 10**7, transcendentals=0)
+        weights2 = call(load, loaded, cost=long)(taps(second_kernel), early)
+        both, both_all = (pltpu.VMEM((2, *half.shape), BF16) for half in (packed, packed_all))
+        two_frames, all_frames = (pltpu.VMEM((k, height + 2, cols, 256), BF16) for k in (2, 4))
+        near_total = call(second_conv_near, tall, (both_all, all_frames))(m, active2, mate, weights2)
+        early_beside = over_core(early)
         late_beside = over_core(held_until(late, near_total))
-        both = pltpu.VMEM((2, 2, height, cols, 128), BF16)
-        last = pltpu.VMEM((2, 1, height, cols, 128), BF16)
         early_total = call(second_conv_early, tall, (both, two_frames))(
             m, near_total, early, early_beside, weights2
         )
@@ -609,8 +618,8 @@
         pieces = call(
             second_conv_late,
             [piece] * frames,
-            (both, last, two_frames, tall_scratch, pltpu.VMEM((frames, n * plane, outputs), BF16)),
-        )(m, early_total, early, early_beside, late, late_beside, weights2, second_bias)
+            (both, two_frames, pltpu.VMEM(tall.shape, F32), pltpu.VMEM((frames, n * plane, outputs), BF16)),
+        )(m, early_total, late, late_beside, weights2, second_bias)
         pieces = [pieces[0]] + [swapped(pieces[k], "tm", lambda i, k=k: i ^ k) for k in range(1, frames)]
         decoded = call(
             frame_attention,

time: 49.8 us -> 47.8 us (0.960)
  waiting for transfers between devices: 17 us -> 12.2 us
  starting transfers between devices: 12.9 us -> 14.8 us
  Pallas kernels: 17.1 us -> 17.9 us
    ppermute x14 -> x15, waiting for transfers between devices: 17 us -> 12.2 us  [swapped(): lax.ppermute(value, axis, [(i, partner(i)) for i in range(lax.axis_size(a...]
    ppermute x14 -> x15, starting transfers between devices: 12.9 us -> 14.8 us  [swapped(): lax.ppermute(value, axis, [(i, partner(i)) for i in range(lax.axis_size(a...]
    pallas_call x13, Pallas kernels: 17.1 us -> 17.9 us  [run(): pl.pallas_call(functools.partial(body, *axes), out_shape=outs, in_specs=[...]
  transfers between devices with their start and end apart: 14 -> 15, of which waited for: 8 -> 8; matrix products, arithmetic and copies ran while one was open for 2% -> 2% of each run, Pallas kernels for 20% -> 24%
where the time goes in v5:
time: 47.8 us; the launch traced here: 47.6 us
  Pallas kernels  17.9 us (37%)
  starting transfers between devices  14.8 us (31%)
  waiting for transfers between devices  12.2 us (26%)
  local copies, waits for them, and re-layouts  1.6 us (3%)
  other arithmetic  0.86 us (2%)
    pallas_call x13, Pallas kernels, run(): pl.pallas_call(functools.partial(body, *axes), out_shape=outs, in_specs=[...  17.9 us
    ppermute x15, starting transfers between devices, swapped(): lax.ppermute(value, axis, [(i, partner(i)) for i in range(lax.axis_size(a...  14.8 us
    ppermute x15, waiting for transfers between devices, swapped(): lax.ppermute(value, axis, [(i, partner(i)) for i in range(lax.axis_size(a...  12.2 us
    unnamed x18, local copies, waits for them, and re-layouts  1.6 us
  transfers between devices with their start and end apart: 15, of which 8 were waited for; matrix products, arithmetic and copies ran while one was open for 2% of the time, Pallas kernels for 24%

profile of v5, /device:TPU:0, one launch (start us, length us, event | category | flops | bytes accessed | tf_op | source)
XLA Modules:
  0.0 47.6 jit_solution(6259720996258138540)
XLA Ops:
  0.0 3.0 %collective-permute-start = (bf16[1,2,48,384]{3,2,1,0:T(8,128)(2,1)}, bf16[1,2,48,384]{3,2,1,0:T(8,128)(2,1)S(1)}, u32[]{:S(2)}, u32[]{:S(2)}) collective-permute-start(bf16[1,2,48,384]{3,2,1,0:T(8,128)(2,1)} %own_ref.1), channel_id=1, source_target_pairs={{0,1},{1,0},{2,3},{3,2},{4,5},{5,4},{6,7},{7,6},{8,9},{9,8},{10,11... | collective-permute-start | bytes 221192 | tf_op jit(solution)/shard_map/ppermute | solution.py:513
  3.0 2.6 %collective-permute-start.1 = (bf16[1,2,48,384]{3,2,1,0:T(8,128)(2,1)}, bf16[1,2,48,384]{3,2,1,0:T(8,128)(2,1)S(1)}, u32[]{:S(2)}, u32[]{:S(2)}) collective-permute-start(bf16[1,2,48,384]{3,2,1,0:T(8,128)(2,1)} %own_ref.1), channel_id=1, source_target_pairs={{0,2},{1,3},{2,0},{3,1},{4,6},{5,7},{6,4},{7,5},{8,10},{9,11},{10,... | collective-permute-start | bytes 221192 | tf_op jit(solution)/shard_map/ppermute | solution.py:513
  5.6 0.0 collective-permute-start.2
  5.6 1.7 %collective-permute-start.3 = (bf16[1,2,48,384]{3,2,1,0:T(8,128)(2,1)}, bf16[1,2,48,384]{3,2,1,0:T(8,128)(2,1)S(1)}, u32[]{:S(2)}, u32[]{:S(2)}) collective-permute-start(bf16[1,2,48,384]{3,2,1,0:T(8,128)(2,1)} %own_ref.1), channel_id=1, source_target_pairs={{0,8},{4,12},{8,0},{12,4},{1,9},{5,13},{9,1},{13,5},{2,10},{6,14},... | collective-permute-start | bytes 221192 | tf_op jit(solution)/shard_map/ppermute | solution.py:513
  7.4 0.8 %select_select_fusion.table_ref = f32[8,384]{1,0:T(8,128)S(1)} fusion(f32[384]{0:T(512)} %param.16, f32[384]{0:T(512)} %param.17, f32[384]{0:T(512)} %param.20, f32[384]{0:T(512)} %param.21, f32[384]{0:T(512)} %param.24, f32[384]{0:T(512)} %param.25, pred[8]{0:T(512)(128)(4,1)S(1)} %get-tuple-element.23, pred[8]{0:T(512)(128)(4,1)S(1)} %get-tuple-element.24, ...), kind=kLoop, calls=%fused_computation | loop fusion | flops 18432 | bytes 21552 | tf_op jit(solution)/shard_map/jit(_where)/select_n | solution.py:554
  8.2 1.5 %copy-done = bf16[96,3,3,3,384]{4,0,3,2,1:T(8,128)(2,1)S(1)} copy-done((bf16[96,3,3,3,384]{4,0,3,2,1:T(8,128)(2,1)S(1)}, bf16[96,3,3,3,384]{4,0,3,2,1:T(8,128)(2,1)}, u32[]{:S(2)}) %copy-start) | copy-done | bytes 1990680
  9.8 0.2 shard_map.145.loaded_ref.w_ref
  10.0 1.0 %collective-permute-done.1.two_ref = bf16[1,2,48,384]{3,2,1,0:T(8,128)(2,1)S(1)} collective-permute-done((bf16[1,2,48,384]{3,2,1,0:T(8,128)(2,1)}, bf16[1,2,48,384]{3,2,1,0:T(8,128)(2,1)S(1)}, u32[]{:S(2)}, u32[]{:S(2)}) %collective-permute-start.1) | collective-permute-done | bytes 73760 | tf_op jit(solution)/shard_map/ppermute | solution.py:513
  11.0 1.0 %collective-permute-done.2.three_ref = bf16[1,2,48,384]{3,2,1,0:T(8,128)(2,1)S(1)} collective-permute-done((bf16[1,2,48,384]{3,2,1,0:T(8,128)(2,1)}, bf16[1,2,48,384]{3,2,1,0:T(8,128)(2,1)S(1)}, u32[]{:S(2)}, u32[]{:S(2)}) %collective-permute-start.2) | collective-permute-done | bytes 73760 | tf_op jit(solution)/shard_map/ppermute | solution.py:513
  12.1 0.0 collective-permute-done.3.across_ref.own_ref
  12.1 0.7 %shard_map.146 = (bf16[1,8,48,384]{3,2,1,0:T(8,128)(2,1)S(1)}, bf16[8,48,384]{2,1,0:T(8,128)(2,1)S(1)}, bf16[3,2,48,384]{3,2,1,0:T(8,128)(2,1)S(1)}) custom-call(bf16[1,2,48,384]{3,2,1,0:T(8,128)(2,1)S(1)} %copy-done.5, bf16[1,2,48,384]{3,2,1,0:T(8,128)(2,1)S(1)} %collective-permute-done.one_ref, bf16[1,2,48,384]{3,2,1,0:T(8,128)(2,1)S(1)} %collective-permute-done.1.two_ref, ...), custom_call_target="tpu_custom_call" | custom-call | tf_op jit(solution)/shard_map/pallas_call | solution.py:31
  12.8 0.1 collective-permute-start.4
  12.9 1.6 %collective-permute-start.5 = (bf16[3,2,48,384]{3,2,1,0:T(8,128)(2,1)S(1)}, bf16[3,2,48,384]{3,2,1,0:T(8,128)(2,1)S(1)}, u32[]{:S(2)}, u32[]{:S(2)}) collective-permute-start(bf16[3,2,48,384]{3,2,1,0:T(8,128)(2,1)S(1)} %get-tuple-element.16), channel_id=1, source_target_pairs={{0,8},{4,12},{8,0},{12,4},{1,9},{5,13},{9,1},{13,5},{2,10},{6,14},... | collective-permute-start | bytes 663560 | tf_op jit(solution)/shard_map/ppermute | solution.py:513
  14.5 0.0 collective-permute-done.4.mate_ref
  14.5 3.2 %shard_map.147.after_ref.near_total_ref = f32[4,384,384]{2,1,0:T(8,128)S(1)} custom-call(bf16[1,8,48,384]{3,2,1,0:T(8,128)(2,1)S(1)} %get-tuple-element.15.own_ref, bf16[1,8,48,384]{3,2,1,0:T(8,128)(2,1)S(1)} %collective-permute-done.4.mate_ref, bf16[3,3,384,384]{3,2,1,0:T(8,128)(2,1)S(1)} %shard_map.145.loaded_ref.w_ref), custom_call_target="tpu_custom_call" | custom-call | tf_op jit(solution)/shard_map/pallas_call | solution.py:31
  17.7 3.1 %collective-permute-done.5.blocks_ref = bf16[3,2,48,384]{3,2,1,0:T(8,128)(2,1)S(1)} collective-permute-done((bf16[3,2,48,384]{3,2,1,0:T(8,128)(2,1)S(1)}, bf16[3,2,48,384]{3,2,1,0:T(8,128)(2,1)S(1)}, u32[]{:S(2)}, u32[]{:S(2)}) %collective-permute-start.5) | collective-permute-done | bytes 221216 | tf_op jit(solution)/shard_map/ppermute | solution.py:513
  20.8 0.7 %shard_map.148.a_ref = bf16[1,8,48,384]{3,2,1,0:T(8,128)(2,1)S(1)} custom-call(bf16[1,2,48,384]{3,2,1,0:T(8,128)(2,1)S(1)} %collective-permute-done.3.across_ref.own_ref, bf16[3,2,48,384]{3,2,1,0:T(8,128)(2,1)S(1)} %collective-permute-done.5.blocks_ref, f32[8,384]{1,0:T(8,128)S(1)} %select_select_fusion.table_ref, ...), custom_call_target="tpu_custom_call" | custom-call | tf_op jit(solution)/shard_map/pallas_call | solution.py:31
  21.4 0.0 copy-start.6
  21.4 0.1 collective-permute-start.6
  21.5 1.3 %shard_map.149.base_ref = f32[4,384,384]{2,1,0:T(8,128)S(1)} custom-call(f32[4,384,384]{2,1,0:T(8,128)S(1)} %shard_map.147.after_ref.near_total_ref, bf16[1,8,48,384]{3,2,1,0:T(8,128)(2,1)S(1)} %shard_map.148.a_ref, bf16[3,3,384,384]{3,2,1,0:T(8,128)(2,1)S(1)} %shard_map.145.loaded_ref.w_ref), custom_call_target="tpu_custom_call" | custom-call | tf_op jit(solution)/shard_map/pallas_call | solution.py:31
  22.8 0.3 collective-permute-done.6.a_ref
  23.1 0.8 %shard_map.150.early_ref = bf16[2,6,48,128]{3,2,1,0:T(8,128)(2,1)S(1)} custom-call(f32[4,384,384]{2,1,0:T(8,128)S(1)} %shard_map.149.base_ref, bf16[1,8,48,384]{3,2,1,0:T(8,128)(2,1)S(1)} %collective-permute-done.6.a_ref, bf16[3,3,384,384]{3,2,1,0:T(8,128)(2,1)S(1)} %shard_map.145.loaded_ref.w_ref, f32[96]{0:T(128)S(1)} %copy-done.6, ...), custom_call_target="tpu_custom_call" | custom-call | tf_op jit(solution)/shard_map/pallas_call | solution.py:31
  23.9 0.0 copy-start.8
  23.9 2.3 %collective-permute-start.8 = (bf16[2,6,48,128]{3,2,1,0:T(8,128)(2,1)S(1)}, bf16[2,6,48,128]{3,2,1,0:T(8,128)(2,1)S(1)}, u32[]{:S(2)}, u32[]{:S(2)}) collective-permute-start(bf16[2,6,48,128]{3,2,1,0:T(8,128)(2,1)S(1)} %shard_map.150.early_ref), channel_id=1, source_target_pairs={{0,8},{4,12},{8,0},{12,4},{1,9},{5,13},{9,1},{13,5},{2,10},{6,14},... | collective-permute-start | bytes 442376 | tf_op jit(solution)/shard_map/ppermute | solution.py:513
  26.2 1.6 %shard_map.151 = (bf16[2,6,48,128]{3,2,1,0:T(8,128)(2,1)S(1)}, bf16[4,6,48,128]{3,2,1,0:T(8,128)(2,1)S(1)}) custom-call(f32[4,384,384]{2,1,0:T(8,128)S(1)} %shard_map.149.base_ref, bf16[1,8,48,384]{3,2,1,0:T(8,128)(2,1)S(1)} %collective-permute-done.6.a_ref, bf16[3,3,384,384]{3,2,1,0:T(8,128)(2,1)S(1)} %shard_map.145.loaded_ref.w_ref, f32[96]{0:T(128)S(1)} %copy-done.6, ...), custom_call_target="tpu_custom_call" | custom-call | tf_op jit(solution)/shard_map/pallas_call | solution.py:31
  27.9 1.2 %collective-permute-start.7 = (bf16[4,6,48,128]{3,2,1,0:T(8,128)(2,1)S(1)}, bf16[4,6,48,128]{3,2,1,0:T(8,128)(2,1)S(1)}, u32[]{:S(2)}, u32[]{:S(2)}) collective-permute-start(bf16[4,6,48,128]{3,2,1,0:T(8,128)(2,1)S(1)} %get-tuple-element.17.own_ref), channel_id=1, source_target_pairs={{0,4},{4,0},{8,12},{12,8},{1,5},{5,1},{9,13},{13,9},{2,6},{6,2},{1... | collective-permute-start | bytes 884744 | tf_op jit(solution)/shard_map/ppermute | solution.py:513
  29.1 1.5 %collective-permute-done.8.refs_0_.own_ref = bf16[2,6,48,128]{3,2,1,0:T(8,128)(2,1)S(1)} collective-permute-done((bf16[2,6,48,128]{3,2,1,0:T(8,128)(2,1)S(1)}, bf16[2,6,48,128]{3,2,1,0:T(8,128)(2,1)S(1)}, u32[]{:S(2)}, u32[]{:S(2)}) %collective-permute-start.8) | collective-permute-done | bytes 147488 | tf_op jit(solution)/shard_map/ppermute | solution.py:513
  30.6 0.1 collective-permute-start.9
  30.8 0.2 shard_map.152.w_ref
  31.0 0.0 collective-permute-done.7.mate_ref
  31.0 3.0 %shard_map.153.near_total_ref.after_ref = f32[4,384,384]{2,1,0:T(8,128)S(1)} custom-call(bf16[4,6,48,128]{3,2,1,0:T(8,128)(2,1)S(1)} %get-tuple-element.17.own_ref, bf16[4,6,48,128]{3,2,1,0:T(8,128)(2,1)S(1)} %collective-permute-done.7.mate_ref, bf16[3,3,384,384]{3,2,1,0:T(8,128)(2,1)S(1)} %shard_map.152.w_ref), custom_call_target="tpu_custom_call" | custom-call | tf_op jit(solution)/shard_map/pallas_call | solution.py:31
  34.0 0.9 %collective-permute-done.10.x_ref.own_ref = bf16[2,6,48,128]{3,2,1,0:T(8,128)(2,1)S(1)} collective-permute-done((bf16[2,6,48,128]{3,2,1,0:T(8,128)(2,1)S(1)}, bf16[2,6,48,128]{3,2,1,0:T(8,128)(2,1)S(1)}, u32[]{:S(2)}, u32[]{:S(2)}) %collective-permute-start.10) | collective-permute-done | bytes 147488 | tf_op jit(solution)/shard_map/ppermute | solution.py:513
  35.0 0.0 copy-start.7
  35.0 0.1 collective-permute-start.11
  35.1 0.0 collective-permute-done.9.mate_ref
  35.1 2.1 %shard_map.154.total_ref = f32[4,384,384]{2,1,0:T(8,128)S(1)} custom-call(f32[4,384,384]{2,1,0:T(8,128)S(1)} %shard_map.153.near_total_ref.after_ref, bf16[2,6,48,128]{3,2,1,0:T(8,128)(2,1)S(1)} %collective-permute-done.8.refs_0_.own_ref, bf16[2,6,48,128]{3,2,1,0:T(8,128)(2,1)S(1)} %collective-permute-done.9.mate_ref, ...), custom_call_target="tpu_custom_call" | custom-call | tf_op jit(solution)/shard_map/pallas_call | solution.py:31
  37.1 0.0 copy-start.1
  37.2 0.0 copy-start.2
  37.2 0.0 copy-start.3
  37.2 0.0 copy-start.4
  37.2 0.0 collective-permute-done.11.mate_ref
  37.2 1.8 %shard_map.156 = (bf16[288,128]{1,0:T(8,128)(2,1)S(1)}, bf16[288,128]{1,0:T(8,128)(2,1)S(1)}, bf16[288,128]{1,0:T(8,128)(2,1)S(1)}, bf16[288,128]{1,0:T(8,128)(2,1)S(1)}) custom-call(f32[4,384,384]{2,1,0:T(8,128)S(1)} %shard_map.154.total_ref, bf16[2,6,48,128]{3,2,1,0:T(8,128)(2,1)S(1)} %collective-permute-done.10.x_ref.own_ref, ...), custom_call_target="tpu_custom_call" | custom-call | tf_op jit(solution)/shard_map/pallas_call | solution.py:31
  39.0 0.6 %collective-permute-start.12 = (bf16[288,128]{1,0:T(8,128)(2,1)S(1)}, bf16[288,128]{1,0:T(8,128)(2,1)S(1)}, u32[]{:S(2)}, u32[]{:S(2)}) collective-permute-start(bf16[288,128]{1,0:T(8,128)(2,1)S(1)} %get-tuple-element.20), channel_id=1, source_target_pairs={{0,4},{4,0},{8,12},{12,8},{1,5},{5,1},{9,13},{13,9},{2,6},{6,2},{1... | collective-permute-start | bytes 221192 | tf_op jit(solution)/shard_map/ppermute | solution.py:513
  39.6 1.4 %collective-permute-start.13 = (bf16[288,128]{1,0:T(8,128)(2,1)S(1)}, bf16[288,128]{1,0:T(8,128)(2,1)S(1)}, u32[]{:S(2)}, u32[]{:S(2)}) collective-permute-start(bf16[288,128]{1,0:T(8,128)(2,1)S(1)} %get-tuple-element.21), channel_id=1, source_target_pairs={{0,8},{4,12},{8,0},{12,4},{1,9},{5,13},{9,1},{13,5},{2,10},{6,14},... | collective-permute-start | bytes 221192 | tf_op jit(solution)/shard_map/ppermute | solution.py:513
  41.0 0.0 collective-permute-start.14
  41.0 2.9 %collective-permute-done.13.p2 = bf16[288,128]{1,0:T(8,128)(2,1)S(1)} collective-permute-done((bf16[288,128]{1,0:T(8,128)(2,1)S(1)}, bf16[288,128]{1,0:T(8,128)(2,1)S(1)}, u32[]{:S(2)}, u32[]{:S(2)}) %collective-permute-start.13) | collective-permute-done | bytes 73760 | tf_op jit(solution)/shard_map/ppermute | solution.py:513
  43.9 1.4 %collective-permute-done.14.p3 = bf16[288,128]{1,0:T(8,128)(2,1)S(1)} collective-permute-done((bf16[288,128]{1,0:T(8,128)(2,1)S(1)}, bf16[288,128]{1,0:T(8,128)(2,1)S(1)}, u32[]{:S(2)}, u32[]{:S(2)}) %collective-permute-start.14) | collective-permute-done | bytes 73760 | tf_op jit(solution)/shard_map/ppermute | solution.py:513
  45.3 2.3 %shard_map.157 = bf16[96,384]{1,0:T(8,128)(2,1)} custom-call(bf16[8,48,384]{2,1,0:T(8,128)(2,1)S(1)} %get-tuple-element.14.raw_ref, bf16[288,128]{1,0:T(8,128)(2,1)S(1)} %get-tuple-element.19.p0, bf16[288,128]{1,0:T(8,128)(2,1)S(1)} %collective-permute-done.12.p1, bf16[288,128]{1,0:T(8,128)(2,1)S(1)} %collective-permute-done.13.p2, ...), custom_call_target="tpu_custom_call" | custom-call | tf_op jit(solution)/shard_map/pallas_call | solution.py:31
  (17 shorter events, 0.1 us)
Async XLA Ops:
  0.0 10.0 %collective-permute-start = (bf16[1,2,48,384]{3,2,1,0:T(8,128)(2,1)}, bf16[1,2,48,384]{3,2,1,0:T(8,128)(2,1)S(1)}, u32[]{:S(2)}, u32[]{:S(2)}) collective-permute-start(bf16[1,2,48,384]{3,2,1,0:T(8,128)(2,1)} %own_ref.1), channel_id=1, source_target_pairs={{0,1},{1,0},{2,3},{3,2},{4,5},{5,4},{6,7},{7,6},{8,9},{9,8},{10,11... | collective-permute-start | bytes 221192 | tf_op jit(solution)/shard_map/ppermute | solution.py:513
  3.0 8.0 %collective-permute-start.1 = (bf16[1,2,48,384]{3,2,1,0:T(8,128)(2,1)}, bf16[1,2,48,384]{3,2,1,0:T(8,128)(2,1)S(1)}, u32[]{:S(2)}, u32[]{:S(2)}) collective-permute-start(bf16[1,2,48,384]{3,2,1,0:T(8,128)(2,1)} %own_ref.1), channel_id=1, source_target_pairs={{0,2},{1,3},{2,0},{3,1},{4,6},{5,7},{6,4},{7,5},{8,10},{9,11},{10,... | collective-permute-start | bytes 221192 | tf_op jit(solution)/shard_map/ppermute | solution.py:513
  5.6 6.5 %collective-permute-start.2 = (bf16[1,2,48,384]{3,2,1,0:T(8,128)(2,1)}, bf16[1,2,48,384]{3,2,1,0:T(8,128)(2,1)S(1)}, u32[]{:S(2)}, u32[]{:S(2)}) collective-permute-start(bf16[1,2,48,384]{3,2,1,0:T(8,128)(2,1)} %own_ref.1), channel_id=1, source_target_pairs={{0,3},{1,2},{2,1},{3,0},{4,7},{5,6},{6,5},{7,4},{8,11},{9,10},{10,... | collective-permute-start | bytes 221192 | tf_op jit(solution)/shard_map/ppermute | solution.py:513
  5.6 6.5 %collective-permute-start.3 = (bf16[1,2,48,384]{3,2,1,0:T(8,128)(2,1)}, bf16[1,2,48,384]{3,2,1,0:T(8,128)(2,1)S(1)}, u32[]{:S(2)}, u32[]{:S(2)}) collective-permute-start(bf16[1,2,48,384]{3,2,1,0:T(8,128)(2,1)} %own_ref.1), channel_id=1, source_target_pairs={{0,8},{4,12},{8,0},{12,4},{1,9},{5,13},{9,1},{13,5},{2,10},{6,14},... | collective-permute-start | bytes 221192 | tf_op jit(solution)/shard_map/ppermute | solution.py:513
  8.2 1.6 %copy-start = (bf16[96,3,3,3,384]{4,0,3,2,1:T(8,128)(2,1)S(1)}, bf16[96,3,3,3,384]{4,0,3,2,1:T(8,128)(2,1)}, u32[]{:S(2)}) copy-start(bf16[96,3,3,3,384]{4,0,3,2,1:T(8,128)(2,1)} %param.18) | copy-start | bytes 5971972
  9.8 2.3 %copy-start.5 = (bf16[1,2,48,384]{3,2,1,0:T(8,128)(2,1)S(1)}, bf16[1,2,48,384]{3,2,1,0:T(8,128)(2,1)}, u32[]{:S(2)}) copy-start(bf16[1,2,48,384]{3,2,1,0:T(8,128)(2,1)} %own_ref.1) | copy-start | bytes 221188
  12.8 1.6 %collective-permute-start.4 = (bf16[1,8,48,384]{3,2,1,0:T(8,128)(2,1)S(1)}, bf16[1,8,48,384]{3,2,1,0:T(8,128)(2,1)S(1)}, u32[]{:S(2)}, u32[]{:S(2)}) collective-permute-start(bf16[1,8,48,384]{3,2,1,0:T(8,128)(2,1)S(1)} %get-tuple-element.15.own_ref), channel_id=1, source_target_pairs={{0,4},{4,0},{8,12},{12,8},{1,5},{5,1},{9,13},{13,9},{2,6},{6,2},{1... | collective-permute-start | bytes 884744 | tf_op jit(solution)/shard_map/ppermute | solution.py:513
  12.9 7.8 %collective-permute-start.5 = (bf16[3,2,48,384]{3,2,1,0:T(8,128)(2,1)S(1)}, bf16[3,2,48,384]{3,2,1,0:T(8,128)(2,1)S(1)}, u32[]{:S(2)}, u32[]{:S(2)}) collective-permute-start(bf16[3,2,48,384]{3,2,1,0:T(8,128)(2,1)S(1)} %get-tuple-element.16), channel_id=1, source_target_pairs={{0,8},{4,12},{8,0},{12,4},{1,9},{5,13},{9,1},{13,5},{2,10},{6,14},... | collective-permute-start | bytes 663560 | tf_op jit(solution)/shard_map/ppermute | solution.py:513
  21.4 1.7 %copy-start.6 = (f32[96]{0:T(128)S(1)}, f32[96]{0:T(128)}, u32[]{:S(2)}) copy-start(f32[96]{0:T(128)} %bias_ref.4) | copy-start | bytes 1156
  21.4 1.6 %collective-permute-start.6 = (bf16[1,8,48,384]{3,2,1,0:T(8,128)(2,1)S(1)}, bf16[1,8,48,384]{3,2,1,0:T(8,128)(2,1)S(1)}, u32[]{:S(2)}, u32[]{:S(2)}) collective-permute-start(bf16[1,8,48,384]{3,2,1,0:T(8,128)(2,1)S(1)} %shard_map.148.a_ref), channel_id=1, source_target_pairs={{0,4},{4,0},{8,12},{12,8},{1,5},{5,1},{9,13},{13,9},{2,6},{6,2},{1... | collective-permute-start | bytes 884744 | tf_op jit(solution)/shard_map/ppermute | solution.py:513
  23.9 6.9 %copy-start.8 = (bf16[96,3,3,3,384]{4,0,3,2,1:T(8,128)(2,1)S(1)}, bf16[96,3,3,3,384]{4,0,3,2,1:T(8,128)(2,1)}, u32[]{:S(2)}) copy-start(bf16[96,3,3,3,384]{4,0,3,2,1:T(8,128)(2,1)} %param.22) | copy-start | bytes 5971972
  23.9 6.7 %collective-permute-start.8 = (bf16[2,6,48,128]{3,2,1,0:T(8,128)(2,1)S(1)}, bf16[2,6,48,128]{3,2,1,0:T(8,128)(2,1)S(1)}, u32[]{:S(2)}, u32[]{:S(2)}) collective-permute-start(bf16[2,6,48,128]{3,2,1,0:T(8,128)(2,1)S(1)} %shard_map.150.early_ref), channel_id=1, source_target_pairs={{0,8},{4,12},{8,0},{12,4},{1,9},{5,13},{9,1},{13,5},{2,10},{6,14},... | collective-permute-start | bytes 442376 | tf_op jit(solution)/shard_map/ppermute | solution.py:513
  27.9 3.1 %collective-permute-start.7 = (bf16[4,6,48,128]{3,2,1,0:T(8,128)(2,1)S(1)}, bf16[4,6,48,128]{3,2,1,0:T(8,128)(2,1)S(1)}, u32[]{:S(2)}, u32[]{:S(2)}) collective-permute-start(bf16[4,6,48,128]{3,2,1,0:T(8,128)(2,1)S(1)} %get-tuple-element.17.own_ref), channel_id=1, source_target_pairs={{0,4},{4,0},{8,12},{12,8},{1,5},{5,1},{9,13},{13,9},{2,6},{6,2},{1... | collective-permute-start | bytes 884744 | tf_op jit(solution)/shard_map/ppermute | solution.py:513
  29.1 5.8 %collective-permute-start.10 = (bf16[2,6,48,128]{3,2,1,0:T(8,128)(2,1)S(1)}, bf16[2,6,48,128]{3,2,1,0:T(8,128)(2,1)S(1)}, u32[]{:S(2)}, u32[]{:S(2)}) collective-permute-start(bf16[2,6,48,128]{3,2,1,0:T(8,128)(2,1)S(1)} %get-tuple-element.18), channel_id=1, source_target_pairs={{0,8},{4,12},{8,0},{12,4},{1,9},{5,13},{9,1},{13,5},{2,10},{6,14},... | collective-permute-start | bytes 442376 | tf_op jit(solution)/shard_map/ppermute | solution.py:513
  30.6 4.4 %collective-permute-start.9 = (bf16[2,6,48,128]{3,2,1,0:T(8,128)(2,1)S(1)}, bf16[2,6,48,128]{3,2,1,0:T(8,128)(2,1)S(1)}, u32[]{:S(2)}, u32[]{:S(2)}) collective-permute-start(bf16[2,6,48,128]{3,2,1,0:T(8,128)(2,1)S(1)} %collective-permute-done.8.refs_0_.own_ref), channel_id=1, source_target_pairs={{0,4},{4,0},{8,12},{12,8},{1,5},{5,1},{9,13},{13,9},{2,6},{6,2},{1... | collective-permute-start | bytes 442376 | tf_op jit(solution)/shard_map/ppermute | solution.py:513
  35.0 2.2 %copy-start.7 = (f32[96]{0:T(128)S(1)}, f32[96]{0:T(128)}, u32[]{:S(2)}) copy-start(f32[96]{0:T(128)} %bias_ref.5) | copy-start | bytes 1156
  35.0 2.2 %collective-permute-start.11 = (bf16[2,6,48,128]{3,2,1,0:T(8,128)(2,1)S(1)}, bf16[2,6,48,128]{3,2,1,0:T(8,128)(2,1)S(1)}, u32[]{:S(2)}, u32[]{:S(2)}) collective-permute-start(bf16[2,6,48,128]{3,2,1,0:T(8,128)(2,1)S(1)} %shard_map.155), channel_id=1, source_target_pairs={{0,4},{4,0},{8,12},{12,8},{1,5},{5,1},{9,13},{13,9},{2,6},{6,2},{1... | collective-permute-start | bytes 442376 | tf_op jit(solution)/shard_map/ppermute | solution.py:513
  37.1 8.2 %copy-start.1 = (bf16[384,384]{1,0:T(8,128)(2,1)S(1)}, bf16[384,384]{1,0:T(8,128)(2,1)}, u32[]{:S(2)}) copy-start(bf16[384,384]{1,0:T(8,128)(2,1)} %wq_ref.1) | copy-start | bytes 884740
  37.2 8.2 %copy-start.2 = (bf16[384,384]{1,0:T(8,128)(2,1)S(1)}, bf16[384,384]{1,0:T(8,128)(2,1)}, u32[]{:S(2)}) copy-start(bf16[384,384]{1,0:T(8,128)(2,1)} %wk_ref.1) | copy-start | bytes 884740
  37.2 8.1 %copy-start.3 = (bf16[384,384]{1,0:T(8,128)(2,1)S(1)}, bf16[384,384]{1,0:T(8,128)(2,1)}, u32[]{:S(2)}) copy-start(bf16[384,384]{1,0:T(8,128)(2,1)} %wv_ref.1) | copy-start | bytes 884740
  37.2 8.1 %copy-start.4 = (bf16[384,384]{1,0:T(8,128)(2,1)S(1)}, bf16[384,384]{1,0:T(8,128)(2,1)}, u32[]{:S(2)}) copy-start(bf16[384,384]{1,0:T(8,128)(2,1)} %wo_ref.1) | copy-start | bytes 884740
  39.0 2.0 %collective-permute-start.12 = (bf16[288,128]{1,0:T(8,128)(2,1)S(1)}, bf16[288,128]{1,0:T(8,128)(2,1)S(1)}, u32[]{:S(2)}, u32[]{:S(2)}) collective-permute-start(bf16[288,128]{1,0:T(8,128)(2,1)S(1)} %get-tuple-element.20), channel_id=1, source_target_pairs={{0,4},{4,0},{8,12},{12,8},{1,5},{5,1},{9,13},{13,9},{2,6},{6,2},{1... | collective-permute-start | bytes 221192 | tf_op jit(solution)/shard_map/ppermute | solution.py:513
  39.6 4.4 %collective-permute-start.13 = (bf16[288,128]{1,0:T(8,128)(2,1)S(1)}, bf16[288,128]{1,0:T(8,128)(2,1)S(1)}, u32[]{:S(2)}, u32[]{:S(2)}) collective-permute-start(bf16[288,128]{1,0:T(8,128)(2,1)S(1)} %get-tuple-element.21), channel_id=1, source_target_pairs={{0,8},{4,12},{8,0},{12,4},{1,9},{5,13},{9,1},{13,5},{2,10},{6,14},... | collective-permute-start | bytes 221192 | tf_op jit(solution)/shard_map/ppermute | solution.py:513
  41.0 4.3 %collective-permute-start.14 = (bf16[288,128]{1,0:T(8,128)(2,1)S(1)}, bf16[288,128]{1,0:T(8,128)(2,1)S(1)}, u32[]{:S(2)}, u32[]{:S(2)}) collective-permute-start(bf16[288,128]{1,0:T(8,128)(2,1)S(1)} %get-tuple-element.22), channel_id=1, source_target_pairs={{0,12},{4,8},{8,4},{12,0},{1,13},{5,9},{9,5},{13,1},{2,14},{6,10},... | collective-permute-start | bytes 221192 | tf_op jit(solution)/shard_map/ppermute | solution.py:513

commit v6 on v5

--- a/solution.py
+++ b/solution.py
@@ -45,13 +45,20 @@
     return jax.ShapeDtypeStruct(shape, dtype)
 
 
-def group_sums(rows):
-    channels = rows.shape[-1]
+def same_group(channels):
     first = lax.broadcasted_iota(jnp.int32, (channels, channels), 0)
     second = lax.broadcasted_iota(jnp.int32, (channels, channels), 1)
-    same = ((first * 43691) >> 19) == ((second * 43691) >> 19)
+    return (((first * 43691) >> 19) == ((second * 43691) >> 19)).astype(BF16)
+
+
+def channel_groups(out_ref):
+    out_ref[...] = same_group(out_ref.shape[0])
+
+
+def group_sums(rows, groups=None):
+    groups = same_group(rows.shape[-1]) if groups is None else groups
     terms = jnp.concatenate(split3(rows), axis=0).astype(BF16)
-    sums = jnp.dot(terms, same.astype(BF16), preferred_element_type=F32)
+    sums = jnp.dot(terms, groups, preferred_element_type=F32)
     size = rows.shape[0]
     return sums[0:size] + sums[size : 2 * size] + sums[2 * size :]
 
@@ -100,7 +107,7 @@
 
 
 def own_frame(
-    r_ref, own_ref, one_ref, two_ref, three_ref, table_ref, loaded_ref, across_ref, out_ref, raw_ref, blocks_ref
+    r_ref, own_ref, one_ref, two_ref, three_ref, table_ref, loaded_ref, across_ref, groups_ref, out_ref, raw_ref, blocks_ref
 ):
     blocks = [ref[0] for ref in (own_ref, one_ref, two_ref, three_ref)]
     rows = blocks[0].shape[0]
@@ -108,20 +115,20 @@
         raw_ref[pl.ds((r_ref[0] ^ k) * rows, rows)] = block
         if k > 0:
             blocks_ref[k - 1] = block
-    frame_norm(r_ref, blocks, table_ref, out_ref)
-
-
-def across_frame(r_ref, own_ref, blocks_ref, table_ref, after_ref, out_ref):
-    frame_norm(r_ref, [own_ref[0]] + [blocks_ref[k] for k in range(3)], table_ref, out_ref)
-
-
-def frame_norm(r_ref, blocks, table_ref, out_ref):
+    frame_norm(r_ref, blocks, table_ref, groups_ref[...], out_ref)
+
+
+def across_frame(r_ref, own_ref, blocks_ref, table_ref, after_ref, groups_ref, out_ref):
+    frame_norm(r_ref, [own_ref[0]] + [blocks_ref[k] for k in range(3)], table_ref, groups_ref[...], out_ref)
+
+
+def frame_norm(r_ref, blocks, table_ref, groups, out_ref):
     rows, cols, channels = blocks[0].shape
     wide = [block.astype(F32).reshape(rows * cols, channels) for block in blocks]
     count = len(wide) * rows * cols * GROUP
-    mean = group_sums(eight(sum(jnp.sum(x, axis=0, keepdims=True) for x in wide)))[0:1] / count
+    mean = group_sums(eight(sum(jnp.sum(x, axis=0, keepdims=True) for x in wide)), groups)[0:1] / count
     squares = sum(jnp.sum(jnp.square(x - mean), axis=0, keepdims=True) for x in wide)
-    variance = group_sums(eight(squares))[0:1] / count
+    variance = group_sums(eight(squares), groups)[0:1] / count
     scale = lax.rsqrt(variance + EPSILON) * table_ref[0:1]
     shift = table_ref[1:2]
     for k, x in enumerate(wide):
@@ -253,10 +260,8 @@
     first_conv_rest(0, m_ref, base_ref, a_ref, w_ref, bias_ref, table_ref, out_ref, *scratch)
 
 
-def first_conv_late(m_ref, base_ref, a_ref, w_ref, bias_ref, table_ref, early_ref, out_ref, all_ref, *scratch):
+def first_conv_late(m_ref, base_ref, a_ref, w_ref, bias_ref, table_ref, after_ref, out_ref, *scratch):
     first_conv_rest(2, m_ref, base_ref, a_ref, w_ref, bias_ref, table_ref, out_ref, *scratch)
-    all_ref[0:2] = early_ref[...]
-    all_ref[2:4] = out_ref[...]
 
 
 def first_conv_rest(
@@ -409,12 +414,16 @@
     on_half(m_ref, other, body)
 
 
-def second_conv_near(m_ref, own_ref, mate_ref, w_ref, total_ref, both, a_ref):
-    half_taps(m_ref, False, own_ref, mate_ref, (0, 1, 2, 3), None, w_ref, total_ref, both, a_ref)
-
-
-def second_conv_early(m_ref, near_total_ref, own_ref, mate_ref, w_ref, total_ref, both, a_ref):
-    half_taps(m_ref, True, own_ref, mate_ref, (0, 1), near_total_ref, w_ref, total_ref, both, a_ref)
+def second_conv_near_early(m_ref, own_ref, mate_ref, w_ref, total_ref, both, a_ref):
+    half_taps(m_ref, False, own_ref, mate_ref, (0, 1), None, w_ref, total_ref, both, a_ref)
+
+
+def second_conv_near_late(m_ref, base_ref, own_ref, mate_ref, w_ref, total_ref, both, a_ref):
+    half_taps(m_ref, False, own_ref, mate_ref, (2, 3), base_ref, w_ref, total_ref, both, a_ref)
+
+
+def second_conv_early(m_ref, base_ref, own_ref, mate_ref, w_ref, total_ref, both, a_ref):
+    half_taps(m_ref, True, own_ref, mate_ref, (0, 1), base_ref, w_ref, total_ref, both, a_ref)
 
 
 def second_conv_late(m_ref, total_ref, own_ref, mate_ref, w_ref, bias_ref, *refs):
@@ -466,7 +475,7 @@
 
 
 def frame_attention(
-    r_ref, m_ref, raw_ref, p0, p1, p2, p3, table_ref, wq_ref, wk_ref, wv_ref, wo_ref, out_ref, held, hidden
+    r_ref, m_ref, raw_ref, p0, p1, p2, p3, table_ref, wq_ref, wk_ref, wv_ref, wo_ref, groups_ref, out_ref, held, hidden
 ):
     height, cols, channels = raw_ref.shape
     rows = height // 4
@@ -485,15 +494,15 @@
         raw = raw_ref[b * rows : (b + 1) * rows].reshape(quarter, channels).astype(F32)
         hidden[b * quarter : (b + 1) * quarter] = (raw + update).astype(BF16).astype(F32)
     own = hidden[pl.ds(r_ref[0] * quarter, quarter)]
-    out_ref[...] = attend(own, hidden[...], table_ref, wq_ref, wk_ref, wv_ref, wo_ref)
-
-
-def attend(own, wide, table_ref, wq_ref, wk_ref, wv_ref, wo_ref):
+    out_ref[...] = attend(own, hidden[...], table_ref, wq_ref, wk_ref, wv_ref, wo_ref, groups_ref[...])
+
+
+def attend(own, wide, table_ref, wq_ref, wk_ref, wv_ref, wo_ref, groups=None):
     gain, shift = table_ref[4:5], table_ref[5:6]
     count = wide.shape[0] * GROUP
-    mean = group_sums(eight(jnp.sum(wide, axis=0, keepdims=True)))[0:1] / count
+    mean = group_sums(eight(jnp.sum(wide, axis=0, keepdims=True)), groups)[0:1] / count
     centered = wide - mean
-    variance = group_sums(eight(jnp.sum(centered * centered, axis=0, keepdims=True)))[0:1] / count
+    variance = group_sums(eight(jnp.sum(centered * centered, axis=0, keepdims=True)), groups)[0:1] / count
     scale = lax.rsqrt(variance + EPSILON) * gain
     normed = (centered * scale + shift).astype(BF16)
     mine = ((own - mean) * scale + shift).astype(BF16)
@@ -556,7 +565,6 @@
     split = n == 4 and frames == 4 and channels == 384 and packs(frames, outputs)
     lanes = 128 * (-(-outputs // 128)) if split else outputs
     loaded = struct((3, 3, 3 * lanes, channels))
-    weights1 = call(load, loaded)(taps(first_kernel))
     step = 8 * (-(-frames // 8))
     size = 6 * step
     stats_scratch = pltpu.VMEM((step, outputs), F32)
@@ -578,16 +586,18 @@
 
         height = n * rows
         one, two, three = (over_rows(features, k) for k in (1, 2, 3))
+        weights1 = call(load, loaded)(taps(first_kernel))
+        groups = call(channel_groups, struct((channels, channels)))()
         frame = struct((1, height, cols, channels))
         across_own = over_x(features)
         active1, raw, blocks = call(
             own_frame, (frame, struct((height, cols, channels)), struct((n - 1, rows, cols, channels)))
-        )(r, features, one, two, three, table, weights1, across_own)
+        )(r, features, one, two, three, table, weights1, across_own, groups)
         across_blocks, mate = over_x(blocks), over_core(active1)
         pair, rimmed = (pltpu.VMEM((k, height + 2, cols, channels), BF16) for k in (2, 1))
         tall = struct((frames, n * plane, 3 * lanes), F32)
         near_total = call(first_conv_near, tall, (pair,))(m, active1, mate, weights1)
-        across = call(across_frame, frame)(r, across_own, across_blocks, table, near_total)
+        across = call(across_frame, frame)(r, across_own, across_blocks, table, near_total, groups)
         beside = over_core(across)
         across_total = call(first_conv_across, tall, (rimmed,))(m, near_total, across, weights1)
         scratch = (
@@ -597,36 +607,41 @@
             stats_scratch,
         )
         packed = struct((2, 3 * height // 4, cols, 128))
-        packed_all = struct((4, 3 * height // 4, cols, 128))
         early = call(first_conv_early, packed, scratch)(m, across_total, beside, weights1, first_bias, table)
-        late, active2 = call(first_conv_late, (packed, packed_all), scratch)(
+        late = call(first_conv_late, packed, scratch)(
             m, across_total, beside, weights1, first_bias, table, early
         )
 
-        early, late, mate = over_x(early), over_x(late), over_core(active2)
+        early_mate, late_mate = over_core(early), over_core(late)
+        early_across, late_across = over_x(early), over_x(late)
+        weights2 = call(load, loaded)(taps(second_kernel), early)
+        both, two_frames = pltpu.VMEM((2, *packed.shape), BF16), pltpu.VMEM((2, height + 2, cols, 256), BF16)
+        near_early = call(second_conv_near_early, tall, (both, two_frames))(m, early, early_mate, weights2)
         long = pl.CostEstimate(flops=10**10, bytes_accessed=4 * 10**7, transcendentals=0)
-        weights2 = call(load, loaded, cost=long)(taps(second_kernel), early)
-        both, both_all = (pltpu.VMEM((2, *half.shape), BF16) for half in (packed, packed_all))
-        two_frames, all_frames = (pltpu.VMEM((k, height + 2, cols, 256), BF16) for k in (2, 4))
-        near_total = call(second_conv_near, tall, (both_all, all_frames))(m, active2, mate, weights2)
-        early_beside = over_core(early)
-        late_beside = over_core(held_until(late, near_total))
+        early_across = call(hand_on, packed, cost=long)(early_across, near_early)
+        early_beside = over_core(early_across)
+        near_total = call(second_conv_near_late, tall, (both, two_frames))(
+            m, near_early, late, late_mate, weights2
+        )
+        late_across = held_until(late_across, near_total)
+        late_beside = over_core(late_across)
         early_total = call(second_conv_early, tall, (both, two_frames))(
-            m, near_total, early, early_beside, weights2
+            m, near_total, early_across, early_beside, weights2
         )
         piece = struct((3 * plane, 128))
         pieces = call(
             second_conv_late,
             [piece] * frames,
             (both, two_frames, pltpu.VMEM(tall.shape, F32), pltpu.VMEM((frames, n * plane, outputs), BF16)),
-        )(m, early_total, late, late_beside, weights2, second_bias)
+        )(m, early_total, late_across, late_beside, weights2, second_bias)
         pieces = [pieces[0]] + [swapped(pieces[k], "tm", lambda i, k=k: i ^ k) for k in range(1, frames)]
         decoded = call(
             frame_attention,
             struct((plane, channels)),
             (pltpu.VMEM((frames, 3 * plane, 128), BF16), pltpu.VMEM((n * plane, channels), F32)),
-        )(r, m, raw, *pieces, table, query_weight, key_weight, value_weight, output_weight)
+        )(r, m, raw, *pieces, table, query_weight, key_weight, value_weight, output_weight, groups)
     else:
+        weights1 = taps(first_kernel)
         halo = struct((cols, channels))
         near, far, block = call(first_stats, (halo, halo, struct((16, channels))))(r, features)
         active1 = call(functools.partial(first_norm, n), struct((1, rows + 2, cols, channels)))(

time: 47.8 us -> 47.1 us (0.985)
  waiting for transfers between devices: 12.2 us -> 10.6 us
  starting transfers between devices: 14.8 us -> 15.5 us
    ppermute x15 -> x16, waiting for transfers between devices: 12.2 us -> 10.6 us  [swapped(): lax.ppermute(value, axis, [(i, partner(i)) for i in range(lax.axis_size(a...]
    ppermute x15 -> x16, starting transfers between devices: 14.8 us -> 15.5 us  [swapped(): lax.ppermute(value, axis, [(i, partner(i)) for i in range(lax.axis_size(a...]
    pallas_call x13 -> x16, Pallas kernels: 17.9 us -> 18.2 us  [run(): pl.pallas_call(functools.partial(body, *axes), out_shape=outs, in_specs=[...]
  transfers between devices with their start and end apart: 15 -> 16, of which waited for: 8 -> 6; matrix products, arithmetic and copies ran while one was open for 2% -> 2% of each run, Pallas kernels for 24% -> 25%
where the time goes in v6:
time: 47.1 us; the launch traced here: 47 us
  Pallas kernels  18.2 us (39%)
  starting transfers between devices  15.5 us (33%)
  waiting for transfers between devices  10.6 us (23%)
  local copies, waits for them, and re-layouts  1.6 us (3%)
  other arithmetic  0.86 us (2%)
    pallas_call x16, Pallas kernels, run(): pl.pallas_call(functools.partial(body, *axes), out_shape=outs, in_specs=[...  18.2 us
    ppermute x16, starting transfers between devices, swapped(): lax.ppermute(value, axis, [(i, partner(i)) for i in range(lax.axis_size(a...  15.5 us
    ppermute x16, waiting for transfers between devices, swapped(): lax.ppermute(value, axis, [(i, partner(i)) for i in range(lax.axis_size(a...  10.6 us
    unnamed x18, local copies, waits for them, and re-layouts  1.6 us
  transfers between devices with their start and end apart: 16, of which 6 were waited for; matrix products, arithmetic and copies ran while one was open for 2% of the time, Pallas kernels for 25%

profile of v6, /device:TPU:0, one launch (start us, length us, event | category | flops | bytes accessed | tf_op | source)
XLA Modules:
  0.0 47.0 jit_solution(6789125047052451385)
XLA Ops:
  0.0 5.0 %collective-permute-start.2 = (bf16[1,2,48,384]{3,2,1,0:T(8,128)(2,1)}, bf16[1,2,48,384]{3,2,1,0:T(8,128)(2,1)S(1)}, u32[]{:S(2)}, u32[]{:S(2)}) collective-permute-start(bf16[1,2,48,384]{3,2,1,0:T(8,128)(2,1)} %own_ref.1), channel_id=1, source_target_pairs={{0,3},{1,2},{2,1},{3,0},{4,7},{5,6},{6,5},{7,4},{8,11},{9,10},{10,... | collective-permute-start | bytes 221192 | tf_op jit(solution)/shard_map/ppermute | solution.py:522
  5.1 0.6 %collective-permute-start = (bf16[1,2,48,384]{3,2,1,0:T(8,128)(2,1)}, bf16[1,2,48,384]{3,2,1,0:T(8,128)(2,1)S(1)}, u32[]{:S(2)}, u32[]{:S(2)}) collective-permute-start(bf16[1,2,48,384]{3,2,1,0:T(8,128)(2,1)} %own_ref.1), channel_id=1, source_target_pairs={{0,1},{1,0},{2,3},{3,2},{4,5},{5,4},{6,7},{7,6},{8,9},{9,8},{10,11... | collective-permute-start | bytes 221192 | tf_op jit(solution)/shard_map/ppermute | solution.py:522
  5.6 1.7 %collective-permute-start.3 = (bf16[1,2,48,384]{3,2,1,0:T(8,128)(2,1)}, bf16[1,2,48,384]{3,2,1,0:T(8,128)(2,1)S(1)}, u32[]{:S(2)}, u32[]{:S(2)}) collective-permute-start(bf16[1,2,48,384]{3,2,1,0:T(8,128)(2,1)} %own_ref.1), channel_id=1, source_target_pairs={{0,8},{4,12},{8,0},{12,4},{1,9},{5,13},{9,1},{13,5},{2,10},{6,14},... | collective-permute-start | bytes 221192 | tf_op jit(solution)/shard_map/ppermute | solution.py:522
  7.4 0.8 %select_select_fusion.table_ref = f32[8,384]{1,0:T(8,128)S(1)} fusion(f32[384]{0:T(512)} %param.16, f32[384]{0:T(512)} %param.17, f32[384]{0:T(512)} %param.20, f32[384]{0:T(512)} %param.21, f32[384]{0:T(512)} %param.24, f32[384]{0:T(512)} %param.25, pred[8]{0:T(512)(128)(4,1)S(1)} %get-tuple-element.19, pred[8]{0:T(512)(128)(4,1)S(1)} %get-tuple-element.20, ...), kind=kLoop, calls=%fused_computation | loop fusion | flops 18432 | bytes 21552 | tf_op jit(solution)/shard_map/jit(_where)/select_n | solution.py:563
  8.2 0.1 shard_map.146.groups_ref
  8.3 0.0 copy-start
  8.3 1.5 %copy-done = bf16[96,3,3,3,384]{4,0,3,2,1:T(8,128)(2,1)S(1)} copy-done((bf16[96,3,3,3,384]{4,0,3,2,1:T(8,128)(2,1)S(1)}, bf16[96,3,3,3,384]{4,0,3,2,1:T(8,128)(2,1)}, u32[]{:S(2)}) %copy-start) | copy-done | bytes 1990680
  9.8 0.2 shard_map.145.loaded_ref.w_ref
  10.1 1.4 %collective-permute-done.1.two_ref = bf16[1,2,48,384]{3,2,1,0:T(8,128)(2,1)S(1)} collective-permute-done((bf16[1,2,48,384]{3,2,1,0:T(8,128)(2,1)}, bf16[1,2,48,384]{3,2,1,0:T(8,128)(2,1)S(1)}, u32[]{:S(2)}, u32[]{:S(2)}) %collective-permute-start.1) | collective-permute-done | bytes 73760 | tf_op jit(solution)/shard_map/ppermute | solution.py:522
  11.5 0.0 collective-permute-done.one_ref
  11.5 0.7 %shard_map.147 = (bf16[1,8,48,384]{3,2,1,0:T(8,128)(2,1)S(1)}, bf16[8,48,384]{2,1,0:T(8,128)(2,1)S(1)}, bf16[3,2,48,384]{3,2,1,0:T(8,128)(2,1)S(1)}) custom-call(bf16[1,2,48,384]{3,2,1,0:T(8,128)(2,1)S(1)} %copy-done.6, bf16[1,2,48,384]{3,2,1,0:T(8,128)(2,1)S(1)} %collective-permute-done.one_ref, bf16[1,2,48,384]{3,2,1,0:T(8,128)(2,1)S(1)} %collective-permute-done.1.two_ref, ...), custom_call_target="tpu_custom_call" | custom-call | tf_op jit(solution)/shard_map/pallas_call | solution.py:31
  12.2 0.1 collective-permute-start.4
  12.2 1.6 %collective-permute-start.5 = (bf16[3,2,48,384]{3,2,1,0:T(8,128)(2,1)S(1)}, bf16[3,2,48,384]{3,2,1,0:T(8,128)(2,1)S(1)}, u32[]{:S(2)}, u32[]{:S(2)}) collective-permute-start(bf16[3,2,48,384]{3,2,1,0:T(8,128)(2,1)S(1)} %get-tuple-element.14), channel_id=1, source_target_pairs={{0,8},{4,12},{8,0},{12,4},{1,9},{5,13},{9,1},{13,5},{2,10},{6,14},... | collective-permute-start | bytes 663560 | tf_op jit(solution)/shard_map/ppermute | solution.py:522
  13.8 0.0 collective-permute-done.4.mate_ref
  13.8 3.2 %shard_map.148.after_ref.near_total_ref = f32[4,384,384]{2,1,0:T(8,128)S(1)} custom-call(bf16[1,8,48,384]{3,2,1,0:T(8,128)(2,1)S(1)} %get-tuple-element.13.own_ref, bf16[1,8,48,384]{3,2,1,0:T(8,128)(2,1)S(1)} %collective-permute-done.4.mate_ref, bf16[3,3,384,384]{3,2,1,0:T(8,128)(2,1)S(1)} %shard_map.145.loaded_ref.w_ref), custom_call_target="tpu_custom_call" | custom-call | tf_op jit(solution)/shard_map/pallas_call | solution.py:31
  17.0 3.1 %collective-permute-done.5.blocks_ref = bf16[3,2,48,384]{3,2,1,0:T(8,128)(2,1)S(1)} collective-permute-done((bf16[3,2,48,384]{3,2,1,0:T(8,128)(2,1)S(1)}, bf16[3,2,48,384]{3,2,1,0:T(8,128)(2,1)S(1)}, u32[]{:S(2)}, u32[]{:S(2)}) %collective-permute-start.5) | collective-permute-done | bytes 221216 | tf_op jit(solution)/shard_map/ppermute | solution.py:522
  20.1 0.7 %shard_map.149.a_ref = bf16[1,8,48,384]{3,2,1,0:T(8,128)(2,1)S(1)} custom-call(bf16[1,2,48,384]{3,2,1,0:T(8,128)(2,1)S(1)} %collective-permute-done.3.across_ref.own_ref, bf16[3,2,48,384]{3,2,1,0:T(8,128)(2,1)S(1)} %collective-permute-done.5.blocks_ref, f32[8,384]{1,0:T(8,128)S(1)} %select_select_fusion.table_ref, ...), custom_call_target="tpu_custom_call" | custom-call | tf_op jit(solution)/shard_map/pallas_call | solution.py:31
  20.8 0.0 copy-start.7
  20.8 0.1 collective-permute-start.6
  20.8 1.3 %shard_map.150.base_ref = f32[4,384,384]{2,1,0:T(8,128)S(1)} custom-call(f32[4,384,384]{2,1,0:T(8,128)S(1)} %shard_map.148.after_ref.near_total_ref, bf16[1,8,48,384]{3,2,1,0:T(8,128)(2,1)S(1)} %shard_map.149.a_ref, bf16[3,3,384,384]{3,2,1,0:T(8,128)(2,1)S(1)} %shard_map.145.loaded_ref.w_ref), custom_call_target="tpu_custom_call" | custom-call | tf_op jit(solution)/shard_map/pallas_call | solution.py:31
  22.1 0.3 collective-permute-done.6.a_ref
  22.4 0.8 %shard_map.151.refs_0_.own_ref.after_ref = bf16[2,6,48,128]{3,2,1,0:T(8,128)(2,1)S(1)} custom-call(f32[4,384,384]{2,1,0:T(8,128)S(1)} %shard_map.150.base_ref, bf16[1,8,48,384]{3,2,1,0:T(8,128)(2,1)S(1)} %collective-permute-done.6.a_ref, bf16[3,3,384,384]{3,2,1,0:T(8,128)(2,1)S(1)} %shard_map.145.loaded_ref.w_ref, f32[96]{0:T(128)S(1)} %copy-done.7, ...), custom_call_target="tpu_custom_call" | custom-call | tf_op jit(solution)/shard_map/pallas_call | solution.py:31
  23.2 0.0 copy-start.1
  23.2 0.2 collective-permute-start.7
  23.4 3.1 %collective-permute-start.9 = (bf16[2,6,48,128]{3,2,1,0:T(8,128)(2,1)S(1)}, bf16[2,6,48,128]{3,2,1,0:T(8,128)(2,1)S(1)}, u32[]{:S(2)}, u32[]{:S(2)}) collective-permute-start(bf16[2,6,48,128]{3,2,1,0:T(8,128)(2,1)S(1)} %shard_map.151.refs_0_.own_ref.after_ref), channel_id=1, source_target_pairs={{0,8},{4,12},{8,0},{12,4},{1,9},{5,13},{9,1},{13,5},{2,10},{6,14},... | collective-permute-start | bytes 442376 | tf_op jit(solution)/shard_map/ppermute | solution.py:522
  26.6 1.6 %shard_map.154.own_ref = bf16[2,6,48,128]{3,2,1,0:T(8,128)(2,1)S(1)} custom-call(f32[4,384,384]{2,1,0:T(8,128)S(1)} %shard_map.150.base_ref, bf16[1,8,48,384]{3,2,1,0:T(8,128)(2,1)S(1)} %collective-permute-done.6.a_ref, bf16[3,3,384,384]{3,2,1,0:T(8,128)(2,1)S(1)} %shard_map.145.loaded_ref.w_ref, f32[96]{0:T(128)S(1)} %copy-done.7, ...), custom_call_target="tpu_custom_call" | custom-call | tf_op jit(solution)/shard_map/pallas_call | solution.py:31
  28.2 0.5 %collective-permute-start.11 = (bf16[2,6,48,128]{3,2,1,0:T(8,128)(2,1)S(1)}, bf16[2,6,48,128]{3,2,1,0:T(8,128)(2,1)S(1)}, u32[]{:S(2)}, u32[]{:S(2)}) collective-permute-start(bf16[2,6,48,128]{3,2,1,0:T(8,128)(2,1)S(1)} %shard_map.154.own_ref), channel_id=1, source_target_pairs={{0,8},{4,12},{8,0},{12,4},{1,9},{5,13},{9,1},{13,5},{2,10},{6,14},... | collective-permute-start | bytes 442376 | tf_op jit(solution)/shard_map/ppermute | solution.py:522
  28.7 0.0 collective-permute-start.8
  28.7 0.2 shard_map.152.w_ref
  28.9 2.1 %shard_map.153.base_ref.after_ref = f32[4,384,384]{2,1,0:T(8,128)S(1)} custom-call(bf16[2,6,48,128]{3,2,1,0:T(8,128)(2,1)S(1)} %shard_map.151.refs_0_.own_ref.after_ref, bf16[2,6,48,128]{3,2,1,0:T(8,128)(2,1)S(1)} %collective-permute-done.7.mate_ref, bf16[3,3,384,384]{3,2,1,0:T(8,128)(2,1)S(1)} %shard_map.152.w_ref), custom_call_target="tpu_custom_call" | custom-call | tf_op jit(solution)/shard_map/pallas_call | solution.py:31
  31.0 0.6 %collective-permute-start.10 = (bf16[2,6,48,128]{3,2,1,0:T(8,128)(2,1)S(1)}, bf16[2,6,48,128]{3,2,1,0:T(8,128)(2,1)S(1)}, u32[]{:S(2)}, u32[]{:S(2)}) collective-permute-start(bf16[2,6,48,128]{3,2,1,0:T(8,128)(2,1)S(1)} %shard_map.156.own_ref), channel_id=1, source_target_pairs={{0,4},{4,0},{8,12},{12,8},{1,5},{5,1},{9,13},{13,9},{2,6},{6,2},{1... | collective-permute-start | bytes 442376 | tf_op jit(solution)/shard_map/ppermute | solution.py:522
  31.6 0.0 collective-permute-done.8.mate_ref
  31.6 1.2 %shard_map.155.base_ref.after_ref = f32[4,384,384]{2,1,0:T(8,128)S(1)} custom-call(f32[4,384,384]{2,1,0:T(8,128)S(1)} %shard_map.153.base_ref.after_ref, bf16[2,6,48,128]{3,2,1,0:T(8,128)(2,1)S(1)} %shard_map.154.own_ref, bf16[2,6,48,128]{3,2,1,0:T(8,128)(2,1)S(1)} %collective-permute-done.8.mate_ref, bf16[3,3,384,384]{3,2,1,0:T(8,128)(2,1)S(1)} %shard_map.152.w_ref), custom_call_target="tpu_custom_call" | custom-call | tf_op jit(solution)/shard_map/pallas_call | solution.py:31
  32.9 1.4 %collective-permute-done.11.x_ref = bf16[2,6,48,128]{3,2,1,0:T(8,128)(2,1)S(1)} collective-permute-done((bf16[2,6,48,128]{3,2,1,0:T(8,128)(2,1)S(1)}, bf16[2,6,48,128]{3,2,1,0:T(8,128)(2,1)S(1)}, u32[]{:S(2)}, u32[]{:S(2)}) %collective-permute-start.11) | collective-permute-done | bytes 147488 | tf_op jit(solution)/shard_map/ppermute | solution.py:522
  34.3 0.0 copy-start.8
  34.3 0.1 collective-permute-start.12
  34.4 2.1 %shard_map.157.total_ref = f32[4,384,384]{2,1,0:T(8,128)S(1)} custom-call(f32[4,384,384]{2,1,0:T(8,128)S(1)} %shard_map.155.base_ref.after_ref, bf16[2,6,48,128]{3,2,1,0:T(8,128)(2,1)S(1)} %shard_map.156.own_ref, bf16[2,6,48,128]{3,2,1,0:T(8,128)(2,1)S(1)} %collective-permute-done.10.mate_ref, bf16[3,3,384,384]{3,2,1,0:T(8,128)(2,1)S(1)} %shard_map.152.w_ref), custom_call_target="tpu_custom_call" | custom-call | tf_op jit(solution)/shard_map/pallas_call | solution.py:31
  36.4 0.0 copy-start.2
  36.5 0.0 copy-start.3
  36.5 0.0 copy-start.4
  36.5 0.0 copy-start.5
  36.5 1.8 %shard_map.159 = (bf16[288,128]{1,0:T(8,128)(2,1)S(1)}, bf16[288,128]{1,0:T(8,128)(2,1)S(1)}, bf16[288,128]{1,0:T(8,128)(2,1)S(1)}, bf16[288,128]{1,0:T(8,128)(2,1)S(1)}) custom-call(f32[4,384,384]{2,1,0:T(8,128)S(1)} %shard_map.157.total_ref, bf16[2,6,48,128]{3,2,1,0:T(8,128)(2,1)S(1)} %shard_map.158.own_ref, ...), custom_call_target="tpu_custom_call" | custom-call | tf_op jit(solution)/shard_map/pallas_call | solution.py:31
  38.3 0.6 %collective-permute-start.13 = (bf16[288,128]{1,0:T(8,128)(2,1)S(1)}, bf16[288,128]{1,0:T(8,128)(2,1)S(1)}, u32[]{:S(2)}, u32[]{:S(2)}) collective-permute-start(bf16[288,128]{1,0:T(8,128)(2,1)S(1)} %get-tuple-element.16), channel_id=1, source_target_pairs={{0,4},{4,0},{8,12},{12,8},{1,5},{5,1},{9,13},{13,9},{2,6},{6,2},{1... | collective-permute-start | bytes 221192 | tf_op jit(solution)/shard_map/ppermute | solution.py:522
  38.8 1.3 %collective-permute-start.14 = (bf16[288,128]{1,0:T(8,128)(2,1)S(1)}, bf16[288,128]{1,0:T(8,128)(2,1)S(1)}, u32[]{:S(2)}, u32[]{:S(2)}) collective-permute-start(bf16[288,128]{1,0:T(8,128)(2,1)S(1)} %get-tuple-element.17), channel_id=1, source_target_pairs={{0,8},{4,12},{8,0},{12,4},{1,9},{5,13},{9,1},{13,5},{2,10},{6,14},... | collective-permute-start | bytes 221192 | tf_op jit(solution)/shard_map/ppermute | solution.py:522
  40.2 0.1 collective-permute-start.15
  40.3 3.0 %collective-permute-done.14.p2 = bf16[288,128]{1,0:T(8,128)(2,1)S(1)} collective-permute-done((bf16[288,128]{1,0:T(8,128)(2,1)S(1)}, bf16[288,128]{1,0:T(8,128)(2,1)S(1)}, u32[]{:S(2)}, u32[]{:S(2)}) %collective-permute-start.14) | collective-permute-done | bytes 73760 | tf_op jit(solution)/shard_map/ppermute | solution.py:522
  43.3 1.4 %collective-permute-done.15.p3 = bf16[288,128]{1,0:T(8,128)(2,1)S(1)} collective-permute-done((bf16[288,128]{1,0:T(8,128)(2,1)S(1)}, bf16[288,128]{1,0:T(8,128)(2,1)S(1)}, u32[]{:S(2)}, u32[]{:S(2)}) %collective-permute-start.15) | collective-permute-done | bytes 73760 | tf_op jit(solution)/shard_map/ppermute | solution.py:522
  44.7 2.3 %shard_map.160 = bf16[96,384]{1,0:T(8,128)(2,1)} custom-call(bf16[8,48,384]{2,1,0:T(8,128)(2,1)S(1)} %get-tuple-element.12.raw_ref, bf16[288,128]{1,0:T(8,128)(2,1)S(1)} %get-tuple-element.15.p0, bf16[288,128]{1,0:T(8,128)(2,1)S(1)} %collective-permute-done.13.p1, bf16[288,128]{1,0:T(8,128)(2,1)S(1)} %collective-permute-done.14.p2, ...), custom_call_target="tpu_custom_call" | custom-call | tf_op jit(solution)/shard_map/pallas_call | solution.py:31
  (22 shorter events, 0.1 us)
Async XLA Ops:
  0.0 10.1 %collective-permute-start.2 = (bf16[1,2,48,384]{3,2,1,0:T(8,128)(2,1)}, bf16[1,2,48,384]{3,2,1,0:T(8,128)(2,1)S(1)}, u32[]{:S(2)}, u32[]{:S(2)}) collective-permute-start(bf16[1,2,48,384]{3,2,1,0:T(8,128)(2,1)} %own_ref.1), channel_id=1, source_target_pairs={{0,3},{1,2},{2,1},{3,0},{4,7},{5,6},{6,5},{7,4},{8,11},{9,10},{10,... | collective-permute-start | bytes 221192 | tf_op jit(solution)/shard_map/ppermute | solution.py:522
  5.0 6.4 %collective-permute-start.1 = (bf16[1,2,48,384]{3,2,1,0:T(8,128)(2,1)}, bf16[1,2,48,384]{3,2,1,0:T(8,128)(2,1)S(1)}, u32[]{:S(2)}, u32[]{:S(2)}) collective-permute-start(bf16[1,2,48,384]{3,2,1,0:T(8,128)(2,1)} %own_ref.1), channel_id=1, source_target_pairs={{0,2},{1,3},{2,0},{3,1},{4,6},{5,7},{6,4},{7,5},{8,10},{9,11},{10,... | collective-permute-start | bytes 221192 | tf_op jit(solution)/shard_map/ppermute | solution.py:522
  5.1 6.4 %collective-permute-start = (bf16[1,2,48,384]{3,2,1,0:T(8,128)(2,1)}, bf16[1,2,48,384]{3,2,1,0:T(8,128)(2,1)S(1)}, u32[]{:S(2)}, u32[]{:S(2)}) collective-permute-start(bf16[1,2,48,384]{3,2,1,0:T(8,128)(2,1)} %own_ref.1), channel_id=1, source_target_pairs={{0,1},{1,0},{2,3},{3,2},{4,5},{5,4},{6,7},{7,6},{8,9},{9,8},{10,11... | collective-permute-start | bytes 221192 | tf_op jit(solution)/shard_map/ppermute | solution.py:522
  5.6 5.9 %collective-permute-start.3 = (bf16[1,2,48,384]{3,2,1,0:T(8,128)(2,1)}, bf16[1,2,48,384]{3,2,1,0:T(8,128)(2,1)S(1)}, u32[]{:S(2)}, u32[]{:S(2)}) collective-permute-start(bf16[1,2,48,384]{3,2,1,0:T(8,128)(2,1)} %own_ref.1), channel_id=1, source_target_pairs={{0,8},{4,12},{8,0},{12,4},{1,9},{5,13},{9,1},{13,5},{2,10},{6,14},... | collective-permute-start | bytes 221192 | tf_op jit(solution)/shard_map/ppermute | solution.py:522
  8.3 1.6 %copy-start = (bf16[96,3,3,3,384]{4,0,3,2,1:T(8,128)(2,1)S(1)}, bf16[96,3,3,3,384]{4,0,3,2,1:T(8,128)(2,1)}, u32[]{:S(2)}) copy-start(bf16[96,3,3,3,384]{4,0,3,2,1:T(8,128)(2,1)} %param.18) | copy-start | bytes 5971972
  9.8 1.6 %copy-start.6 = (bf16[1,2,48,384]{3,2,1,0:T(8,128)(2,1)S(1)}, bf16[1,2,48,384]{3,2,1,0:T(8,128)(2,1)}, u32[]{:S(2)}) copy-start(bf16[1,2,48,384]{3,2,1,0:T(8,128)(2,1)} %own_ref.1) | copy-start | bytes 221188
  12.2 1.6 %collective-permute-start.4 = (bf16[1,8,48,384]{3,2,1,0:T(8,128)(2,1)S(1)}, bf16[1,8,48,384]{3,2,1,0:T(8,128)(2,1)S(1)}, u32[]{:S(2)}, u32[]{:S(2)}) collective-permute-start(bf16[1,8,48,384]{3,2,1,0:T(8,128)(2,1)S(1)} %get-tuple-element.13.own_ref), channel_id=1, source_target_pairs={{0,4},{4,0},{8,12},{12,8},{1,5},{5,1},{9,13},{13,9},{2,6},{6,2},{1... | collective-permute-start | bytes 884744 | tf_op jit(solution)/shard_map/ppermute | solution.py:522
  12.2 7.8 %collective-permute-start.5 = (bf16[3,2,48,384]{3,2,1,0:T(8,128)(2,1)S(1)}, bf16[3,2,48,384]{3,2,1,0:T(8,128)(2,1)S(1)}, u32[]{:S(2)}, u32[]{:S(2)}) collective-permute-start(bf16[3,2,48,384]{3,2,1,0:T(8,128)(2,1)S(1)} %get-tuple-element.14), channel_id=1, source_target_pairs={{0,8},{4,12},{8,0},{12,4},{1,9},{5,13},{9,1},{13,5},{2,10},{6,14},... | collective-permute-start | bytes 663560 | tf_op jit(solution)/shard_map/ppermute | solution.py:522
  20.8 1.7 %copy-start.7 = (f32[96]{0:T(128)S(1)}, f32[96]{0:T(128)}, u32[]{:S(2)}) copy-start(f32[96]{0:T(128)} %bias_ref.4) | copy-start | bytes 1156
  20.8 1.6 %collective-permute-start.6 = (bf16[1,8,48,384]{3,2,1,0:T(8,128)(2,1)S(1)}, bf16[1,8,48,384]{3,2,1,0:T(8,128)(2,1)S(1)}, u32[]{:S(2)}, u32[]{:S(2)}) collective-permute-start(bf16[1,8,48,384]{3,2,1,0:T(8,128)(2,1)S(1)} %shard_map.149.a_ref), channel_id=1, source_target_pairs={{0,4},{4,0},{8,12},{12,8},{1,5},{5,1},{9,13},{13,9},{2,6},{6,2},{1... | collective-permute-start | bytes 884744 | tf_op jit(solution)/shard_map/ppermute | solution.py:522
  23.2 5.5 %copy-start.1 = (bf16[96,3,3,3,384]{4,0,3,2,1:T(8,128)(2,1)S(1)}, bf16[96,3,3,3,384]{4,0,3,2,1:T(8,128)(2,1)}, u32[]{:S(2)}) copy-start(bf16[96,3,3,3,384]{4,0,3,2,1:T(8,128)(2,1)} %param.22) | copy-start | bytes 5971972
  23.2 5.7 %collective-permute-start.7 = (bf16[2,6,48,128]{3,2,1,0:T(8,128)(2,1)S(1)}, bf16[2,6,48,128]{3,2,1,0:T(8,128)(2,1)S(1)}, u32[]{:S(2)}, u32[]{:S(2)}) collective-permute-start(bf16[2,6,48,128]{3,2,1,0:T(8,128)(2,1)S(1)} %shard_map.151.refs_0_.own_ref.after_ref), channel_id=1, source_target_pairs={{0,4},{4,0},{8,12},{12,8},{1,5},{5,1},{9,13},{13,9},{2,6},{6,2},{1... | collective-permute-start | bytes 442376 | tf_op jit(solution)/shard_map/ppermute | solution.py:522
  23.4 7.6 %collective-permute-start.9 = (bf16[2,6,48,128]{3,2,1,0:T(8,128)(2,1)S(1)}, bf16[2,6,48,128]{3,2,1,0:T(8,128)(2,1)S(1)}, u32[]{:S(2)}, u32[]{:S(2)}) collective-permute-start(bf16[2,6,48,128]{3,2,1,0:T(8,128)(2,1)S(1)} %shard_map.151.refs_0_.own_ref.after_ref), channel_id=1, source_target_pairs={{0,8},{4,12},{8,0},{12,4},{1,9},{5,13},{9,1},{13,5},{2,10},{6,14},... | collective-permute-start | bytes 442376 | tf_op jit(solution)/shard_map/ppermute | solution.py:522
  28.2 6.1 %collective-permute-start.11 = (bf16[2,6,48,128]{3,2,1,0:T(8,128)(2,1)S(1)}, bf16[2,6,48,128]{3,2,1,0:T(8,128)(2,1)S(1)}, u32[]{:S(2)}, u32[]{:S(2)}) collective-permute-start(bf16[2,6,48,128]{3,2,1,0:T(8,128)(2,1)S(1)} %shard_map.154.own_ref), channel_id=1, source_target_pairs={{0,8},{4,12},{8,0},{12,4},{1,9},{5,13},{9,1},{13,5},{2,10},{6,14},... | collective-permute-start | bytes 442376 | tf_op jit(solution)/shard_map/ppermute | solution.py:522
  28.7 2.9 %collective-permute-start.8 = (bf16[2,6,48,128]{3,2,1,0:T(8,128)(2,1)S(1)}, bf16[2,6,48,128]{3,2,1,0:T(8,128)(2,1)S(1)}, u32[]{:S(2)}, u32[]{:S(2)}) collective-permute-start(bf16[2,6,48,128]{3,2,1,0:T(8,128)(2,1)S(1)} %shard_map.154.own_ref), channel_id=1, source_target_pairs={{0,4},{4,0},{8,12},{12,8},{1,5},{5,1},{9,13},{13,9},{2,6},{6,2},{1... | collective-permute-start | bytes 442376 | tf_op jit(solution)/shard_map/ppermute | solution.py:522
  31.0 3.3 %collective-permute-start.10 = (bf16[2,6,48,128]{3,2,1,0:T(8,128)(2,1)S(1)}, bf16[2,6,48,128]{3,2,1,0:T(8,128)(2,1)S(1)}, u32[]{:S(2)}, u32[]{:S(2)}) collective-permute-start(bf16[2,6,48,128]{3,2,1,0:T(8,128)(2,1)S(1)} %shard_map.156.own_ref), channel_id=1, source_target_pairs={{0,4},{4,0},{8,12},{12,8},{1,5},{5,1},{9,13},{13,9},{2,6},{6,2},{1... | collective-permute-start | bytes 442376 | tf_op jit(solution)/shard_map/ppermute | solution.py:522
  34.3 2.2 %copy-start.8 = (f32[96]{0:T(128)S(1)}, f32[96]{0:T(128)}, u32[]{:S(2)}) copy-start(f32[96]{0:T(128)} %bias_ref.5) | copy-start | bytes 1156
  34.3 2.2 %collective-permute-start.12 = (bf16[2,6,48,128]{3,2,1,0:T(8,128)(2,1)S(1)}, bf16[2,6,48,128]{3,2,1,0:T(8,128)(2,1)S(1)}, u32[]{:S(2)}, u32[]{:S(2)}) collective-permute-start(bf16[2,6,48,128]{3,2,1,0:T(8,128)(2,1)S(1)} %shard_map.158.own_ref), channel_id=1, source_target_pairs={{0,4},{4,0},{8,12},{12,8},{1,5},{5,1},{9,13},{13,9},{2,6},{6,2},{1... | collective-permute-start | bytes 442376 | tf_op jit(solution)/shard_map/ppermute | solution.py:522
  36.4 8.2 %copy-start.2 = (bf16[384,384]{1,0:T(8,128)(2,1)S(1)}, bf16[384,384]{1,0:T(8,128)(2,1)}, u32[]{:S(2)}) copy-start(bf16[384,384]{1,0:T(8,128)(2,1)} %wq_ref.1) | copy-start | bytes 884740
  36.5 8.2 %copy-start.3 = (bf16[384,384]{1,0:T(8,128)(2,1)S(1)}, bf16[384,384]{1,0:T(8,128)(2,1)}, u32[]{:S(2)}) copy-start(bf16[384,384]{1,0:T(8,128)(2,1)} %wk_ref.1) | copy-start | bytes 884740
  36.5 8.2 %copy-start.4 = (bf16[384,384]{1,0:T(8,128)(2,1)S(1)}, bf16[384,384]{1,0:T(8,128)(2,1)}, u32[]{:S(2)}) copy-start(bf16[384,384]{1,0:T(8,128)(2,1)} %wv_ref.1) | copy-start | bytes 884740
  36.5 8.2 %copy-start.5 = (bf16[384,384]{1,0:T(8,128)(2,1)S(1)}, bf16[384,384]{1,0:T(8,128)(2,1)}, u32[]{:S(2)}) copy-start(bf16[384,384]{1,0:T(8,128)(2,1)} %wo_ref.1) | copy-start | bytes 884740
  38.3 2.0 %collective-permute-start.13 = (bf16[288,128]{1,0:T(8,128)(2,1)S(1)}, bf16[288,128]{1,0:T(8,128)(2,1)S(1)}, u32[]{:S(2)}, u32[]{:S(2)}) collective-permute-start(bf16[288,128]{1,0:T(8,128)(2,1)S(1)} %get-tuple-element.16), channel_id=1, source_target_pairs={{0,4},{4,0},{8,12},{12,8},{1,5},{5,1},{9,13},{13,9},{2,6},{6,2},{1... | collective-permute-start | bytes 221192 | tf_op jit(solution)/shard_map/ppermute | solution.py:522
  38.8 4.4 %collective-permute-start.14 = (bf16[288,128]{1,0:T(8,128)(2,1)S(1)}, bf16[288,128]{1,0:T(8,128)(2,1)S(1)}, u32[]{:S(2)}, u32[]{:S(2)}) collective-permute-start(bf16[288,128]{1,0:T(8,128)(2,1)S(1)} %get-tuple-element.17), channel_id=1, source_target_pairs={{0,8},{4,12},{8,0},{12,4},{1,9},{5,13},{9,1},{13,5},{2,10},{6,14},... | collective-permute-start | bytes 221192 | tf_op jit(solution)/shard_map/ppermute | solution.py:522
  40.2 4.5 %collective-permute-start.15 = (bf16[288,128]{1,0:T(8,128)(2,1)S(1)}, bf16[288,128]{1,0:T(8,128)(2,1)S(1)}, u32[]{:S(2)}, u32[]{:S(2)}) collective-permute-start(bf16[288,128]{1,0:T(8,128)(2,1)S(1)} %get-tuple-element.18), channel_id=1, source_target_pairs={{0,12},{4,8},{8,4},{12,0},{1,13},{5,9},{9,5},{13,1},{2,14},{6,10},... | collective-permute-start | bytes 221192 | tf_op jit(solution)/shard_map/ppermute | solution.py:522

commit v7 on v6

--- a/solution.py
+++ b/solution.py
@@ -107,19 +107,19 @@
 
 
 def own_frame(
-    r_ref, own_ref, one_ref, two_ref, three_ref, table_ref, loaded_ref, across_ref, groups_ref, out_ref, raw_ref, blocks_ref
+    r_ref, own_ref, one_ref, two_ref, three_ref, table_ref, groups_ref, loaded_ref, across_ref, across_one_ref, out_ref, raw_ref, blocks_ref
 ):
     blocks = [ref[0] for ref in (own_ref, one_ref, two_ref, three_ref)]
     rows = blocks[0].shape[0]
     for k, block in enumerate(blocks):
         raw_ref[pl.ds((r_ref[0] ^ k) * rows, rows)] = block
-        if k > 0:
-            blocks_ref[k - 1] = block
+        if k > 1:
+            blocks_ref[k - 2] = block
     frame_norm(r_ref, blocks, table_ref, groups_ref[...], out_ref)
 
 
-def across_frame(r_ref, own_ref, blocks_ref, table_ref, after_ref, groups_ref, out_ref):
-    frame_norm(r_ref, [own_ref[0]] + [blocks_ref[k] for k in range(3)], table_ref, groups_ref[...], out_ref)
+def across_frame(r_ref, own_ref, one_ref, blocks_ref, table_ref, groups_ref, after_ref, out_ref):
+    frame_norm(r_ref, [own_ref[0], one_ref[0], blocks_ref[0], blocks_ref[1]], table_ref, groups_ref[...], out_ref)
 
 
 def frame_norm(r_ref, blocks, table_ref, groups, out_ref):
@@ -590,14 +590,17 @@
         groups = call(channel_groups, struct((channels, channels)))()
         frame = struct((1, height, cols, channels))
         across_own = over_x(features)
+        across_one = lax.ppermute(
+            features, ("tm", "rows"), [(i * n + k, (i ^ 2) * n + (k ^ 1)) for i in range(frames) for k in range(n)]
+        )
         active1, raw, blocks = call(
-            own_frame, (frame, struct((height, cols, channels)), struct((n - 1, rows, cols, channels)))
-        )(r, features, one, two, three, table, weights1, across_own, groups)
+            own_frame, (frame, struct((height, cols, channels)), struct((2, rows, cols, channels)))
+        )(r, features, one, two, three, table, groups, weights1, across_own, across_one)
         across_blocks, mate = over_x(blocks), over_core(active1)
         pair, rimmed = (pltpu.VMEM((k, height + 2, cols, channels), BF16) for k in (2, 1))
         tall = struct((frames, n * plane, 3 * lanes), F32)
         near_total = call(first_conv_near, tall, (pair,))(m, active1, mate, weights1)
-        across = call(across_frame, frame)(r, across_own, across_blocks, table, near_total, groups)
+        across = call(across_frame, frame)(r, across_own, across_one, across_blocks, table, groups, near_total)
         beside = over_core(across)
         across_total = call(first_conv_across, tall, (rimmed,))(m, near_total, across, weights1)
         scratch = (

time: 47.1 us -> 48.2 us (1.023)
  starting transfers between devices: 15.5 us -> 17.1 us
  waiting for transfers between devices: 10.6 us -> 9.99 us
    ppermute x0 -> x1, starting transfers between devices: none -> 1.21 us  [per_device(): lax.ppermute(features, ('tm', 'rows'), [(i * n + k, (i ^ 2) * n + (k ^ 1)...]
    ppermute x16, waiting for transfers between devices: 10.6 us -> 9.45 us  [swapped(): lax.ppermute(value, axis, [(i, partner(i)) for i in range(lax.axis_size(a...]
    ppermute x0 -> x1, waiting for transfers between devices: none -> 0.54 us  [per_device(): lax.ppermute(features, ('tm', 'rows'), [(i * n + k, (i ^ 2) * n + (k ^ 1)...]
  transfers between devices with their start and end apart: 16 -> 17, of which waited for: 6 -> 8; matrix products, arithmetic and copies ran while one was open for 2% -> 2% of each run, Pallas kernels for 25% -> 25%
where the time goes in v7:
time: 48.2 us; the launch traced here: 48 us
  Pallas kernels  18.2 us (38%)
  starting transfers between devices  17.1 us (35%)
  waiting for transfers between devices  9.99 us (21%)
  local copies, waits for them, and re-layouts  1.6 us (3%)
  other arithmetic  0.86 us (2%)
    pallas_call x16, Pallas kernels, run(): pl.pallas_call(functools.partial(body, *axes), out_shape=outs, in_specs=[...  18.2 us
    ppermute x16, starting transfers between devices, swapped(): lax.ppermute(value, axis, [(i, partner(i)) for i in range(lax.axis_size(a...  15.9 us
    ppermute x16, waiting for transfers between devices, swapped(): lax.ppermute(value, axis, [(i, partner(i)) for i in range(lax.axis_size(a...  9.45 us
    unnamed x18, local copies, waits for them, and re-layouts  1.6 us
    ppermute x1, starting transfers between devices, per_device(): lax.ppermute(features, ('tm', 'rows'), [(i * n + k, (i ^ 2) * n + (k ^ 1)...  1.21 us
  transfers between devices with their start and end apart: 17, of which 8 were waited for; matrix products, arithmetic and copies ran while one was open for 2% of the time, Pallas kernels for 25%

profile of v7, /device:TPU:0, one launch (start us, length us, event | category | flops | bytes accessed | tf_op | source)
XLA Modules:
  0.0 48.0 jit_solution(16984876221648589421)
XLA Ops:
  0.0 2.9 %collective-permute-start.3 = (bf16[1,2,48,384]{3,2,1,0:T(8,128)(2,1)}, bf16[1,2,48,384]{3,2,1,0:T(8,128)(2,1)S(1)}, u32[]{:S(2)}, u32[]{:S(2)}) collective-permute-start(bf16[1,2,48,384]{3,2,1,0:T(8,128)(2,1)} %own_ref.1), channel_id=1, source_target_pairs={{0,8},{4,12},{8,0},{12,4},{1,9},{5,13},{9,1},{13,5},{2,10},{6,14},... | collective-permute-start | bytes 221192 | tf_op jit(solution)/shard_map/ppermute | solution.py:522
  2.9 3.6 %collective-permute-start.2 = (bf16[1,2,48,384]{3,2,1,0:T(8,128)(2,1)}, bf16[1,2,48,384]{3,2,1,0:T(8,128)(2,1)S(1)}, u32[]{:S(2)}, u32[]{:S(2)}) collective-permute-start(bf16[1,2,48,384]{3,2,1,0:T(8,128)(2,1)} %own_ref.1), channel_id=1, source_target_pairs={{0,3},{1,2},{2,1},{3,0},{4,7},{5,6},{6,5},{7,4},{8,11},{9,10},{10,... | collective-permute-start | bytes 221192 | tf_op jit(solution)/shard_map/ppermute | solution.py:522
  6.5 0.8 %collective-permute-start = (bf16[1,2,48,384]{3,2,1,0:T(8,128)(2,1)}, bf16[1,2,48,384]{3,2,1,0:T(8,128)(2,1)S(1)}, u32[]{:S(2)}, u32[]{:S(2)}) collective-permute-start(bf16[1,2,48,384]{3,2,1,0:T(8,128)(2,1)} %own_ref.1), channel_id=1, source_target_pairs={{0,1},{1,0},{2,3},{3,2},{4,5},{5,4},{6,7},{7,6},{8,9},{9,8},{10,11... | collective-permute-start | bytes 221192 | tf_op jit(solution)/shard_map/ppermute | solution.py:522
  7.3 1.2 %collective-permute-start.4 = (bf16[1,2,48,384]{3,2,1,0:T(8,128)(2,1)}, bf16[1,2,48,384]{3,2,1,0:T(8,128)(2,1)S(1)}, u32[]{:S(2)}, u32[]{:S(2)}) collective-permute-start(bf16[1,2,48,384]{3,2,1,0:T(8,128)(2,1)} %own_ref.1), channel_id=1, source_target_pairs={{0,9},{1,8},{2,11},{3,10},{4,13},{5,12},{6,15},{7,14},{8,1},{9,0},... | collective-permute-start | bytes 221192 | tf_op jit(solution)/shard_map/ppermute | solution.py:593
  8.6 0.8 %select_select_fusion.table_ref = f32[8,384]{1,0:T(8,128)S(1)} fusion(f32[384]{0:T(512)} %param.16, f32[384]{0:T(512)} %param.17, f32[384]{0:T(512)} %param.20, f32[384]{0:T(512)} %param.21, f32[384]{0:T(512)} %param.24, f32[384]{0:T(512)} %param.25, pred[8]{0:T(512)(128)(4,1)S(1)} %get-tuple-element.19, pred[8]{0:T(512)(128)(4,1)S(1)} %get-tuple-element.20, ...), kind=kLoop, calls=%fused_computation | loop fusion | flops 18432 | bytes 21552 | tf_op jit(solution)/shard_map/jit(_where)/select_n | solution.py:563
  9.4 0.1 shard_map.145.groups_ref
  9.5 0.0 copy-start
  9.5 1.5 %copy-done = bf16[96,3,3,3,384]{4,0,3,2,1:T(8,128)(2,1)S(1)} copy-done((bf16[96,3,3,3,384]{4,0,3,2,1:T(8,128)(2,1)S(1)}, bf16[96,3,3,3,384]{4,0,3,2,1:T(8,128)(2,1)}, u32[]{:S(2)}) %copy-start) | copy-done | bytes 1990680
  11.1 0.2 shard_map.146.loaded_ref.w_ref
  11.3 0.0 collective-permute-done.3.across_ref.own_ref
  11.3 1.5 %collective-permute-done.1.two_ref = bf16[1,2,48,384]{3,2,1,0:T(8,128)(2,1)S(1)} collective-permute-done((bf16[1,2,48,384]{3,2,1,0:T(8,128)(2,1)}, bf16[1,2,48,384]{3,2,1,0:T(8,128)(2,1)S(1)}, u32[]{:S(2)}, u32[]{:S(2)}) %collective-permute-start.1) | collective-permute-done | bytes 73760 | tf_op jit(solution)/shard_map/ppermute | solution.py:522
  12.8 0.5 %collective-permute-done.one_ref = bf16[1,2,48,384]{3,2,1,0:T(8,128)(2,1)S(1)} collective-permute-done((bf16[1,2,48,384]{3,2,1,0:T(8,128)(2,1)}, bf16[1,2,48,384]{3,2,1,0:T(8,128)(2,1)S(1)}, u32[]{:S(2)}, u32[]{:S(2)}) %collective-permute-start) | collective-permute-done | bytes 73760 | tf_op jit(solution)/shard_map/ppermute | solution.py:522
  13.4 0.5 %collective-permute-done.4.across_one_ref.one_ref = bf16[1,2,48,384]{3,2,1,0:T(8,128)(2,1)S(1)} collective-permute-done((bf16[1,2,48,384]{3,2,1,0:T(8,128)(2,1)}, bf16[1,2,48,384]{3,2,1,0:T(8,128)(2,1)S(1)}, u32[]{:S(2)}, u32[]{:S(2)}) %collective-permute-start.4) | collective-permute-done | bytes 73760 | tf_op jit(solution)/shard_map/ppermute | solution.py:593
  13.9 0.7 %shard_map.147 = (bf16[1,8,48,384]{3,2,1,0:T(8,128)(2,1)S(1)}, bf16[8,48,384]{2,1,0:T(8,128)(2,1)S(1)}, bf16[2,2,48,384]{3,2,1,0:T(8,128)(2,1)S(1)}) custom-call(bf16[1,2,48,384]{3,2,1,0:T(8,128)(2,1)S(1)} %copy-done.6, bf16[1,2,48,384]{3,2,1,0:T(8,128)(2,1)S(1)} %collective-permute-done.one_ref, bf16[1,2,48,384]{3,2,1,0:T(8,128)(2,1)S(1)} %collective-permute-done.1.two_ref, ...), custom_call_target="tpu_custom_call" | custom-call | tf_op jit(solution)/shard_map/pallas_call | solution.py:31
  14.6 0.1 collective-permute-start.5
  14.7 1.8 %collective-permute-start.6 = (bf16[2,2,48,384]{3,2,1,0:T(8,128)(2,1)S(1)}, bf16[2,2,48,384]{3,2,1,0:T(8,128)(2,1)S(1)}, u32[]{:S(2)}, u32[]{:S(2)}) collective-permute-start(bf16[2,2,48,384]{3,2,1,0:T(8,128)(2,1)S(1)} %get-tuple-element.14), channel_id=1, source_target_pairs={{0,8},{4,12},{8,0},{12,4},{1,9},{5,13},{9,1},{13,5},{2,10},{6,14},... | collective-permute-start | bytes 442376 | tf_op jit(solution)/shard_map/ppermute | solution.py:522
  16.4 3.2 %shard_map.148.after_ref.near_total_ref = f32[4,384,384]{2,1,0:T(8,128)S(1)} custom-call(bf16[1,8,48,384]{3,2,1,0:T(8,128)(2,1)S(1)} %get-tuple-element.13.own_ref, bf16[1,8,48,384]{3,2,1,0:T(8,128)(2,1)S(1)} %collective-permute-done.5.mate_ref, bf16[3,3,384,384]{3,2,1,0:T(8,128)(2,1)S(1)} %shard_map.146.loaded_ref.w_ref), custom_call_target="tpu_custom_call" | custom-call | tf_op jit(solution)/shard_map/pallas_call | solution.py:31
  19.6 1.3 %collective-permute-done.6.blocks_ref = bf16[2,2,48,384]{3,2,1,0:T(8,128)(2,1)S(1)} collective-permute-done((bf16[2,2,48,384]{3,2,1,0:T(8,128)(2,1)S(1)}, bf16[2,2,48,384]{3,2,1,0:T(8,128)(2,1)S(1)}, u32[]{:S(2)}, u32[]{:S(2)}) %collective-permute-start.6) | collective-permute-done | bytes 147488 | tf_op jit(solution)/shard_map/ppermute | solution.py:522
  20.9 0.7 %shard_map.149.a_ref = bf16[1,8,48,384]{3,2,1,0:T(8,128)(2,1)S(1)} custom-call(bf16[1,2,48,384]{3,2,1,0:T(8,128)(2,1)S(1)} %collective-permute-done.3.across_ref.own_ref, bf16[1,2,48,384]{3,2,1,0:T(8,128)(2,1)S(1)} %collective-permute-done.4.across_one_ref.one_ref, bf16[2,2,48,384]{3,2,1,0:T(8,128)(2,1)S(1)} %collective-permute-done.6.blocks_ref, ...), custom_call_target="tpu_custom_call" | custom-call | tf_op jit(solution)/shard_map/pallas_call | solution.py:31
  21.6 0.0 copy-start.7
  21.6 0.1 collective-permute-start.7
  21.7 1.3 %shard_map.150.base_ref = f32[4,384,384]{2,1,0:T(8,128)S(1)} custom-call(f32[4,384,384]{2,1,0:T(8,128)S(1)} %shard_map.148.after_ref.near_total_ref, bf16[1,8,48,384]{3,2,1,0:T(8,128)(2,1)S(1)} %shard_map.149.a_ref, bf16[3,3,384,384]{3,2,1,0:T(8,128)(2,1)S(1)} %shard_map.146.loaded_ref.w_ref), custom_call_target="tpu_custom_call" | custom-call | tf_op jit(solution)/shard_map/pallas_call | solution.py:31
  22.9 0.3 collective-permute-done.7.a_ref
  23.2 0.8 %shard_map.151.refs_0_.own_ref.after_ref = bf16[2,6,48,128]{3,2,1,0:T(8,128)(2,1)S(1)} custom-call(f32[4,384,384]{2,1,0:T(8,128)S(1)} %shard_map.150.base_ref, bf16[1,8,48,384]{3,2,1,0:T(8,128)(2,1)S(1)} %collective-permute-done.7.a_ref, bf16[3,3,384,384]{3,2,1,0:T(8,128)(2,1)S(1)} %shard_map.146.loaded_ref.w_ref, f32[96]{0:T(128)S(1)} %copy-done.7, ...), custom_call_target="tpu_custom_call" | custom-call | tf_op jit(solution)/shard_map/pallas_call | solution.py:31
  24.1 0.0 copy-start.1
  24.1 0.2 collective-permute-start.8
  24.3 3.3 %collective-permute-start.10 = (bf16[2,6,48,128]{3,2,1,0:T(8,128)(2,1)S(1)}, bf16[2,6,48,128]{3,2,1,0:T(8,128)(2,1)S(1)}, u32[]{:S(2)}, u32[]{:S(2)}) collective-permute-start(bf16[2,6,48,128]{3,2,1,0:T(8,128)(2,1)S(1)} %shard_map.151.refs_0_.own_ref.after_ref), channel_id=1, source_target_pairs={{0,8},{4,12},{8,0},{12,4},{1,9},{5,13},{9,1},{13,5},{2,10},{6,14},... | collective-permute-start | bytes 442376 | tf_op jit(solution)/shard_map/ppermute | solution.py:522
  27.6 1.6 %shard_map.154.own_ref = bf16[2,6,48,128]{3,2,1,0:T(8,128)(2,1)S(1)} custom-call(f32[4,384,384]{2,1,0:T(8,128)S(1)} %shard_map.150.base_ref, bf16[1,8,48,384]{3,2,1,0:T(8,128)(2,1)S(1)} %collective-permute-done.7.a_ref, bf16[3,3,384,384]{3,2,1,0:T(8,128)(2,1)S(1)} %shard_map.146.loaded_ref.w_ref, f32[96]{0:T(128)S(1)} %copy-done.7, ...), custom_call_target="tpu_custom_call" | custom-call | tf_op jit(solution)/shard_map/pallas_call | solution.py:31
  29.2 0.5 %collective-permute-start.12 = (bf16[2,6,48,128]{3,2,1,0:T(8,128)(2,1)S(1)}, bf16[2,6,48,128]{3,2,1,0:T(8,128)(2,1)S(1)}, u32[]{:S(2)}, u32[]{:S(2)}) collective-permute-start(bf16[2,6,48,128]{3,2,1,0:T(8,128)(2,1)S(1)} %shard_map.154.own_ref), channel_id=1, source_target_pairs={{0,8},{4,12},{8,0},{12,4},{1,9},{5,13},{9,1},{13,5},{2,10},{6,14},... | collective-permute-start | bytes 442376 | tf_op jit(solution)/shard_map/ppermute | solution.py:522
  29.8 0.2 shard_map.152.w_ref
  30.0 2.1 %shard_map.153.base_ref.after_ref = f32[4,384,384]{2,1,0:T(8,128)S(1)} custom-call(bf16[2,6,48,128]{3,2,1,0:T(8,128)(2,1)S(1)} %shard_map.151.refs_0_.own_ref.after_ref, bf16[2,6,48,128]{3,2,1,0:T(8,128)(2,1)S(1)} %collective-permute-done.8.mate_ref, bf16[3,3,384,384]{3,2,1,0:T(8,128)(2,1)S(1)} %shard_map.152.w_ref), custom_call_target="tpu_custom_call" | custom-call | tf_op jit(solution)/shard_map/pallas_call | solution.py:31
  32.1 0.6 %collective-permute-start.11 = (bf16[2,6,48,128]{3,2,1,0:T(8,128)(2,1)S(1)}, bf16[2,6,48,128]{3,2,1,0:T(8,128)(2,1)S(1)}, u32[]{:S(2)}, u32[]{:S(2)}) collective-permute-start(bf16[2,6,48,128]{3,2,1,0:T(8,128)(2,1)S(1)} %shard_map.156.own_ref), channel_id=1, source_target_pairs={{0,4},{4,0},{8,12},{12,8},{1,5},{5,1},{9,13},{13,9},{2,6},{6,2},{1... | collective-permute-start | bytes 442376 | tf_op jit(solution)/shard_map/ppermute | solution.py:522
  32.7 1.2 %shard_map.155.base_ref.after_ref = f32[4,384,384]{2,1,0:T(8,128)S(1)} custom-call(f32[4,384,384]{2,1,0:T(8,128)S(1)} %shard_map.153.base_ref.after_ref, bf16[2,6,48,128]{3,2,1,0:T(8,128)(2,1)S(1)} %shard_map.154.own_ref, bf16[2,6,48,128]{3,2,1,0:T(8,128)(2,1)S(1)} %collective-permute-done.9.mate_ref, bf16[3,3,384,384]{3,2,1,0:T(8,128)(2,1)S(1)} %shard_map.152.w_ref), custom_call_target="tpu_custom_call" | custom-call | tf_op jit(solution)/shard_map/pallas_call | solution.py:31
  33.9 1.4 %collective-permute-done.12.x_ref = bf16[2,6,48,128]{3,2,1,0:T(8,128)(2,1)S(1)} collective-permute-done((bf16[2,6,48,128]{3,2,1,0:T(8,128)(2,1)S(1)}, bf16[2,6,48,128]{3,2,1,0:T(8,128)(2,1)S(1)}, u32[]{:S(2)}, u32[]{:S(2)}) %collective-permute-start.12) | collective-permute-done | bytes 147488 | tf_op jit(solution)/shard_map/ppermute | solution.py:522
  35.3 0.0 copy-start.8
  35.3 0.1 collective-permute-start.13
  35.4 2.1 %shard_map.157.total_ref = f32[4,384,384]{2,1,0:T(8,128)S(1)} custom-call(f32[4,384,384]{2,1,0:T(8,128)S(1)} %shard_map.155.base_ref.after_ref, bf16[2,6,48,128]{3,2,1,0:T(8,128)(2,1)S(1)} %shard_map.156.own_ref, bf16[2,6,48,128]{3,2,1,0:T(8,128)(2,1)S(1)} %collective-permute-done.11.mate_ref, bf16[3,3,384,384]{3,2,1,0:T(8,128)(2,1)S(1)} %shard_map.152.w_ref), custom_call_target="tpu_custom_call" | custom-call | tf_op jit(solution)/shard_map/pallas_call | solution.py:31
  37.5 0.0 copy-start.2
  37.5 0.0 copy-start.3
  37.5 0.0 copy-start.4
  37.5 0.0 copy-start.5
  37.6 1.8 %shard_map.159 = (bf16[288,128]{1,0:T(8,128)(2,1)S(1)}, bf16[288,128]{1,0:T(8,128)(2,1)S(1)}, bf16[288,128]{1,0:T(8,128)(2,1)S(1)}, bf16[288,128]{1,0:T(8,128)(2,1)S(1)}) custom-call(f32[4,384,384]{2,1,0:T(8,128)S(1)} %shard_map.157.total_ref, bf16[2,6,48,128]{3,2,1,0:T(8,128)(2,1)S(1)} %shard_map.158.own_ref, ...), custom_call_target="tpu_custom_call" | custom-call | tf_op jit(solution)/shard_map/pallas_call | solution.py:31
  39.3 0.6 %collective-permute-start.14 = (bf16[288,128]{1,0:T(8,128)(2,1)S(1)}, bf16[288,128]{1,0:T(8,128)(2,1)S(1)}, u32[]{:S(2)}, u32[]{:S(2)}) collective-permute-start(bf16[288,128]{1,0:T(8,128)(2,1)S(1)} %get-tuple-element.16), channel_id=1, source_target_pairs={{0,4},{4,0},{8,12},{12,8},{1,5},{5,1},{9,13},{13,9},{2,6},{6,2},{1... | collective-permute-start | bytes 221192 | tf_op jit(solution)/shard_map/ppermute | solution.py:522
  39.9 1.3 %collective-permute-start.15 = (bf16[288,128]{1,0:T(8,128)(2,1)S(1)}, bf16[288,128]{1,0:T(8,128)(2,1)S(1)}, u32[]{:S(2)}, u32[]{:S(2)}) collective-permute-start(bf16[288,128]{1,0:T(8,128)(2,1)S(1)} %get-tuple-element.17), channel_id=1, source_target_pairs={{0,8},{4,12},{8,0},{12,4},{1,9},{5,13},{9,1},{13,5},{2,10},{6,14},... | collective-permute-start | bytes 221192 | tf_op jit(solution)/shard_map/ppermute | solution.py:522
  41.2 0.1 collective-permute-start.16
  41.3 3.0 %collective-permute-done.15.p2 = bf16[288,128]{1,0:T(8,128)(2,1)S(1)} collective-permute-done((bf16[288,128]{1,0:T(8,128)(2,1)S(1)}, bf16[288,128]{1,0:T(8,128)(2,1)S(1)}, u32[]{:S(2)}, u32[]{:S(2)}) %collective-permute-start.15) | collective-permute-done | bytes 73760 | tf_op jit(solution)/shard_map/ppermute | solution.py:522
  44.3 1.4 %collective-permute-done.16.p3 = bf16[288,128]{1,0:T(8,128)(2,1)S(1)} collective-permute-done((bf16[288,128]{1,0:T(8,128)(2,1)S(1)}, bf16[288,128]{1,0:T(8,128)(2,1)S(1)}, u32[]{:S(2)}, u32[]{:S(2)}) %collective-permute-start.16) | collective-permute-done | bytes 73760 | tf_op jit(solution)/shard_map/ppermute | solution.py:522
  45.7 2.3 %shard_map.160 = bf16[96,384]{1,0:T(8,128)(2,1)} custom-call(bf16[8,48,384]{2,1,0:T(8,128)(2,1)S(1)} %get-tuple-element.12.raw_ref, bf16[288,128]{1,0:T(8,128)(2,1)S(1)} %get-tuple-element.15.p0, bf16[288,128]{1,0:T(8,128)(2,1)S(1)} %collective-permute-done.14.p1, bf16[288,128]{1,0:T(8,128)(2,1)S(1)} %collective-permute-done.15.p2, ...), custom_call_target="tpu_custom_call" | custom-call | tf_op jit(solution)/shard_map/pallas_call | solution.py:31
  (24 shorter events, 0.1 us)
Async XLA Ops:
  0.0 11.3 %collective-permute-start.3 = (bf16[1,2,48,384]{3,2,1,0:T(8,128)(2,1)}, bf16[1,2,48,384]{3,2,1,0:T(8,128)(2,1)S(1)}, u32[]{:S(2)}, u32[]{:S(2)}) collective-permute-start(bf16[1,2,48,384]{3,2,1,0:T(8,128)(2,1)} %own_ref.1), channel_id=1, source_target_pairs={{0,8},{4,12},{8,0},{12,4},{1,9},{5,13},{9,1},{13,5},{2,10},{6,14},... | collective-permute-start | bytes 221192 | tf_op jit(solution)/shard_map/ppermute | solution.py:522
  2.9 8.4 %collective-permute-start.2 = (bf16[1,2,48,384]{3,2,1,0:T(8,128)(2,1)}, bf16[1,2,48,384]{3,2,1,0:T(8,128)(2,1)S(1)}, u32[]{:S(2)}, u32[]{:S(2)}) collective-permute-start(bf16[1,2,48,384]{3,2,1,0:T(8,128)(2,1)} %own_ref.1), channel_id=1, source_target_pairs={{0,3},{1,2},{2,1},{3,0},{4,7},{5,6},{6,5},{7,4},{8,11},{9,10},{10,... | collective-permute-start | bytes 221192 | tf_op jit(solution)/shard_map/ppermute | solution.py:522
  6.5 6.3 %collective-permute-start.1 = (bf16[1,2,48,384]{3,2,1,0:T(8,128)(2,1)}, bf16[1,2,48,384]{3,2,1,0:T(8,128)(2,1)S(1)}, u32[]{:S(2)}, u32[]{:S(2)}) collective-permute-start(bf16[1,2,48,384]{3,2,1,0:T(8,128)(2,1)} %own_ref.1), channel_id=1, source_target_pairs={{0,2},{1,3},{2,0},{3,1},{4,6},{5,7},{6,4},{7,5},{8,10},{9,11},{10,... | collective-permute-start | bytes 221192 | tf_op jit(solution)/shard_map/ppermute | solution.py:522
  6.5 6.8 %collective-permute-start = (bf16[1,2,48,384]{3,2,1,0:T(8,128)(2,1)}, bf16[1,2,48,384]{3,2,1,0:T(8,128)(2,1)S(1)}, u32[]{:S(2)}, u32[]{:S(2)}) collective-permute-start(bf16[1,2,48,384]{3,2,1,0:T(8,128)(2,1)} %own_ref.1), channel_id=1, source_target_pairs={{0,1},{1,0},{2,3},{3,2},{4,5},{5,4},{6,7},{7,6},{8,9},{9,8},{10,11... | collective-permute-start | bytes 221192 | tf_op jit(solution)/shard_map/ppermute | solution.py:522
  7.3 6.6 %collective-permute-start.4 = (bf16[1,2,48,384]{3,2,1,0:T(8,128)(2,1)}, bf16[1,2,48,384]{3,2,1,0:T(8,128)(2,1)S(1)}, u32[]{:S(2)}, u32[]{:S(2)}) collective-permute-start(bf16[1,2,48,384]{3,2,1,0:T(8,128)(2,1)} %own_ref.1), channel_id=1, source_target_pairs={{0,9},{1,8},{2,11},{3,10},{4,13},{5,12},{6,15},{7,14},{8,1},{9,0},... | collective-permute-start | bytes 221192 | tf_op jit(solution)/shard_map/ppermute | solution.py:593
  9.5 1.6 %copy-start = (bf16[96,3,3,3,384]{4,0,3,2,1:T(8,128)(2,1)S(1)}, bf16[96,3,3,3,384]{4,0,3,2,1:T(8,128)(2,1)}, u32[]{:S(2)}) copy-start(bf16[96,3,3,3,384]{4,0,3,2,1:T(8,128)(2,1)} %param.18) | copy-start | bytes 5971972
  11.0 2.9 %copy-start.6 = (bf16[1,2,48,384]{3,2,1,0:T(8,128)(2,1)S(1)}, bf16[1,2,48,384]{3,2,1,0:T(8,128)(2,1)}, u32[]{:S(2)}) copy-start(bf16[1,2,48,384]{3,2,1,0:T(8,128)(2,1)} %own_ref.1) | copy-start | bytes 221188
  14.6 1.9 %collective-permute-start.5 = (bf16[1,8,48,384]{3,2,1,0:T(8,128)(2,1)S(1)}, bf16[1,8,48,384]{3,2,1,0:T(8,128)(2,1)S(1)}, u32[]{:S(2)}, u32[]{:S(2)}) collective-permute-start(bf16[1,8,48,384]{3,2,1,0:T(8,128)(2,1)S(1)} %get-tuple-element.13.own_ref), channel_id=1, source_target_pairs={{0,4},{4,0},{8,12},{12,8},{1,5},{5,1},{9,13},{13,9},{2,6},{6,2},{1... | collective-permute-start | bytes 884744 | tf_op jit(solution)/shard_map/ppermute | solution.py:522
  14.7 6.3 %collective-permute-start.6 = (bf16[2,2,48,384]{3,2,1,0:T(8,128)(2,1)S(1)}, bf16[2,2,48,384]{3,2,1,0:T(8,128)(2,1)S(1)}, u32[]{:S(2)}, u32[]{:S(2)}) collective-permute-start(bf16[2,2,48,384]{3,2,1,0:T(8,128)(2,1)S(1)} %get-tuple-element.14), channel_id=1, source_target_pairs={{0,8},{4,12},{8,0},{12,4},{1,9},{5,13},{9,1},{13,5},{2,10},{6,14},... | collective-permute-start | bytes 442376 | tf_op jit(solution)/shard_map/ppermute | solution.py:522
  21.6 1.7 %copy-start.7 = (f32[96]{0:T(128)S(1)}, f32[96]{0:T(128)}, u32[]{:S(2)}) copy-start(f32[96]{0:T(128)} %bias_ref.4) | copy-start | bytes 1156
  21.6 1.6 %collective-permute-start.7 = (bf16[1,8,48,384]{3,2,1,0:T(8,128)(2,1)S(1)}, bf16[1,8,48,384]{3,2,1,0:T(8,128)(2,1)S(1)}, u32[]{:S(2)}, u32[]{:S(2)}) collective-permute-start(bf16[1,8,48,384]{3,2,1,0:T(8,128)(2,1)S(1)} %shard_map.149.a_ref), channel_id=1, source_target_pairs={{0,4},{4,0},{8,12},{12,8},{1,5},{5,1},{9,13},{13,9},{2,6},{6,2},{1... | collective-permute-start | bytes 884744 | tf_op jit(solution)/shard_map/ppermute | solution.py:522
  24.1 5.7 %copy-start.1 = (bf16[96,3,3,3,384]{4,0,3,2,1:T(8,128)(2,1)S(1)}, bf16[96,3,3,3,384]{4,0,3,2,1:T(8,128)(2,1)}, u32[]{:S(2)}) copy-start(bf16[96,3,3,3,384]{4,0,3,2,1:T(8,128)(2,1)} %param.22) | copy-start | bytes 5971972
  24.1 5.9 %collective-permute-start.8 = (bf16[2,6,48,128]{3,2,1,0:T(8,128)(2,1)S(1)}, bf16[2,6,48,128]{3,2,1,0:T(8,128)(2,1)S(1)}, u32[]{:S(2)}, u32[]{:S(2)}) collective-permute-start(bf16[2,6,48,128]{3,2,1,0:T(8,128)(2,1)S(1)} %shard_map.151.refs_0_.own_ref.after_ref), channel_id=1, source_target_pairs={{0,4},{4,0},{8,12},{12,8},{1,5},{5,1},{9,13},{13,9},{2,6},{6,2},{1... | collective-permute-start | bytes 442376 | tf_op jit(solution)/shard_map/ppermute | solution.py:522
  24.3 7.8 %collective-permute-start.10 = (bf16[2,6,48,128]{3,2,1,0:T(8,128)(2,1)S(1)}, bf16[2,6,48,128]{3,2,1,0:T(8,128)(2,1)S(1)}, u32[]{:S(2)}, u32[]{:S(2)}) collective-permute-start(bf16[2,6,48,128]{3,2,1,0:T(8,128)(2,1)S(1)} %shard_map.151.refs_0_.own_ref.after_ref), channel_id=1, source_target_pairs={{0,8},{4,12},{8,0},{12,4},{1,9},{5,13},{9,1},{13,5},{2,10},{6,14},... | collective-permute-start | bytes 442376 | tf_op jit(solution)/shard_map/ppermute | solution.py:522
  29.2 6.1 %collective-permute-start.12 = (bf16[2,6,48,128]{3,2,1,0:T(8,128)(2,1)S(1)}, bf16[2,6,48,128]{3,2,1,0:T(8,128)(2,1)S(1)}, u32[]{:S(2)}, u32[]{:S(2)}) collective-permute-start(bf16[2,6,48,128]{3,2,1,0:T(8,128)(2,1)S(1)} %shard_map.154.own_ref), channel_id=1, source_target_pairs={{0,8},{4,12},{8,0},{12,4},{1,9},{5,13},{9,1},{13,5},{2,10},{6,14},... | collective-permute-start | bytes 442376 | tf_op jit(solution)/shard_map/ppermute | solution.py:522
  29.7 2.9 %collective-permute-start.9 = (bf16[2,6,48,128]{3,2,1,0:T(8,128)(2,1)S(1)}, bf16[2,6,48,128]{3,2,1,0:T(8,128)(2,1)S(1)}, u32[]{:S(2)}, u32[]{:S(2)}) collective-permute-start(bf16[2,6,48,128]{3,2,1,0:T(8,128)(2,1)S(1)} %shard_map.154.own_ref), channel_id=1, source_target_pairs={{0,4},{4,0},{8,12},{12,8},{1,5},{5,1},{9,13},{13,9},{2,6},{6,2},{1... | collective-permute-start | bytes 442376 | tf_op jit(solution)/shard_map/ppermute | solution.py:522
  32.1 3.3 %collective-permute-start.11 = (bf16[2,6,48,128]{3,2,1,0:T(8,128)(2,1)S(1)}, bf16[2,6,48,128]{3,2,1,0:T(8,128)(2,1)S(1)}, u32[]{:S(2)}, u32[]{:S(2)}) collective-permute-start(bf16[2,6,48,128]{3,2,1,0:T(8,128)(2,1)S(1)} %shard_map.156.own_ref), channel_id=1, source_target_pairs={{0,4},{4,0},{8,12},{12,8},{1,5},{5,1},{9,13},{13,9},{2,6},{6,2},{1... | collective-permute-start | bytes 442376 | tf_op jit(solution)/shard_map/ppermute | solution.py:522
  35.3 2.2 %copy-start.8 = (f32[96]{0:T(128)S(1)}, f32[96]{0:T(128)}, u32[]{:S(2)}) copy-start(f32[96]{0:T(128)} %bias_ref.5) | copy-start | bytes 1156
  35.3 2.2 %collective-permute-start.13 = (bf16[2,6,48,128]{3,2,1,0:T(8,128)(2,1)S(1)}, bf16[2,6,48,128]{3,2,1,0:T(8,128)(2,1)S(1)}, u32[]{:S(2)}, u32[]{:S(2)}) collective-permute-start(bf16[2,6,48,128]{3,2,1,0:T(8,128)(2,1)S(1)} %shard_map.158.own_ref), channel_id=1, source_target_pairs={{0,4},{4,0},{8,12},{12,8},{1,5},{5,1},{9,13},{13,9},{2,6},{6,2},{1... | collective-permute-start | bytes 442376 | tf_op jit(solution)/shard_map/ppermute | solution.py:522
  37.5 8.2 %copy-start.2 = (bf16[384,384]{1,0:T(8,128)(2,1)S(1)}, bf16[384,384]{1,0:T(8,128)(2,1)}, u32[]{:S(2)}) copy-start(bf16[384,384]{1,0:T(8,128)(2,1)} %wq_ref.1) | copy-start | bytes 884740
  37.5 8.2 %copy-start.3 = (bf16[384,384]{1,0:T(8,128)(2,1)S(1)}, bf16[384,384]{1,0:T(8,128)(2,1)}, u32[]{:S(2)}) copy-start(bf16[384,384]{1,0:T(8,128)(2,1)} %wk_ref.1) | copy-start | bytes 884740
  37.5 8.2 %copy-start.4 = (bf16[384,384]{1,0:T(8,128)(2,1)S(1)}, bf16[384,384]{1,0:T(8,128)(2,1)}, u32[]{:S(2)}) copy-start(bf16[384,384]{1,0:T(8,128)(2,1)} %wv_ref.1) | copy-start | bytes 884740
  37.5 8.2 %copy-start.5 = (bf16[384,384]{1,0:T(8,128)(2,1)S(1)}, bf16[384,384]{1,0:T(8,128)(2,1)}, u32[]{:S(2)}) copy-start(bf16[384,384]{1,0:T(8,128)(2,1)} %wo_ref.1) | copy-start | bytes 884740
  39.3 2.0 %collective-permute-start.14 = (bf16[288,128]{1,0:T(8,128)(2,1)S(1)}, bf16[288,128]{1,0:T(8,128)(2,1)S(1)}, u32[]{:S(2)}, u32[]{:S(2)}) collective-permute-start(bf16[288,128]{1,0:T(8,128)(2,1)S(1)} %get-tuple-element.16), channel_id=1, source_target_pairs={{0,4},{4,0},{8,12},{12,8},{1,5},{5,1},{9,13},{13,9},{2,6},{6,2},{1... | collective-permute-start | bytes 221192 | tf_op jit(solution)/shard_map/ppermute | solution.py:522
  39.9 4.4 %collective-permute-start.15 = (bf16[288,128]{1,0:T(8,128)(2,1)S(1)}, bf16[288,128]{1,0:T(8,128)(2,1)S(1)}, u32[]{:S(2)}, u32[]{:S(2)}) collective-permute-start(bf16[288,128]{1,0:T(8,128)(2,1)S(1)} %get-tuple-element.17), channel_id=1, source_target_pairs={{0,8},{4,12},{8,0},{12,4},{1,9},{5,13},{9,1},{13,5},{2,10},{6,14},... | collective-permute-start | bytes 221192 | tf_op jit(solution)/shard_map/ppermute | solution.py:522
  41.2 4.5 %collective-permute-start.16 = (bf16[288,128]{1,0:T(8,128)(2,1)S(1)}, bf16[288,128]{1,0:T(8,128)(2,1)S(1)}, u32[]{:S(2)}, u32[]{:S(2)}) collective-permute-start(bf16[288,128]{1,0:T(8,128)(2,1)S(1)} %get-tuple-element.18), channel_id=1, source_target_pairs={{0,12},{4,8},{8,4},{12,0},{1,13},{5,9},{9,5},{13,1},{2,14},{6,10},... | collective-permute-start | bytes 221192 | tf_op jit(solution)/shard_map/ppermute | solution.py:522

commit v8 on v6

--- a/solution.py
+++ b/solution.py
@@ -401,7 +401,7 @@
     return slice(channels - lanes, channels) if h else slice(0, lanes)
 
 
-def half_taps(m_ref, other, own_ref, mate_ref, held, base_ref, w_ref, total_ref, both, a_ref):
+def half_taps(m_ref, other, own_ref, mate_ref, held, base_ref, w_ref, total_ref, both, a_ref, first=lambda h: 0):
     odd = m_ref[0] & 1
     both[odd] = own_ref[...]
     both[1 - odd] = mate_ref[...]
@@ -409,7 +409,7 @@
 
     def body(h):
         half_channels(h, (both.at[0], both.at[1]), a_ref)
-        frame_taps(total_ref, base_ref, a_ref, held, w_ref, half_lanes(h, lanes, channels))
+        frame_taps(total_ref, base_ref, a_ref, held, w_ref, half_lanes(h, lanes, channels), first=first(h))
 
     on_half(m_ref, other, body)
 
@@ -426,15 +426,17 @@
     half_taps(m_ref, True, own_ref, mate_ref, (0, 1), base_ref, w_ref, total_ref, both, a_ref)
 
 
-def second_conv_late(m_ref, total_ref, own_ref, mate_ref, w_ref, bias_ref, *refs):
-    outs, (both, a_ref, total, done) = refs[:-4], refs[-4:]
-    half_taps(m_ref, True, own_ref, mate_ref, (2, 3), total_ref, w_ref, total, both, a_ref)
-    cols = a_ref.shape[2]
-    for t in range(total.shape[0]):
-        done[t] = finish((total if t >= 2 else total_ref).at[t], cols, bias_ref)
+def second_conv_late(own, m_ref, base_ref, own_ref, mate_ref, w_ref, bias_ref, *refs):
+    one_ref, other_ref, both, a_ref, total, done = refs[-6:]
+    half_taps(
+        m_ref, True, own_ref, mate_ref, (2, 3), base_ref, w_ref, total, both, a_ref,
+        first=lambda h: 2 * (1 - h) if own else 2 * h,
+    )
+    for t in range(2):
+        done[t] = finish(total.at[t], a_ref.shape[2], bias_ref)
+    odd = m_ref[0] & 1
     quarter = done.shape[1] // 4
-    for k, out_ref in enumerate(outs):
-        frame = m_ref[0] ^ k
+    for frame, out_ref in ((odd, one_ref), (1 - odd, other_ref)):
         tail = done[frame, 3 * quarter :]
         for b in range(3):
             at = slice(b * quarter, (b + 1) * quarter)
@@ -629,17 +631,23 @@
             m, near_total, early_across, early_beside, weights2
         )
         piece = struct((3 * plane, 128))
-        pieces = call(
-            second_conv_late,
-            [piece] * frames,
-            (both, two_frames, pltpu.VMEM(tall.shape, F32), pltpu.VMEM((frames, n * plane, outputs), BF16)),
-        )(m, early_total, late_across, late_beside, weights2, second_bias)
-        pieces = [pieces[0]] + [swapped(pieces[k], "tm", lambda i, k=k: i ^ k) for k in range(1, frames)]
+        scratch = (both, two_frames, pltpu.VMEM((2, n * plane, 3 * lanes), F32), pltpu.VMEM((2, n * plane, outputs), BF16))
+        across, cross = call(functools.partial(second_conv_late, False), (piece, piece), scratch)(
+            m, early_total, late_across, late_beside, weights2, second_bias
+        )
+        own, beside = call(functools.partial(second_conv_late, True), (piece, piece), scratch)(
+            m, early_total, late_across, late_beside, weights2, second_bias, across
+        )
+        beside = over_core(beside)
+        across, cross = over_x(across), swapped(cross, "tm", lambda i: i ^ 3)
+        across = call(hand_on, piece, cost=long)(across, cross)
         decoded = call(
             frame_attention,
             struct((plane, channels)),
             (pltpu.VMEM((frames, 3 * plane, 128), BF16), pltpu.VMEM((n * plane, channels), F32)),
-        )(r, m, raw, *pieces, table, query_weight, key_weight, value_weight, output_weight, groups)
+        )(
+            r, m, raw, own, beside, across, cross, table, query_weight, key_weight, value_weight, output_weight, groups
+        )
     else:
         weights1 = taps(first_kernel)
         halo = struct((cols, channels))

time: 47.1 us -> 46.7 us (level)
  waiting for transfers between devices: 10.6 us -> 9.7 us
    ppermute x16, waiting for transfers between devices: 10.6 us -> 9.7 us  [swapped(): lax.ppermute(value, axis, [(i, partner(i)) for i in range(lax.axis_size(a...]
    pallas_call x16 -> x18, Pallas kernels: 18.2 us -> 18.3 us  [run(): pl.pallas_call(functools.partial(body, *axes), out_shape=outs, in_specs=[...]
  transfers between devices with their start and end apart: 16 -> 16, of which waited for: 6 -> 6; matrix products, arithmetic and copies ran while one was open for 2% -> 2% of each run, Pallas kernels for 25% -> 27%
where the time goes in v8:
time: 46.7 us; the launch traced here: 46.6 us
  Pallas kernels  18.3 us (39%)
  starting transfers between devices  15.8 us (34%)
  waiting for transfers between devices  9.7 us (21%)
  local copies, waits for them, and re-layouts  1.6 us (3%)
  other arithmetic  0.86 us (2%)
    pallas_call x18, Pallas kernels, run(): pl.pallas_call(functools.partial(body, *axes), out_shape=outs, in_specs=[...  18.3 us
    ppermute x16, starting transfers between devices, swapped(): lax.ppermute(value, axis, [(i, partner(i)) for i in range(lax.axis_size(a...  15.8 us
    ppermute x16, waiting for transfers between devices, swapped(): lax.ppermute(value, axis, [(i, partner(i)) for i in range(lax.axis_size(a...  9.7 us
    unnamed x18, local copies, waits for them, and re-layouts  1.6 us
  transfers between devices with their start and end apart: 16, of which 6 were waited for; matrix products, arithmetic and copies ran while one was open for 2% of the time, Pallas kernels for 27%

profile of v8, /device:TPU:0, one launch (start us, length us, event | category | flops | bytes accessed | tf_op | source)
XLA Modules:
  0.0 46.6 jit_solution(9225115105818308249)
XLA Ops:
  0.0 5.0 %collective-permute-start.2 = (bf16[1,2,48,384]{3,2,1,0:T(8,128)(2,1)}, bf16[1,2,48,384]{3,2,1,0:T(8,128)(2,1)S(1)}, u32[]{:S(2)}, u32[]{:S(2)}) collective-permute-start(bf16[1,2,48,384]{3,2,1,0:T(8,128)(2,1)} %own_ref.1), channel_id=1, source_target_pairs={{0,3},{1,2},{2,1},{3,0},{4,7},{5,6},{6,5},{7,4},{8,11},{9,10},{10,... | collective-permute-start | bytes 221192 | tf_op jit(solution)/shard_map/ppermute | solution.py:524
  5.1 0.6 %collective-permute-start = (bf16[1,2,48,384]{3,2,1,0:T(8,128)(2,1)}, bf16[1,2,48,384]{3,2,1,0:T(8,128)(2,1)S(1)}, u32[]{:S(2)}, u32[]{:S(2)}) collective-permute-start(bf16[1,2,48,384]{3,2,1,0:T(8,128)(2,1)} %own_ref.1), channel_id=1, source_target_pairs={{0,1},{1,0},{2,3},{3,2},{4,5},{5,4},{6,7},{7,6},{8,9},{9,8},{10,11... | collective-permute-start | bytes 221192 | tf_op jit(solution)/shard_map/ppermute | solution.py:524
  5.6 1.7 %collective-permute-start.3 = (bf16[1,2,48,384]{3,2,1,0:T(8,128)(2,1)}, bf16[1,2,48,384]{3,2,1,0:T(8,128)(2,1)S(1)}, u32[]{:S(2)}, u32[]{:S(2)}) collective-permute-start(bf16[1,2,48,384]{3,2,1,0:T(8,128)(2,1)} %own_ref.1), channel_id=1, source_target_pairs={{0,8},{4,12},{8,0},{12,4},{1,9},{5,13},{9,1},{13,5},{2,10},{6,14},... | collective-permute-start | bytes 221192 | tf_op jit(solution)/shard_map/ppermute | solution.py:524
  7.4 0.8 %select_select_fusion.table_ref = f32[8,384]{1,0:T(8,128)S(1)} fusion(f32[384]{0:T(512)} %param.16, f32[384]{0:T(512)} %param.17, f32[384]{0:T(512)} %param.20, f32[384]{0:T(512)} %param.21, f32[384]{0:T(512)} %param.24, f32[384]{0:T(512)} %param.25, pred[8]{0:T(512)(128)(4,1)S(1)} %get-tuple-element.19, pred[8]{0:T(512)(128)(4,1)S(1)} %get-tuple-element.20, ...), kind=kLoop, calls=%fused_computation | loop fusion | flops 18432 | bytes 21552 | tf_op jit(solution)/shard_map/jit(_where)/select_n | solution.py:565
  8.2 0.1 shard_map.146.groups_ref
  8.3 0.0 copy-start
  8.3 1.5 %copy-done = bf16[96,3,3,3,384]{4,0,3,2,1:T(8,128)(2,1)S(1)} copy-done((bf16[96,3,3,3,384]{4,0,3,2,1:T(8,128)(2,1)S(1)}, bf16[96,3,3,3,384]{4,0,3,2,1:T(8,128)(2,1)}, u32[]{:S(2)}) %copy-start) | copy-done | bytes 1990680
  9.8 0.2 shard_map.145.loaded_ref.w_ref
  10.1 1.4 %collective-permute-done.1.two_ref = bf16[1,2,48,384]{3,2,1,0:T(8,128)(2,1)S(1)} collective-permute-done((bf16[1,2,48,384]{3,2,1,0:T(8,128)(2,1)}, bf16[1,2,48,384]{3,2,1,0:T(8,128)(2,1)S(1)}, u32[]{:S(2)}, u32[]{:S(2)}) %collective-permute-start.1) | collective-permute-done | bytes 73760 | tf_op jit(solution)/shard_map/ppermute | solution.py:524
  11.5 0.0 collective-permute-done.one_ref
  11.5 0.7 %shard_map.147 = (bf16[1,8,48,384]{3,2,1,0:T(8,128)(2,1)S(1)}, bf16[8,48,384]{2,1,0:T(8,128)(2,1)S(1)}, bf16[3,2,48,384]{3,2,1,0:T(8,128)(2,1)S(1)}) custom-call(bf16[1,2,48,384]{3,2,1,0:T(8,128)(2,1)S(1)} %copy-done.6, bf16[1,2,48,384]{3,2,1,0:T(8,128)(2,1)S(1)} %collective-permute-done.one_ref, bf16[1,2,48,384]{3,2,1,0:T(8,128)(2,1)S(1)} %collective-permute-done.1.two_ref, ...), custom_call_target="tpu_custom_call" | custom-call | tf_op jit(solution)/shard_map/pallas_call | solution.py:31
  12.2 0.1 collective-permute-start.4
  12.2 1.6 %collective-permute-start.5 = (bf16[3,2,48,384]{3,2,1,0:T(8,128)(2,1)S(1)}, bf16[3,2,48,384]{3,2,1,0:T(8,128)(2,1)S(1)}, u32[]{:S(2)}, u32[]{:S(2)}) collective-permute-start(bf16[3,2,48,384]{3,2,1,0:T(8,128)(2,1)S(1)} %get-tuple-element.14), channel_id=1, source_target_pairs={{0,8},{4,12},{8,0},{12,4},{1,9},{5,13},{9,1},{13,5},{2,10},{6,14},... | collective-permute-start | bytes 663560 | tf_op jit(solution)/shard_map/ppermute | solution.py:524
  13.8 0.0 collective-permute-done.4.mate_ref
  13.8 3.2 %shard_map.148.after_ref.near_total_ref = f32[4,384,384]{2,1,0:T(8,128)S(1)} custom-call(bf16[1,8,48,384]{3,2,1,0:T(8,128)(2,1)S(1)} %get-tuple-element.13.own_ref, bf16[1,8,48,384]{3,2,1,0:T(8,128)(2,1)S(1)} %collective-permute-done.4.mate_ref, bf16[3,3,384,384]{3,2,1,0:T(8,128)(2,1)S(1)} %shard_map.145.loaded_ref.w_ref), custom_call_target="tpu_custom_call" | custom-call | tf_op jit(solution)/shard_map/pallas_call | solution.py:31
  17.0 3.1 %collective-permute-done.5.blocks_ref = bf16[3,2,48,384]{3,2,1,0:T(8,128)(2,1)S(1)} collective-permute-done((bf16[3,2,48,384]{3,2,1,0:T(8,128)(2,1)S(1)}, bf16[3,2,48,384]{3,2,1,0:T(8,128)(2,1)S(1)}, u32[]{:S(2)}, u32[]{:S(2)}) %collective-permute-start.5) | collective-permute-done | bytes 221216 | tf_op jit(solution)/shard_map/ppermute | solution.py:524
  20.1 0.7 %shard_map.149.a_ref = bf16[1,8,48,384]{3,2,1,0:T(8,128)(2,1)S(1)} custom-call(bf16[1,2,48,384]{3,2,1,0:T(8,128)(2,1)S(1)} %collective-permute-done.3.across_ref.own_ref, bf16[3,2,48,384]{3,2,1,0:T(8,128)(2,1)S(1)} %collective-permute-done.5.blocks_ref, f32[8,384]{1,0:T(8,128)S(1)} %select_select_fusion.table_ref, ...), custom_call_target="tpu_custom_call" | custom-call | tf_op jit(solution)/shard_map/pallas_call | solution.py:31
  20.8 0.0 copy-start.7
  20.8 0.1 collective-permute-start.6
  20.8 1.3 %shard_map.150.base_ref = f32[4,384,384]{2,1,0:T(8,128)S(1)} custom-call(f32[4,384,384]{2,1,0:T(8,128)S(1)} %shard_map.148.after_ref.near_total_ref, bf16[1,8,48,384]{3,2,1,0:T(8,128)(2,1)S(1)} %shard_map.149.a_ref, bf16[3,3,384,384]{3,2,1,0:T(8,128)(2,1)S(1)} %shard_map.145.loaded_ref.w_ref), custom_call_target="tpu_custom_call" | custom-call | tf_op jit(solution)/shard_map/pallas_call | solution.py:31
  22.1 0.3 collective-permute-done.6.a_ref
  22.4 0.8 %shard_map.151.refs_0_.own_ref.after_ref = bf16[2,6,48,128]{3,2,1,0:T(8,128)(2,1)S(1)} custom-call(f32[4,384,384]{2,1,0:T(8,128)S(1)} %shard_map.150.base_ref, bf16[1,8,48,384]{3,2,1,0:T(8,128)(2,1)S(1)} %collective-permute-done.6.a_ref, bf16[3,3,384,384]{3,2,1,0:T(8,128)(2,1)S(1)} %shard_map.145.loaded_ref.w_ref, f32[96]{0:T(128)S(1)} %copy-done.7, ...), custom_call_target="tpu_custom_call" | custom-call | tf_op jit(solution)/shard_map/pallas_call | solution.py:31
  23.2 0.0 copy-start.1
  23.3 0.2 collective-permute-start.7
  23.5 3.1 %collective-permute-start.9 = (bf16[2,6,48,128]{3,2,1,0:T(8,128)(2,1)S(1)}, bf16[2,6,48,128]{3,2,1,0:T(8,128)(2,1)S(1)}, u32[]{:S(2)}, u32[]{:S(2)}) collective-permute-start(bf16[2,6,48,128]{3,2,1,0:T(8,128)(2,1)S(1)} %shard_map.151.refs_0_.own_ref.after_ref), channel_id=1, source_target_pairs={{0,8},{4,12},{8,0},{12,4},{1,9},{5,13},{9,1},{13,5},{2,10},{6,14},... | collective-permute-start | bytes 442376 | tf_op jit(solution)/shard_map/ppermute | solution.py:524
  26.6 1.6 %shard_map.154.own_ref = bf16[2,6,48,128]{3,2,1,0:T(8,128)(2,1)S(1)} custom-call(f32[4,384,384]{2,1,0:T(8,128)S(1)} %shard_map.150.base_ref, bf16[1,8,48,384]{3,2,1,0:T(8,128)(2,1)S(1)} %collective-permute-done.6.a_ref, bf16[3,3,384,384]{3,2,1,0:T(8,128)(2,1)S(1)} %shard_map.145.loaded_ref.w_ref, f32[96]{0:T(128)S(1)} %copy-done.7, ...), custom_call_target="tpu_custom_call" | custom-call | tf_op jit(solution)/shard_map/pallas_call | solution.py:31
  28.2 0.5 %collective-permute-start.11 = (bf16[2,6,48,128]{3,2,1,0:T(8,128)(2,1)S(1)}, bf16[2,6,48,128]{3,2,1,0:T(8,128)(2,1)S(1)}, u32[]{:S(2)}, u32[]{:S(2)}) collective-permute-start(bf16[2,6,48,128]{3,2,1,0:T(8,128)(2,1)S(1)} %shard_map.154.own_ref), channel_id=1, source_target_pairs={{0,8},{4,12},{8,0},{12,4},{1,9},{5,13},{9,1},{13,5},{2,10},{6,14},... | collective-permute-start | bytes 442376 | tf_op jit(solution)/shard_map/ppermute | solution.py:524
  28.7 0.0 collective-permute-start.8
  28.7 0.2 shard_map.152.w_ref
  28.9 2.1 %shard_map.153.base_ref.after_ref = f32[4,384,384]{2,1,0:T(8,128)S(1)} custom-call(bf16[2,6,48,128]{3,2,1,0:T(8,128)(2,1)S(1)} %shard_map.151.refs_0_.own_ref.after_ref, bf16[2,6,48,128]{3,2,1,0:T(8,128)(2,1)S(1)} %collective-permute-done.7.mate_ref, bf16[3,3,384,384]{3,2,1,0:T(8,128)(2,1)S(1)} %shard_map.152.w_ref), custom_call_target="tpu_custom_call" | custom-call | tf_op jit(solution)/shard_map/pallas_call | solution.py:31
  31.0 0.6 %collective-permute-start.10 = (bf16[2,6,48,128]{3,2,1,0:T(8,128)(2,1)S(1)}, bf16[2,6,48,128]{3,2,1,0:T(8,128)(2,1)S(1)}, u32[]{:S(2)}, u32[]{:S(2)}) collective-permute-start(bf16[2,6,48,128]{3,2,1,0:T(8,128)(2,1)S(1)} %shard_map.156.own_ref), channel_id=1, source_target_pairs={{0,4},{4,0},{8,12},{12,8},{1,5},{5,1},{9,13},{13,9},{2,6},{6,2},{1... | collective-permute-start | bytes 442376 | tf_op jit(solution)/shard_map/ppermute | solution.py:524
  31.6 1.2 %shard_map.155.base_ref.after_ref = f32[4,384,384]{2,1,0:T(8,128)S(1)} custom-call(f32[4,384,384]{2,1,0:T(8,128)S(1)} %shard_map.153.base_ref.after_ref, bf16[2,6,48,128]{3,2,1,0:T(8,128)(2,1)S(1)} %shard_map.154.own_ref, bf16[2,6,48,128]{3,2,1,0:T(8,128)(2,1)S(1)} %collective-permute-done.8.mate_ref, bf16[3,3,384,384]{3,2,1,0:T(8,128)(2,1)S(1)} %shard_map.152.w_ref), custom_call_target="tpu_custom_call" | custom-call | tf_op jit(solution)/shard_map/pallas_call | solution.py:31
  32.8 1.4 %collective-permute-done.11.x_ref = bf16[2,6,48,128]{3,2,1,0:T(8,128)(2,1)S(1)} collective-permute-done((bf16[2,6,48,128]{3,2,1,0:T(8,128)(2,1)S(1)}, bf16[2,6,48,128]{3,2,1,0:T(8,128)(2,1)S(1)}, u32[]{:S(2)}, u32[]{:S(2)}) %collective-permute-start.11) | collective-permute-done | bytes 147488 | tf_op jit(solution)/shard_map/ppermute | solution.py:524
  34.3 0.0 copy-start.8
  34.3 0.1 collective-permute-start.12
  34.4 2.1 %shard_map.157.base_ref = f32[4,384,384]{2,1,0:T(8,128)S(1)} custom-call(f32[4,384,384]{2,1,0:T(8,128)S(1)} %shard_map.155.base_ref.after_ref, bf16[2,6,48,128]{3,2,1,0:T(8,128)(2,1)S(1)} %shard_map.156.own_ref, bf16[2,6,48,128]{3,2,1,0:T(8,128)(2,1)S(1)} %collective-permute-done.10.mate_ref, bf16[3,3,384,384]{3,2,1,0:T(8,128)(2,1)S(1)} %shard_map.152.w_ref), custom_call_target="tpu_custom_call" | custom-call | tf_op jit(solution)/shard_map/pallas_call | solution.py:31
  36.5 1.6 %shard_map.159 = (bf16[288,128]{1,0:T(8,128)(2,1)S(1)}, bf16[288,128]{1,0:T(8,128)(2,1)S(1)}) custom-call(f32[4,384,384]{2,1,0:T(8,128)S(1)} %shard_map.157.base_ref, bf16[2,6,48,128]{3,2,1,0:T(8,128)(2,1)S(1)} %shard_map.158.own_ref, bf16[2,6,48,128]{3,2,1,0:T(8,128)(2,1)S(1)} %collective-permute-done.12.mate_ref, ...), custom_call_target="tpu_custom_call" | custom-call | tf_op jit(solution)/shard_map/pallas_call | solution.py:31
  38.0 0.5 %collective-permute-start.15 = (bf16[288,128]{1,0:T(8,128)(2,1)S(1)}, bf16[288,128]{1,0:T(8,128)(2,1)S(1)}, u32[]{:S(2)}, u32[]{:S(2)}) collective-permute-start(bf16[288,128]{1,0:T(8,128)(2,1)S(1)} %get-tuple-element.18), channel_id=1, source_target_pairs={{0,12},{4,8},{8,4},{12,0},{1,13},{5,9},{9,5},{13,1},{2,14},{6,10},... | collective-permute-start | bytes 221192 | tf_op jit(solution)/shard_map/ppermute | solution.py:524
  38.5 1.7 %collective-permute-start.14 = (bf16[288,128]{1,0:T(8,128)(2,1)S(1)}, bf16[288,128]{1,0:T(8,128)(2,1)S(1)}, u32[]{:S(2)}, u32[]{:S(2)}) collective-permute-start(bf16[288,128]{1,0:T(8,128)(2,1)S(1)} %get-tuple-element.15.refs_0_), channel_id=1, source_target_pairs={{0,8},{4,12},{8,0},{12,4},{1,9},{5,13},{9,1},{13,5},{2,10},{6,14},... | collective-permute-start | bytes 221192 | tf_op jit(solution)/shard_map/ppermute | solution.py:524
  40.2 0.4 shard_map.160
  40.6 0.0 copy-start.2
  40.6 0.0 copy-start.3
  40.6 0.0 copy-start.4
  40.7 0.0 copy-start.5
  40.7 0.1 collective-permute-start.13
  40.7 1.3 %collective-permute-done.15.after_ref.p3 = bf16[288,128]{1,0:T(8,128)(2,1)S(1)} collective-permute-done((bf16[288,128]{1,0:T(8,128)(2,1)S(1)}, bf16[288,128]{1,0:T(8,128)(2,1)S(1)}, u32[]{:S(2)}, u32[]{:S(2)}) %collective-permute-start.15) | collective-permute-done | bytes 73760 | tf_op jit(solution)/shard_map/ppermute | solution.py:524
  42.0 2.2 %collective-permute-done.14.x_ref = bf16[288,128]{1,0:T(8,128)(2,1)S(1)} collective-permute-done((bf16[288,128]{1,0:T(8,128)(2,1)S(1)}, bf16[288,128]{1,0:T(8,128)(2,1)S(1)}, u32[]{:S(2)}, u32[]{:S(2)}) %collective-permute-start.14) | collective-permute-done | bytes 73760 | tf_op jit(solution)/shard_map/ppermute | solution.py:524
  44.3 2.3 %shard_map.162 = bf16[96,384]{1,0:T(8,128)(2,1)} custom-call(bf16[8,48,384]{2,1,0:T(8,128)(2,1)S(1)} %get-tuple-element.12.raw_ref, bf16[288,128]{1,0:T(8,128)(2,1)S(1)} %get-tuple-element.16.p0, bf16[288,128]{1,0:T(8,128)(2,1)S(1)} %collective-permute-done.13.p1, bf16[288,128]{1,0:T(8,128)(2,1)S(1)} %shard_map.161.p2, ...), custom_call_target="tpu_custom_call" | custom-call | tf_op jit(solution)/shard_map/pallas_call | solution.py:31
  (24 shorter events, 0.1 us)
Async XLA Ops:
  0.0 10.1 %collective-permute-start.2 = (bf16[1,2,48,384]{3,2,1,0:T(8,128)(2,1)}, bf16[1,2,48,384]{3,2,1,0:T(8,128)(2,1)S(1)}, u32[]{:S(2)}, u32[]{:S(2)}) collective-permute-start(bf16[1,2,48,384]{3,2,1,0:T(8,128)(2,1)} %own_ref.1), channel_id=1, source_target_pairs={{0,3},{1,2},{2,1},{3,0},{4,7},{5,6},{6,5},{7,4},{8,11},{9,10},{10,... | collective-permute-start | bytes 221192 | tf_op jit(solution)/shard_map/ppermute | solution.py:524
  5.0 6.4 %collective-permute-start.1 = (bf16[1,2,48,384]{3,2,1,0:T(8,128)(2,1)}, bf16[1,2,48,384]{3,2,1,0:T(8,128)(2,1)S(1)}, u32[]{:S(2)}, u32[]{:S(2)}) collective-permute-start(bf16[1,2,48,384]{3,2,1,0:T(8,128)(2,1)} %own_ref.1), channel_id=1, source_target_pairs={{0,2},{1,3},{2,0},{3,1},{4,6},{5,7},{6,4},{7,5},{8,10},{9,11},{10,... | collective-permute-start | bytes 221192 | tf_op jit(solution)/shard_map/ppermute | solution.py:524
  5.1 6.4 %collective-permute-start = (bf16[1,2,48,384]{3,2,1,0:T(8,128)(2,1)}, bf16[1,2,48,384]{3,2,1,0:T(8,128)(2,1)S(1)}, u32[]{:S(2)}, u32[]{:S(2)}) collective-permute-start(bf16[1,2,48,384]{3,2,1,0:T(8,128)(2,1)} %own_ref.1), channel_id=1, source_target_pairs={{0,1},{1,0},{2,3},{3,2},{4,5},{5,4},{6,7},{7,6},{8,9},{9,8},{10,11... | collective-permute-start | bytes 221192 | tf_op jit(solution)/shard_map/ppermute | solution.py:524
  5.6 5.9 %collective-permute-start.3 = (bf16[1,2,48,384]{3,2,1,0:T(8,128)(2,1)}, bf16[1,2,48,384]{3,2,1,0:T(8,128)(2,1)S(1)}, u32[]{:S(2)}, u32[]{:S(2)}) collective-permute-start(bf16[1,2,48,384]{3,2,1,0:T(8,128)(2,1)} %own_ref.1), channel_id=1, source_target_pairs={{0,8},{4,12},{8,0},{12,4},{1,9},{5,13},{9,1},{13,5},{2,10},{6,14},... | collective-permute-start | bytes 221192 | tf_op jit(solution)/shard_map/ppermute | solution.py:524
  8.3 1.6 %copy-start = (bf16[96,3,3,3,384]{4,0,3,2,1:T(8,128)(2,1)S(1)}, bf16[96,3,3,3,384]{4,0,3,2,1:T(8,128)(2,1)}, u32[]{:S(2)}) copy-start(bf16[96,3,3,3,384]{4,0,3,2,1:T(8,128)(2,1)} %param.18) | copy-start | bytes 5971972
  9.8 1.6 %copy-start.6 = (bf16[1,2,48,384]{3,2,1,0:T(8,128)(2,1)S(1)}, bf16[1,2,48,384]{3,2,1,0:T(8,128)(2,1)}, u32[]{:S(2)}) copy-start(bf16[1,2,48,384]{3,2,1,0:T(8,128)(2,1)} %own_ref.1) | copy-start | bytes 221188
  12.2 1.6 %collective-permute-start.4 = (bf16[1,8,48,384]{3,2,1,0:T(8,128)(2,1)S(1)}, bf16[1,8,48,384]{3,2,1,0:T(8,128)(2,1)S(1)}, u32[]{:S(2)}, u32[]{:S(2)}) collective-permute-start(bf16[1,8,48,384]{3,2,1,0:T(8,128)(2,1)S(1)} %get-tuple-element.13.own_ref), channel_id=1, source_target_pairs={{0,4},{4,0},{8,12},{12,8},{1,5},{5,1},{9,13},{13,9},{2,6},{6,2},{1... | collective-permute-start | bytes 884744 | tf_op jit(solution)/shard_map/ppermute | solution.py:524
  12.2 7.8 %collective-permute-start.5 = (bf16[3,2,48,384]{3,2,1,0:T(8,128)(2,1)S(1)}, bf16[3,2,48,384]{3,2,1,0:T(8,128)(2,1)S(1)}, u32[]{:S(2)}, u32[]{:S(2)}) collective-permute-start(bf16[3,2,48,384]{3,2,1,0:T(8,128)(2,1)S(1)} %get-tuple-element.14), channel_id=1, source_target_pairs={{0,8},{4,12},{8,0},{12,4},{1,9},{5,13},{9,1},{13,5},{2,10},{6,14},... | collective-permute-start | bytes 663560 | tf_op jit(solution)/shard_map/ppermute | solution.py:524
  20.8 1.7 %copy-start.7 = (f32[96]{0:T(128)S(1)}, f32[96]{0:T(128)}, u32[]{:S(2)}) copy-start(f32[96]{0:T(128)} %bias_ref.5) | copy-start | bytes 1156
  20.8 1.6 %collective-permute-start.6 = (bf16[1,8,48,384]{3,2,1,0:T(8,128)(2,1)S(1)}, bf16[1,8,48,384]{3,2,1,0:T(8,128)(2,1)S(1)}, u32[]{:S(2)}, u32[]{:S(2)}) collective-permute-start(bf16[1,8,48,384]{3,2,1,0:T(8,128)(2,1)S(1)} %shard_map.149.a_ref), channel_id=1, source_target_pairs={{0,4},{4,0},{8,12},{12,8},{1,5},{5,1},{9,13},{13,9},{2,6},{6,2},{1... | collective-permute-start | bytes 884744 | tf_op jit(solution)/shard_map/ppermute | solution.py:524
  23.2 5.5 %copy-start.1 = (bf16[96,3,3,3,384]{4,0,3,2,1:T(8,128)(2,1)S(1)}, bf16[96,3,3,3,384]{4,0,3,2,1:T(8,128)(2,1)}, u32[]{:S(2)}) copy-start(bf16[96,3,3,3,384]{4,0,3,2,1:T(8,128)(2,1)} %param.22) | copy-start | bytes 5971972
  23.3 5.7 %collective-permute-start.7 = (bf16[2,6,48,128]{3,2,1,0:T(8,128)(2,1)S(1)}, bf16[2,6,48,128]{3,2,1,0:T(8,128)(2,1)S(1)}, u32[]{:S(2)}, u32[]{:S(2)}) collective-permute-start(bf16[2,6,48,128]{3,2,1,0:T(8,128)(2,1)S(1)} %shard_map.151.refs_0_.own_ref.after_ref), channel_id=1, source_target_pairs={{0,4},{4,0},{8,12},{12,8},{1,5},{5,1},{9,13},{13,9},{2,6},{6,2},{1... | collective-permute-start | bytes 442376 | tf_op jit(solution)/shard_map/ppermute | solution.py:524
  23.5 7.6 %collective-permute-start.9 = (bf16[2,6,48,128]{3,2,1,0:T(8,128)(2,1)S(1)}, bf16[2,6,48,128]{3,2,1,0:T(8,128)(2,1)S(1)}, u32[]{:S(2)}, u32[]{:S(2)}) collective-permute-start(bf16[2,6,48,128]{3,2,1,0:T(8,128)(2,1)S(1)} %shard_map.151.refs_0_.own_ref.after_ref), channel_id=1, source_target_pairs={{0,8},{4,12},{8,0},{12,4},{1,9},{5,13},{9,1},{13,5},{2,10},{6,14},... | collective-permute-start | bytes 442376 | tf_op jit(solution)/shard_map/ppermute | solution.py:524
  28.2 6.1 %collective-permute-start.11 = (bf16[2,6,48,128]{3,2,1,0:T(8,128)(2,1)S(1)}, bf16[2,6,48,128]{3,2,1,0:T(8,128)(2,1)S(1)}, u32[]{:S(2)}, u32[]{:S(2)}) collective-permute-start(bf16[2,6,48,128]{3,2,1,0:T(8,128)(2,1)S(1)} %shard_map.154.own_ref), channel_id=1, source_target_pairs={{0,8},{4,12},{8,0},{12,4},{1,9},{5,13},{9,1},{13,5},{2,10},{6,14},... | collective-permute-start | bytes 442376 | tf_op jit(solution)/shard_map/ppermute | solution.py:524
  28.7 2.9 %collective-permute-start.8 = (bf16[2,6,48,128]{3,2,1,0:T(8,128)(2,1)S(1)}, bf16[2,6,48,128]{3,2,1,0:T(8,128)(2,1)S(1)}, u32[]{:S(2)}, u32[]{:S(2)}) collective-permute-start(bf16[2,6,48,128]{3,2,1,0:T(8,128)(2,1)S(1)} %shard_map.154.own_ref), channel_id=1, source_target_pairs={{0,4},{4,0},{8,12},{12,8},{1,5},{5,1},{9,13},{13,9},{2,6},{6,2},{1... | collective-permute-start | bytes 442376 | tf_op jit(solution)/shard_map/ppermute | solution.py:524
  31.0 3.3 %collective-permute-start.10 = (bf16[2,6,48,128]{3,2,1,0:T(8,128)(2,1)S(1)}, bf16[2,6,48,128]{3,2,1,0:T(8,128)(2,1)S(1)}, u32[]{:S(2)}, u32[]{:S(2)}) collective-permute-start(bf16[2,6,48,128]{3,2,1,0:T(8,128)(2,1)S(1)} %shard_map.156.own_ref), channel_id=1, source_target_pairs={{0,4},{4,0},{8,12},{12,8},{1,5},{5,1},{9,13},{13,9},{2,6},{6,2},{1... | collective-permute-start | bytes 442376 | tf_op jit(solution)/shard_map/ppermute | solution.py:524
  34.3 2.2 %copy-start.8 = (f32[96]{0:T(128)S(1)}, f32[96]{0:T(128)}, u32[]{:S(2)}) copy-start(f32[96]{0:T(128)} %bias_ref.7) | copy-start | bytes 1156
  34.3 2.2 %collective-permute-start.12 = (bf16[2,6,48,128]{3,2,1,0:T(8,128)(2,1)S(1)}, bf16[2,6,48,128]{3,2,1,0:T(8,128)(2,1)S(1)}, u32[]{:S(2)}, u32[]{:S(2)}) collective-permute-start(bf16[2,6,48,128]{3,2,1,0:T(8,128)(2,1)S(1)} %shard_map.158.own_ref), channel_id=1, source_target_pairs={{0,4},{4,0},{8,12},{12,8},{1,5},{5,1},{9,13},{13,9},{2,6},{6,2},{1... | collective-permute-start | bytes 442376 | tf_op jit(solution)/shard_map/ppermute | solution.py:524
  38.0 4.0 %collective-permute-start.15 = (bf16[288,128]{1,0:T(8,128)(2,1)S(1)}, bf16[288,128]{1,0:T(8,128)(2,1)S(1)}, u32[]{:S(2)}, u32[]{:S(2)}) collective-permute-start(bf16[288,128]{1,0:T(8,128)(2,1)S(1)} %get-tuple-element.18), channel_id=1, source_target_pairs={{0,12},{4,8},{8,4},{12,0},{1,13},{5,9},{9,5},{13,1},{2,14},{6,10},... | collective-permute-start | bytes 221192 | tf_op jit(solution)/shard_map/ppermute | solution.py:524
  38.5 5.7 %collective-permute-start.14 = (bf16[288,128]{1,0:T(8,128)(2,1)S(1)}, bf16[288,128]{1,0:T(8,128)(2,1)S(1)}, u32[]{:S(2)}, u32[]{:S(2)}) collective-permute-start(bf16[288,128]{1,0:T(8,128)(2,1)S(1)} %get-tuple-element.15.refs_0_), channel_id=1, source_target_pairs={{0,8},{4,12},{8,0},{12,4},{1,9},{5,13},{9,1},{13,5},{2,10},{6,14},... | collective-permute-start | bytes 221192 | tf_op jit(solution)/shard_map/ppermute | solution.py:524
  40.6 3.6 %copy-start.2 = (bf16[384,384]{1,0:T(8,128)(2,1)S(1)}, bf16[384,384]{1,0:T(8,128)(2,1)}, u32[]{:S(2)}) copy-start(bf16[384,384]{1,0:T(8,128)(2,1)} %wq_ref.1) | copy-start | bytes 884740
  40.6 3.6 %copy-start.3 = (bf16[384,384]{1,0:T(8,128)(2,1)S(1)}, bf16[384,384]{1,0:T(8,128)(2,1)}, u32[]{:S(2)}) copy-start(bf16[384,384]{1,0:T(8,128)(2,1)} %wk_ref.1) | copy-start | bytes 884740
  40.6 3.6 %copy-start.4 = (bf16[384,384]{1,0:T(8,128)(2,1)S(1)}, bf16[384,384]{1,0:T(8,128)(2,1)}, u32[]{:S(2)}) copy-start(bf16[384,384]{1,0:T(8,128)(2,1)} %wv_ref.1) | copy-start | bytes 884740
  40.7 3.6 %copy-start.5 = (bf16[384,384]{1,0:T(8,128)(2,1)S(1)}, bf16[384,384]{1,0:T(8,128)(2,1)}, u32[]{:S(2)}) copy-start(bf16[384,384]{1,0:T(8,128)(2,1)} %wo_ref.1) | copy-start | bytes 884740
  40.7 3.6 %collective-permute-start.13 = (bf16[288,128]{1,0:T(8,128)(2,1)S(1)}, bf16[288,128]{1,0:T(8,128)(2,1)S(1)}, u32[]{:S(2)}, u32[]{:S(2)}) collective-permute-start(bf16[288,128]{1,0:T(8,128)(2,1)S(1)} %get-tuple-element.17), channel_id=1, source_target_pairs={{0,4},{4,0},{8,12},{12,8},{1,5},{5,1},{9,13},{13,9},{2,6},{6,2},{1... | collective-permute-start | bytes 221192 | tf_op jit(solution)/shard_map/ppermute | solution.py:524

commit v9 on v8

--- a/solution.py
+++ b/solution.py
@@ -211,19 +211,25 @@
 
 
 def frame_taps(total_ref, base_ref, a_ref, held, w_ref, lanes=slice(None), first=0):
-    frames, plane, _ = total_ref.shape
+    frames, plane, width = total_ref.shape
     _, padded, cols, channels = a_ref.shape
-    for t in range(first, first + frames):
-        total = None if base_ref is None else base_ref[t]
-        terms = [(g, 2 - (t - f)) for g, f in enumerate(held) if 0 <= t - f <= 2]
-        for g, i in terms:
-            window = jnp.concatenate(
-                [a_ref[g, j : j + padded - 2].reshape(plane, channels) for j in range(3)], axis=1
-            )
-            weight = jnp.concatenate([w_ref[i, j, :, lanes] for j in range(3)], axis=1)
-            term = lax.dot_general(window, weight, (((1,), (1,)), ((), ())), preferred_element_type=F32)
-            total = term if total is None else total + term
-        total_ref[t - first] = jnp.zeros(total_ref.shape[1:], F32) if total is None else total
+    totals = [None if base_ref is None else base_ref[first + t] for t in range(frames)]
+    for g, f in enumerate(held):
+        taken = [(t, 2 - (first + t - f)) for t in range(frames) if 0 <= first + t - f <= 2]
+        if not taken:
+            continue
+        window = jnp.concatenate(
+            [a_ref[g, j : j + padded - 2].reshape(plane, channels) for j in range(3)], axis=1
+        )
+        weight = jnp.concatenate(
+            [jnp.concatenate([w_ref[i, j, :, lanes] for j in range(3)], axis=1) for _, i in taken], axis=0
+        )
+        term = lax.dot_general(window, weight, (((1,), (1,)), ((), ())), preferred_element_type=F32)
+        for k, (t, _) in enumerate(taken):
+            part = term[:, k * width : (k + 1) * width]
+            totals[t] = part if totals[t] is None else totals[t] + part
+    for t in range(frames):
+        total_ref[t] = jnp.zeros((plane, width), F32) if totals[t] is None else totals[t]
 
 
 def lay_out(m_ref, own_ref, mate_ref, pair):

time: 46.7 us -> 45.5 us (0.974)
  Pallas kernels: 18.3 us -> 16.6 us
  waiting for transfers between devices: 9.7 us -> 11 us
  starting transfers between devices: 15.8 us -> 15 us
    pallas_call x18, Pallas kernels: 18.3 us -> 16.6 us  [run(): pl.pallas_call(functools.partial(body, *axes), out_shape=outs, in_specs=[...]
    ppermute x16, waiting for transfers between devices: 9.7 us -> 11 us  [swapped(): lax.ppermute(value, axis, [(i, partner(i)) for i in range(lax.axis_size(a...]
    ppermute x16, starting transfers between devices: 15.8 us -> 15 us  [swapped(): lax.ppermute(value, axis, [(i, partner(i)) for i in range(lax.axis_size(a...]
  transfers between devices with their start and end apart: 16 -> 16, of which waited for: 6 -> 7; matrix products, arithmetic and copies ran while one was open for 2% -> 2% of each run, Pallas kernels for 27% -> 24%
where the time goes in v9:
time: 45.5 us; the launch traced here: 45.3 us
  Pallas kernels  16.6 us (36%)
  starting transfers between devices  15 us (33%)
  waiting for transfers between devices  11 us (24%)
  local copies, waits for them, and re-layouts  1.6 us (4%)
  other arithmetic  0.86 us (2%)
    pallas_call x18, Pallas kernels, run(): pl.pallas_call(functools.partial(body, *axes), out_shape=outs, in_specs=[...  16.6 us
    ppermute x16, starting transfers between devices, swapped(): lax.ppermute(value, axis, [(i, partner(i)) for i in range(lax.axis_size(a...  15 us
    ppermute x16, waiting for transfers between devices, swapped(): lax.ppermute(value, axis, [(i, partner(i)) for i in range(lax.axis_size(a...  11 us
    unnamed x18, local copies, waits for them, and re-layouts  1.6 us
  transfers between devices with their start and end apart: 16, of which 7 were waited for; matrix products, arithmetic and copies ran while one was open for 2% of the time, Pallas kernels for 24%

profile of v9, /device:TPU:0, one launch (start us, length us, event | category | flops | bytes accessed | tf_op | source)
XLA Modules:
  0.0 45.3 jit_solution(1668873317024823748)
XLA Ops:
  0.0 5.0 %collective-permute-start.2 = (bf16[1,2,48,384]{3,2,1,0:T(8,128)(2,1)}, bf16[1,2,48,384]{3,2,1,0:T(8,128)(2,1)S(1)}, u32[]{:S(2)}, u32[]{:S(2)}) collective-permute-start(bf16[1,2,48,384]{3,2,1,0:T(8,128)(2,1)} %own_ref.1), channel_id=1, source_target_pairs={{0,3},{1,2},{2,1},{3,0},{4,7},{5,6},{6,5},{7,4},{8,11},{9,10},{10,... | collective-permute-start | bytes 221192 | tf_op jit(solution)/shard_map/ppermute | solution.py:530
  5.0 0.0 collective-permute-start.1
  5.1 0.6 %collective-permute-start = (bf16[1,2,48,384]{3,2,1,0:T(8,128)(2,1)}, bf16[1,2,48,384]{3,2,1,0:T(8,128)(2,1)S(1)}, u32[]{:S(2)}, u32[]{:S(2)}) collective-permute-start(bf16[1,2,48,384]{3,2,1,0:T(8,128)(2,1)} %own_ref.1), channel_id=1, source_target_pairs={{0,1},{1,0},{2,3},{3,2},{4,5},{5,4},{6,7},{7,6},{8,9},{9,8},{10,11... | collective-permute-start | bytes 221192 | tf_op jit(solution)/shard_map/ppermute | solution.py:530
  5.6 1.7 %collective-permute-start.3 = (bf16[1,2,48,384]{3,2,1,0:T(8,128)(2,1)}, bf16[1,2,48,384]{3,2,1,0:T(8,128)(2,1)S(1)}, u32[]{:S(2)}, u32[]{:S(2)}) collective-permute-start(bf16[1,2,48,384]{3,2,1,0:T(8,128)(2,1)} %own_ref.1), channel_id=1, source_target_pairs={{0,8},{4,12},{8,0},{12,4},{1,9},{5,13},{9,1},{13,5},{2,10},{6,14},... | collective-permute-start | bytes 221192 | tf_op jit(solution)/shard_map/ppermute | solution.py:530
  7.4 0.8 %select_select_fusion.table_ref = f32[8,384]{1,0:T(8,128)S(1)} fusion(f32[384]{0:T(512)} %param.16, f32[384]{0:T(512)} %param.17, f32[384]{0:T(512)} %param.20, f32[384]{0:T(512)} %param.21, f32[384]{0:T(512)} %param.24, f32[384]{0:T(512)} %param.25, pred[8]{0:T(512)(128)(4,1)S(1)} %get-tuple-element.19, pred[8]{0:T(512)(128)(4,1)S(1)} %get-tuple-element.20, ...), kind=kLoop, calls=%fused_computation | loop fusion | flops 18432 | bytes 21552 | tf_op jit(solution)/shard_map/jit(_where)/select_n | solution.py:571
  8.2 0.1 shard_map.146.groups_ref
  8.3 0.0 copy-start
  8.3 1.5 %copy-done = bf16[96,3,3,3,384]{4,0,3,2,1:T(8,128)(2,1)S(1)} copy-done((bf16[96,3,3,3,384]{4,0,3,2,1:T(8,128)(2,1)S(1)}, bf16[96,3,3,3,384]{4,0,3,2,1:T(8,128)(2,1)}, u32[]{:S(2)}) %copy-start) | copy-done | bytes 1990680
  9.8 0.2 shard_map.145.loaded_ref.w_ref
  10.1 1.4 %collective-permute-done.1.two_ref = bf16[1,2,48,384]{3,2,1,0:T(8,128)(2,1)S(1)} collective-permute-done((bf16[1,2,48,384]{3,2,1,0:T(8,128)(2,1)}, bf16[1,2,48,384]{3,2,1,0:T(8,128)(2,1)S(1)}, u32[]{:S(2)}, u32[]{:S(2)}) %collective-permute-start.1) | collective-permute-done | bytes 73760 | tf_op jit(solution)/shard_map/ppermute | solution.py:530
  11.5 0.7 %shard_map.147 = (bf16[1,8,48,384]{3,2,1,0:T(8,128)(2,1)S(1)}, bf16[8,48,384]{2,1,0:T(8,128)(2,1)S(1)}, bf16[3,2,48,384]{3,2,1,0:T(8,128)(2,1)S(1)}) custom-call(bf16[1,2,48,384]{3,2,1,0:T(8,128)(2,1)S(1)} %copy-done.6, bf16[1,2,48,384]{3,2,1,0:T(8,128)(2,1)S(1)} %collective-permute-done.one_ref, bf16[1,2,48,384]{3,2,1,0:T(8,128)(2,1)S(1)} %collective-permute-done.1.two_ref, ...), custom_call_target="tpu_custom_call" | custom-call | tf_op jit(solution)/shard_map/pallas_call | solution.py:31
  12.2 0.1 collective-permute-start.4
  12.2 1.6 %collective-permute-start.5 = (bf16[3,2,48,384]{3,2,1,0:T(8,128)(2,1)S(1)}, bf16[3,2,48,384]{3,2,1,0:T(8,128)(2,1)S(1)}, u32[]{:S(2)}, u32[]{:S(2)}) collective-permute-start(bf16[3,2,48,384]{3,2,1,0:T(8,128)(2,1)S(1)} %get-tuple-element.14), channel_id=1, source_target_pairs={{0,8},{4,12},{8,0},{12,4},{1,9},{5,13},{9,1},{13,5},{2,10},{6,14},... | collective-permute-start | bytes 663560 | tf_op jit(solution)/shard_map/ppermute | solution.py:530
  13.8 0.0 collective-permute-done.4.mate_ref
  13.8 2.8 %shard_map.148.after_ref.near_total_ref = f32[4,384,384]{2,1,0:T(8,128)S(1)} custom-call(bf16[1,8,48,384]{3,2,1,0:T(8,128)(2,1)S(1)} %get-tuple-element.13.own_ref, bf16[1,8,48,384]{3,2,1,0:T(8,128)(2,1)S(1)} %collective-permute-done.4.mate_ref, bf16[3,3,384,384]{3,2,1,0:T(8,128)(2,1)S(1)} %shard_map.145.loaded_ref.w_ref), custom_call_target="tpu_custom_call" | custom-call | tf_op jit(solution)/shard_map/pallas_call | solution.py:31
  16.6 3.5 %collective-permute-done.5.blocks_ref = bf16[3,2,48,384]{3,2,1,0:T(8,128)(2,1)S(1)} collective-permute-done((bf16[3,2,48,384]{3,2,1,0:T(8,128)(2,1)S(1)}, bf16[3,2,48,384]{3,2,1,0:T(8,128)(2,1)S(1)}, u32[]{:S(2)}, u32[]{:S(2)}) %collective-permute-start.5) | collective-permute-done | bytes 221216 | tf_op jit(solution)/shard_map/ppermute | solution.py:530
  20.1 0.7 %shard_map.149.a_ref = bf16[1,8,48,384]{3,2,1,0:T(8,128)(2,1)S(1)} custom-call(bf16[1,2,48,384]{3,2,1,0:T(8,128)(2,1)S(1)} %collective-permute-done.3.across_ref.own_ref, bf16[3,2,48,384]{3,2,1,0:T(8,128)(2,1)S(1)} %collective-permute-done.5.blocks_ref, f32[8,384]{1,0:T(8,128)S(1)} %select_select_fusion.table_ref, ...), custom_call_target="tpu_custom_call" | custom-call | tf_op jit(solution)/shard_map/pallas_call | solution.py:31
  20.8 0.0 copy-start.7
  20.8 0.1 collective-permute-start.6
  20.8 1.1 %shard_map.150.base_ref = f32[4,384,384]{2,1,0:T(8,128)S(1)} custom-call(f32[4,384,384]{2,1,0:T(8,128)S(1)} %shard_map.148.after_ref.near_total_ref, bf16[1,8,48,384]{3,2,1,0:T(8,128)(2,1)S(1)} %shard_map.149.a_ref, bf16[3,3,384,384]{3,2,1,0:T(8,128)(2,1)S(1)} %shard_map.145.loaded_ref.w_ref), custom_call_target="tpu_custom_call" | custom-call | tf_op jit(solution)/shard_map/pallas_call | solution.py:31
  21.9 0.5 %collective-permute-done.6.a_ref = bf16[1,8,48,384]{3,2,1,0:T(8,128)(2,1)S(1)} collective-permute-done((bf16[1,8,48,384]{3,2,1,0:T(8,128)(2,1)S(1)}, bf16[1,8,48,384]{3,2,1,0:T(8,128)(2,1)S(1)}, u32[]{:S(2)}, u32[]{:S(2)}) %collective-permute-start.6) | collective-permute-done | bytes 294944 | tf_op jit(solution)/shard_map/ppermute | solution.py:530
  22.4 0.8 %shard_map.151.refs_0_.own_ref.after_ref = bf16[2,6,48,128]{3,2,1,0:T(8,128)(2,1)S(1)} custom-call(f32[4,384,384]{2,1,0:T(8,128)S(1)} %shard_map.150.base_ref, bf16[1,8,48,384]{3,2,1,0:T(8,128)(2,1)S(1)} %collective-permute-done.6.a_ref, bf16[3,3,384,384]{3,2,1,0:T(8,128)(2,1)S(1)} %shard_map.145.loaded_ref.w_ref, f32[96]{0:T(128)S(1)} %copy-done.7, ...), custom_call_target="tpu_custom_call" | custom-call | tf_op jit(solution)/shard_map/pallas_call | solution.py:31
  23.2 0.0 copy-start.1
  23.3 0.2 collective-permute-start.7
  23.5 2.7 %collective-permute-start.9 = (bf16[2,6,48,128]{3,2,1,0:T(8,128)(2,1)S(1)}, bf16[2,6,48,128]{3,2,1,0:T(8,128)(2,1)S(1)}, u32[]{:S(2)}, u32[]{:S(2)}) collective-permute-start(bf16[2,6,48,128]{3,2,1,0:T(8,128)(2,1)S(1)} %shard_map.151.refs_0_.own_ref.after_ref), channel_id=1, source_target_pairs={{0,8},{4,12},{8,0},{12,4},{1,9},{5,13},{9,1},{13,5},{2,10},{6,14},... | collective-permute-start | bytes 442376 | tf_op jit(solution)/shard_map/ppermute | solution.py:530
  26.2 1.6 %shard_map.154.own_ref = bf16[2,6,48,128]{3,2,1,0:T(8,128)(2,1)S(1)} custom-call(f32[4,384,384]{2,1,0:T(8,128)S(1)} %shard_map.150.base_ref, bf16[1,8,48,384]{3,2,1,0:T(8,128)(2,1)S(1)} %collective-permute-done.6.a_ref, bf16[3,3,384,384]{3,2,1,0:T(8,128)(2,1)S(1)} %shard_map.145.loaded_ref.w_ref, f32[96]{0:T(128)S(1)} %copy-done.7, ...), custom_call_target="tpu_custom_call" | custom-call | tf_op jit(solution)/shard_map/pallas_call | solution.py:31
  27.8 0.3 collective-permute-start.11
  28.2 0.2 shard_map.152.w_ref
  28.4 1.8 %shard_map.153.base_ref.after_ref = f32[4,384,384]{2,1,0:T(8,128)S(1)} custom-call(bf16[2,6,48,128]{3,2,1,0:T(8,128)(2,1)S(1)} %shard_map.151.refs_0_.own_ref.after_ref, bf16[2,6,48,128]{3,2,1,0:T(8,128)(2,1)S(1)} %collective-permute-done.7.mate_ref, bf16[3,3,384,384]{3,2,1,0:T(8,128)(2,1)S(1)} %shard_map.152.w_ref), custom_call_target="tpu_custom_call" | custom-call | tf_op jit(solution)/shard_map/pallas_call | solution.py:31
  30.2 0.3 collective-permute-done.9.x_ref
  30.4 0.3 collective-permute-start.10
  30.8 1.1 %shard_map.155.base_ref.after_ref = f32[4,384,384]{2,1,0:T(8,128)S(1)} custom-call(f32[4,384,384]{2,1,0:T(8,128)S(1)} %shard_map.153.base_ref.after_ref, bf16[2,6,48,128]{3,2,1,0:T(8,128)(2,1)S(1)} %shard_map.154.own_ref, bf16[2,6,48,128]{3,2,1,0:T(8,128)(2,1)S(1)} %collective-permute-done.8.mate_ref, bf16[3,3,384,384]{3,2,1,0:T(8,128)(2,1)S(1)} %shard_map.152.w_ref), custom_call_target="tpu_custom_call" | custom-call | tf_op jit(solution)/shard_map/pallas_call | solution.py:31
  31.9 1.8 %collective-permute-done.11.x_ref = bf16[2,6,48,128]{3,2,1,0:T(8,128)(2,1)S(1)} collective-permute-done((bf16[2,6,48,128]{3,2,1,0:T(8,128)(2,1)S(1)}, bf16[2,6,48,128]{3,2,1,0:T(8,128)(2,1)S(1)}, u32[]{:S(2)}, u32[]{:S(2)}) %collective-permute-start.11) | collective-permute-done | bytes 147488 | tf_op jit(solution)/shard_map/ppermute | solution.py:530
  33.7 0.0 copy-start.8
  33.7 0.1 collective-permute-start.12
  33.8 1.8 %shard_map.157.base_ref = f32[4,384,384]{2,1,0:T(8,128)S(1)} custom-call(f32[4,384,384]{2,1,0:T(8,128)S(1)} %shard_map.155.base_ref.after_ref, bf16[2,6,48,128]{3,2,1,0:T(8,128)(2,1)S(1)} %shard_map.156.own_ref, bf16[2,6,48,128]{3,2,1,0:T(8,128)(2,1)S(1)} %collective-permute-done.10.mate_ref, bf16[3,3,384,384]{3,2,1,0:T(8,128)(2,1)S(1)} %shard_map.152.w_ref), custom_call_target="tpu_custom_call" | custom-call | tf_op jit(solution)/shard_map/pallas_call | solution.py:31
  35.6 1.2 %shard_map.159 = (bf16[288,128]{1,0:T(8,128)(2,1)S(1)}, bf16[288,128]{1,0:T(8,128)(2,1)S(1)}) custom-call(f32[4,384,384]{2,1,0:T(8,128)S(1)} %shard_map.157.base_ref, bf16[2,6,48,128]{3,2,1,0:T(8,128)(2,1)S(1)} %shard_map.158.own_ref, bf16[2,6,48,128]{3,2,1,0:T(8,128)(2,1)S(1)} %collective-permute-done.12.mate_ref, ...), custom_call_target="tpu_custom_call" | custom-call | tf_op jit(solution)/shard_map/pallas_call | solution.py:31
  36.8 0.8 %collective-permute-start.15 = (bf16[288,128]{1,0:T(8,128)(2,1)S(1)}, bf16[288,128]{1,0:T(8,128)(2,1)S(1)}, u32[]{:S(2)}, u32[]{:S(2)}) collective-permute-start(bf16[288,128]{1,0:T(8,128)(2,1)S(1)} %get-tuple-element.18), channel_id=1, source_target_pairs={{0,12},{4,8},{8,4},{12,0},{1,13},{5,9},{9,5},{13,1},{2,14},{6,10},... | collective-permute-start | bytes 221192 | tf_op jit(solution)/shard_map/ppermute | solution.py:530
  37.6 1.3 %collective-permute-start.14 = (bf16[288,128]{1,0:T(8,128)(2,1)S(1)}, bf16[288,128]{1,0:T(8,128)(2,1)S(1)}, u32[]{:S(2)}, u32[]{:S(2)}) collective-permute-start(bf16[288,128]{1,0:T(8,128)(2,1)S(1)} %get-tuple-element.15.refs_0_), channel_id=1, source_target_pairs={{0,8},{4,12},{8,0},{12,4},{1,9},{5,13},{9,1},{13,5},{2,10},{6,14},... | collective-permute-start | bytes 221192 | tf_op jit(solution)/shard_map/ppermute | solution.py:530
  39.0 0.4 shard_map.160
  39.4 0.0 copy-start.2
  39.4 0.0 copy-start.3
  39.4 0.0 copy-start.4
  39.4 0.0 copy-start.5
  39.4 0.1 collective-permute-start.13
  39.5 1.3 %collective-permute-done.15.after_ref.p3 = bf16[288,128]{1,0:T(8,128)(2,1)S(1)} collective-permute-done((bf16[288,128]{1,0:T(8,128)(2,1)S(1)}, bf16[288,128]{1,0:T(8,128)(2,1)S(1)}, u32[]{:S(2)}, u32[]{:S(2)}) %collective-permute-start.15) | collective-permute-done | bytes 73760 | tf_op jit(solution)/shard_map/ppermute | solution.py:530
  40.8 2.2 %collective-permute-done.14.x_ref = bf16[288,128]{1,0:T(8,128)(2,1)S(1)} collective-permute-done((bf16[288,128]{1,0:T(8,128)(2,1)S(1)}, bf16[288,128]{1,0:T(8,128)(2,1)S(1)}, u32[]{:S(2)}, u32[]{:S(2)}) %collective-permute-start.14) | collective-permute-done | bytes 73760 | tf_op jit(solution)/shard_map/ppermute | solution.py:530
  43.1 2.3 %shard_map.162 = bf16[96,384]{1,0:T(8,128)(2,1)} custom-call(bf16[8,48,384]{2,1,0:T(8,128)(2,1)S(1)} %get-tuple-element.12.raw_ref, bf16[288,128]{1,0:T(8,128)(2,1)S(1)} %get-tuple-element.16.p0, bf16[288,128]{1,0:T(8,128)(2,1)S(1)} %collective-permute-done.13.p1, bf16[288,128]{1,0:T(8,128)(2,1)S(1)} %shard_map.161.p2, ...), custom_call_target="tpu_custom_call" | custom-call | tf_op jit(solution)/shard_map/pallas_call | solution.py:31
  (24 shorter events, 0.1 us)
Async XLA Ops:
  0.0 10.1 %collective-permute-start.2 = (bf16[1,2,48,384]{3,2,1,0:T(8,128)(2,1)}, bf16[1,2,48,384]{3,2,1,0:T(8,128)(2,1)S(1)}, u32[]{:S(2)}, u32[]{:S(2)}) collective-permute-start(bf16[1,2,48,384]{3,2,1,0:T(8,128)(2,1)} %own_ref.1), channel_id=1, source_target_pairs={{0,3},{1,2},{2,1},{3,0},{4,7},{5,6},{6,5},{7,4},{8,11},{9,10},{10,... | collective-permute-start | bytes 221192 | tf_op jit(solution)/shard_map/ppermute | solution.py:530
  5.0 6.4 %collective-permute-start.1 = (bf16[1,2,48,384]{3,2,1,0:T(8,128)(2,1)}, bf16[1,2,48,384]{3,2,1,0:T(8,128)(2,1)S(1)}, u32[]{:S(2)}, u32[]{:S(2)}) collective-permute-start(bf16[1,2,48,384]{3,2,1,0:T(8,128)(2,1)} %own_ref.1), channel_id=1, source_target_pairs={{0,2},{1,3},{2,0},{3,1},{4,6},{5,7},{6,4},{7,5},{8,10},{9,11},{10,... | collective-permute-start | bytes 221192 | tf_op jit(solution)/shard_map/ppermute | solution.py:530
  5.1 6.4 %collective-permute-start = (bf16[1,2,48,384]{3,2,1,0:T(8,128)(2,1)}, bf16[1,2,48,384]{3,2,1,0:T(8,128)(2,1)S(1)}, u32[]{:S(2)}, u32[]{:S(2)}) collective-permute-start(bf16[1,2,48,384]{3,2,1,0:T(8,128)(2,1)} %own_ref.1), channel_id=1, source_target_pairs={{0,1},{1,0},{2,3},{3,2},{4,5},{5,4},{6,7},{7,6},{8,9},{9,8},{10,11... | collective-permute-start | bytes 221192 | tf_op jit(solution)/shard_map/ppermute | solution.py:530
  5.6 5.9 %collective-permute-start.3 = (bf16[1,2,48,384]{3,2,1,0:T(8,128)(2,1)}, bf16[1,2,48,384]{3,2,1,0:T(8,128)(2,1)S(1)}, u32[]{:S(2)}, u32[]{:S(2)}) collective-permute-start(bf16[1,2,48,384]{3,2,1,0:T(8,128)(2,1)} %own_ref.1), channel_id=1, source_target_pairs={{0,8},{4,12},{8,0},{12,4},{1,9},{5,13},{9,1},{13,5},{2,10},{6,14},... | collective-permute-start | bytes 221192 | tf_op jit(solution)/shard_map/ppermute | solution.py:530
  8.3 1.6 %copy-start = (bf16[96,3,3,3,384]{4,0,3,2,1:T(8,128)(2,1)S(1)}, bf16[96,3,3,3,384]{4,0,3,2,1:T(8,128)(2,1)}, u32[]{:S(2)}) copy-start(bf16[96,3,3,3,384]{4,0,3,2,1:T(8,128)(2,1)} %param.18) | copy-start | bytes 5971972
  9.8 1.6 %copy-start.6 = (bf16[1,2,48,384]{3,2,1,0:T(8,128)(2,1)S(1)}, bf16[1,2,48,384]{3,2,1,0:T(8,128)(2,1)}, u32[]{:S(2)}) copy-start(bf16[1,2,48,384]{3,2,1,0:T(8,128)(2,1)} %own_ref.1) | copy-start | bytes 221188
  12.2 1.6 %collective-permute-start.4 = (bf16[1,8,48,384]{3,2,1,0:T(8,128)(2,1)S(1)}, bf16[1,8,48,384]{3,2,1,0:T(8,128)(2,1)S(1)}, u32[]{:S(2)}, u32[]{:S(2)}) collective-permute-start(bf16[1,8,48,384]{3,2,1,0:T(8,128)(2,1)S(1)} %get-tuple-element.13.own_ref), channel_id=1, source_target_pairs={{0,4},{4,0},{8,12},{12,8},{1,5},{5,1},{9,13},{13,9},{2,6},{6,2},{1... | collective-permute-start | bytes 884744 | tf_op jit(solution)/shard_map/ppermute | solution.py:530
  12.2 7.8 %collective-permute-start.5 = (bf16[3,2,48,384]{3,2,1,0:T(8,128)(2,1)S(1)}, bf16[3,2,48,384]{3,2,1,0:T(8,128)(2,1)S(1)}, u32[]{:S(2)}, u32[]{:S(2)}) collective-permute-start(bf16[3,2,48,384]{3,2,1,0:T(8,128)(2,1)S(1)} %get-tuple-element.14), channel_id=1, source_target_pairs={{0,8},{4,12},{8,0},{12,4},{1,9},{5,13},{9,1},{13,5},{2,10},{6,14},... | collective-permute-start | bytes 663560 | tf_op jit(solution)/shard_map/ppermute | solution.py:530
  20.8 1.7 %copy-start.7 = (f32[96]{0:T(128)S(1)}, f32[96]{0:T(128)}, u32[]{:S(2)}) copy-start(f32[96]{0:T(128)} %bias_ref.5) | copy-start | bytes 1156
  20.8 1.6 %collective-permute-start.6 = (bf16[1,8,48,384]{3,2,1,0:T(8,128)(2,1)S(1)}, bf16[1,8,48,384]{3,2,1,0:T(8,128)(2,1)S(1)}, u32[]{:S(2)}, u32[]{:S(2)}) collective-permute-start(bf16[1,8,48,384]{3,2,1,0:T(8,128)(2,1)S(1)} %shard_map.149.a_ref), channel_id=1, source_target_pairs={{0,4},{4,0},{8,12},{12,8},{1,5},{5,1},{9,13},{13,9},{2,6},{6,2},{1... | collective-permute-start | bytes 884744 | tf_op jit(solution)/shard_map/ppermute | solution.py:530
  23.2 4.9 %copy-start.1 = (bf16[96,3,3,3,384]{4,0,3,2,1:T(8,128)(2,1)S(1)}, bf16[96,3,3,3,384]{4,0,3,2,1:T(8,128)(2,1)}, u32[]{:S(2)}) copy-start(bf16[96,3,3,3,384]{4,0,3,2,1:T(8,128)(2,1)} %param.22) | copy-start | bytes 5971972
  23.3 5.1 %collective-permute-start.7 = (bf16[2,6,48,128]{3,2,1,0:T(8,128)(2,1)S(1)}, bf16[2,6,48,128]{3,2,1,0:T(8,128)(2,1)S(1)}, u32[]{:S(2)}, u32[]{:S(2)}) collective-permute-start(bf16[2,6,48,128]{3,2,1,0:T(8,128)(2,1)S(1)} %shard_map.151.refs_0_.own_ref.after_ref), channel_id=1, source_target_pairs={{0,4},{4,0},{8,12},{12,8},{1,5},{5,1},{9,13},{13,9},{2,6},{6,2},{1... | collective-permute-start | bytes 442376 | tf_op jit(solution)/shard_map/ppermute | solution.py:530
  23.5 7.0 %collective-permute-start.9 = (bf16[2,6,48,128]{3,2,1,0:T(8,128)(2,1)S(1)}, bf16[2,6,48,128]{3,2,1,0:T(8,128)(2,1)S(1)}, u32[]{:S(2)}, u32[]{:S(2)}) collective-permute-start(bf16[2,6,48,128]{3,2,1,0:T(8,128)(2,1)S(1)} %shard_map.151.refs_0_.own_ref.after_ref), channel_id=1, source_target_pairs={{0,8},{4,12},{8,0},{12,4},{1,9},{5,13},{9,1},{13,5},{2,10},{6,14},... | collective-permute-start | bytes 442376 | tf_op jit(solution)/shard_map/ppermute | solution.py:530
  27.8 5.9 %collective-permute-start.11 = (bf16[2,6,48,128]{3,2,1,0:T(8,128)(2,1)S(1)}, bf16[2,6,48,128]{3,2,1,0:T(8,128)(2,1)S(1)}, u32[]{:S(2)}, u32[]{:S(2)}) collective-permute-start(bf16[2,6,48,128]{3,2,1,0:T(8,128)(2,1)S(1)} %shard_map.154.own_ref), channel_id=1, source_target_pairs={{0,8},{4,12},{8,0},{12,4},{1,9},{5,13},{9,1},{13,5},{2,10},{6,14},... | collective-permute-start | bytes 442376 | tf_op jit(solution)/shard_map/ppermute | solution.py:530
  28.1 2.6 %collective-permute-start.8 = (bf16[2,6,48,128]{3,2,1,0:T(8,128)(2,1)S(1)}, bf16[2,6,48,128]{3,2,1,0:T(8,128)(2,1)S(1)}, u32[]{:S(2)}, u32[]{:S(2)}) collective-permute-start(bf16[2,6,48,128]{3,2,1,0:T(8,128)(2,1)S(1)} %shard_map.154.own_ref), channel_id=1, source_target_pairs={{0,4},{4,0},{8,12},{12,8},{1,5},{5,1},{9,13},{13,9},{2,6},{6,2},{1... | collective-permute-start | bytes 442376 | tf_op jit(solution)/shard_map/ppermute | solution.py:530
  30.4 3.4 %collective-permute-start.10 = (bf16[2,6,48,128]{3,2,1,0:T(8,128)(2,1)S(1)}, bf16[2,6,48,128]{3,2,1,0:T(8,128)(2,1)S(1)}, u32[]{:S(2)}, u32[]{:S(2)}) collective-permute-start(bf16[2,6,48,128]{3,2,1,0:T(8,128)(2,1)S(1)} %shard_map.156.own_ref), channel_id=1, source_target_pairs={{0,4},{4,0},{8,12},{12,8},{1,5},{5,1},{9,13},{13,9},{2,6},{6,2},{1... | collective-permute-start | bytes 442376 | tf_op jit(solution)/shard_map/ppermute | solution.py:530
  33.7 1.9 %copy-start.8 = (f32[96]{0:T(128)S(1)}, f32[96]{0:T(128)}, u32[]{:S(2)}) copy-start(f32[96]{0:T(128)} %bias_ref.7) | copy-start | bytes 1156
  33.7 1.9 %collective-permute-start.12 = (bf16[2,6,48,128]{3,2,1,0:T(8,128)(2,1)S(1)}, bf16[2,6,48,128]{3,2,1,0:T(8,128)(2,1)S(1)}, u32[]{:S(2)}, u32[]{:S(2)}) collective-permute-start(bf16[2,6,48,128]{3,2,1,0:T(8,128)(2,1)S(1)} %shard_map.158.own_ref), channel_id=1, source_target_pairs={{0,4},{4,0},{8,12},{12,8},{1,5},{5,1},{9,13},{13,9},{2,6},{6,2},{1... | collective-permute-start | bytes 442376 | tf_op jit(solution)/shard_map/ppermute | solution.py:530
  36.8 4.0 %collective-permute-start.15 = (bf16[288,128]{1,0:T(8,128)(2,1)S(1)}, bf16[288,128]{1,0:T(8,128)(2,1)S(1)}, u32[]{:S(2)}, u32[]{:S(2)}) collective-permute-start(bf16[288,128]{1,0:T(8,128)(2,1)S(1)} %get-tuple-element.18), channel_id=1, source_target_pairs={{0,12},{4,8},{8,4},{12,0},{1,13},{5,9},{9,5},{13,1},{2,14},{6,10},... | collective-permute-start | bytes 221192 | tf_op jit(solution)/shard_map/ppermute | solution.py:530
  37.6 5.4 %collective-permute-start.14 = (bf16[288,128]{1,0:T(8,128)(2,1)S(1)}, bf16[288,128]{1,0:T(8,128)(2,1)S(1)}, u32[]{:S(2)}, u32[]{:S(2)}) collective-permute-start(bf16[288,128]{1,0:T(8,128)(2,1)S(1)} %get-tuple-element.15.refs_0_), channel_id=1, source_target_pairs={{0,8},{4,12},{8,0},{12,4},{1,9},{5,13},{9,1},{13,5},{2,10},{6,14},... | collective-permute-start | bytes 221192 | tf_op jit(solution)/shard_map/ppermute | solution.py:530
  39.4 3.6 %copy-start.2 = (bf16[384,384]{1,0:T(8,128)(2,1)S(1)}, bf16[384,384]{1,0:T(8,128)(2,1)}, u32[]{:S(2)}) copy-start(bf16[384,384]{1,0:T(8,128)(2,1)} %wq_ref.1) | copy-start | bytes 884740
  39.4 3.6 %copy-start.3 = (bf16[384,384]{1,0:T(8,128)(2,1)S(1)}, bf16[384,384]{1,0:T(8,128)(2,1)}, u32[]{:S(2)}) copy-start(bf16[384,384]{1,0:T(8,128)(2,1)} %wk_ref.1) | copy-start | bytes 884740
  39.4 3.6 %copy-start.4 = (bf16[384,384]{1,0:T(8,128)(2,1)S(1)}, bf16[384,384]{1,0:T(8,128)(2,1)}, u32[]{:S(2)}) copy-start(bf16[384,384]{1,0:T(8,128)(2,1)} %wv_ref.1) | copy-start | bytes 884740
  39.4 3.6 %copy-start.5 = (bf16[384,384]{1,0:T(8,128)(2,1)S(1)}, bf16[384,384]{1,0:T(8,128)(2,1)}, u32[]{:S(2)}) copy-start(bf16[384,384]{1,0:T(8,128)(2,1)} %wo_ref.1) | copy-start | bytes 884740
  39.4 3.6 %collective-permute-start.13 = (bf16[288,128]{1,0:T(8,128)(2,1)S(1)}, bf16[288,128]{1,0:T(8,128)(2,1)S(1)}, u32[]{:S(2)}, u32[]{:S(2)}) collective-permute-start(bf16[288,128]{1,0:T(8,128)(2,1)S(1)} %get-tuple-element.17), channel_id=1, source_target_pairs={{0,4},{4,0},{8,12},{12,8},{1,5},{5,1},{9,13},{13,9},{2,6},{6,2},{1... | collective-permute-start | bytes 221192 | tf_op jit(solution)/shard_map/ppermute | solution.py:530

commit v10 on v9

--- a/solution.py
+++ b/solution.py
@@ -516,8 +516,8 @@
     mine = ((own - mean) * scale + shift).astype(BF16)
     dot = functools.partial(jnp.dot, preferred_element_type=F32)
     queries = (dot(mine, wq_ref[...]) * C ** (-0.5)).astype(BF16)
-    keys = dot(normed, wk_ref[...]).astype(BF16)
-    values = dot(normed, wv_ref[...]).astype(BF16)
+    both = dot(normed, jnp.concatenate([wk_ref[...], wv_ref[...]], axis=1)).astype(BF16)
+    keys, values = both[:, : both.shape[1] // 2], both[:, both.shape[1] // 2 :]
     scores = lax.dot_general(queries, keys, (((1,), (1,)), ((), ())), preferred_element_type=F32)
     peak = jnp.max(scores, axis=-1, keepdims=True)
     weights = jnp.exp(scores - peak)

time: 45.5 us -> 45.5 us (level)
  no operation moved by 1% of the time
where the time goes in v10:
time: 45.5 us; the launch traced here: 45.3 us
  Pallas kernels  16.6 us (36%)
  starting transfers between devices  15 us (33%)
  waiting for transfers between devices  11 us (24%)
  local copies, waits for them, and re-layouts  1.6 us (4%)
  other arithmetic  0.86 us (2%)
    pallas_call x18, Pallas kernels, run(): pl.pallas_call(functools.partial(body, *axes), out_shape=outs, in_specs=[...  16.6 us
    ppermute x16, starting transfers between devices, swapped(): lax.ppermute(value, axis, [(i, partner(i)) for i in range(lax.axis_size(a...  15 us
    ppermute x16, waiting for transfers between devices, swapped(): lax.ppermute(value, axis, [(i, partner(i)) for i in range(lax.axis_size(a...  11 us
    unnamed x18, local copies, waits for them, and re-layouts  1.6 us
  transfers between devices with their start and end apart: 16, of which 7 were waited for; matrix products, arithmetic and copies ran while one was open for 2% of the time, Pallas kernels for 24%

profile of v10, /device:TPU:0, one launch (start us, length us, event | category | flops | bytes accessed | tf_op | source)
XLA Modules:
  0.0 45.3 jit_solution(4276181300595020807)
XLA Ops:
  0.0 5.0 %collective-permute-start.2 = (bf16[1,2,48,384]{3,2,1,0:T(8,128)(2,1)}, bf16[1,2,48,384]{3,2,1,0:T(8,128)(2,1)S(1)}, u32[]{:S(2)}, u32[]{:S(2)}) collective-permute-start(bf16[1,2,48,384]{3,2,1,0:T(8,128)(2,1)} %own_ref.1), channel_id=1, source_target_pairs={{0,3},{1,2},{2,1},{3,0},{4,7},{5,6},{6,5},{7,4},{8,11},{9,10},{10,... | collective-permute-start | bytes 221192 | tf_op jit(solution)/shard_map/ppermute | solution.py:530
  5.1 0.6 %collective-permute-start = (bf16[1,2,48,384]{3,2,1,0:T(8,128)(2,1)}, bf16[1,2,48,384]{3,2,1,0:T(8,128)(2,1)S(1)}, u32[]{:S(2)}, u32[]{:S(2)}) collective-permute-start(bf16[1,2,48,384]{3,2,1,0:T(8,128)(2,1)} %own_ref.1), channel_id=1, source_target_pairs={{0,1},{1,0},{2,3},{3,2},{4,5},{5,4},{6,7},{7,6},{8,9},{9,8},{10,11... | collective-permute-start | bytes 221192 | tf_op jit(solution)/shard_map/ppermute | solution.py:530
  5.6 1.7 %collective-permute-start.3 = (bf16[1,2,48,384]{3,2,1,0:T(8,128)(2,1)}, bf16[1,2,48,384]{3,2,1,0:T(8,128)(2,1)S(1)}, u32[]{:S(2)}, u32[]{:S(2)}) collective-permute-start(bf16[1,2,48,384]{3,2,1,0:T(8,128)(2,1)} %own_ref.1), channel_id=1, source_target_pairs={{0,8},{4,12},{8,0},{12,4},{1,9},{5,13},{9,1},{13,5},{2,10},{6,14},... | collective-permute-start | bytes 221192 | tf_op jit(solution)/shard_map/ppermute | solution.py:530
  7.4 0.8 %select_select_fusion.table_ref = f32[8,384]{1,0:T(8,128)S(1)} fusion(f32[384]{0:T(512)} %param.16, f32[384]{0:T(512)} %param.17, f32[384]{0:T(512)} %param.20, f32[384]{0:T(512)} %param.21, f32[384]{0:T(512)} %param.24, f32[384]{0:T(512)} %param.25, pred[8]{0:T(512)(128)(4,1)S(1)} %get-tuple-element.19, pred[8]{0:T(512)(128)(4,1)S(1)} %get-tuple-element.20, ...), kind=kLoop, calls=%fused_computation | loop fusion | flops 18432 | bytes 21552 | tf_op jit(solution)/shard_map/jit(_where)/select_n | solution.py:571
  8.2 0.1 shard_map.146.groups_ref
  8.3 0.0 copy-start
  8.3 1.5 %copy-done = bf16[96,3,3,3,384]{4,0,3,2,1:T(8,128)(2,1)S(1)} copy-done((bf16[96,3,3,3,384]{4,0,3,2,1:T(8,128)(2,1)S(1)}, bf16[96,3,3,3,384]{4,0,3,2,1:T(8,128)(2,1)}, u32[]{:S(2)}) %copy-start) | copy-done | bytes 1990680
  9.8 0.2 shard_map.145.loaded_ref.w_ref
  10.1 1.4 %collective-permute-done.1.two_ref = bf16[1,2,48,384]{3,2,1,0:T(8,128)(2,1)S(1)} collective-permute-done((bf16[1,2,48,384]{3,2,1,0:T(8,128)(2,1)}, bf16[1,2,48,384]{3,2,1,0:T(8,128)(2,1)S(1)}, u32[]{:S(2)}, u32[]{:S(2)}) %collective-permute-start.1) | collective-permute-done | bytes 73760 | tf_op jit(solution)/shard_map/ppermute | solution.py:530
  11.5 0.0 collective-permute-done.one_ref
  11.5 0.7 %shard_map.147 = (bf16[1,8,48,384]{3,2,1,0:T(8,128)(2,1)S(1)}, bf16[8,48,384]{2,1,0:T(8,128)(2,1)S(1)}, bf16[3,2,48,384]{3,2,1,0:T(8,128)(2,1)S(1)}) custom-call(bf16[1,2,48,384]{3,2,1,0:T(8,128)(2,1)S(1)} %copy-done.6, bf16[1,2,48,384]{3,2,1,0:T(8,128)(2,1)S(1)} %collective-permute-done.one_ref, bf16[1,2,48,384]{3,2,1,0:T(8,128)(2,1)S(1)} %collective-permute-done.1.two_ref, ...), custom_call_target="tpu_custom_call" | custom-call | tf_op jit(solution)/shard_map/pallas_call | solution.py:31
  12.2 0.1 collective-permute-start.4
  12.2 1.6 %collective-permute-start.5 = (bf16[3,2,48,384]{3,2,1,0:T(8,128)(2,1)S(1)}, bf16[3,2,48,384]{3,2,1,0:T(8,128)(2,1)S(1)}, u32[]{:S(2)}, u32[]{:S(2)}) collective-permute-start(bf16[3,2,48,384]{3,2,1,0:T(8,128)(2,1)S(1)} %get-tuple-element.14), channel_id=1, source_target_pairs={{0,8},{4,12},{8,0},{12,4},{1,9},{5,13},{9,1},{13,5},{2,10},{6,14},... | collective-permute-start | bytes 663560 | tf_op jit(solution)/shard_map/ppermute | solution.py:530
  13.8 0.0 collective-permute-done.4.mate_ref
  13.8 2.8 %shard_map.148.after_ref.near_total_ref = f32[4,384,384]{2,1,0:T(8,128)S(1)} custom-call(bf16[1,8,48,384]{3,2,1,0:T(8,128)(2,1)S(1)} %get-tuple-element.13.own_ref, bf16[1,8,48,384]{3,2,1,0:T(8,128)(2,1)S(1)} %collective-permute-done.4.mate_ref, bf16[3,3,384,384]{3,2,1,0:T(8,128)(2,1)S(1)} %shard_map.145.loaded_ref.w_ref), custom_call_target="tpu_custom_call" | custom-call | tf_op jit(solution)/shard_map/pallas_call | solution.py:31
  16.6 3.5 %collective-permute-done.5.blocks_ref = bf16[3,2,48,384]{3,2,1,0:T(8,128)(2,1)S(1)} collective-permute-done((bf16[3,2,48,384]{3,2,1,0:T(8,128)(2,1)S(1)}, bf16[3,2,48,384]{3,2,1,0:T(8,128)(2,1)S(1)}, u32[]{:S(2)}, u32[]{:S(2)}) %collective-permute-start.5) | collective-permute-done | bytes 221216 | tf_op jit(solution)/shard_map/ppermute | solution.py:530
  20.1 0.7 %shard_map.149.a_ref = bf16[1,8,48,384]{3,2,1,0:T(8,128)(2,1)S(1)} custom-call(bf16[1,2,48,384]{3,2,1,0:T(8,128)(2,1)S(1)} %collective-permute-done.3.across_ref.own_ref, bf16[3,2,48,384]{3,2,1,0:T(8,128)(2,1)S(1)} %collective-permute-done.5.blocks_ref, f32[8,384]{1,0:T(8,128)S(1)} %select_select_fusion.table_ref, ...), custom_call_target="tpu_custom_call" | custom-call | tf_op jit(solution)/shard_map/pallas_call | solution.py:31
  20.8 0.0 copy-start.7
  20.8 0.1 collective-permute-start.6
  20.8 1.1 %shard_map.150.base_ref = f32[4,384,384]{2,1,0:T(8,128)S(1)} custom-call(f32[4,384,384]{2,1,0:T(8,128)S(1)} %shard_map.148.after_ref.near_total_ref, bf16[1,8,48,384]{3,2,1,0:T(8,128)(2,1)S(1)} %shard_map.149.a_ref, bf16[3,3,384,384]{3,2,1,0:T(8,128)(2,1)S(1)} %shard_map.145.loaded_ref.w_ref), custom_call_target="tpu_custom_call" | custom-call | tf_op jit(solution)/shard_map/pallas_call | solution.py:31
  21.9 0.5 %collective-permute-done.6.a_ref = bf16[1,8,48,384]{3,2,1,0:T(8,128)(2,1)S(1)} collective-permute-done((bf16[1,8,48,384]{3,2,1,0:T(8,128)(2,1)S(1)}, bf16[1,8,48,384]{3,2,1,0:T(8,128)(2,1)S(1)}, u32[]{:S(2)}, u32[]{:S(2)}) %collective-permute-start.6) | collective-permute-done | bytes 294944 | tf_op jit(solution)/shard_map/ppermute | solution.py:530
  22.4 0.8 %shard_map.151.refs_0_.own_ref.after_ref = bf16[2,6,48,128]{3,2,1,0:T(8,128)(2,1)S(1)} custom-call(f32[4,384,384]{2,1,0:T(8,128)S(1)} %shard_map.150.base_ref, bf16[1,8,48,384]{3,2,1,0:T(8,128)(2,1)S(1)} %collective-permute-done.6.a_ref, bf16[3,3,384,384]{3,2,1,0:T(8,128)(2,1)S(1)} %shard_map.145.loaded_ref.w_ref, f32[96]{0:T(128)S(1)} %copy-done.7, ...), custom_call_target="tpu_custom_call" | custom-call | tf_op jit(solution)/shard_map/pallas_call | solution.py:31
  23.2 0.0 copy-start.1
  23.3 0.2 collective-permute-start.7
  23.5 2.7 %collective-permute-start.9 = (bf16[2,6,48,128]{3,2,1,0:T(8,128)(2,1)S(1)}, bf16[2,6,48,128]{3,2,1,0:T(8,128)(2,1)S(1)}, u32[]{:S(2)}, u32[]{:S(2)}) collective-permute-start(bf16[2,6,48,128]{3,2,1,0:T(8,128)(2,1)S(1)} %shard_map.151.refs_0_.own_ref.after_ref), channel_id=1, source_target_pairs={{0,8},{4,12},{8,0},{12,4},{1,9},{5,13},{9,1},{13,5},{2,10},{6,14},... | collective-permute-start | bytes 442376 | tf_op jit(solution)/shard_map/ppermute | solution.py:530
  26.2 1.6 %shard_map.154.own_ref = bf16[2,6,48,128]{3,2,1,0:T(8,128)(2,1)S(1)} custom-call(f32[4,384,384]{2,1,0:T(8,128)S(1)} %shard_map.150.base_ref, bf16[1,8,48,384]{3,2,1,0:T(8,128)(2,1)S(1)} %collective-permute-done.6.a_ref, bf16[3,3,384,384]{3,2,1,0:T(8,128)(2,1)S(1)} %shard_map.145.loaded_ref.w_ref, f32[96]{0:T(128)S(1)} %copy-done.7, ...), custom_call_target="tpu_custom_call" | custom-call | tf_op jit(solution)/shard_map/pallas_call | solution.py:31
  27.8 0.3 collective-permute-start.11
  28.2 0.2 shard_map.152.w_ref
  28.4 1.8 %shard_map.153.base_ref.after_ref = f32[4,384,384]{2,1,0:T(8,128)S(1)} custom-call(bf16[2,6,48,128]{3,2,1,0:T(8,128)(2,1)S(1)} %shard_map.151.refs_0_.own_ref.after_ref, bf16[2,6,48,128]{3,2,1,0:T(8,128)(2,1)S(1)} %collective-permute-done.7.mate_ref, bf16[3,3,384,384]{3,2,1,0:T(8,128)(2,1)S(1)} %shard_map.152.w_ref), custom_call_target="tpu_custom_call" | custom-call | tf_op jit(solution)/shard_map/pallas_call | solution.py:31
  30.2 0.3 collective-permute-done.9.x_ref
  30.4 0.3 collective-permute-start.10
  30.8 1.1 %shard_map.155.base_ref.after_ref = f32[4,384,384]{2,1,0:T(8,128)S(1)} custom-call(f32[4,384,384]{2,1,0:T(8,128)S(1)} %shard_map.153.base_ref.after_ref, bf16[2,6,48,128]{3,2,1,0:T(8,128)(2,1)S(1)} %shard_map.154.own_ref, bf16[2,6,48,128]{3,2,1,0:T(8,128)(2,1)S(1)} %collective-permute-done.8.mate_ref, bf16[3,3,384,384]{3,2,1,0:T(8,128)(2,1)S(1)} %shard_map.152.w_ref), custom_call_target="tpu_custom_call" | custom-call | tf_op jit(solution)/shard_map/pallas_call | solution.py:31
  31.9 1.8 %collective-permute-done.11.x_ref = bf16[2,6,48,128]{3,2,1,0:T(8,128)(2,1)S(1)} collective-permute-done((bf16[2,6,48,128]{3,2,1,0:T(8,128)(2,1)S(1)}, bf16[2,6,48,128]{3,2,1,0:T(8,128)(2,1)S(1)}, u32[]{:S(2)}, u32[]{:S(2)}) %collective-permute-start.11) | collective-permute-done | bytes 147488 | tf_op jit(solution)/shard_map/ppermute | solution.py:530
  33.7 0.0 copy-start.8
  33.7 0.1 collective-permute-start.12
  33.8 1.8 %shard_map.157.base_ref = f32[4,384,384]{2,1,0:T(8,128)S(1)} custom-call(f32[4,384,384]{2,1,0:T(8,128)S(1)} %shard_map.155.base_ref.after_ref, bf16[2,6,48,128]{3,2,1,0:T(8,128)(2,1)S(1)} %shard_map.156.own_ref, bf16[2,6,48,128]{3,2,1,0:T(8,128)(2,1)S(1)} %collective-permute-done.10.mate_ref, bf16[3,3,384,384]{3,2,1,0:T(8,128)(2,1)S(1)} %shard_map.152.w_ref), custom_call_target="tpu_custom_call" | custom-call | tf_op jit(solution)/shard_map/pallas_call | solution.py:31
  35.6 1.2 %shard_map.159 = (bf16[288,128]{1,0:T(8,128)(2,1)S(1)}, bf16[288,128]{1,0:T(8,128)(2,1)S(1)}) custom-call(f32[4,384,384]{2,1,0:T(8,128)S(1)} %shard_map.157.base_ref, bf16[2,6,48,128]{3,2,1,0:T(8,128)(2,1)S(1)} %shard_map.158.own_ref, bf16[2,6,48,128]{3,2,1,0:T(8,128)(2,1)S(1)} %collective-permute-done.12.mate_ref, ...), custom_call_target="tpu_custom_call" | custom-call | tf_op jit(solution)/shard_map/pallas_call | solution.py:31
  36.8 0.8 %collective-permute-start.15 = (bf16[288,128]{1,0:T(8,128)(2,1)S(1)}, bf16[288,128]{1,0:T(8,128)(2,1)S(1)}, u32[]{:S(2)}, u32[]{:S(2)}) collective-permute-start(bf16[288,128]{1,0:T(8,128)(2,1)S(1)} %get-tuple-element.18), channel_id=1, source_target_pairs={{0,12},{4,8},{8,4},{12,0},{1,13},{5,9},{9,5},{13,1},{2,14},{6,10},... | collective-permute-start | bytes 221192 | tf_op jit(solution)/shard_map/ppermute | solution.py:530
  37.6 1.3 %collective-permute-start.14 = (bf16[288,128]{1,0:T(8,128)(2,1)S(1)}, bf16[288,128]{1,0:T(8,128)(2,1)S(1)}, u32[]{:S(2)}, u32[]{:S(2)}) collective-permute-start(bf16[288,128]{1,0:T(8,128)(2,1)S(1)} %get-tuple-element.15.refs_0_), channel_id=1, source_target_pairs={{0,8},{4,12},{8,0},{12,4},{1,9},{5,13},{9,1},{13,5},{2,10},{6,14},... | collective-permute-start | bytes 221192 | tf_op jit(solution)/shard_map/ppermute | solution.py:530
  39.0 0.4 shard_map.160
  39.4 0.0 copy-start.2
  39.4 0.0 copy-start.3
  39.4 0.0 copy-start.4
  39.4 0.0 copy-start.5
  39.4 0.1 collective-permute-start.13
  39.5 1.3 %collective-permute-done.15.after_ref.p3 = bf16[288,128]{1,0:T(8,128)(2,1)S(1)} collective-permute-done((bf16[288,128]{1,0:T(8,128)(2,1)S(1)}, bf16[288,128]{1,0:T(8,128)(2,1)S(1)}, u32[]{:S(2)}, u32[]{:S(2)}) %collective-permute-start.15) | collective-permute-done | bytes 73760 | tf_op jit(solution)/shard_map/ppermute | solution.py:530
  40.8 2.2 %collective-permute-done.14.x_ref = bf16[288,128]{1,0:T(8,128)(2,1)S(1)} collective-permute-done((bf16[288,128]{1,0:T(8,128)(2,1)S(1)}, bf16[288,128]{1,0:T(8,128)(2,1)S(1)}, u32[]{:S(2)}, u32[]{:S(2)}) %collective-permute-start.14) | collective-permute-done | bytes 73760 | tf_op jit(solution)/shard_map/ppermute | solution.py:530
  43.1 2.3 %shard_map.162 = bf16[96,384]{1,0:T(8,128)(2,1)} custom-call(bf16[8,48,384]{2,1,0:T(8,128)(2,1)S(1)} %get-tuple-element.12.raw_ref, bf16[288,128]{1,0:T(8,128)(2,1)S(1)} %get-tuple-element.16.p0, bf16[288,128]{1,0:T(8,128)(2,1)S(1)} %collective-permute-done.13.p1, bf16[288,128]{1,0:T(8,128)(2,1)S(1)} %shard_map.161.p2, ...), custom_call_target="tpu_custom_call" | custom-call | tf_op jit(solution)/shard_map/pallas_call | solution.py:31
  (24 shorter events, 0.1 us)
Async XLA Ops:
  0.0 10.1 %collective-permute-start.2 = (bf16[1,2,48,384]{3,2,1,0:T(8,128)(2,1)}, bf16[1,2,48,384]{3,2,1,0:T(8,128)(2,1)S(1)}, u32[]{:S(2)}, u32[]{:S(2)}) collective-permute-start(bf16[1,2,48,384]{3,2,1,0:T(8,128)(2,1)} %own_ref.1), channel_id=1, source_target_pairs={{0,3},{1,2},{2,1},{3,0},{4,7},{5,6},{6,5},{7,4},{8,11},{9,10},{10,... | collective-permute-start | bytes 221192 | tf_op jit(solution)/shard_map/ppermute | solution.py:530
  5.0 6.4 %collective-permute-start.1 = (bf16[1,2,48,384]{3,2,1,0:T(8,128)(2,1)}, bf16[1,2,48,384]{3,2,1,0:T(8,128)(2,1)S(1)}, u32[]{:S(2)}, u32[]{:S(2)}) collective-permute-start(bf16[1,2,48,384]{3,2,1,0:T(8,128)(2,1)} %own_ref.1), channel_id=1, source_target_pairs={{0,2},{1,3},{2,0},{3,1},{4,6},{5,7},{6,4},{7,5},{8,10},{9,11},{10,... | collective-permute-start | bytes 221192 | tf_op jit(solution)/shard_map/ppermute | solution.py:530
  5.1 6.4 %collective-permute-start = (bf16[1,2,48,384]{3,2,1,0:T(8,128)(2,1)}, bf16[1,2,48,384]{3,2,1,0:T(8,128)(2,1)S(1)}, u32[]{:S(2)}, u32[]{:S(2)}) collective-permute-start(bf16[1,2,48,384]{3,2,1,0:T(8,128)(2,1)} %own_ref.1), channel_id=1, source_target_pairs={{0,1},{1,0},{2,3},{3,2},{4,5},{5,4},{6,7},{7,6},{8,9},{9,8},{10,11... | collective-permute-start | bytes 221192 | tf_op jit(solution)/shard_map/ppermute | solution.py:530
  5.6 5.9 %collective-permute-start.3 = (bf16[1,2,48,384]{3,2,1,0:T(8,128)(2,1)}, bf16[1,2,48,384]{3,2,1,0:T(8,128)(2,1)S(1)}, u32[]{:S(2)}, u32[]{:S(2)}) collective-permute-start(bf16[1,2,48,384]{3,2,1,0:T(8,128)(2,1)} %own_ref.1), channel_id=1, source_target_pairs={{0,8},{4,12},{8,0},{12,4},{1,9},{5,13},{9,1},{13,5},{2,10},{6,14},... | collective-permute-start | bytes 221192 | tf_op jit(solution)/shard_map/ppermute | solution.py:530
  8.3 1.6 %copy-start = (bf16[96,3,3,3,384]{4,0,3,2,1:T(8,128)(2,1)S(1)}, bf16[96,3,3,3,384]{4,0,3,2,1:T(8,128)(2,1)}, u32[]{:S(2)}) copy-start(bf16[96,3,3,3,384]{4,0,3,2,1:T(8,128)(2,1)} %param.18) | copy-start | bytes 5971972
  9.8 1.6 %copy-start.6 = (bf16[1,2,48,384]{3,2,1,0:T(8,128)(2,1)S(1)}, bf16[1,2,48,384]{3,2,1,0:T(8,128)(2,1)}, u32[]{:S(2)}) copy-start(bf16[1,2,48,384]{3,2,1,0:T(8,128)(2,1)} %own_ref.1) | copy-start | bytes 221188
  12.2 1.6 %collective-permute-start.4 = (bf16[1,8,48,384]{3,2,1,0:T(8,128)(2,1)S(1)}, bf16[1,8,48,384]{3,2,1,0:T(8,128)(2,1)S(1)}, u32[]{:S(2)}, u32[]{:S(2)}) collective-permute-start(bf16[1,8,48,384]{3,2,1,0:T(8,128)(2,1)S(1)} %get-tuple-element.13.own_ref), channel_id=1, source_target_pairs={{0,4},{4,0},{8,12},{12,8},{1,5},{5,1},{9,13},{13,9},{2,6},{6,2},{1... | collective-permute-start | bytes 884744 | tf_op jit(solution)/shard_map/ppermute | solution.py:530
  12.2 7.8 %collective-permute-start.5 = (bf16[3,2,48,384]{3,2,1,0:T(8,128)(2,1)S(1)}, bf16[3,2,48,384]{3,2,1,0:T(8,128)(2,1)S(1)}, u32[]{:S(2)}, u32[]{:S(2)}) collective-permute-start(bf16[3,2,48,384]{3,2,1,0:T(8,128)(2,1)S(1)} %get-tuple-element.14), channel_id=1, source_target_pairs={{0,8},{4,12},{8,0},{12,4},{1,9},{5,13},{9,1},{13,5},{2,10},{6,14},... | collective-permute-start | bytes 663560 | tf_op jit(solution)/shard_map/ppermute | solution.py:530
  20.8 1.7 %copy-start.7 = (f32[96]{0:T(128)S(1)}, f32[96]{0:T(128)}, u32[]{:S(2)}) copy-start(f32[96]{0:T(128)} %bias_ref.5) | copy-start | bytes 1156
  20.8 1.6 %collective-permute-start.6 = (bf16[1,8,48,384]{3,2,1,0:T(8,128)(2,1)S(1)}, bf16[1,8,48,384]{3,2,1,0:T(8,128)(2,1)S(1)}, u32[]{:S(2)}, u32[]{:S(2)}) collective-permute-start(bf16[1,8,48,384]{3,2,1,0:T(8,128)(2,1)S(1)} %shard_map.149.a_ref), channel_id=1, source_target_pairs={{0,4},{4,0},{8,12},{12,8},{1,5},{5,1},{9,13},{13,9},{2,6},{6,2},{1... | collective-permute-start | bytes 884744 | tf_op jit(solution)/shard_map/ppermute | solution.py:530
  23.2 4.9 %copy-start.1 = (bf16[96,3,3,3,384]{4,0,3,2,1:T(8,128)(2,1)S(1)}, bf16[96,3,3,3,384]{4,0,3,2,1:T(8,128)(2,1)}, u32[]{:S(2)}) copy-start(bf16[96,3,3,3,384]{4,0,3,2,1:T(8,128)(2,1)} %param.22) | copy-start | bytes 5971972
  23.3 5.1 %collective-permute-start.7 = (bf16[2,6,48,128]{3,2,1,0:T(8,128)(2,1)S(1)}, bf16[2,6,48,128]{3,2,1,0:T(8,128)(2,1)S(1)}, u32[]{:S(2)}, u32[]{:S(2)}) collective-permute-start(bf16[2,6,48,128]{3,2,1,0:T(8,128)(2,1)S(1)} %shard_map.151.refs_0_.own_ref.after_ref), channel_id=1, source_target_pairs={{0,4},{4,0},{8,12},{12,8},{1,5},{5,1},{9,13},{13,9},{2,6},{6,2},{1... | collective-permute-start | bytes 442376 | tf_op jit(solution)/shard_map/ppermute | solution.py:530
  23.5 7.0 %collective-permute-start.9 = (bf16[2,6,48,128]{3,2,1,0:T(8,128)(2,1)S(1)}, bf16[2,6,48,128]{3,2,1,0:T(8,128)(2,1)S(1)}, u32[]{:S(2)}, u32[]{:S(2)}) collective-permute-start(bf16[2,6,48,128]{3,2,1,0:T(8,128)(2,1)S(1)} %shard_map.151.refs_0_.own_ref.after_ref), channel_id=1, source_target_pairs={{0,8},{4,12},{8,0},{12,4},{1,9},{5,13},{9,1},{13,5},{2,10},{6,14},... | collective-permute-start | bytes 442376 | tf_op jit(solution)/shard_map/ppermute | solution.py:530
  27.8 5.9 %collective-permute-start.11 = (bf16[2,6,48,128]{3,2,1,0:T(8,128)(2,1)S(1)}, bf16[2,6,48,128]{3,2,1,0:T(8,128)(2,1)S(1)}, u32[]{:S(2)}, u32[]{:S(2)}) collective-permute-start(bf16[2,6,48,128]{3,2,1,0:T(8,128)(2,1)S(1)} %shard_map.154.own_ref), channel_id=1, source_target_pairs={{0,8},{4,12},{8,0},{12,4},{1,9},{5,13},{9,1},{13,5},{2,10},{6,14},... | collective-permute-start | bytes 442376 | tf_op jit(solution)/shard_map/ppermute | solution.py:530
  28.1 2.6 %collective-permute-start.8 = (bf16[2,6,48,128]{3,2,1,0:T(8,128)(2,1)S(1)}, bf16[2,6,48,128]{3,2,1,0:T(8,128)(2,1)S(1)}, u32[]{:S(2)}, u32[]{:S(2)}) collective-permute-start(bf16[2,6,48,128]{3,2,1,0:T(8,128)(2,1)S(1)} %shard_map.154.own_ref), channel_id=1, source_target_pairs={{0,4},{4,0},{8,12},{12,8},{1,5},{5,1},{9,13},{13,9},{2,6},{6,2},{1... | collective-permute-start | bytes 442376 | tf_op jit(solution)/shard_map/ppermute | solution.py:530
  30.4 3.4 %collective-permute-start.10 = (bf16[2,6,48,128]{3,2,1,0:T(8,128)(2,1)S(1)}, bf16[2,6,48,128]{3,2,1,0:T(8,128)(2,1)S(1)}, u32[]{:S(2)}, u32[]{:S(2)}) collective-permute-start(bf16[2,6,48,128]{3,2,1,0:T(8,128)(2,1)S(1)} %shard_map.156.own_ref), channel_id=1, source_target_pairs={{0,4},{4,0},{8,12},{12,8},{1,5},{5,1},{9,13},{13,9},{2,6},{6,2},{1... | collective-permute-start | bytes 442376 | tf_op jit(solution)/shard_map/ppermute | solution.py:530
  33.7 1.9 %copy-start.8 = (f32[96]{0:T(128)S(1)}, f32[96]{0:T(128)}, u32[]{:S(2)}) copy-start(f32[96]{0:T(128)} %bias_ref.7) | copy-start | bytes 1156
  33.7 1.9 %collective-permute-start.12 = (bf16[2,6,48,128]{3,2,1,0:T(8,128)(2,1)S(1)}, bf16[2,6,48,128]{3,2,1,0:T(8,128)(2,1)S(1)}, u32[]{:S(2)}, u32[]{:S(2)}) collective-permute-start(bf16[2,6,48,128]{3,2,1,0:T(8,128)(2,1)S(1)} %shard_map.158.own_ref), channel_id=1, source_target_pairs={{0,4},{4,0},{8,12},{12,8},{1,5},{5,1},{9,13},{13,9},{2,6},{6,2},{1... | collective-permute-start | bytes 442376 | tf_op jit(solution)/shard_map/ppermute | solution.py:530
  36.8 4.0 %collective-permute-start.15 = (bf16[288,128]{1,0:T(8,128)(2,1)S(1)}, bf16[288,128]{1,0:T(8,128)(2,1)S(1)}, u32[]{:S(2)}, u32[]{:S(2)}) collective-permute-start(bf16[288,128]{1,0:T(8,128)(2,1)S(1)} %get-tuple-element.18), channel_id=1, source_target_pairs={{0,12},{4,8},{8,4},{12,0},{1,13},{5,9},{9,5},{13,1},{2,14},{6,10},... | collective-permute-start | bytes 221192 | tf_op jit(solution)/shard_map/ppermute | solution.py:530
  37.6 5.4 %collective-permute-start.14 = (bf16[288,128]{1,0:T(8,128)(2,1)S(1)}, bf16[288,128]{1,0:T(8,128)(2,1)S(1)}, u32[]{:S(2)}, u32[]{:S(2)}) collective-permute-start(bf16[288,128]{1,0:T(8,128)(2,1)S(1)} %get-tuple-element.15.refs_0_), channel_id=1, source_target_pairs={{0,8},{4,12},{8,0},{12,4},{1,9},{5,13},{9,1},{13,5},{2,10},{6,14},... | collective-permute-start | bytes 221192 | tf_op jit(solution)/shard_map/ppermute | solution.py:530
  39.4 3.6 %copy-start.2 = (bf16[384,384]{1,0:T(8,128)(2,1)S(1)}, bf16[384,384]{1,0:T(8,128)(2,1)}, u32[]{:S(2)}) copy-start(bf16[384,384]{1,0:T(8,128)(2,1)} %wq_ref.1) | copy-start | bytes 884740
  39.4 3.6 %copy-start.3 = (bf16[384,384]{1,0:T(8,128)(2,1)S(1)}, bf16[384,384]{1,0:T(8,128)(2,1)}, u32[]{:S(2)}) copy-start(bf16[384,384]{1,0:T(8,128)(2,1)} %wk_ref.1) | copy-start | bytes 884740
  39.4 3.6 %copy-start.4 = (bf16[384,384]{1,0:T(8,128)(2,1)S(1)}, bf16[384,384]{1,0:T(8,128)(2,1)}, u32[]{:S(2)}) copy-start(bf16[384,384]{1,0:T(8,128)(2,1)} %wv_ref.1) | copy-start | bytes 884740
  39.4 3.6 %copy-start.5 = (bf16[384,384]{1,0:T(8,128)(2,1)S(1)}, bf16[384,384]{1,0:T(8,128)(2,1)}, u32[]{:S(2)}) copy-start(bf16[384,384]{1,0:T(8,128)(2,1)} %wo_ref.1) | copy-start | bytes 884740
  39.4 3.6 %collective-permute-start.13 = (bf16[288,128]{1,0:T(8,128)(2,1)S(1)}, bf16[288,128]{1,0:T(8,128)(2,1)S(1)}, u32[]{:S(2)}, u32[]{:S(2)}) collective-permute-start(bf16[288,128]{1,0:T(8,128)(2,1)S(1)} %get-tuple-element.17), channel_id=1, source_target_pairs={{0,4},{4,0},{8,12},{12,8},{1,5},{5,1},{9,13},{13,9},{2,6},{6,2},{1... | collective-permute-start | bytes 221192 | tf_op jit(solution)/shard_map/ppermute | solution.py:530

commit v11 on v10

--- a/solution.py
+++ b/solution.py
@@ -386,56 +386,56 @@
     return jnp.concatenate([part_ref[g, row][:, part:] for g in range(frames - 1)], axis=1)
 
 
-def half_channels(h, parts, a_ref):
+def half_channels(h, odd, own_ref, mate_ref, a_ref):
     frames, padded, cols, lanes = a_ref.shape
     fill = jnp.zeros((cols, lanes - 192), BF16)
     for f in range(frames):
         a_ref[f, 0] = jnp.zeros((cols, lanes), BF16)
         a_ref[f, padded - 1] = jnp.zeros((cols, lanes), BF16)
-        for row in range(padded - 2):
-            q, i = divmod(row, 4)
-            pieces = []
-            for part in parts:
-                if i < 3:
-                    pieces.append(part[f, 3 * q + i][:, 0:96])
-                else:
-                    pieces += [part[f, 3 * q + g][:, 96:] for g in range(3)]
-            a_ref[f, row + 1] = jnp.concatenate([fill] + pieces if h else pieces + [fill], axis=1)
+        for q in range((padded - 2) // 4):
+            planes = [(own_ref[f, 3 * q + g], mate_ref[f, 3 * q + g]) for g in range(3)]
+            parts = [
+                [jnp.where(odd == place, own, mate) for own, mate in planes] for place in (0, 1)
+            ]
+            for i in range(4):
+                pieces = []
+                for part in parts:
+                    pieces += [part[i][:, 0:96]] if i < 3 else [plane[:, 96:] for plane in part]
+                a_ref[f, 4 * q + i + 1] = jnp.concatenate([fill] + pieces if h else pieces + [fill], axis=1)
 
 
 def half_lanes(h, lanes, channels):
     return slice(channels - lanes, channels) if h else slice(0, lanes)
 
 
-def half_taps(m_ref, other, own_ref, mate_ref, held, base_ref, w_ref, total_ref, both, a_ref, first=lambda h: 0):
+def half_taps(m_ref, other, own_ref, mate_ref, held, base_ref, w_ref, total_ref, a_ref, first=lambda h: 0):
     odd = m_ref[0] & 1
-    both[odd] = own_ref[...]
-    both[1 - odd] = mate_ref[...]
     lanes, channels = a_ref.shape[3], w_ref.shape[3]
 
     def body(h):
-        half_channels(h, (both.at[0], both.at[1]), a_ref)
+        if first(h) + total_ref.shape[0] > held[0]:
+            half_channels(h, odd, own_ref, mate_ref, a_ref)
         frame_taps(total_ref, base_ref, a_ref, held, w_ref, half_lanes(h, lanes, channels), first=first(h))
 
     on_half(m_ref, other, body)
 
 
-def second_conv_near_early(m_ref, own_ref, mate_ref, w_ref, total_ref, both, a_ref):
-    half_taps(m_ref, False, own_ref, mate_ref, (0, 1), None, w_ref, total_ref, both, a_ref)
-
-
-def second_conv_near_late(m_ref, base_ref, own_ref, mate_ref, w_ref, total_ref, both, a_ref):
-    half_taps(m_ref, False, own_ref, mate_ref, (2, 3), base_ref, w_ref, total_ref, both, a_ref)
-
-
-def second_conv_early(m_ref, base_ref, own_ref, mate_ref, w_ref, total_ref, both, a_ref):
-    half_taps(m_ref, True, own_ref, mate_ref, (0, 1), base_ref, w_ref, total_ref, both, a_ref)
+def second_conv_near_early(m_ref, own_ref, mate_ref, w_ref, total_ref, a_ref):
+    half_taps(m_ref, False, own_ref, mate_ref, (0, 1), None, w_ref, total_ref, a_ref)
+
+
+def second_conv_near_late(m_ref, base_ref, own_ref, mate_ref, w_ref, total_ref, a_ref):
+    half_taps(m_ref, False, own_ref, mate_ref, (2, 3), base_ref, w_ref, total_ref, a_ref)
+
+
+def second_conv_early(m_ref, base_ref, own_ref, mate_ref, w_ref, total_ref, a_ref):
+    half_taps(m_ref, True, own_ref, mate_ref, (0, 1), base_ref, w_ref, total_ref, a_ref)
 
 
 def second_conv_late(own, m_ref, base_ref, own_ref, mate_ref, w_ref, bias_ref, *refs):
-    one_ref, other_ref, both, a_ref, total, done = refs[-6:]
+    one_ref, other_ref, a_ref, total, done = refs[-5:]
     half_taps(
-        m_ref, True, own_ref, mate_ref, (2, 3), base_ref, w_ref, total, both, a_ref,
+        m_ref, True, own_ref, mate_ref, (2, 3), base_ref, w_ref, total, a_ref,
         first=lambda h: 2 * (1 - h) if own else 2 * h,
     )
     for t in range(2):
@@ -623,21 +623,21 @@
         early_mate, late_mate = over_core(early), over_core(late)
         early_across, late_across = over_x(early), over_x(late)
         weights2 = call(load, loaded)(taps(second_kernel), early)
-        both, two_frames = pltpu.VMEM((2, *packed.shape), BF16), pltpu.VMEM((2, height + 2, cols, 256), BF16)
-        near_early = call(second_conv_near_early, tall, (both, two_frames))(m, early, early_mate, weights2)
+        two_frames = pltpu.VMEM((2, height + 2, cols, 256), BF16)
+        near_early = call(second_conv_near_early, tall, (two_frames,))(m, early, early_mate, weights2)
         long = pl.CostEstimate(flops=10**10, bytes_accessed=4 * 10**7, transcendentals=0)
         early_across = call(hand_on, packed, cost=long)(early_across, near_early)
         early_beside = over_core(early_across)
-        near_total = call(second_conv_near_late, tall, (both, two_frames))(
+        near_total = call(second_conv_near_late, tall, (two_frames,))(
             m, near_early, late, late_mate, weights2
         )
         late_across = held_until(late_across, near_total)
         late_beside = over_core(late_across)
-        early_total = call(second_conv_early, tall, (both, two_frames))(
+        early_total = call(second_conv_early, tall, (two_frames,))(
             m, near_total, early_across, early_beside, weights2
         )
         piece = struct((3 * plane, 128))
-        scratch = (both, two_frames, pltpu.VMEM((2, n * plane, 3 * lanes), F32), pltpu.VMEM((2, n * plane, outputs), BF16))
+        scratch = (two_frames, pltpu.VMEM((2, n * plane, 3 * lanes), F32), pltpu.VMEM((2, n * plane, outputs), BF16))
         across, cross = call(functools.partial(second_conv_late, False), (piece, piece), scratch)(
             m, early_total, late_across, late_beside, weights2, second_bias
         )

time: 45.5 us -> 45.5 us (level)
  no operation moved by 1% of the time
where the time goes in v11:
time: 45.5 us; the launch traced here: 45.3 us
  Pallas kernels  16.4 us (36%)
  starting transfers between devices  14.9 us (33%)
  waiting for transfers between devices  11.2 us (25%)
  local copies, waits for them, and re-layouts  1.6 us (4%)
  other arithmetic  0.86 us (2%)
    pallas_call x18, Pallas kernels, run(): pl.pallas_call(functools.partial(body, *axes), out_shape=outs, in_specs=[...  16.4 us
    ppermute x16, starting transfers between devices, swapped(): lax.ppermute(value, axis, [(i, partner(i)) for i in range(lax.axis_size(a...  14.9 us
    ppermute x16, waiting for transfers between devices, swapped(): lax.ppermute(value, axis, [(i, partner(i)) for i in range(lax.axis_size(a...  11.2 us
    unnamed x18, local copies, waits for them, and re-layouts  1.6 us
  transfers between devices with their start and end apart: 16, of which 7 were waited for; matrix products, arithmetic and copies ran while one was open for 2% of the time, Pallas kernels for 24%

profile of v11, /device:TPU:0, one launch (start us, length us, event | category | flops | bytes accessed | tf_op | source)
XLA Modules:
  0.0 45.3 jit_solution(3742333136002853389)
XLA Ops:
  0.0 5.0 %collective-permute-start.2 = (bf16[1,2,48,384]{3,2,1,0:T(8,128)(2,1)}, bf16[1,2,48,384]{3,2,1,0:T(8,128)(2,1)S(1)}, u32[]{:S(2)}, u32[]{:S(2)}) collective-permute-start(bf16[1,2,48,384]{3,2,1,0:T(8,128)(2,1)} %own_ref.1), channel_id=1, source_target_pairs={{0,3},{1,2},{2,1},{3,0},{4,7},{5,6},{6,5},{7,4},{8,11},{9,10},{10,... | collective-permute-start | bytes 221192 | tf_op jit(solution)/shard_map/ppermute | solution.py:530
  5.1 0.6 %collective-permute-start = (bf16[1,2,48,384]{3,2,1,0:T(8,128)(2,1)}, bf16[1,2,48,384]{3,2,1,0:T(8,128)(2,1)S(1)}, u32[]{:S(2)}, u32[]{:S(2)}) collective-permute-start(bf16[1,2,48,384]{3,2,1,0:T(8,128)(2,1)} %own_ref.1), channel_id=1, source_target_pairs={{0,1},{1,0},{2,3},{3,2},{4,5},{5,4},{6,7},{7,6},{8,9},{9,8},{10,11... | collective-permute-start | bytes 221192 | tf_op jit(solution)/shard_map/ppermute | solution.py:530
  5.6 1.7 %collective-permute-start.3 = (bf16[1,2,48,384]{3,2,1,0:T(8,128)(2,1)}, bf16[1,2,48,384]{3,2,1,0:T(8,128)(2,1)S(1)}, u32[]{:S(2)}, u32[]{:S(2)}) collective-permute-start(bf16[1,2,48,384]{3,2,1,0:T(8,128)(2,1)} %own_ref.1), channel_id=1, source_target_pairs={{0,8},{4,12},{8,0},{12,4},{1,9},{5,13},{9,1},{13,5},{2,10},{6,14},... | collective-permute-start | bytes 221192 | tf_op jit(solution)/shard_map/ppermute | solution.py:530
  7.4 0.8 %select_select_fusion.table_ref = f32[8,384]{1,0:T(8,128)S(1)} fusion(f32[384]{0:T(512)} %param.16, f32[384]{0:T(512)} %param.17, f32[384]{0:T(512)} %param.20, f32[384]{0:T(512)} %param.21, f32[384]{0:T(512)} %param.24, f32[384]{0:T(512)} %param.25, pred[8]{0:T(512)(128)(4,1)S(1)} %get-tuple-element.19, pred[8]{0:T(512)(128)(4,1)S(1)} %get-tuple-element.20, ...), kind=kLoop, calls=%fused_computation | loop fusion | flops 18432 | bytes 21552 | tf_op jit(solution)/shard_map/jit(_where)/select_n | solution.py:571
  8.2 0.1 shard_map.146.groups_ref
  8.3 0.0 copy-start
  8.3 1.5 %copy-done = bf16[96,3,3,3,384]{4,0,3,2,1:T(8,128)(2,1)S(1)} copy-done((bf16[96,3,3,3,384]{4,0,3,2,1:T(8,128)(2,1)S(1)}, bf16[96,3,3,3,384]{4,0,3,2,1:T(8,128)(2,1)}, u32[]{:S(2)}) %copy-start) | copy-done | bytes 1990680
  9.8 0.2 shard_map.145.loaded_ref.w_ref
  10.1 1.4 %collective-permute-done.1.two_ref = bf16[1,2,48,384]{3,2,1,0:T(8,128)(2,1)S(1)} collective-permute-done((bf16[1,2,48,384]{3,2,1,0:T(8,128)(2,1)}, bf16[1,2,48,384]{3,2,1,0:T(8,128)(2,1)S(1)}, u32[]{:S(2)}, u32[]{:S(2)}) %collective-permute-start.1) | collective-permute-done | bytes 73760 | tf_op jit(solution)/shard_map/ppermute | solution.py:530
  11.5 0.7 %shard_map.147 = (bf16[1,8,48,384]{3,2,1,0:T(8,128)(2,1)S(1)}, bf16[8,48,384]{2,1,0:T(8,128)(2,1)S(1)}, bf16[3,2,48,384]{3,2,1,0:T(8,128)(2,1)S(1)}) custom-call(bf16[1,2,48,384]{3,2,1,0:T(8,128)(2,1)S(1)} %copy-done.6, bf16[1,2,48,384]{3,2,1,0:T(8,128)(2,1)S(1)} %collective-permute-done.one_ref, bf16[1,2,48,384]{3,2,1,0:T(8,128)(2,1)S(1)} %collective-permute-done.1.two_ref, ...), custom_call_target="tpu_custom_call" | custom-call | tf_op jit(solution)/shard_map/pallas_call | solution.py:31
  12.2 0.1 collective-permute-start.4
  12.2 1.6 %collective-permute-start.5 = (bf16[3,2,48,384]{3,2,1,0:T(8,128)(2,1)S(1)}, bf16[3,2,48,384]{3,2,1,0:T(8,128)(2,1)S(1)}, u32[]{:S(2)}, u32[]{:S(2)}) collective-permute-start(bf16[3,2,48,384]{3,2,1,0:T(8,128)(2,1)S(1)} %get-tuple-element.14), channel_id=1, source_target_pairs={{0,8},{4,12},{8,0},{12,4},{1,9},{5,13},{9,1},{13,5},{2,10},{6,14},... | collective-permute-start | bytes 663560 | tf_op jit(solution)/shard_map/ppermute | solution.py:530
  13.8 0.0 collective-permute-done.4.mate_ref
  13.8 2.8 %shard_map.148.after_ref.near_total_ref = f32[4,384,384]{2,1,0:T(8,128)S(1)} custom-call(bf16[1,8,48,384]{3,2,1,0:T(8,128)(2,1)S(1)} %get-tuple-element.13.own_ref, bf16[1,8,48,384]{3,2,1,0:T(8,128)(2,1)S(1)} %collective-permute-done.4.mate_ref, bf16[3,3,384,384]{3,2,1,0:T(8,128)(2,1)S(1)} %shard_map.145.loaded_ref.w_ref), custom_call_target="tpu_custom_call" | custom-call | tf_op jit(solution)/shard_map/pallas_call | solution.py:31
  16.6 3.5 %collective-permute-done.5.blocks_ref = bf16[3,2,48,384]{3,2,1,0:T(8,128)(2,1)S(1)} collective-permute-done((bf16[3,2,48,384]{3,2,1,0:T(8,128)(2,1)S(1)}, bf16[3,2,48,384]{3,2,1,0:T(8,128)(2,1)S(1)}, u32[]{:S(2)}, u32[]{:S(2)}) %collective-permute-start.5) | collective-permute-done | bytes 221216 | tf_op jit(solution)/shard_map/ppermute | solution.py:530
  20.1 0.7 %shard_map.149.a_ref = bf16[1,8,48,384]{3,2,1,0:T(8,128)(2,1)S(1)} custom-call(bf16[1,2,48,384]{3,2,1,0:T(8,128)(2,1)S(1)} %collective-permute-done.3.across_ref.own_ref, bf16[3,2,48,384]{3,2,1,0:T(8,128)(2,1)S(1)} %collective-permute-done.5.blocks_ref, f32[8,384]{1,0:T(8,128)S(1)} %select_select_fusion.table_ref, ...), custom_call_target="tpu_custom_call" | custom-call | tf_op jit(solution)/shard_map/pallas_call | solution.py:31
  20.8 0.0 copy-start.7
  20.8 0.1 collective-permute-start.6
  20.8 1.1 %shard_map.150.base_ref = f32[4,384,384]{2,1,0:T(8,128)S(1)} custom-call(f32[4,384,384]{2,1,0:T(8,128)S(1)} %shard_map.148.after_ref.near_total_ref, bf16[1,8,48,384]{3,2,1,0:T(8,128)(2,1)S(1)} %shard_map.149.a_ref, bf16[3,3,384,384]{3,2,1,0:T(8,128)(2,1)S(1)} %shard_map.145.loaded_ref.w_ref), custom_call_target="tpu_custom_call" | custom-call | tf_op jit(solution)/shard_map/pallas_call | solution.py:31
  21.9 0.5 %collective-permute-done.6.a_ref = bf16[1,8,48,384]{3,2,1,0:T(8,128)(2,1)S(1)} collective-permute-done((bf16[1,8,48,384]{3,2,1,0:T(8,128)(2,1)S(1)}, bf16[1,8,48,384]{3,2,1,0:T(8,128)(2,1)S(1)}, u32[]{:S(2)}, u32[]{:S(2)}) %collective-permute-start.6) | collective-permute-done | bytes 294944 | tf_op jit(solution)/shard_map/ppermute | solution.py:530
  22.4 0.8 %shard_map.151.refs_0_.own_ref.after_ref = bf16[2,6,48,128]{3,2,1,0:T(8,128)(2,1)S(1)} custom-call(f32[4,384,384]{2,1,0:T(8,128)S(1)} %shard_map.150.base_ref, bf16[1,8,48,384]{3,2,1,0:T(8,128)(2,1)S(1)} %collective-permute-done.6.a_ref, bf16[3,3,384,384]{3,2,1,0:T(8,128)(2,1)S(1)} %shard_map.145.loaded_ref.w_ref, f32[96]{0:T(128)S(1)} %copy-done.7, ...), custom_call_target="tpu_custom_call" | custom-call | tf_op jit(solution)/shard_map/pallas_call | solution.py:31
  23.2 0.0 copy-start.1
  23.3 0.2 collective-permute-start.7
  23.5 2.7 %collective-permute-start.9 = (bf16[2,6,48,128]{3,2,1,0:T(8,128)(2,1)S(1)}, bf16[2,6,48,128]{3,2,1,0:T(8,128)(2,1)S(1)}, u32[]{:S(2)}, u32[]{:S(2)}) collective-permute-start(bf16[2,6,48,128]{3,2,1,0:T(8,128)(2,1)S(1)} %shard_map.151.refs_0_.own_ref.after_ref), channel_id=1, source_target_pairs={{0,8},{4,12},{8,0},{12,4},{1,9},{5,13},{9,1},{13,5},{2,10},{6,14},... | collective-permute-start | bytes 442376 | tf_op jit(solution)/shard_map/ppermute | solution.py:530
  26.2 1.6 %shard_map.154.own_ref = bf16[2,6,48,128]{3,2,1,0:T(8,128)(2,1)S(1)} custom-call(f32[4,384,384]{2,1,0:T(8,128)S(1)} %shard_map.150.base_ref, bf16[1,8,48,384]{3,2,1,0:T(8,128)(2,1)S(1)} %collective-permute-done.6.a_ref, bf16[3,3,384,384]{3,2,1,0:T(8,128)(2,1)S(1)} %shard_map.145.loaded_ref.w_ref, f32[96]{0:T(128)S(1)} %copy-done.7, ...), custom_call_target="tpu_custom_call" | custom-call | tf_op jit(solution)/shard_map/pallas_call | solution.py:31
  27.8 0.3 collective-permute-start.11
  28.1 0.0 collective-permute-start.8
  28.2 0.2 shard_map.152.w_ref
  28.4 1.7 %shard_map.153.base_ref.after_ref = f32[4,384,384]{2,1,0:T(8,128)S(1)} custom-call(bf16[2,6,48,128]{3,2,1,0:T(8,128)(2,1)S(1)} %shard_map.151.refs_0_.own_ref.after_ref, bf16[2,6,48,128]{3,2,1,0:T(8,128)(2,1)S(1)} %collective-permute-done.7.mate_ref, bf16[3,3,384,384]{3,2,1,0:T(8,128)(2,1)S(1)} %shard_map.152.w_ref), custom_call_target="tpu_custom_call" | custom-call | tf_op jit(solution)/shard_map/pallas_call | solution.py:31
  30.1 0.3 collective-permute-done.9.x_ref
  30.4 0.3 collective-permute-start.10
  30.7 1.1 %shard_map.155.base_ref.after_ref = f32[4,384,384]{2,1,0:T(8,128)S(1)} custom-call(f32[4,384,384]{2,1,0:T(8,128)S(1)} %shard_map.153.base_ref.after_ref, bf16[2,6,48,128]{3,2,1,0:T(8,128)(2,1)S(1)} %shard_map.154.own_ref, bf16[2,6,48,128]{3,2,1,0:T(8,128)(2,1)S(1)} %collective-permute-done.8.mate_ref, bf16[3,3,384,384]{3,2,1,0:T(8,128)(2,1)S(1)} %shard_map.152.w_ref), custom_call_target="tpu_custom_call" | custom-call | tf_op jit(solution)/shard_map/pallas_call | solution.py:31
  31.8 1.9 %collective-permute-done.11.x_ref = bf16[2,6,48,128]{3,2,1,0:T(8,128)(2,1)S(1)} collective-permute-done((bf16[2,6,48,128]{3,2,1,0:T(8,128)(2,1)S(1)}, bf16[2,6,48,128]{3,2,1,0:T(8,128)(2,1)S(1)}, u32[]{:S(2)}, u32[]{:S(2)}) %collective-permute-start.11) | collective-permute-done | bytes 147488 | tf_op jit(solution)/shard_map/ppermute | solution.py:530
  33.7 0.0 copy-start.8
  33.7 0.1 collective-permute-start.12
  33.8 1.8 %shard_map.157.base_ref = f32[4,384,384]{2,1,0:T(8,128)S(1)} custom-call(f32[4,384,384]{2,1,0:T(8,128)S(1)} %shard_map.155.base_ref.after_ref, bf16[2,6,48,128]{3,2,1,0:T(8,128)(2,1)S(1)} %shard_map.156.own_ref, bf16[2,6,48,128]{3,2,1,0:T(8,128)(2,1)S(1)} %collective-permute-done.10.mate_ref, bf16[3,3,384,384]{3,2,1,0:T(8,128)(2,1)S(1)} %shard_map.152.w_ref), custom_call_target="tpu_custom_call" | custom-call | tf_op jit(solution)/shard_map/pallas_call | solution.py:31
  35.6 1.2 %shard_map.159 = (bf16[288,128]{1,0:T(8,128)(2,1)S(1)}, bf16[288,128]{1,0:T(8,128)(2,1)S(1)}) custom-call(f32[4,384,384]{2,1,0:T(8,128)S(1)} %shard_map.157.base_ref, bf16[2,6,48,128]{3,2,1,0:T(8,128)(2,1)S(1)} %shard_map.158.own_ref, bf16[2,6,48,128]{3,2,1,0:T(8,128)(2,1)S(1)} %collective-permute-done.12.mate_ref, ...), custom_call_target="tpu_custom_call" | custom-call | tf_op jit(solution)/shard_map/pallas_call | solution.py:31
  36.8 0.7 %collective-permute-start.15 = (bf16[288,128]{1,0:T(8,128)(2,1)S(1)}, bf16[288,128]{1,0:T(8,128)(2,1)S(1)}, u32[]{:S(2)}, u32[]{:S(2)}) collective-permute-start(bf16[288,128]{1,0:T(8,128)(2,1)S(1)} %get-tuple-element.18), channel_id=1, source_target_pairs={{0,12},{4,8},{8,4},{12,0},{1,13},{5,9},{9,5},{13,1},{2,14},{6,10},... | collective-permute-start | bytes 221192 | tf_op jit(solution)/shard_map/ppermute | solution.py:530
  37.5 1.5 %collective-permute-start.14 = (bf16[288,128]{1,0:T(8,128)(2,1)S(1)}, bf16[288,128]{1,0:T(8,128)(2,1)S(1)}, u32[]{:S(2)}, u32[]{:S(2)}) collective-permute-start(bf16[288,128]{1,0:T(8,128)(2,1)S(1)} %get-tuple-element.15.refs_0_), channel_id=1, source_target_pairs={{0,8},{4,12},{8,0},{12,4},{1,9},{5,13},{9,1},{13,5},{2,10},{6,14},... | collective-permute-start | bytes 221192 | tf_op jit(solution)/shard_map/ppermute | solution.py:530
  38.9 0.2 shard_map.160
  39.2 0.0 copy-start.2
  39.2 0.0 copy-start.3
  39.2 0.0 copy-start.4
  39.2 0.0 copy-start.5
  39.2 0.1 collective-permute-start.13
  39.3 1.5 %collective-permute-done.15.after_ref.p3 = bf16[288,128]{1,0:T(8,128)(2,1)S(1)} collective-permute-done((bf16[288,128]{1,0:T(8,128)(2,1)S(1)}, bf16[288,128]{1,0:T(8,128)(2,1)S(1)}, u32[]{:S(2)}, u32[]{:S(2)}) %collective-permute-start.15) | collective-permute-done | bytes 73760 | tf_op jit(solution)/shard_map/ppermute | solution.py:530
  40.8 2.2 %collective-permute-done.14.x_ref = bf16[288,128]{1,0:T(8,128)(2,1)S(1)} collective-permute-done((bf16[288,128]{1,0:T(8,128)(2,1)S(1)}, bf16[288,128]{1,0:T(8,128)(2,1)S(1)}, u32[]{:S(2)}, u32[]{:S(2)}) %collective-permute-start.14) | collective-permute-done | bytes 73760 | tf_op jit(solution)/shard_map/ppermute | solution.py:530
  43.0 2.3 %shard_map.162 = bf16[96,384]{1,0:T(8,128)(2,1)} custom-call(bf16[8,48,384]{2,1,0:T(8,128)(2,1)S(1)} %get-tuple-element.12.raw_ref, bf16[288,128]{1,0:T(8,128)(2,1)S(1)} %get-tuple-element.16.p0, bf16[288,128]{1,0:T(8,128)(2,1)S(1)} %collective-permute-done.13.p1, bf16[288,128]{1,0:T(8,128)(2,1)S(1)} %shard_map.161.p2, ...), custom_call_target="tpu_custom_call" | custom-call | tf_op jit(solution)/shard_map/pallas_call | solution.py:31
  (24 shorter events, 0.1 us)
Async XLA Ops:
  0.0 10.1 %collective-permute-start.2 = (bf16[1,2,48,384]{3,2,1,0:T(8,128)(2,1)}, bf16[1,2,48,384]{3,2,1,0:T(8,128)(2,1)S(1)}, u32[]{:S(2)}, u32[]{:S(2)}) collective-permute-start(bf16[1,2,48,384]{3,2,1,0:T(8,128)(2,1)} %own_ref.1), channel_id=1, source_target_pairs={{0,3},{1,2},{2,1},{3,0},{4,7},{5,6},{6,5},{7,4},{8,11},{9,10},{10,... | collective-permute-start | bytes 221192 | tf_op jit(solution)/shard_map/ppermute | solution.py:530
  5.0 6.4 %collective-permute-start.1 = (bf16[1,2,48,384]{3,2,1,0:T(8,128)(2,1)}, bf16[1,2,48,384]{3,2,1,0:T(8,128)(2,1)S(1)}, u32[]{:S(2)}, u32[]{:S(2)}) collective-permute-start(bf16[1,2,48,384]{3,2,1,0:T(8,128)(2,1)} %own_ref.1), channel_id=1, source_target_pairs={{0,2},{1,3},{2,0},{3,1},{4,6},{5,7},{6,4},{7,5},{8,10},{9,11},{10,... | collective-permute-start | bytes 221192 | tf_op jit(solution)/shard_map/ppermute | solution.py:530
  5.1 6.4 %collective-permute-start = (bf16[1,2,48,384]{3,2,1,0:T(8,128)(2,1)}, bf16[1,2,48,384]{3,2,1,0:T(8,128)(2,1)S(1)}, u32[]{:S(2)}, u32[]{:S(2)}) collective-permute-start(bf16[1,2,48,384]{3,2,1,0:T(8,128)(2,1)} %own_ref.1), channel_id=1, source_target_pairs={{0,1},{1,0},{2,3},{3,2},{4,5},{5,4},{6,7},{7,6},{8,9},{9,8},{10,11... | collective-permute-start | bytes 221192 | tf_op jit(solution)/shard_map/ppermute | solution.py:530
  5.6 5.9 %collective-permute-start.3 = (bf16[1,2,48,384]{3,2,1,0:T(8,128)(2,1)}, bf16[1,2,48,384]{3,2,1,0:T(8,128)(2,1)S(1)}, u32[]{:S(2)}, u32[]{:S(2)}) collective-permute-start(bf16[1,2,48,384]{3,2,1,0:T(8,128)(2,1)} %own_ref.1), channel_id=1, source_target_pairs={{0,8},{4,12},{8,0},{12,4},{1,9},{5,13},{9,1},{13,5},{2,10},{6,14},... | collective-permute-start | bytes 221192 | tf_op jit(solution)/shard_map/ppermute | solution.py:530
  8.3 1.6 %copy-start = (bf16[96,3,3,3,384]{4,0,3,2,1:T(8,128)(2,1)S(1)}, bf16[96,3,3,3,384]{4,0,3,2,1:T(8,128)(2,1)}, u32[]{:S(2)}) copy-start(bf16[96,3,3,3,384]{4,0,3,2,1:T(8,128)(2,1)} %param.18) | copy-start | bytes 5971972
  9.8 1.6 %copy-start.6 = (bf16[1,2,48,384]{3,2,1,0:T(8,128)(2,1)S(1)}, bf16[1,2,48,384]{3,2,1,0:T(8,128)(2,1)}, u32[]{:S(2)}) copy-start(bf16[1,2,48,384]{3,2,1,0:T(8,128)(2,1)} %own_ref.1) | copy-start | bytes 221188
  12.2 1.6 %collective-permute-start.4 = (bf16[1,8,48,384]{3,2,1,0:T(8,128)(2,1)S(1)}, bf16[1,8,48,384]{3,2,1,0:T(8,128)(2,1)S(1)}, u32[]{:S(2)}, u32[]{:S(2)}) collective-permute-start(bf16[1,8,48,384]{3,2,1,0:T(8,128)(2,1)S(1)} %get-tuple-element.13.own_ref), channel_id=1, source_target_pairs={{0,4},{4,0},{8,12},{12,8},{1,5},{5,1},{9,13},{13,9},{2,6},{6,2},{1... | collective-permute-start | bytes 884744 | tf_op jit(solution)/shard_map/ppermute | solution.py:530
  12.2 7.8 %collective-permute-start.5 = (bf16[3,2,48,384]{3,2,1,0:T(8,128)(2,1)S(1)}, bf16[3,2,48,384]{3,2,1,0:T(8,128)(2,1)S(1)}, u32[]{:S(2)}, u32[]{:S(2)}) collective-permute-start(bf16[3,2,48,384]{3,2,1,0:T(8,128)(2,1)S(1)} %get-tuple-element.14), channel_id=1, source_target_pairs={{0,8},{4,12},{8,0},{12,4},{1,9},{5,13},{9,1},{13,5},{2,10},{6,14},... | collective-permute-start | bytes 663560 | tf_op jit(solution)/shard_map/ppermute | solution.py:530
  20.8 1.7 %copy-start.7 = (f32[96]{0:T(128)S(1)}, f32[96]{0:T(128)}, u32[]{:S(2)}) copy-start(f32[96]{0:T(128)} %bias_ref.5) | copy-start | bytes 1156
  20.8 1.6 %collective-permute-start.6 = (bf16[1,8,48,384]{3,2,1,0:T(8,128)(2,1)S(1)}, bf16[1,8,48,384]{3,2,1,0:T(8,128)(2,1)S(1)}, u32[]{:S(2)}, u32[]{:S(2)}) collective-permute-start(bf16[1,8,48,384]{3,2,1,0:T(8,128)(2,1)S(1)} %shard_map.149.a_ref), channel_id=1, source_target_pairs={{0,4},{4,0},{8,12},{12,8},{1,5},{5,1},{9,13},{13,9},{2,6},{6,2},{1... | collective-permute-start | bytes 884744 | tf_op jit(solution)/shard_map/ppermute | solution.py:530
  23.2 4.9 %copy-start.1 = (bf16[96,3,3,3,384]{4,0,3,2,1:T(8,128)(2,1)S(1)}, bf16[96,3,3,3,384]{4,0,3,2,1:T(8,128)(2,1)}, u32[]{:S(2)}) copy-start(bf16[96,3,3,3,384]{4,0,3,2,1:T(8,128)(2,1)} %param.22) | copy-start | bytes 5971972
  23.3 5.1 %collective-permute-start.7 = (bf16[2,6,48,128]{3,2,1,0:T(8,128)(2,1)S(1)}, bf16[2,6,48,128]{3,2,1,0:T(8,128)(2,1)S(1)}, u32[]{:S(2)}, u32[]{:S(2)}) collective-permute-start(bf16[2,6,48,128]{3,2,1,0:T(8,128)(2,1)S(1)} %shard_map.151.refs_0_.own_ref.after_ref), channel_id=1, source_target_pairs={{0,4},{4,0},{8,12},{12,8},{1,5},{5,1},{9,13},{13,9},{2,6},{6,2},{1... | collective-permute-start | bytes 442376 | tf_op jit(solution)/shard_map/ppermute | solution.py:530
  23.5 7.0 %collective-permute-start.9 = (bf16[2,6,48,128]{3,2,1,0:T(8,128)(2,1)S(1)}, bf16[2,6,48,128]{3,2,1,0:T(8,128)(2,1)S(1)}, u32[]{:S(2)}, u32[]{:S(2)}) collective-permute-start(bf16[2,6,48,128]{3,2,1,0:T(8,128)(2,1)S(1)} %shard_map.151.refs_0_.own_ref.after_ref), channel_id=1, source_target_pairs={{0,8},{4,12},{8,0},{12,4},{1,9},{5,13},{9,1},{13,5},{2,10},{6,14},... | collective-permute-start | bytes 442376 | tf_op jit(solution)/shard_map/ppermute | solution.py:530
  27.8 5.9 %collective-permute-start.11 = (bf16[2,6,48,128]{3,2,1,0:T(8,128)(2,1)S(1)}, bf16[2,6,48,128]{3,2,1,0:T(8,128)(2,1)S(1)}, u32[]{:S(2)}, u32[]{:S(2)}) collective-permute-start(bf16[2,6,48,128]{3,2,1,0:T(8,128)(2,1)S(1)} %shard_map.154.own_ref), channel_id=1, source_target_pairs={{0,8},{4,12},{8,0},{12,4},{1,9},{5,13},{9,1},{13,5},{2,10},{6,14},... | collective-permute-start | bytes 442376 | tf_op jit(solution)/shard_map/ppermute | solution.py:530
  28.1 2.6 %collective-permute-start.8 = (bf16[2,6,48,128]{3,2,1,0:T(8,128)(2,1)S(1)}, bf16[2,6,48,128]{3,2,1,0:T(8,128)(2,1)S(1)}, u32[]{:S(2)}, u32[]{:S(2)}) collective-permute-start(bf16[2,6,48,128]{3,2,1,0:T(8,128)(2,1)S(1)} %shard_map.154.own_ref), channel_id=1, source_target_pairs={{0,4},{4,0},{8,12},{12,8},{1,5},{5,1},{9,13},{13,9},{2,6},{6,2},{1... | collective-permute-start | bytes 442376 | tf_op jit(solution)/shard_map/ppermute | solution.py:530
  30.4 3.4 %collective-permute-start.10 = (bf16[2,6,48,128]{3,2,1,0:T(8,128)(2,1)S(1)}, bf16[2,6,48,128]{3,2,1,0:T(8,128)(2,1)S(1)}, u32[]{:S(2)}, u32[]{:S(2)}) collective-permute-start(bf16[2,6,48,128]{3,2,1,0:T(8,128)(2,1)S(1)} %shard_map.156.own_ref), channel_id=1, source_target_pairs={{0,4},{4,0},{8,12},{12,8},{1,5},{5,1},{9,13},{13,9},{2,6},{6,2},{1... | collective-permute-start | bytes 442376 | tf_op jit(solution)/shard_map/ppermute | solution.py:530
  33.7 1.9 %copy-start.8 = (f32[96]{0:T(128)S(1)}, f32[96]{0:T(128)}, u32[]{:S(2)}) copy-start(f32[96]{0:T(128)} %bias_ref.7) | copy-start | bytes 1156
  33.7 1.9 %collective-permute-start.12 = (bf16[2,6,48,128]{3,2,1,0:T(8,128)(2,1)S(1)}, bf16[2,6,48,128]{3,2,1,0:T(8,128)(2,1)S(1)}, u32[]{:S(2)}, u32[]{:S(2)}) collective-permute-start(bf16[2,6,48,128]{3,2,1,0:T(8,128)(2,1)S(1)} %shard_map.158.own_ref), channel_id=1, source_target_pairs={{0,4},{4,0},{8,12},{12,8},{1,5},{5,1},{9,13},{13,9},{2,6},{6,2},{1... | collective-permute-start | bytes 442376 | tf_op jit(solution)/shard_map/ppermute | solution.py:530
  36.8 4.0 %collective-permute-start.15 = (bf16[288,128]{1,0:T(8,128)(2,1)S(1)}, bf16[288,128]{1,0:T(8,128)(2,1)S(1)}, u32[]{:S(2)}, u32[]{:S(2)}) collective-permute-start(bf16[288,128]{1,0:T(8,128)(2,1)S(1)} %get-tuple-element.18), channel_id=1, source_target_pairs={{0,12},{4,8},{8,4},{12,0},{1,13},{5,9},{9,5},{13,1},{2,14},{6,10},... | collective-permute-start | bytes 221192 | tf_op jit(solution)/shard_map/ppermute | solution.py:530
  37.5 5.5 %collective-permute-start.14 = (bf16[288,128]{1,0:T(8,128)(2,1)S(1)}, bf16[288,128]{1,0:T(8,128)(2,1)S(1)}, u32[]{:S(2)}, u32[]{:S(2)}) collective-permute-start(bf16[288,128]{1,0:T(8,128)(2,1)S(1)} %get-tuple-element.15.refs_0_), channel_id=1, source_target_pairs={{0,8},{4,12},{8,0},{12,4},{1,9},{5,13},{9,1},{13,5},{2,10},{6,14},... | collective-permute-start | bytes 221192 | tf_op jit(solution)/shard_map/ppermute | solution.py:530
  39.2 3.8 %copy-start.2 = (bf16[384,384]{1,0:T(8,128)(2,1)S(1)}, bf16[384,384]{1,0:T(8,128)(2,1)}, u32[]{:S(2)}) copy-start(bf16[384,384]{1,0:T(8,128)(2,1)} %wq_ref.1) | copy-start | bytes 884740
  39.2 3.8 %copy-start.3 = (bf16[384,384]{1,0:T(8,128)(2,1)S(1)}, bf16[384,384]{1,0:T(8,128)(2,1)}, u32[]{:S(2)}) copy-start(bf16[384,384]{1,0:T(8,128)(2,1)} %wk_ref.1) | copy-start | bytes 884740
  39.2 3.8 %copy-start.4 = (bf16[384,384]{1,0:T(8,128)(2,1)S(1)}, bf16[384,384]{1,0:T(8,128)(2,1)}, u32[]{:S(2)}) copy-start(bf16[384,384]{1,0:T(8,128)(2,1)} %wv_ref.1) | copy-start | bytes 884740
  39.2 3.8 %copy-start.5 = (bf16[384,384]{1,0:T(8,128)(2,1)S(1)}, bf16[384,384]{1,0:T(8,128)(2,1)}, u32[]{:S(2)}) copy-start(bf16[384,384]{1,0:T(8,128)(2,1)} %wo_ref.1) | copy-start | bytes 884740
  39.2 3.8 %collective-permute-start.13 = (bf16[288,128]{1,0:T(8,128)(2,1)S(1)}, bf16[288,128]{1,0:T(8,128)(2,1)S(1)}, u32[]{:S(2)}, u32[]{:S(2)}) collective-permute-start(bf16[288,128]{1,0:T(8,128)(2,1)S(1)} %get-tuple-element.17), channel_id=1, source_target_pairs={{0,4},{4,0},{8,12},{12,8},{1,5},{5,1},{9,13},{13,9},{2,6},{6,2},{1... | collective-permute-start | bytes 221192 | tf_op jit(solution)/shard_map/ppermute | solution.py:530

commit v12 on v11

--- a/solution.py
+++ b/solution.py
@@ -82,7 +82,8 @@
 
 
 def silu(value):
-    return value / (1.0 + jnp.exp(-value))
+    half = 0.5 * value
+    return half + half * jnp.tanh(half)
 
 
 def plane_block(x, count):

time: 45.5 us -> 45.4 us (level)
  no operation moved by 1% of the time
where the time goes in v12:
time: 45.4 us; the launch traced here: 45.2 us
  Pallas kernels  16.4 us (36%)
  starting transfers between devices  14.9 us (33%)
  waiting for transfers between devices  11.2 us (25%)
  local copies, waits for them, and re-layouts  1.6 us (4%)
  other arithmetic  0.86 us (2%)
    pallas_call x18, Pallas kernels, run(): pl.pallas_call(functools.partial(body, *axes), out_shape=outs, in_specs=[...  16.4 us
    ppermute x16, starting transfers between devices, swapped(): lax.ppermute(value, axis, [(i, partner(i)) for i in range(lax.axis_size(a...  14.9 us
    ppermute x16, waiting for transfers between devices, swapped(): lax.ppermute(value, axis, [(i, partner(i)) for i in range(lax.axis_size(a...  11.2 us
    unnamed x18, local copies, waits for them, and re-layouts  1.6 us
  transfers between devices with their start and end apart: 16, of which 7 were waited for; matrix products, arithmetic and copies ran while one was open for 2% of the time, Pallas kernels for 24%

profile of v12, /device:TPU:0, one launch (start us, length us, event | category | flops | bytes accessed | tf_op | source)
XLA Modules:
  0.0 45.2 jit_solution(3588233705981779168)
XLA Ops:
  0.0 5.0 %collective-permute-start.2 = (bf16[1,2,48,384]{3,2,1,0:T(8,128)(2,1)}, bf16[1,2,48,384]{3,2,1,0:T(8,128)(2,1)S(1)}, u32[]{:S(2)}, u32[]{:S(2)}) collective-permute-start(bf16[1,2,48,384]{3,2,1,0:T(8,128)(2,1)} %own_ref.1), channel_id=1, source_target_pairs={{0,3},{1,2},{2,1},{3,0},{4,7},{5,6},{6,5},{7,4},{8,11},{9,10},{10,... | collective-permute-start | bytes 221192 | tf_op jit(solution)/shard_map/ppermute | solution.py:531
  5.0 0.0 collective-permute-start.1
  5.1 0.6 %collective-permute-start = (bf16[1,2,48,384]{3,2,1,0:T(8,128)(2,1)}, bf16[1,2,48,384]{3,2,1,0:T(8,128)(2,1)S(1)}, u32[]{:S(2)}, u32[]{:S(2)}) collective-permute-start(bf16[1,2,48,384]{3,2,1,0:T(8,128)(2,1)} %own_ref.1), channel_id=1, source_target_pairs={{0,1},{1,0},{2,3},{3,2},{4,5},{5,4},{6,7},{7,6},{8,9},{9,8},{10,11... | collective-permute-start | bytes 221192 | tf_op jit(solution)/shard_map/ppermute | solution.py:531
  5.6 1.7 %collective-permute-start.3 = (bf16[1,2,48,384]{3,2,1,0:T(8,128)(2,1)}, bf16[1,2,48,384]{3,2,1,0:T(8,128)(2,1)S(1)}, u32[]{:S(2)}, u32[]{:S(2)}) collective-permute-start(bf16[1,2,48,384]{3,2,1,0:T(8,128)(2,1)} %own_ref.1), channel_id=1, source_target_pairs={{0,8},{4,12},{8,0},{12,4},{1,9},{5,13},{9,1},{13,5},{2,10},{6,14},... | collective-permute-start | bytes 221192 | tf_op jit(solution)/shard_map/ppermute | solution.py:531
  7.4 0.8 %select_select_fusion.table_ref = f32[8,384]{1,0:T(8,128)S(1)} fusion(f32[384]{0:T(512)} %param.16, f32[384]{0:T(512)} %param.17, f32[384]{0:T(512)} %param.20, f32[384]{0:T(512)} %param.21, f32[384]{0:T(512)} %param.24, f32[384]{0:T(512)} %param.25, pred[8]{0:T(512)(128)(4,1)S(1)} %get-tuple-element.19, pred[8]{0:T(512)(128)(4,1)S(1)} %get-tuple-element.20, ...), kind=kLoop, calls=%fused_computation | loop fusion | flops 18432 | bytes 21552 | tf_op jit(solution)/shard_map/jit(_where)/select_n | solution.py:572
  8.2 0.1 shard_map.146.groups_ref
  8.3 0.0 copy-start
  8.3 1.5 %copy-done = bf16[96,3,3,3,384]{4,0,3,2,1:T(8,128)(2,1)S(1)} copy-done((bf16[96,3,3,3,384]{4,0,3,2,1:T(8,128)(2,1)S(1)}, bf16[96,3,3,3,384]{4,0,3,2,1:T(8,128)(2,1)}, u32[]{:S(2)}) %copy-start) | copy-done | bytes 1990680
  9.8 0.2 shard_map.145.loaded_ref.w_ref
  10.1 1.4 %collective-permute-done.1.two_ref = bf16[1,2,48,384]{3,2,1,0:T(8,128)(2,1)S(1)} collective-permute-done((bf16[1,2,48,384]{3,2,1,0:T(8,128)(2,1)}, bf16[1,2,48,384]{3,2,1,0:T(8,128)(2,1)S(1)}, u32[]{:S(2)}, u32[]{:S(2)}) %collective-permute-start.1) | collective-permute-done | bytes 73760 | tf_op jit(solution)/shard_map/ppermute | solution.py:531
  11.5 0.7 %shard_map.147 = (bf16[1,8,48,384]{3,2,1,0:T(8,128)(2,1)S(1)}, bf16[8,48,384]{2,1,0:T(8,128)(2,1)S(1)}, bf16[3,2,48,384]{3,2,1,0:T(8,128)(2,1)S(1)}) custom-call(bf16[1,2,48,384]{3,2,1,0:T(8,128)(2,1)S(1)} %copy-done.6, bf16[1,2,48,384]{3,2,1,0:T(8,128)(2,1)S(1)} %collective-permute-done.one_ref, bf16[1,2,48,384]{3,2,1,0:T(8,128)(2,1)S(1)} %collective-permute-done.1.two_ref, ...), custom_call_target="tpu_custom_call" | custom-call | tf_op jit(solution)/shard_map/pallas_call | solution.py:31
  12.2 0.1 collective-permute-start.4
  12.2 1.6 %collective-permute-start.5 = (bf16[3,2,48,384]{3,2,1,0:T(8,128)(2,1)S(1)}, bf16[3,2,48,384]{3,2,1,0:T(8,128)(2,1)S(1)}, u32[]{:S(2)}, u32[]{:S(2)}) collective-permute-start(bf16[3,2,48,384]{3,2,1,0:T(8,128)(2,1)S(1)} %get-tuple-element.14), channel_id=1, source_target_pairs={{0,8},{4,12},{8,0},{12,4},{1,9},{5,13},{9,1},{13,5},{2,10},{6,14},... | collective-permute-start | bytes 663560 | tf_op jit(solution)/shard_map/ppermute | solution.py:531
  13.8 0.0 collective-permute-done.4.mate_ref
  13.8 2.8 %shard_map.148.after_ref.near_total_ref = f32[4,384,384]{2,1,0:T(8,128)S(1)} custom-call(bf16[1,8,48,384]{3,2,1,0:T(8,128)(2,1)S(1)} %get-tuple-element.13.own_ref, bf16[1,8,48,384]{3,2,1,0:T(8,128)(2,1)S(1)} %collective-permute-done.4.mate_ref, bf16[3,3,384,384]{3,2,1,0:T(8,128)(2,1)S(1)} %shard_map.145.loaded_ref.w_ref), custom_call_target="tpu_custom_call" | custom-call | tf_op jit(solution)/shard_map/pallas_call | solution.py:31
  16.6 3.5 %collective-permute-done.5.blocks_ref = bf16[3,2,48,384]{3,2,1,0:T(8,128)(2,1)S(1)} collective-permute-done((bf16[3,2,48,384]{3,2,1,0:T(8,128)(2,1)S(1)}, bf16[3,2,48,384]{3,2,1,0:T(8,128)(2,1)S(1)}, u32[]{:S(2)}, u32[]{:S(2)}) %collective-permute-start.5) | collective-permute-done | bytes 221216 | tf_op jit(solution)/shard_map/ppermute | solution.py:531
  20.1 0.6 %shard_map.149.a_ref = bf16[1,8,48,384]{3,2,1,0:T(8,128)(2,1)S(1)} custom-call(bf16[1,2,48,384]{3,2,1,0:T(8,128)(2,1)S(1)} %collective-permute-done.3.across_ref.own_ref, bf16[3,2,48,384]{3,2,1,0:T(8,128)(2,1)S(1)} %collective-permute-done.5.blocks_ref, f32[8,384]{1,0:T(8,128)S(1)} %select_select_fusion.table_ref, ...), custom_call_target="tpu_custom_call" | custom-call | tf_op jit(solution)/shard_map/pallas_call | solution.py:31
  20.7 0.0 copy-start.7
  20.7 0.1 collective-permute-start.6
  20.8 1.1 %shard_map.150.base_ref = f32[4,384,384]{2,1,0:T(8,128)S(1)} custom-call(f32[4,384,384]{2,1,0:T(8,128)S(1)} %shard_map.148.after_ref.near_total_ref, bf16[1,8,48,384]{3,2,1,0:T(8,128)(2,1)S(1)} %shard_map.149.a_ref, bf16[3,3,384,384]{3,2,1,0:T(8,128)(2,1)S(1)} %shard_map.145.loaded_ref.w_ref), custom_call_target="tpu_custom_call" | custom-call | tf_op jit(solution)/shard_map/pallas_call | solution.py:31
  21.9 0.5 %collective-permute-done.6.a_ref = bf16[1,8,48,384]{3,2,1,0:T(8,128)(2,1)S(1)} collective-permute-done((bf16[1,8,48,384]{3,2,1,0:T(8,128)(2,1)S(1)}, bf16[1,8,48,384]{3,2,1,0:T(8,128)(2,1)S(1)}, u32[]{:S(2)}, u32[]{:S(2)}) %collective-permute-start.6) | collective-permute-done | bytes 294944 | tf_op jit(solution)/shard_map/ppermute | solution.py:531
  22.4 0.8 %shard_map.151.refs_0_.own_ref.after_ref = bf16[2,6,48,128]{3,2,1,0:T(8,128)(2,1)S(1)} custom-call(f32[4,384,384]{2,1,0:T(8,128)S(1)} %shard_map.150.base_ref, bf16[1,8,48,384]{3,2,1,0:T(8,128)(2,1)S(1)} %collective-permute-done.6.a_ref, bf16[3,3,384,384]{3,2,1,0:T(8,128)(2,1)S(1)} %shard_map.145.loaded_ref.w_ref, f32[96]{0:T(128)S(1)} %copy-done.7, ...), custom_call_target="tpu_custom_call" | custom-call | tf_op jit(solution)/shard_map/pallas_call | solution.py:31
  23.2 0.0 copy-start.1
  23.2 0.2 collective-permute-start.7
  23.4 2.7 %collective-permute-start.9 = (bf16[2,6,48,128]{3,2,1,0:T(8,128)(2,1)S(1)}, bf16[2,6,48,128]{3,2,1,0:T(8,128)(2,1)S(1)}, u32[]{:S(2)}, u32[]{:S(2)}) collective-permute-start(bf16[2,6,48,128]{3,2,1,0:T(8,128)(2,1)S(1)} %shard_map.151.refs_0_.own_ref.after_ref), channel_id=1, source_target_pairs={{0,8},{4,12},{8,0},{12,4},{1,9},{5,13},{9,1},{13,5},{2,10},{6,14},... | collective-permute-start | bytes 442376 | tf_op jit(solution)/shard_map/ppermute | solution.py:531
  26.1 1.6 %shard_map.154.own_ref = bf16[2,6,48,128]{3,2,1,0:T(8,128)(2,1)S(1)} custom-call(f32[4,384,384]{2,1,0:T(8,128)S(1)} %shard_map.150.base_ref, bf16[1,8,48,384]{3,2,1,0:T(8,128)(2,1)S(1)} %collective-permute-done.6.a_ref, bf16[3,3,384,384]{3,2,1,0:T(8,128)(2,1)S(1)} %shard_map.145.loaded_ref.w_ref, f32[96]{0:T(128)S(1)} %copy-done.7, ...), custom_call_target="tpu_custom_call" | custom-call | tf_op jit(solution)/shard_map/pallas_call | solution.py:31
  27.8 0.3 collective-permute-start.11
  28.1 0.2 shard_map.152.w_ref
  28.3 1.7 %shard_map.153.base_ref.after_ref = f32[4,384,384]{2,1,0:T(8,128)S(1)} custom-call(bf16[2,6,48,128]{3,2,1,0:T(8,128)(2,1)S(1)} %shard_map.151.refs_0_.own_ref.after_ref, bf16[2,6,48,128]{3,2,1,0:T(8,128)(2,1)S(1)} %collective-permute-done.7.mate_ref, bf16[3,3,384,384]{3,2,1,0:T(8,128)(2,1)S(1)} %shard_map.152.w_ref), custom_call_target="tpu_custom_call" | custom-call | tf_op jit(solution)/shard_map/pallas_call | solution.py:31
  30.1 0.3 collective-permute-done.9.x_ref
  30.4 0.3 collective-permute-start.10
  30.7 1.1 %shard_map.155.base_ref.after_ref = f32[4,384,384]{2,1,0:T(8,128)S(1)} custom-call(f32[4,384,384]{2,1,0:T(8,128)S(1)} %shard_map.153.base_ref.after_ref, bf16[2,6,48,128]{3,2,1,0:T(8,128)(2,1)S(1)} %shard_map.154.own_ref, bf16[2,6,48,128]{3,2,1,0:T(8,128)(2,1)S(1)} %collective-permute-done.8.mate_ref, bf16[3,3,384,384]{3,2,1,0:T(8,128)(2,1)S(1)} %shard_map.152.w_ref), custom_call_target="tpu_custom_call" | custom-call | tf_op jit(solution)/shard_map/pallas_call | solution.py:31
  31.8 1.9 %collective-permute-done.11.x_ref = bf16[2,6,48,128]{3,2,1,0:T(8,128)(2,1)S(1)} collective-permute-done((bf16[2,6,48,128]{3,2,1,0:T(8,128)(2,1)S(1)}, bf16[2,6,48,128]{3,2,1,0:T(8,128)(2,1)S(1)}, u32[]{:S(2)}, u32[]{:S(2)}) %collective-permute-start.11) | collective-permute-done | bytes 147488 | tf_op jit(solution)/shard_map/ppermute | solution.py:531
  33.6 0.0 copy-start.8
  33.7 0.1 collective-permute-start.12
  33.7 1.8 %shard_map.157.base_ref = f32[4,384,384]{2,1,0:T(8,128)S(1)} custom-call(f32[4,384,384]{2,1,0:T(8,128)S(1)} %shard_map.155.base_ref.after_ref, bf16[2,6,48,128]{3,2,1,0:T(8,128)(2,1)S(1)} %shard_map.156.own_ref, bf16[2,6,48,128]{3,2,1,0:T(8,128)(2,1)S(1)} %collective-permute-done.10.mate_ref, bf16[3,3,384,384]{3,2,1,0:T(8,128)(2,1)S(1)} %shard_map.152.w_ref), custom_call_target="tpu_custom_call" | custom-call | tf_op jit(solution)/shard_map/pallas_call | solution.py:31
  35.5 1.2 %shard_map.159 = (bf16[288,128]{1,0:T(8,128)(2,1)S(1)}, bf16[288,128]{1,0:T(8,128)(2,1)S(1)}) custom-call(f32[4,384,384]{2,1,0:T(8,128)S(1)} %shard_map.157.base_ref, bf16[2,6,48,128]{3,2,1,0:T(8,128)(2,1)S(1)} %shard_map.158.own_ref, bf16[2,6,48,128]{3,2,1,0:T(8,128)(2,1)S(1)} %collective-permute-done.12.mate_ref, ...), custom_call_target="tpu_custom_call" | custom-call | tf_op jit(solution)/shard_map/pallas_call | solution.py:31
  36.7 0.7 %collective-permute-start.15 = (bf16[288,128]{1,0:T(8,128)(2,1)S(1)}, bf16[288,128]{1,0:T(8,128)(2,1)S(1)}, u32[]{:S(2)}, u32[]{:S(2)}) collective-permute-start(bf16[288,128]{1,0:T(8,128)(2,1)S(1)} %get-tuple-element.18), channel_id=1, source_target_pairs={{0,12},{4,8},{8,4},{12,0},{1,13},{5,9},{9,5},{13,1},{2,14},{6,10},... | collective-permute-start | bytes 221192 | tf_op jit(solution)/shard_map/ppermute | solution.py:531
  37.4 1.4 %collective-permute-start.14 = (bf16[288,128]{1,0:T(8,128)(2,1)S(1)}, bf16[288,128]{1,0:T(8,128)(2,1)S(1)}, u32[]{:S(2)}, u32[]{:S(2)}) collective-permute-start(bf16[288,128]{1,0:T(8,128)(2,1)S(1)} %get-tuple-element.15.refs_0_), channel_id=1, source_target_pairs={{0,8},{4,12},{8,0},{12,4},{1,9},{5,13},{9,1},{13,5},{2,10},{6,14},... | collective-permute-start | bytes 221192 | tf_op jit(solution)/shard_map/ppermute | solution.py:531
  38.9 0.2 shard_map.160
  39.1 0.0 copy-start.2
  39.1 0.0 copy-start.3
  39.1 0.0 copy-start.4
  39.2 0.0 copy-start.5
  39.2 0.1 collective-permute-start.13
  39.3 1.5 %collective-permute-done.15.after_ref.p3 = bf16[288,128]{1,0:T(8,128)(2,1)S(1)} collective-permute-done((bf16[288,128]{1,0:T(8,128)(2,1)S(1)}, bf16[288,128]{1,0:T(8,128)(2,1)S(1)}, u32[]{:S(2)}, u32[]{:S(2)}) %collective-permute-start.15) | collective-permute-done | bytes 73760 | tf_op jit(solution)/shard_map/ppermute | solution.py:531
  40.7 2.2 %collective-permute-done.14.x_ref = bf16[288,128]{1,0:T(8,128)(2,1)S(1)} collective-permute-done((bf16[288,128]{1,0:T(8,128)(2,1)S(1)}, bf16[288,128]{1,0:T(8,128)(2,1)S(1)}, u32[]{:S(2)}, u32[]{:S(2)}) %collective-permute-start.14) | collective-permute-done | bytes 73760 | tf_op jit(solution)/shard_map/ppermute | solution.py:531
  43.0 2.3 %shard_map.162 = bf16[96,384]{1,0:T(8,128)(2,1)} custom-call(bf16[8,48,384]{2,1,0:T(8,128)(2,1)S(1)} %get-tuple-element.12.raw_ref, bf16[288,128]{1,0:T(8,128)(2,1)S(1)} %get-tuple-element.16.p0, bf16[288,128]{1,0:T(8,128)(2,1)S(1)} %collective-permute-done.13.p1, bf16[288,128]{1,0:T(8,128)(2,1)S(1)} %shard_map.161.p2, ...), custom_call_target="tpu_custom_call" | custom-call | tf_op jit(solution)/shard_map/pallas_call | solution.py:31
  (24 shorter events, 0.1 us)
Async XLA Ops:
  0.0 10.1 %collective-permute-start.2 = (bf16[1,2,48,384]{3,2,1,0:T(8,128)(2,1)}, bf16[1,2,48,384]{3,2,1,0:T(8,128)(2,1)S(1)}, u32[]{:S(2)}, u32[]{:S(2)}) collective-permute-start(bf16[1,2,48,384]{3,2,1,0:T(8,128)(2,1)} %own_ref.1), channel_id=1, source_target_pairs={{0,3},{1,2},{2,1},{3,0},{4,7},{5,6},{6,5},{7,4},{8,11},{9,10},{10,... | collective-permute-start | bytes 221192 | tf_op jit(solution)/shard_map/ppermute | solution.py:531
  5.0 6.4 %collective-permute-start.1 = (bf16[1,2,48,384]{3,2,1,0:T(8,128)(2,1)}, bf16[1,2,48,384]{3,2,1,0:T(8,128)(2,1)S(1)}, u32[]{:S(2)}, u32[]{:S(2)}) collective-permute-start(bf16[1,2,48,384]{3,2,1,0:T(8,128)(2,1)} %own_ref.1), channel_id=1, source_target_pairs={{0,2},{1,3},{2,0},{3,1},{4,6},{5,7},{6,4},{7,5},{8,10},{9,11},{10,... | collective-permute-start | bytes 221192 | tf_op jit(solution)/shard_map/ppermute | solution.py:531
  5.1 6.4 %collective-permute-start = (bf16[1,2,48,384]{3,2,1,0:T(8,128)(2,1)}, bf16[1,2,48,384]{3,2,1,0:T(8,128)(2,1)S(1)}, u32[]{:S(2)}, u32[]{:S(2)}) collective-permute-start(bf16[1,2,48,384]{3,2,1,0:T(8,128)(2,1)} %own_ref.1), channel_id=1, source_target_pairs={{0,1},{1,0},{2,3},{3,2},{4,5},{5,4},{6,7},{7,6},{8,9},{9,8},{10,11... | collective-permute-start | bytes 221192 | tf_op jit(solution)/shard_map/ppermute | solution.py:531
  5.6 5.9 %collective-permute-start.3 = (bf16[1,2,48,384]{3,2,1,0:T(8,128)(2,1)}, bf16[1,2,48,384]{3,2,1,0:T(8,128)(2,1)S(1)}, u32[]{:S(2)}, u32[]{:S(2)}) collective-permute-start(bf16[1,2,48,384]{3,2,1,0:T(8,128)(2,1)} %own_ref.1), channel_id=1, source_target_pairs={{0,8},{4,12},{8,0},{12,4},{1,9},{5,13},{9,1},{13,5},{2,10},{6,14},... | collective-permute-start | bytes 221192 | tf_op jit(solution)/shard_map/ppermute | solution.py:531
  8.3 1.6 %copy-start = (bf16[96,3,3,3,384]{4,0,3,2,1:T(8,128)(2,1)S(1)}, bf16[96,3,3,3,384]{4,0,3,2,1:T(8,128)(2,1)}, u32[]{:S(2)}) copy-start(bf16[96,3,3,3,384]{4,0,3,2,1:T(8,128)(2,1)} %param.18) | copy-start | bytes 5971972
  9.8 1.6 %copy-start.6 = (bf16[1,2,48,384]{3,2,1,0:T(8,128)(2,1)S(1)}, bf16[1,2,48,384]{3,2,1,0:T(8,128)(2,1)}, u32[]{:S(2)}) copy-start(bf16[1,2,48,384]{3,2,1,0:T(8,128)(2,1)} %own_ref.1) | copy-start | bytes 221188
  12.2 1.6 %collective-permute-start.4 = (bf16[1,8,48,384]{3,2,1,0:T(8,128)(2,1)S(1)}, bf16[1,8,48,384]{3,2,1,0:T(8,128)(2,1)S(1)}, u32[]{:S(2)}, u32[]{:S(2)}) collective-permute-start(bf16[1,8,48,384]{3,2,1,0:T(8,128)(2,1)S(1)} %get-tuple-element.13.own_ref), channel_id=1, source_target_pairs={{0,4},{4,0},{8,12},{12,8},{1,5},{5,1},{9,13},{13,9},{2,6},{6,2},{1... | collective-permute-start | bytes 884744 | tf_op jit(solution)/shard_map/ppermute | solution.py:531
  12.2 7.8 %collective-permute-start.5 = (bf16[3,2,48,384]{3,2,1,0:T(8,128)(2,1)S(1)}, bf16[3,2,48,384]{3,2,1,0:T(8,128)(2,1)S(1)}, u32[]{:S(2)}, u32[]{:S(2)}) collective-permute-start(bf16[3,2,48,384]{3,2,1,0:T(8,128)(2,1)S(1)} %get-tuple-element.14), channel_id=1, source_target_pairs={{0,8},{4,12},{8,0},{12,4},{1,9},{5,13},{9,1},{13,5},{2,10},{6,14},... | collective-permute-start | bytes 663560 | tf_op jit(solution)/shard_map/ppermute | solution.py:531
  20.7 1.7 %copy-start.7 = (f32[96]{0:T(128)S(1)}, f32[96]{0:T(128)}, u32[]{:S(2)}) copy-start(f32[96]{0:T(128)} %bias_ref.5) | copy-start | bytes 1156
  20.7 1.6 %collective-permute-start.6 = (bf16[1,8,48,384]{3,2,1,0:T(8,128)(2,1)S(1)}, bf16[1,8,48,384]{3,2,1,0:T(8,128)(2,1)S(1)}, u32[]{:S(2)}, u32[]{:S(2)}) collective-permute-start(bf16[1,8,48,384]{3,2,1,0:T(8,128)(2,1)S(1)} %shard_map.149.a_ref), channel_id=1, source_target_pairs={{0,4},{4,0},{8,12},{12,8},{1,5},{5,1},{9,13},{13,9},{2,6},{6,2},{1... | collective-permute-start | bytes 884744 | tf_op jit(solution)/shard_map/ppermute | solution.py:531
  23.2 4.9 %copy-start.1 = (bf16[96,3,3,3,384]{4,0,3,2,1:T(8,128)(2,1)S(1)}, bf16[96,3,3,3,384]{4,0,3,2,1:T(8,128)(2,1)}, u32[]{:S(2)}) copy-start(bf16[96,3,3,3,384]{4,0,3,2,1:T(8,128)(2,1)} %param.22) | copy-start | bytes 5971972
  23.2 5.1 %collective-permute-start.7 = (bf16[2,6,48,128]{3,2,1,0:T(8,128)(2,1)S(1)}, bf16[2,6,48,128]{3,2,1,0:T(8,128)(2,1)S(1)}, u32[]{:S(2)}, u32[]{:S(2)}) collective-permute-start(bf16[2,6,48,128]{3,2,1,0:T(8,128)(2,1)S(1)} %shard_map.151.refs_0_.own_ref.after_ref), channel_id=1, source_target_pairs={{0,4},{4,0},{8,12},{12,8},{1,5},{5,1},{9,13},{13,9},{2,6},{6,2},{1... | collective-permute-start | bytes 442376 | tf_op jit(solution)/shard_map/ppermute | solution.py:531
  23.4 6.9 %collective-permute-start.9 = (bf16[2,6,48,128]{3,2,1,0:T(8,128)(2,1)S(1)}, bf16[2,6,48,128]{3,2,1,0:T(8,128)(2,1)S(1)}, u32[]{:S(2)}, u32[]{:S(2)}) collective-permute-start(bf16[2,6,48,128]{3,2,1,0:T(8,128)(2,1)S(1)} %shard_map.151.refs_0_.own_ref.after_ref), channel_id=1, source_target_pairs={{0,8},{4,12},{8,0},{12,4},{1,9},{5,13},{9,1},{13,5},{2,10},{6,14},... | collective-permute-start | bytes 442376 | tf_op jit(solution)/shard_map/ppermute | solution.py:531
  27.8 5.9 %collective-permute-start.11 = (bf16[2,6,48,128]{3,2,1,0:T(8,128)(2,1)S(1)}, bf16[2,6,48,128]{3,2,1,0:T(8,128)(2,1)S(1)}, u32[]{:S(2)}, u32[]{:S(2)}) collective-permute-start(bf16[2,6,48,128]{3,2,1,0:T(8,128)(2,1)S(1)} %shard_map.154.own_ref), channel_id=1, source_target_pairs={{0,8},{4,12},{8,0},{12,4},{1,9},{5,13},{9,1},{13,5},{2,10},{6,14},... | collective-permute-start | bytes 442376 | tf_op jit(solution)/shard_map/ppermute | solution.py:531
  28.1 2.6 %collective-permute-start.8 = (bf16[2,6,48,128]{3,2,1,0:T(8,128)(2,1)S(1)}, bf16[2,6,48,128]{3,2,1,0:T(8,128)(2,1)S(1)}, u32[]{:S(2)}, u32[]{:S(2)}) collective-permute-start(bf16[2,6,48,128]{3,2,1,0:T(8,128)(2,1)S(1)} %shard_map.154.own_ref), channel_id=1, source_target_pairs={{0,4},{4,0},{8,12},{12,8},{1,5},{5,1},{9,13},{13,9},{2,6},{6,2},{1... | collective-permute-start | bytes 442376 | tf_op jit(solution)/shard_map/ppermute | solution.py:531
  30.4 3.4 %collective-permute-start.10 = (bf16[2,6,48,128]{3,2,1,0:T(8,128)(2,1)S(1)}, bf16[2,6,48,128]{3,2,1,0:T(8,128)(2,1)S(1)}, u32[]{:S(2)}, u32[]{:S(2)}) collective-permute-start(bf16[2,6,48,128]{3,2,1,0:T(8,128)(2,1)S(1)} %shard_map.156.own_ref), channel_id=1, source_target_pairs={{0,4},{4,0},{8,12},{12,8},{1,5},{5,1},{9,13},{13,9},{2,6},{6,2},{1... | collective-permute-start | bytes 442376 | tf_op jit(solution)/shard_map/ppermute | solution.py:531
  33.6 1.9 %copy-start.8 = (f32[96]{0:T(128)S(1)}, f32[96]{0:T(128)}, u32[]{:S(2)}) copy-start(f32[96]{0:T(128)} %bias_ref.7) | copy-start | bytes 1156
  33.7 1.9 %collective-permute-start.12 = (bf16[2,6,48,128]{3,2,1,0:T(8,128)(2,1)S(1)}, bf16[2,6,48,128]{3,2,1,0:T(8,128)(2,1)S(1)}, u32[]{:S(2)}, u32[]{:S(2)}) collective-permute-start(bf16[2,6,48,128]{3,2,1,0:T(8,128)(2,1)S(1)} %shard_map.158.own_ref), channel_id=1, source_target_pairs={{0,4},{4,0},{8,12},{12,8},{1,5},{5,1},{9,13},{13,9},{2,6},{6,2},{1... | collective-permute-start | bytes 442376 | tf_op jit(solution)/shard_map/ppermute | solution.py:531
  36.7 4.0 %collective-permute-start.15 = (bf16[288,128]{1,0:T(8,128)(2,1)S(1)}, bf16[288,128]{1,0:T(8,128)(2,1)S(1)}, u32[]{:S(2)}, u32[]{:S(2)}) collective-permute-start(bf16[288,128]{1,0:T(8,128)(2,1)S(1)} %get-tuple-element.18), channel_id=1, source_target_pairs={{0,12},{4,8},{8,4},{12,0},{1,13},{5,9},{9,5},{13,1},{2,14},{6,10},... | collective-permute-start | bytes 221192 | tf_op jit(solution)/shard_map/ppermute | solution.py:531
  37.4 5.5 %collective-permute-start.14 = (bf16[288,128]{1,0:T(8,128)(2,1)S(1)}, bf16[288,128]{1,0:T(8,128)(2,1)S(1)}, u32[]{:S(2)}, u32[]{:S(2)}) collective-permute-start(bf16[288,128]{1,0:T(8,128)(2,1)S(1)} %get-tuple-element.15.refs_0_), channel_id=1, source_target_pairs={{0,8},{4,12},{8,0},{12,4},{1,9},{5,13},{9,1},{13,5},{2,10},{6,14},... | collective-permute-start | bytes 221192 | tf_op jit(solution)/shard_map/ppermute | solution.py:531
  39.1 3.8 %copy-start.2 = (bf16[384,384]{1,0:T(8,128)(2,1)S(1)}, bf16[384,384]{1,0:T(8,128)(2,1)}, u32[]{:S(2)}) copy-start(bf16[384,384]{1,0:T(8,128)(2,1)} %wq_ref.1) | copy-start | bytes 884740
  39.1 3.8 %copy-start.3 = (bf16[384,384]{1,0:T(8,128)(2,1)S(1)}, bf16[384,384]{1,0:T(8,128)(2,1)}, u32[]{:S(2)}) copy-start(bf16[384,384]{1,0:T(8,128)(2,1)} %wk_ref.1) | copy-start | bytes 884740
  39.1 3.8 %copy-start.4 = (bf16[384,384]{1,0:T(8,128)(2,1)S(1)}, bf16[384,384]{1,0:T(8,128)(2,1)}, u32[]{:S(2)}) copy-start(bf16[384,384]{1,0:T(8,128)(2,1)} %wv_ref.1) | copy-start | bytes 884740
  39.2 3.8 %copy-start.5 = (bf16[384,384]{1,0:T(8,128)(2,1)S(1)}, bf16[384,384]{1,0:T(8,128)(2,1)}, u32[]{:S(2)}) copy-start(bf16[384,384]{1,0:T(8,128)(2,1)} %wo_ref.1) | copy-start | bytes 884740
  39.2 3.8 %collective-permute-start.13 = (bf16[288,128]{1,0:T(8,128)(2,1)S(1)}, bf16[288,128]{1,0:T(8,128)(2,1)S(1)}, u32[]{:S(2)}, u32[]{:S(2)}) collective-permute-start(bf16[288,128]{1,0:T(8,128)(2,1)S(1)} %get-tuple-element.17), channel_id=1, source_target_pairs={{0,4},{4,0},{8,12},{12,8},{1,5},{5,1},{9,13},{13,9},{2,6},{6,2},{1... | collective-permute-start | bytes 221192 | tf_op jit(solution)/shard_map/ppermute | solution.py:531
